TPU v7x, 32 devices: a whole 2x2x4 slice. The times are simulated.
32 devices in a mesh: dom: 8 (over z, core), sub: 4 (over y, x).
Axes of the slice: x: 2, y: 2, z: 4, core: 2. Of those that a mesh axis runs over, the one named last changes fastest.
Arguments:
- coupling: bfloat16 [256, 6, 128, 128], P(('dom', 'sub')), may hold values from -0.25 to 0.25
- diag_inv: bfloat16 [256, 128, 128], P(('dom', 'sub')), may hold values from -0.5 to 0.5
- rhs: float32 [256, 64, 128], P(('dom', 'sub')), may hold values from -6 to 6
- color: int32 [256], P(('dom', 'sub')), may hold values from 0 to 3, as said below
- local_target: int32 [256, 2], P(('dom', 'sub')), may hold values from 0 to 7, as said below
- group_peer: int32 [256, 2], P(('dom', 'sub')), may hold values from 0 to 3, as said below
- group_list: int32 [32, 4, 4], P(('dom', 'sub')), may hold values from -1 to 7, as said below
- dom_target: int32 [256, 2], P(('dom', 'sub')), may hold values from 0 to 7, as said below
Outputs:
- solution: float32 [256, 64, 128], P(('dom', 'sub'))
- defect: float32 [256, 64, 128], P(('dom', 'sub'))
Inputs may be any that keep to these rules, and one draw needn't show every extreme that they name: Each partition window of 8 consecutive block rows holds exactly a quarter of its rows of each color. `local_target`: A row of another color than row i, in the same partition window. `group_peer`: never the row's own member of the group; the two entries of a row differ. `group_list`: entry [p, c, q] is the local index on member q of p's group of a row of another color than c that receives all of p's color-c couplings to q, and -1 where p has none; a partition sends at most one row's sum to each member in a color. `dom_target`: groups form a cycle; the row reached is always of another color than row i.
All inputs are finite; a program needn't handle non-finite values.
Results may differ from a plain program's by a relative error of at most 0.012.
Values sent between devices are 32-bit elements; how exact they have to be, the bound alone decides.
No kernel may reach another device: no remote copies, remote signals or barrier semaphores. Data moves between devices by JAX's collectives and lax.ppermute only.
A program may use at most 64 MiB of HBM per device.

v0:
```python
import jax
import jax.numpy as jnp
from jax import lax
from jax.sharding import PartitionSpec as P

COLORS = 4
SWEEPS = 2
COUPLINGS = 6


def extended(value, sides, width):
    for axis, dim in sides:
        devices, length = (lax.axis_size(axis), value.shape[dim])
        up = [(i, (i + 1) % devices) for i in range(devices)]
        down = [(j, i) for i, j in up]
        last = lax.slice_in_dim(value, length - width, length, axis=dim)
        first = lax.slice_in_dim(value, 0, width, axis=dim)
        before = lax.ppermute(last, axis, up)
        after = lax.ppermute(first, axis, down)
        value = jnp.concatenate([before, value, after], axis=dim)
    return value


def on_device(coupling, diag_inv, rhs, color, local_target, group_peer, group_list, dom_target):
    rows_dev, rhs_count, block_width = rhs.shape
    quarter = rows_dev // COLORS
    group_size = lax.axis_size("sub")
    own_member = lax.axis_index("sub")
    members = jnp.arange(group_size, dtype=jnp.int32)
    order_flat = jnp.argsort(color, stable=True)
    rank_of = jnp.argsort(order_flat)
    by_color = order_flat.reshape(COLORS, quarter)
    peer_by = group_peer[by_color]
    local_by = local_target[by_color]
    dom_by = dom_target[by_color]
    sorted_coupling = coupling[order_flat].reshape(
        COLORS, quarter, COUPLINGS, block_width, block_width
    )
    local_tiles = sorted_coupling[:, :, 0:2]
    group_tiles = sorted_coupling[:, :, 2:4]
    cycle_tiles = jnp.stack([sorted_coupling[:, :, 5], sorted_coupling[:, :, 4]], axis=1)
    diag_sorted = diag_inv[order_flat].reshape(COLORS, quarter, block_width, block_width)
    rhs_sorted = rhs[order_flat]
    dom_table = jnp.stack([dom_by[:, :, 1], dom_by[:, :, 0]])
    dom_lists = extended(dom_table, (("dom", 0),), 1)
    from_below = dom_lists[0]
    from_above = dom_lists[3]
    table_rows = jnp.sum(
        jnp.where(peer_by[..., None] == members, group_list[0][:, None, None, :], 0), axis=-1
    )
    gathered_peers, gathered_rows = (
        lax.all_gather(peer_by[None], "sub", axis=0, tiled=True),
        lax.all_gather(table_rows[None], "sub", axis=0, tiled=True),
    )
    solution = jnp.zeros(rhs.shape, jnp.float32).reshape(COLORS, quarter, rhs_count, block_width)
    coupled = jnp.zeros(rhs.shape, jnp.float32)
    for sweep_no in range(SWEEPS):
        for color_now in range(COLORS):
            start_row = color_now * quarter
            current = coupled[start_row : start_row + quarter]
            update_in = (rhs_sorted[start_row : start_row + quarter] - current).astype(jnp.bfloat16)
            updated = jnp.einsum(
                "prb,pbe->pre",
                update_in,
                diag_sorted[color_now],
                preferred_element_type=jnp.float32,
            )
            change = (updated - solution[color_now]).astype(jnp.bfloat16)
            solution = solution.at[color_now].set(updated)
            local_items = jnp.einsum(
                "prb,pkbe->pkre", change, local_tiles[color_now], preferred_element_type=jnp.float32
            ).reshape(2 * quarter, rhs_count * block_width)
            group_terms = jnp.einsum(
                "prb,pkbe->pkre", change, group_tiles[color_now], preferred_element_type=jnp.float32
            ).reshape(2 * quarter, rhs_count * block_width)
            dom_send = jnp.einsum(
                "prb,kpbe->kpre", change, cycle_tiles[color_now], preferred_element_type=jnp.float32
            )
            local_sel = local_by[color_now].reshape(-1)[None, :] == order_flat[:, None]
            arrived = lax.all_gather(
                group_terms.reshape(2 * quarter, rhs_count, block_width), "sub", axis=0, tiled=True
            )
            group_items = arrived.reshape(-1, rhs_count * block_width)
            matches = gathered_peers[:, color_now].reshape(-1) == own_member
            group_sel = (
                gathered_rows[:, color_now].reshape(-1)[None, :] == order_flat[:, None]
            ) & matches[None, :]
            dom_got = extended(dom_send, (("dom", 0),), 1)
            dom_items = jnp.concatenate([dom_got[0], dom_got[3]], axis=0).reshape(
                2 * quarter, rhs_count * block_width
            )
            dom_rows = jnp.concatenate([from_below[color_now], from_above[color_now]], axis=0)
            dom_sel = dom_rows[None, :] == order_flat[:, None]
            selector = jnp.concatenate([local_sel, group_sel, dom_sel], axis=1).astype(jnp.float32)
            arrived_items = jnp.concatenate([local_items, group_items, dom_items], axis=0)
            added = jnp.dot(selector, arrived_items, precision=lax.Precision.HIGHEST)
            coupled = coupled + added.reshape(rows_dev, rhs_count, block_width)
    solution_rows = solution.reshape(rows_dev, rhs_count, block_width)[rank_of]
    defect_rows = (rhs_sorted - coupled)[rank_of]
    return (solution_rows, defect_rows)


def solution(mesh):
    placed = (
        P(("dom", "sub"), None, None, None),
        P(("dom", "sub"), None, None),
        P(("dom", "sub"), None, None),
        P(("dom", "sub")),
        P(("dom", "sub"), None),
        P(("dom", "sub"), None),
        P(("dom", "sub"), None, None),
        P(("dom", "sub"), None),
    )
    return jax.shard_map(
        on_device,
        mesh=mesh,
        in_specs=placed,
        out_specs=(P(("dom", "sub"), None, None), P(("dom", "sub"), None, None)),
        check_vma=False,
    )
```

profile of v0, /device:TPU:0, one launch (start us, length us, event | category | flops | bytes accessed | tf_op | source)
XLA Modules:
  0.0 155.8 jit_solution(6745032428418543364)
XLA Ops:
  0.7 1.7 %sort.34 = (s32[8]{0:T(128)}, s32[8]{0:T(128)S(1)}) sort(s32[8]{0:T(128)} %param.27, s32[8]{0:T(128)S(1)} %iota.12), dimensions={0}, to_apply=%region_0.0 | sort | flops 24 | bytes 128 | tf_op jit(solution)/shard_map/jit(argsort)/sort | solution.py:30
  2.6 0.8 copy.130
  3.3 0.6 gather_fusion.4
  4.6 4.0 %collective-permute-start.1 = (s32[1,4,2]{1,2,0:T(2,128)S(1)}, s32[1,4,2]{1,2,0:T(2,128)S(1)}, u32[]{:S(2)}, u32[]{:S(2)}) collective-permute-start(s32[1,4,2]{1,2,0:T(2,128)S(1)} %bitcast.566), channel_id=1, source_target_pairs={{4,0},{8,4},{12,8},{16,12},{20,16},{24,20},{28,24},{0,28},{5,1},{9... | collective-permute-start | bytes 104 | tf_op jit(solution)/shard_map/ppermute | solution.py:19
  8.6 1.0 sort.35
  9.6 0.9 gather_fusion.5
  10.5 0.8 slice_bitcast_fusion
  11.3 1.5 gather_fusion
  12.9 2.2 %gather_fusion.1 = bf16[8,128,128]{2,1,0:T(8,128)(2,1)} fusion(bf16[8,128,128]{2,1,0:T(8,128)(2,1)} %param.25, s32[1024]{0:T(1024)S(1)} %pad_clamp_fusion.2), kind=kCustom, calls=%fused_computation.1 | custom fusion | bytes 524320 | tf_op jit(solution)/shard_map/gather | solution.py:42
  15.1 1.8 %fusion.64 = (bf16[2,2,128,128]{3,2,1,0:T(8,128)(2,1)}, bf16[2,2,128,128]{3,2,1,0:T(8,128)(2,1)S(1)}, bf16[2,2,128,128]{3,2,1,0:T(8,128)(2,1)}, bf16[2,2,128,128]{3,2,1,0:T(8,128)(2,1)}) fusion(bf16[4,1,2,128,128]{4,3,2,0,1:T(8,128)(2,1)} %get-tuple-element.110, bf16[4,1,2,128,128]{4,3,2,0,1:T(8,128)(2,1)} %get-tuple-element.111), kind=kLoop, calls=%fused_computation.113 | loop fusion | flops 262144 | bytes 1048576 | tf_op jit(solution)/shard_map/squeeze | solution.py:77
  16.9 1.0 fusion.122
  18.1 0.7 fusion.164
  18.8 0.7 collective-permute-start.3
  19.5 0.6 gather_fusion.3
  20.1 8.5 %all-gather.1 = s32[16,2,2]{2,1,0:T(2,128)S(1)} all-gather(s32[4,2,2]{2,1,0:T(2,128)S(1)} %bitcast.562), channel_id=3, replica_groups=mesh['dom'=8,'sub'=4] {'sub'}, dimensions={0}, use_global_device_ids=true | all-gather | bytes 320 | tf_op jit(solution)/shard_map/all_gather | solution.py:52
  28.7 0.8 fusion.67
  29.5 0.8 fusion.65
  30.4 0.6 gather_fusion.2
  31.2 0.6 eq.148
  33.4 8.1 %all-gather = s32[16,2,2]{2,1,0:T(2,128)S(1)} all-gather(s32[4,2,2]{2,1,0:T(2,128)S(1)} %copy.123), channel_id=2, replica_groups=mesh['dom'=8,'sub'=4] {'sub'}, dimensions={0}, use_global_device_ids=true | all-gather | bytes 320 | tf_op jit(solution)/shard_map/all_gather | solution.py:53
  41.9 9.5 %all_gather.32 = f32[16,64,128]{2,1,0:T(8,128)S(1)} all-gather(f32[4,64,128]{2,1,0:T(8,128)} %bitcast.498), channel_id=1, replica_groups=mesh['dom'=8,'sub'=4] {'sub'}, dimensions={0}, use_global_device_ids=true | all-gather | bytes 655360 | tf_op jit(solution)/shard_map/all_gather | solution.py:80
  52.7 0.9 copy.333
  53.6 0.9 copy.334
  54.5 0.5 fusion.1
  55.8 0.5 collective-permute-start.4
  56.3 9.7 %all_gather.33 = f32[16,64,128]{2,1,0:T(8,128)S(1)} all-gather(f32[4,64,128]{2,1,0:T(8,128)S(1)} %bitcast.505), channel_id=1, replica_groups=mesh['dom'=8,'sub'=4] {'sub'}, dimensions={0}, use_global_device_ids=true | all-gather | bytes 655360 | tf_op jit(solution)/shard_map/all_gather | solution.py:80
  66.5 0.5 convolution_add_fusion.6
  67.8 3.2 %collective-permute-start.7 = (f32[1,2,64,128]{3,2,0,1:T(8,128)S(1)}, f32[1,2,64,128]{3,2,0,1:T(8,128)S(1)}, u32[]{:S(2)}, u32[]{:S(2)}) collective-permute-start(f32[1,2,64,128]{3,2,0,1:T(8,128)S(1)} %get-tuple-element.127), channel_id=1, source_target_pairs={{4,0},{8,4},{12,8},{16,12},{20,16},{24,20},{28,24},{0,28},{5,1},{9... | collective-permute-start | bytes 196616 | tf_op jit(solution)/shard_map/ppermute | solution.py:19
  71.1 10.1 %all_gather.34 = f32[16,64,128]{2,1,0:T(8,128)S(1)} all-gather(f32[4,64,128]{2,1,0:T(8,128)S(1)} %bitcast.504), channel_id=1, replica_groups=mesh['dom'=8,'sub'=4] {'sub'}, dimensions={0}, use_global_device_ids=true | all-gather | bytes 655360 | tf_op jit(solution)/shard_map/all_gather | solution.py:80
  81.7 0.5 convolution_add_fusion.5
  83.0 1.5 collective-permute-start.9
  84.4 10.1 %all_gather.35 = f32[16,64,128]{2,1,0:T(8,128)S(1)} all-gather(f32[4,64,128]{2,1,0:T(8,128)S(1)} %bitcast.500), channel_id=1, replica_groups=mesh['dom'=8,'sub'=4] {'sub'}, dimensions={0}, use_global_device_ids=true | all-gather | bytes 655360 | tf_op jit(solution)/shard_map/all_gather | solution.py:80
  95.0 0.5 convolution_add_fusion.4
  96.3 1.6 %collective-permute-start.11 = (f32[1,2,64,128]{3,2,0,1:T(8,128)S(1)}, f32[1,2,64,128]{3,2,0,1:T(8,128)S(1)}, u32[]{:S(2)}, u32[]{:S(2)}) collective-permute-start(f32[1,2,64,128]{3,2,0,1:T(8,128)S(1)} %get-tuple-element.123), channel_id=1, source_target_pairs={{4,0},{8,4},{12,8},{16,12},{20,16},{24,20},{28,24},{0,28},{5,1},{9... | collective-permute-start | bytes 196616 | tf_op jit(solution)/shard_map/ppermute | solution.py:19
  97.9 9.0 %all_gather.36 = f32[16,64,128]{2,1,0:T(8,128)S(1)} all-gather(f32[4,64,128]{2,1,0:T(8,128)S(1)} %bitcast.501), channel_id=1, replica_groups=mesh['dom'=8,'sub'=4] {'sub'}, dimensions={0}, use_global_device_ids=true | all-gather | bytes 655360 | tf_op jit(solution)/shard_map/all_gather | solution.py:80
  107.4 0.5 convolution_add_fusion.3
  108.7 1.9 %collective-permute-start.13 = (f32[1,2,64,128]{3,2,0,1:T(8,128)S(1)}, f32[1,2,64,128]{3,2,0,1:T(8,128)S(1)}, u32[]{:S(2)}, u32[]{:S(2)}) collective-permute-start(f32[1,2,64,128]{3,2,0,1:T(8,128)S(1)} %get-tuple-element.121), channel_id=1, source_target_pairs={{4,0},{8,4},{12,8},{16,12},{20,16},{24,20},{28,24},{0,28},{5,1},{9... | collective-permute-start | bytes 196616 | tf_op jit(solution)/shard_map/ppermute | solution.py:19
  110.5 11.4 %all_gather.37 = f32[16,64,128]{2,1,0:T(8,128)S(1)} all-gather(f32[4,64,128]{2,1,0:T(8,128)S(1)} %bitcast.502), channel_id=1, replica_groups=mesh['dom'=8,'sub'=4] {'sub'}, dimensions={0}, use_global_device_ids=true | all-gather | bytes 655360 | tf_op jit(solution)/shard_map/all_gather | solution.py:80
  122.5 0.5 convolution_add_fusion.2
  123.8 1.9 %collective-permute-start.15 = (f32[1,2,64,128]{3,2,0,1:T(8,128)S(1)}, f32[1,2,64,128]{3,2,0,1:T(8,128)S(1)}, u32[]{:S(2)}, u32[]{:S(2)}) collective-permute-start(f32[1,2,64,128]{3,2,0,1:T(8,128)S(1)} %get-tuple-element.119), channel_id=1, source_target_pairs={{4,0},{8,4},{12,8},{16,12},{20,16},{24,20},{28,24},{0,28},{5,1},{9... | collective-permute-start | bytes 196616 | tf_op jit(solution)/shard_map/ppermute | solution.py:19
  125.7 8.8 %all_gather.38 = f32[16,64,128]{2,1,0:T(8,128)S(1)} all-gather(f32[4,64,128]{2,1,0:T(8,128)S(1)} %bitcast.503), channel_id=1, replica_groups=mesh['dom'=8,'sub'=4] {'sub'}, dimensions={0}, use_global_device_ids=true | all-gather | bytes 655360 | tf_op jit(solution)/shard_map/all_gather | solution.py:80
  134.9 0.5 convolution_add_fusion.1
  135.6 0.5 copy-done.9
  136.7 2.2 %collective-permute-start.17 = (f32[1,2,64,128]{3,2,0,1:T(8,128)S(1)}, f32[1,2,64,128]{3,2,0,1:T(8,128)S(1)}, u32[]{:S(2)}, u32[]{:S(2)}) collective-permute-start(f32[1,2,64,128]{3,2,0,1:T(8,128)S(1)} %get-tuple-element.117), channel_id=1, source_target_pairs={{4,0},{8,4},{12,8},{16,12},{20,16},{24,20},{28,24},{0,28},{5,1},{9... | collective-permute-start | bytes 196616 | tf_op jit(solution)/shard_map/ppermute | solution.py:19
  138.9 11.3 %all_gather.39 = f32[16,64,128]{2,1,0:T(8,128)S(1)} all-gather(f32[4,64,128]{2,1,0:T(8,128)S(1)} %bitcast.499), channel_id=1, replica_groups=mesh['dom'=8,'sub'=4] {'sub'}, dimensions={0}, use_global_device_ids=true | all-gather | bytes 655360 | tf_op jit(solution)/shard_map/all_gather | solution.py:80
  150.6 2.2 %gather_fusion.6 = f32[8,64,128]{2,1,0:T(8,128)} fusion(f32[8,64,128]{2,1,0:T(8,128)} %bitcast.497, s32[1024]{0:T(1024)S(1)} %pad_clamp_fusion), kind=kCustom, calls=%fused_computation.6 | custom fusion | bytes 524320 | tf_op jit(solution)/shard_map/gather | solution.py:98
  152.9 1.5 fusion
  154.5 1.3 gather_fusion.7
  (188 shorter events, 13.2 us)
Async XLA Ops:
  0.6 9.0 %copy-start = (bf16[8,6,128,128]{3,2,1,0:T(8,128)(2,1)S(1)}, bf16[8,6,128,128]{3,2,1,0:T(8,128)(2,1)}, u32[]{:S(2)}) copy-start(bf16[8,6,128,128]{3,2,1,0:T(8,128)(2,1)} %param.24) | copy-start | bytes 4718596
  4.1 48.0 %collective-permute-start = (s32[1,4,2]{1,2,0:T(2,128)S(1)}, s32[1,4,2]{1,2,0:T(2,128)S(1)}, u32[]{:S(2)}, u32[]{:S(2)}) collective-permute-start(s32[1,4,2]{1,2,0:T(2,128)S(1)} %bitcast.567), channel_id=1, source_target_pairs={{0,4},{4,8},{8,12},{12,16},{16,20},{20,24},{24,28},{28,0},{1,5},{5... | collective-permute-start | bytes 104 | tf_op jit(solution)/shard_map/ppermute | solution.py:18
  4.6 47.6 %collective-permute-start.1 = (s32[1,4,2]{1,2,0:T(2,128)S(1)}, s32[1,4,2]{1,2,0:T(2,128)S(1)}, u32[]{:S(2)}, u32[]{:S(2)}) collective-permute-start(s32[1,4,2]{1,2,0:T(2,128)S(1)} %bitcast.566), channel_id=1, source_target_pairs={{4,0},{8,4},{12,8},{16,12},{20,16},{24,20},{28,24},{0,28},{5,1},{9... | collective-permute-start | bytes 104 | tf_op jit(solution)/shard_map/ppermute | solution.py:19
  11.3 8.1 %copy-start.11 = (s32[8,2]{0,1:T(2,128)S(1)}, s32[8,2]{0,1:T(2,128)}, u32[]{:S(2)}) copy-start(s32[8,2]{0,1:T(2,128)} %param.29) | copy-start | bytes 196
  12.9 17.5 %copy-start.12 = (s32[8,2]{0,1:T(2,128)S(1)}, s32[8,2]{0,1:T(2,128)}, u32[]{:S(2)}) copy-start(s32[8,2]{0,1:T(2,128)} %param.28) | copy-start | bytes 196
  12.9 20.1 %copy-start.10 = (s32[1,4,4]{2,1,0:T(4,128)S(1)}, s32[1,4,4]{2,1,0:T(4,128)}, u32[]{:S(2)}) copy-start(s32[1,4,4]{2,1,0:T(4,128)} %param.30) | copy-start | bytes 196
  16.9 1.0 copy-start.5
  18.8 33.9 %collective-permute-start.3 = (f32[1,2,64,128]{3,2,0,1:T(8,128)}, f32[1,2,64,128]{3,2,0,1:T(8,128)}, u32[]{:S(2)}, u32[]{:S(2)}) collective-permute-start(f32[1,2,64,128]{3,2,0,1:T(8,128)} %get-tuple-element.131), channel_id=1, source_target_pairs={{4,0},{8,4},{12,8},{16,12},{20,16},{24,20},{28,24},{0,28},{5,1},{9... | collective-permute-start | bytes 196616 | tf_op jit(solution)/shard_map/ppermute | solution.py:19
  19.5 34.1 %collective-permute-start.2 = (f32[1,2,64,128]{3,2,0,1:T(8,128)}, f32[1,2,64,128]{3,2,0,1:T(8,128)}, u32[]{:S(2)}, u32[]{:S(2)}) collective-permute-start(f32[1,2,64,128]{3,2,0,1:T(8,128)} %get-tuple-element.130), channel_id=1, source_target_pairs={{0,4},{4,8},{8,12},{12,16},{16,20},{20,24},{24,28},{28,0},{1,5},{5... | collective-permute-start | bytes 196616 | tf_op jit(solution)/shard_map/ppermute | solution.py:18
  41.9 9.9 %copy-start.8 = (f32[2,2,128,64]{2,3,1,0:T(8,128)S(1)}, f32[2,2,128,64]{2,3,1,0:T(8,128)}, u32[]{:S(2)}) copy-start(f32[2,2,128,64]{2,3,1,0:T(8,128)} %fusion.65) | copy-start | bytes 393220
  41.9 10.7 %copy-start.13 = (s32[4]{0:T(128)S(1)}, s32[4]{0:T(128)}, u32[]{:S(2)}) copy-start(s32[4]{0:T(128)} %eq.148) | copy-start | bytes 52
  51.5 3.6 %copy-start.1 = (bf16[8,128,128]{2,1,0:T(8,128)(2,1)S(1)}, bf16[8,128,128]{2,1,0:T(8,128)(2,1)}, u32[]{:S(2)}) copy-start(bf16[8,128,128]{2,1,0:T(8,128)(2,1)} %gather_fusion.1) | copy-start | bytes 786436
  51.8 3.7 %copy-start.4 = (bf16[2,2,128,128]{3,2,1,0:T(8,128)(2,1)S(1)}, bf16[2,2,128,128]{3,2,1,0:T(8,128)(2,1)}, u32[]{:S(2)}) copy-start(bf16[2,2,128,128]{3,2,1,0:T(8,128)(2,1)} %get-tuple-element.114) | copy-start | bytes 393220
  55.7 10.7 %collective-permute-start.5 = (f32[1,2,64,128]{3,2,0,1:T(8,128)S(1)}, f32[1,2,64,128]{3,2,0,1:T(8,128)S(1)}, u32[]{:S(2)}, u32[]{:S(2)}) collective-permute-start(f32[1,2,64,128]{3,2,0,1:T(8,128)S(1)} %get-tuple-element.129), channel_id=1, source_target_pairs={{4,0},{8,4},{12,8},{16,12},{20,16},{24,20},{28,24},{0,28},{5,1},{9... | collective-permute-start | bytes 196616 | tf_op jit(solution)/shard_map/ppermute | solution.py:19
  55.8 10.7 %collective-permute-start.4 = (f32[1,2,64,128]{3,2,0,1:T(8,128)S(1)}, f32[1,2,64,128]{3,2,0,1:T(8,128)S(1)}, u32[]{:S(2)}, u32[]{:S(2)}) collective-permute-start(f32[1,2,64,128]{3,2,0,1:T(8,128)S(1)} %get-tuple-element.128), channel_id=1, source_target_pairs={{0,4},{4,8},{8,12},{12,16},{16,20},{20,24},{24,28},{28,0},{1,5},{5... | collective-permute-start | bytes 196616 | tf_op jit(solution)/shard_map/ppermute | solution.py:18
  66.4 1.3 copy-start.3
  67.8 13.7 %collective-permute-start.7 = (f32[1,2,64,128]{3,2,0,1:T(8,128)S(1)}, f32[1,2,64,128]{3,2,0,1:T(8,128)S(1)}, u32[]{:S(2)}, u32[]{:S(2)}) collective-permute-start(f32[1,2,64,128]{3,2,0,1:T(8,128)S(1)} %get-tuple-element.127), channel_id=1, source_target_pairs={{4,0},{8,4},{12,8},{16,12},{20,16},{24,20},{28,24},{0,28},{5,1},{9... | collective-permute-start | bytes 196616 | tf_op jit(solution)/shard_map/ppermute | solution.py:19
  71.1 10.5 %collective-permute-start.6 = (f32[1,2,64,128]{3,2,0,1:T(8,128)S(1)}, f32[1,2,64,128]{3,2,0,1:T(8,128)S(1)}, u32[]{:S(2)}, u32[]{:S(2)}) collective-permute-start(f32[1,2,64,128]{3,2,0,1:T(8,128)S(1)} %get-tuple-element.126), channel_id=1, source_target_pairs={{0,4},{4,8},{8,12},{12,16},{16,20},{20,24},{24,28},{28,0},{1,5},{5... | collective-permute-start | bytes 196616 | tf_op jit(solution)/shard_map/ppermute | solution.py:18
  81.5 1.3 copy-start.2
  83.0 11.9 %collective-permute-start.9 = (f32[1,2,64,128]{3,2,0,1:T(8,128)S(1)}, f32[1,2,64,128]{3,2,0,1:T(8,128)S(1)}, u32[]{:S(2)}, u32[]{:S(2)}) collective-permute-start(f32[1,2,64,128]{3,2,0,1:T(8,128)S(1)} %get-tuple-element.125), channel_id=1, source_target_pairs={{4,0},{8,4},{12,8},{16,12},{20,16},{24,20},{28,24},{0,28},{5,1},{9... | collective-permute-start | bytes 196616 | tf_op jit(solution)/shard_map/ppermute | solution.py:19
  84.4 10.5 %collective-permute-start.8 = (f32[1,2,64,128]{3,2,0,1:T(8,128)S(1)}, f32[1,2,64,128]{3,2,0,1:T(8,128)S(1)}, u32[]{:S(2)}, u32[]{:S(2)}) collective-permute-start(f32[1,2,64,128]{3,2,0,1:T(8,128)S(1)} %get-tuple-element.124), channel_id=1, source_target_pairs={{0,4},{4,8},{8,12},{12,16},{16,20},{20,24},{24,28},{28,0},{1,5},{5... | collective-permute-start | bytes 196616 | tf_op jit(solution)/shard_map/ppermute | solution.py:18
  94.9 1.2 copy-start.6
  96.3 10.9 %collective-permute-start.11 = (f32[1,2,64,128]{3,2,0,1:T(8,128)S(1)}, f32[1,2,64,128]{3,2,0,1:T(8,128)S(1)}, u32[]{:S(2)}, u32[]{:S(2)}) collective-permute-start(f32[1,2,64,128]{3,2,0,1:T(8,128)S(1)} %get-tuple-element.123), channel_id=1, source_target_pairs={{4,0},{8,4},{12,8},{16,12},{20,16},{24,20},{28,24},{0,28},{5,1},{9... | collective-permute-start | bytes 196616 | tf_op jit(solution)/shard_map/ppermute | solution.py:19
  97.9 9.4 %collective-permute-start.10 = (f32[1,2,64,128]{3,2,0,1:T(8,128)S(1)}, f32[1,2,64,128]{3,2,0,1:T(8,128)S(1)}, u32[]{:S(2)}, u32[]{:S(2)}) collective-permute-start(f32[1,2,64,128]{3,2,0,1:T(8,128)S(1)} %get-tuple-element.122), channel_id=1, source_target_pairs={{0,4},{4,8},{8,12},{12,16},{16,20},{20,24},{24,28},{28,0},{1,5},{5... | collective-permute-start | bytes 196616 | tf_op jit(solution)/shard_map/ppermute | solution.py:18
  108.7 13.7 %collective-permute-start.13 = (f32[1,2,64,128]{3,2,0,1:T(8,128)S(1)}, f32[1,2,64,128]{3,2,0,1:T(8,128)S(1)}, u32[]{:S(2)}, u32[]{:S(2)}) collective-permute-start(f32[1,2,64,128]{3,2,0,1:T(8,128)S(1)} %get-tuple-element.121), channel_id=1, source_target_pairs={{4,0},{8,4},{12,8},{16,12},{20,16},{24,20},{28,24},{0,28},{5,1},{9... | collective-permute-start | bytes 196616 | tf_op jit(solution)/shard_map/ppermute | solution.py:19
  110.5 11.9 %collective-permute-start.12 = (f32[1,2,64,128]{3,2,0,1:T(8,128)S(1)}, f32[1,2,64,128]{3,2,0,1:T(8,128)S(1)}, u32[]{:S(2)}, u32[]{:S(2)}) collective-permute-start(f32[1,2,64,128]{3,2,0,1:T(8,128)S(1)} %get-tuple-element.120), channel_id=1, source_target_pairs={{0,4},{4,8},{8,12},{12,16},{16,20},{20,24},{24,28},{28,0},{1,5},{5... | collective-permute-start | bytes 196616 | tf_op jit(solution)/shard_map/ppermute | solution.py:18
  123.8 11.0 %collective-permute-start.15 = (f32[1,2,64,128]{3,2,0,1:T(8,128)S(1)}, f32[1,2,64,128]{3,2,0,1:T(8,128)S(1)}, u32[]{:S(2)}, u32[]{:S(2)}) collective-permute-start(f32[1,2,64,128]{3,2,0,1:T(8,128)S(1)} %get-tuple-element.119), channel_id=1, source_target_pairs={{4,0},{8,4},{12,8},{16,12},{20,16},{24,20},{28,24},{0,28},{5,1},{9... | collective-permute-start | bytes 196616 | tf_op jit(solution)/shard_map/ppermute | solution.py:19
  125.7 9.2 %collective-permute-start.14 = (f32[1,2,64,128]{3,2,0,1:T(8,128)S(1)}, f32[1,2,64,128]{3,2,0,1:T(8,128)S(1)}, u32[]{:S(2)}, u32[]{:S(2)}) collective-permute-start(f32[1,2,64,128]{3,2,0,1:T(8,128)S(1)} %get-tuple-element.118), channel_id=1, source_target_pairs={{0,4},{4,8},{8,12},{12,16},{16,20},{20,24},{24,28},{28,0},{1,5},{5... | collective-permute-start | bytes 196616 | tf_op jit(solution)/shard_map/ppermute | solution.py:18
  135.4 0.7 copy-start.9
  135.6 15.0 %copy-start.7 = (f32[4,2,64,128]{3,2,1,0:T(8,128)}, f32[4,2,64,128]{3,2,1,0:T(8,128)S(1)}, u32[]{:S(2)}) copy-start(f32[4,2,64,128]{3,2,1,0:T(8,128)S(1)} %get-tuple-element.170) | copy-start | bytes 786436
  136.7 16.1 %collective-permute-start.17 = (f32[1,2,64,128]{3,2,0,1:T(8,128)S(1)}, f32[1,2,64,128]{3,2,0,1:T(8,128)S(1)}, u32[]{:S(2)}, u32[]{:S(2)}) collective-permute-start(f32[1,2,64,128]{3,2,0,1:T(8,128)S(1)} %get-tuple-element.117), channel_id=1, source_target_pairs={{4,0},{8,4},{12,8},{16,12},{20,16},{24,20},{28,24},{0,28},{5,1},{9... | collective-permute-start | bytes 196616 | tf_op jit(solution)/shard_map/ppermute | solution.py:19
  138.9 13.9 %collective-permute-start.16 = (f32[1,2,64,128]{3,2,0,1:T(8,128)S(1)}, f32[1,2,64,128]{3,2,0,1:T(8,128)S(1)}, u32[]{:S(2)}, u32[]{:S(2)}) collective-permute-start(f32[1,2,64,128]{3,2,0,1:T(8,128)S(1)} %get-tuple-element.116), channel_id=1, source_target_pairs={{0,4},{4,8},{8,12},{12,16},{16,20},{20,24},{24,28},{28,0},{1,5},{5... | collective-permute-start | bytes 196616 | tf_op jit(solution)/shard_map/ppermute | solution.py:18
where the time goes:
time: 156 us
  blocking collectives  96.6 us (62%)
  local copies, waits for them, and re-layouts  22.4 us (14%)
  starting transfers between devices  18 us (12%)
  matrix products  12 us (8%)
  other arithmetic  5.23 us (3%)
    all_gather x8, blocking collectives, on_device(): lax.all_gather(group_terms.reshape(2 * quarter, rhs_count, block_width),...  79.9 us
    ppermute x9, starting transfers between devices, extended(): after = lax.ppermute(first, axis, down)  17 us
    all_gather x1, blocking collectives, on_device(): lax.all_gather(peer_by[None], 'sub', axis=0, tiled=True)  8.5 us
    all_gather x1, blocking collectives, on_device(): lax.all_gather(table_rows[None], 'sub', axis=0, tiled=True)  8.13 us
    unnamed x80, local copies, waits for them, and re-layouts  7.92 us
    dot_general x8, matrix products, on_device(): added = jnp.dot(selector, arrived_items, precision=lax.Precision.HIGHEST)  5.01 us
  transfers between devices with their start and end apart: 18, of which 0 were waited for; matrix products, arithmetic and copies ran while one was open for 15% of the time, Pallas kernels for 0%

commit v1 on v0

v1 whole, which is shorter than its diff:
```python
import functools

import jax
import jax.numpy as jnp
from jax import lax
from jax.experimental import pallas as pl
from jax.experimental.pallas import tpu as pltpu
from jax.sharding import PartitionSpec as P

COLORS = 4
SWEEPS = 2
COUPLINGS = 6
META = 8

VMEM = pl.BlockSpec(memory_space=pltpu.VMEM)
SMEM = pl.BlockSpec(memory_space=pltpu.SMEM)


def is_pow2(n):
    return n & (n - 1) == 0


def partner(member, shift, size):
    if is_pow2(size):
        return member ^ shift
    return lax.rem(member + shift, size)


def slot_of(member, peer, size):
    if is_pow2(size):
        return (member ^ peer) - 1
    return lax.rem(peer - member + size, size) - 1


def dot(a, b):
    return jnp.dot(a, b, preferred_element_type=jnp.float32)


class Sizes:
    def __init__(self, rows, rhs_count, width, group):
        self.rows, self.n, self.w, self.group = rows, rhs_count, width, group
        self.quarter = rows // COLORS
        self.slots = group - 1
        self.order = 0
        self.local = rows
        self.slot = 3 * rows
        self.table = 5 * rows
        self.dom_meta = -(-rows // 8) * 8


def items_of(sz, color, first, got_group, got_up, got_down, meta):
    metas_group, meta_up, meta_down = meta
    out = []
    for s in range(sz.slots):
        out.append((metas_group[s], sz.n + color, got_group[s], 0))
    for ref, got in ((meta_up, got_up), (meta_down, got_down)):
        for p in range(sz.quarter):
            out.append((ref, sz.quarter * sz.n + color * sz.quarter + p, got, p * sz.n))
    return out


def subtract(sz, value, row, items):
    for meta, at, got, start in items:
        here = meta[pl.ds(at, 1), :] == row
        value = value - jnp.where(here, got[pl.ds(start, sz.n), :], 0.0)
    return value


def products(sz, color, table, changes, coupling, send_group, send_up, send_down):
    group_terms = []
    for p in range(sz.quarter):
        at = color * sz.quarter + p
        j = table[sz.order + at]
        pair = jnp.concatenate([coupling[j, 4], coupling[j, 5]], axis=1)
        both = dot(changes[p], pair)
        send_up[pl.ds(p * sz.n, sz.n), :] = both[:, : sz.w]
        send_down[pl.ds(p * sz.n, sz.n), :] = both[:, sz.w :]
        pair = jnp.concatenate([coupling[j, 2], coupling[j, 3]], axis=1)
        both = dot(changes[p], pair)
        for k in range(2):
            group_terms.append((table[sz.slot + 2 * at + k], both[:, k * sz.w : (k + 1) * sz.w]))
    for s in range(sz.slots):
        total = jnp.zeros((sz.n, sz.w), jnp.float32)
        for slot, term in group_terms:
            total = total + jnp.where(slot == s, term, 0.0)
        send_group[s][pl.ds(0, sz.n), :] = total


def first_kernel(sz, color, local_target, group_peer, group_list, dom_target, rhs, diag, coupling, *outs):
    table, sol, change = outs[:3]
    send_up, send_down = outs[3:5]
    send_group = outs[5:]
    me = lax.axis_index("sub")
    colors = [color[i] for i in range(sz.rows)]
    for i in range(sz.rows):
        before = jnp.int32(0)
        for e in range(i):
            before = before + (colors[e] == colors[i]).astype(jnp.int32)
        at = colors[i] * sz.quarter + before
        table[sz.order + at] = i
        for k in range(2):
            table[sz.local + 2 * at + k] = local_target[i, k]
            table[sz.slot + 2 * at + k] = slot_of(me, group_peer[i, k], sz.group)
    changes = []
    for p in range(sz.quarter):
        j = table[sz.order + p]
        new = dot(rhs[j].astype(jnp.bfloat16), diag[j])
        sol[p] = new
        changes.append(new.astype(jnp.bfloat16))
        change[p] = changes[p]
    products(sz, 0, table, changes, coupling, send_group, send_up, send_down)
    line = lax.broadcasted_iota(jnp.int32, (META, sz.w), 0)
    for s in range(sz.slots):
        q = partner(me, s + 1, sz.group)
        meta = jnp.full((META, sz.w), -1, jnp.int32)
        for c in range(COLORS):
            meta = jnp.where(line == c, group_list[0, c, q], meta)
        send_group[s][pl.ds(sz.n, META), :] = meta.astype(jnp.float32)
    line = lax.broadcasted_iota(jnp.int32, (sz.dom_meta, sz.w), 0)
    for k, send in enumerate((send_up, send_down)):
        meta = jnp.full((sz.dom_meta, sz.w), -1, jnp.int32)
        for at in range(sz.rows):
            meta = jnp.where(line == at, dom_target[table[sz.order + at], k], meta)
        send[pl.ds(sz.quarter * sz.n, sz.dom_meta), :] = meta.astype(jnp.float32)


def split_got(sz, refs):
    up, down = refs[:2]
    return refs[2 : 2 + sz.slots], up, down


def step_kernel(sz, color, prev_color, has_old, table, resid, diag, coupling, *refs):
    lanes = 2 + sz.slots
    got, refs = refs[:lanes], refs[lanes:]
    meta, refs = refs[:lanes], refs[lanes:]
    if has_old:
        old, refs = refs[0], refs[1:]
    sol, change, send_up, send_down = refs[:4]
    send_group = refs[4:]
    items = items_of(sz, prev_color, False, *split_got(sz, got), split_got(sz, meta))
    changes = []
    for p in range(sz.quarter):
        j = table[sz.order + color * sz.quarter + p]
        value = subtract(sz, resid[j], j.astype(jnp.float32), items)
        new = dot(value.astype(jnp.bfloat16), diag[j])
        sol[p] = new
        if has_old:
            new = new - old[p]
        changes.append(new.astype(jnp.bfloat16))
        change[p] = changes[p]
    products(sz, color, table, changes, coupling, send_group, send_up, send_down)


def local_kernel(sz, color, prev_color, last, table, resid, coupling, change, *refs):
    lanes = 2 + sz.slots
    items = []
    if prev_color is not None:
        got, refs = refs[:lanes], refs[lanes:]
        meta, refs = refs[:lanes], refs[lanes:]
        items = items_of(sz, prev_color, False, *split_got(sz, got), split_got(sz, meta))
    if last:
        sols, refs = refs[:COLORS], refs[COLORS:]
        out, sol_out = refs
    else:
        (out,) = refs
    for r in range(sz.rows):
        out[r] = subtract(sz, resid[r], jnp.float32(r), items)
    for p in range(sz.quarter):
        at = color * sz.quarter + p
        j = table[sz.order + at]
        both = dot(change[p], jnp.concatenate([coupling[j, 0], coupling[j, 1]], axis=1))
        for k in range(2):
            t = table[sz.local + 2 * at + k]
            out[t] = out[t] - both[:, k * sz.w : (k + 1) * sz.w]
    if last:
        for c in range(COLORS):
            for p in range(sz.quarter):
                sol_out[table[sz.order + c * sz.quarter + p]] = sols[c][p]


def final_kernel(sz, prev_color, resid, *refs):
    lanes = 2 + sz.slots
    got, refs = refs[:lanes], refs[lanes:]
    meta, refs = refs[:lanes], refs[lanes:]
    (out,) = refs
    items = items_of(sz, prev_color, False, *split_got(sz, got), split_got(sz, meta))
    for r in range(sz.rows):
        out[r] = subtract(sz, resid[r], jnp.float32(r), items)


def exchange(sends):
    doms, group = lax.axis_size("dom"), lax.axis_size("sub")
    up = [(i, (i + 1) % doms) for i in range(doms)]
    down = [(j, i) for i, j in up]
    got = [lax.ppermute(sends[0], "dom", up), lax.ppermute(sends[1], "dom", down)]
    for s, send in enumerate(sends[2:]):
        perm = [(i, int(i ^ (s + 1)) if is_pow2(group) else (i + s + 1) % group) for i in range(group)]
        got.append(lax.ppermute(send, "sub", perm))
    return got


def on_device(coupling, diag_inv, rhs, color, local_target, group_peer, group_list, dom_target):
    rows, rhs_count, width = rhs.shape
    sz = Sizes(rows, rhs_count, width, lax.axis_size("sub"))
    f32 = jnp.float32
    sol_t = pltpu.VMEM((sz.quarter, sz.n, sz.w), f32)
    change_t = pltpu.VMEM((sz.quarter, sz.n, sz.w), jnp.bfloat16)

    def send_types(meta_group, meta_dom):
        dom_t = pltpu.VMEM((sz.quarter * sz.n + meta_dom, sz.w), f32)
        return [dom_t, dom_t] + [pltpu.VMEM((sz.n + meta_group, sz.w), f32)] * sz.slots

    params = pltpu.CompilerParams(vmem_limit_bytes=16 * 1024 * 1024)

    def call(body, ins, smem_ins, outs, **kw):
        specs = [SMEM] * smem_ins + [VMEM] * (len(ins) - smem_ins)
        out_specs = [
            SMEM if getattr(o, "memory_space", None) == pltpu.SMEM else VMEM for o in outs
        ]
        return pl.pallas_call(
            body, in_specs=specs, out_specs=out_specs, out_shape=outs, compiler_params=params, **kw
        )(*ins)

    table, sol, change, *sends = call(
        functools.partial(first_kernel, sz),
        [color, local_target, group_peer, group_list, dom_target, rhs, diag_inv, coupling],
        5,
        [pltpu.SMEM((sz.table,), jnp.int32), sol_t, change_t] + send_types(META, sz.dom_meta),
        name="first",
    )
    tiles = pltpu.with_memory_space_constraint(coupling, pltpu.VMEM)
    diags = pltpu.with_memory_space_constraint(diag_inv, pltpu.VMEM)
    sols = [sol]
    resid = rhs
    resid_t = pltpu.VMEM((sz.rows, sz.n, sz.w), f32)
    meta, got = None, None
    steps = SWEEPS * COLORS
    for step in range(steps):
        c, before = step % COLORS, (step - 1) % COLORS
        if step > 0:
            ins = [table, resid, diags, tiles, *got, *meta]
            has_old = step >= COLORS
            if has_old:
                ins.append(sols[c])
            sol, change, *sends = call(
                functools.partial(step_kernel, sz, c, before, has_old),
                ins,
                1,
                [sol_t, change_t] + send_types(0, 0),
                name=f"step{step}",
            )
            if has_old:
                sols[c] = sol
            else:
                sols.append(sol)
        arriving = exchange(sends)
        ins = [table, resid, tiles, change]
        if step > 0:
            ins += [*got, *meta]
        outs = [resid_t]
        last = step == steps - 1
        if last:
            ins += sols
            outs.append(jax.ShapeDtypeStruct(rhs.shape, f32))
        done = call(
            functools.partial(local_kernel, sz, c, before if step > 0 else None, last),
            ins,
            1,
            outs,
            name=f"local{step}",
            input_output_aliases={1: 0} if step > 0 else {},
        )
        resid = done[0]
        got = arriving
        if step == 0:
            meta = got
    (defect,) = call(
        functools.partial(final_kernel, sz, (steps - 1) % COLORS),
        [resid, *got, *meta],
        0,
        [jax.ShapeDtypeStruct(rhs.shape, f32)],
        name="final",
    )
    return done[1], defect


def solution(mesh):
    placed = (
        P(("dom", "sub"), None, None, None),
        P(("dom", "sub"), None, None),
        P(("dom", "sub"), None, None),
        P(("dom", "sub")),
        P(("dom", "sub"), None),
        P(("dom", "sub"), None),
        P(("dom", "sub"), None, None),
        P(("dom", "sub"), None),
    )
    return jax.shard_map(
        on_device,
        mesh=mesh,
        in_specs=placed,
        out_specs=(P(("dom", "sub"), None, None), P(("dom", "sub"), None, None)),
        check_vma=False,
    )
```

time: 156 us -> 96.7 us (0.62)
  blocking collectives: 96.6 us -> 0 us
  starting transfers between devices: 18 us -> 57.6 us
  waiting for transfers between devices: 0.05 us -> 24.5 us
  local copies, waits for them, and re-layouts: 22.4 us -> 6.92 us
  matrix products: 12 us -> 0 us
  Pallas kernels: 0 us -> 6.43 us
  other arithmetic: 5.23 us -> 0 us
    all_gather x10 -> x0, blocking collectives: 96.6 us -> none  [the longest x8 79.9 us: on_device(): lax.all_gather(group_terms.reshape(2 * quarter, rhs_count, block_width),...]
    ppermute x18 -> x40, starting transfers between devices: 18 us -> 57.6 us  [the longest x8 28.8 us: exchange(): lax.ppermute(sends[1], 'dom', down)]
    ppermute x18 -> x40, waiting for transfers between devices: 0.05 us -> 24.5 us  [the longest x24 24.5 us: exchange(): got.append(lax.ppermute(send, 'sub', perm))]
    dot_general x40 -> x0, matrix products: 12 us -> none  [the longest x8 5.01 us: on_device(): added = jnp.dot(selector, arrived_items, precision=lax.Precision.HIGHEST)]
    gather x9 -> x0, local copies, waits for them, and re-layouts: 9.86 us -> none  [the longest x1 2.24 us: on_device(): diag_inv[order_flat].reshape(COLORS, quarter, block_width, block_width)]
    pallas_call x0 -> x17, Pallas kernels: none -> 6.43 us  [call(): pl.pallas_call(body, in_specs=specs, out_specs=out_specs, out_shape=outs,...]
    sort x2 -> x0, other arithmetic: 2.69 us -> none  [the longest x1 1.73 us: on_device(): order_flat = jnp.argsort(color, stable=True)]
    eq x16 -> x0, local copies, waits for them, and re-layouts: 2.02 us -> none  [the longest x8 0.86 us: on_device(): matches = gathered_peers[:, color_now].reshape(-1) == own_member]
  transfers between devices with their start and end apart: 18 -> 40, of which waited for: 0 -> 23; matrix products, arithmetic and copies ran while one was open for 15% -> 0% of each run, Pallas kernels for 0% -> 2%
where the time goes in v1:
time: 96.7 us; the launch traced here: 96.4 us
  starting transfers between devices  57.6 us (60%)
  waiting for transfers between devices  24.5 us (25%)
  local copies, waits for them, and re-layouts  6.92 us (7%)
  Pallas kernels  6.43 us (7%)
    ppermute x8, starting transfers between devices, exchange(): lax.ppermute(sends[1], 'dom', down)  28.8 us
    ppermute x24, starting transfers between devices, exchange(): got.append(lax.ppermute(send, 'sub', perm))  27.9 us
    ppermute x24, waiting for transfers between devices, exchange(): got.append(lax.ppermute(send, 'sub', perm))  24.5 us
    unnamed x19, local copies, waits for them, and re-layouts  6.92 us
    pallas_call x17, Pallas kernels, call(): pl.pallas_call(body, in_specs=specs, out_specs=out_specs, out_shape=outs,...  6.43 us
  transfers between devices with their start and end apart: 40, of which 23 were waited for; matrix products, arithmetic and copies ran while one was open for 0% of the time, Pallas kernels for 2%

profile of v1, /device:TPU:0, one launch (start us, length us, event | category | flops | bytes accessed | tf_op | source)
XLA Modules:
  0.0 96.4 jit_solution(217206051124511951)
XLA Ops:
  0.6 0.8 copy.17.local_target
  1.4 0.8 copy.18.group_peer
  2.1 0.8 copy.19.dom_target
  2.9 1.4 %copy-done = bf16[8,6,128,128]{3,2,1,0:T(8,128)(2,1)S(1)} copy-done((bf16[8,6,128,128]{3,2,1,0:T(8,128)(2,1)S(1)}, bf16[8,6,128,128]{3,2,1,0:T(8,128)(2,1)}, u32[]{:S(2)}) %copy-start) | copy-done | bytes 1572888
  4.3 0.9 copy-done.2
  5.3 0.9 copy-done.4
  6.2 0.7 copy-done.6
  6.9 0.7 copy-done.7
  7.5 1.2 %first.1 = (s32[40]{0:T(128)S(4)}, f32[2,64,128]{2,1,0:T(8,128)S(1)}, bf16[2,64,128]{2,1,0:T(8,128)(2,1)S(1)}, f32[136,128]{1,0:T(8,128)S(1)}, f32[136,128]{1,0:...) custom-call(s32[8]{0:T(128)S(1)} %copy-done.7, s32[8,2]{1,0:T(8,128)S(1)} %copy.17.local_target, ...), custom_call_target="tpu_custom_call" | custom-call | tf_op jit(solution)/shard_map/first/pallas_call | solution.py:220
  9.2 4.1 %collective-permute-start.1 = (f32[136,128]{1,0:T(8,128)S(1)}, f32[136,128]{1,0:T(8,128)S(1)}, u32[]{:S(2)}, u32[]{:S(2)}) collective-permute-start(f32[136,128]{1,0:T(8,128)S(1)} %get-tuple-element.64), channel_id=1, source_target_pairs={{4,0},{8,4},{12,8},{16,12},{20,16},{24,20},{28,24},{0,28},{5,1},{9... | collective-permute-start | bytes 208904 | tf_op jit(solution)/shard_map/ppermute | solution.py:195
  13.3 1.9 %collective-permute-start.2 = (f32[72,128]{1,0:T(8,128)S(1)}, f32[72,128]{1,0:T(8,128)S(1)}, u32[]{:S(2)}, u32[]{:S(2)}) collective-permute-start(f32[72,128]{1,0:T(8,128)S(1)} %get-tuple-element.65), channel_id=1, source_target_pairs={{0,1},{1,0},{2,3},{3,2},{4,5},{5,4},{6,7},{7,6},{8,9},{9,8},{10,11... | collective-permute-start | bytes 110600 | tf_op jit(solution)/shard_map/ppermute | solution.py:198
  15.3 1.5 %collective-permute-start.3 = (f32[72,128]{1,0:T(8,128)S(1)}, f32[72,128]{1,0:T(8,128)S(1)}, u32[]{:S(2)}, u32[]{:S(2)}) collective-permute-start(f32[72,128]{1,0:T(8,128)S(1)} %get-tuple-element.66), channel_id=1, source_target_pairs={{0,2},{1,3},{2,0},{3,1},{4,6},{5,7},{6,4},{7,5},{8,10},{9,11},{10,... | collective-permute-start | bytes 110600 | tf_op jit(solution)/shard_map/ppermute | solution.py:198
  17.0 0.7 collective-permute-done.2.refs_2_.refs_7_
  17.7 1.5 %collective-permute-done.3.refs_3_.refs_8_ = f32[72,128]{1,0:T(8,128)S(1)} collective-permute-done((f32[72,128]{1,0:T(8,128)S(1)}, f32[72,128]{1,0:T(8,128)S(1)}, u32[]{:S(2)}, u32[]{:S(2)}) %collective-permute-start.3) | collective-permute-done | bytes 36896 | tf_op jit(solution)/shard_map/ppermute | solution.py:198
  19.2 2.4 %collective-permute-done.4.refs_4_.refs_9_ = f32[72,128]{1,0:T(8,128)S(1)} collective-permute-done((f32[72,128]{1,0:T(8,128)S(1)}, f32[72,128]{1,0:T(8,128)S(1)}, u32[]{:S(2)}, u32[]{:S(2)}) %collective-permute-start.4) | collective-permute-done | bytes 36896 | tf_op jit(solution)/shard_map/ppermute | solution.py:198
  22.0 3.5 %collective-permute-start.6 = (f32[128,128]{1,0:T(8,128)S(1)}, f32[128,128]{1,0:T(8,128)S(1)}, u32[]{:S(2)}, u32[]{:S(2)}) collective-permute-start(f32[128,128]{1,0:T(8,128)S(1)} %get-tuple-element.70), channel_id=1, source_target_pairs={{4,0},{8,4},{12,8},{16,12},{20,16},{24,20},{28,24},{0,28},{5,1},{9... | collective-permute-start | bytes 196616 | tf_op jit(solution)/shard_map/ppermute | solution.py:195
  25.6 0.5 collective-permute-start.7
  26.2 2.9 %collective-permute-start.9 = (f32[64,128]{1,0:T(8,128)S(1)}, f32[64,128]{1,0:T(8,128)S(1)}, u32[]{:S(2)}, u32[]{:S(2)}) collective-permute-start(f32[64,128]{1,0:T(8,128)S(1)} %get-tuple-element.73), channel_id=1, source_target_pairs={{0,3},{1,2},{2,1},{3,0},{4,7},{5,6},{6,5},{7,4},{8,11},{9,10},{10,... | collective-permute-start | bytes 98312 | tf_op jit(solution)/shard_map/ppermute | solution.py:198
  29.5 0.5 collective-permute-done.8.refs_3_
  30.0 1.0 %collective-permute-done.9.refs_4_ = f32[64,128]{1,0:T(8,128)S(1)} collective-permute-done((f32[64,128]{1,0:T(8,128)S(1)}, f32[64,128]{1,0:T(8,128)S(1)}, u32[]{:S(2)}, u32[]{:S(2)}) %collective-permute-start.9) | collective-permute-done | bytes 32800 | tf_op jit(solution)/shard_map/ppermute | solution.py:198
  31.4 3.5 %collective-permute-start.11 = (f32[128,128]{1,0:T(8,128)S(1)}, f32[128,128]{1,0:T(8,128)S(1)}, u32[]{:S(2)}, u32[]{:S(2)}) collective-permute-start(f32[128,128]{1,0:T(8,128)S(1)} %get-tuple-element.76), channel_id=1, source_target_pairs={{4,0},{8,4},{12,8},{16,12},{20,16},{24,20},{28,24},{0,28},{5,1},{9... | collective-permute-start | bytes 196616 | tf_op jit(solution)/shard_map/ppermute | solution.py:195
  34.9 1.9 %collective-permute-start.12 = (f32[64,128]{1,0:T(8,128)S(1)}, f32[64,128]{1,0:T(8,128)S(1)}, u32[]{:S(2)}, u32[]{:S(2)}) collective-permute-start(f32[64,128]{1,0:T(8,128)S(1)} %get-tuple-element.77), channel_id=1, source_target_pairs={{0,1},{1,0},{2,3},{3,2},{4,5},{5,4},{6,7},{7,6},{8,9},{9,8},{10,11... | collective-permute-start | bytes 98312 | tf_op jit(solution)/shard_map/ppermute | solution.py:198
  36.8 1.5 %collective-permute-start.13 = (f32[64,128]{1,0:T(8,128)S(1)}, f32[64,128]{1,0:T(8,128)S(1)}, u32[]{:S(2)}, u32[]{:S(2)}) collective-permute-start(f32[64,128]{1,0:T(8,128)S(1)} %get-tuple-element.78), channel_id=1, source_target_pairs={{0,2},{1,3},{2,0},{3,1},{4,6},{5,7},{6,4},{7,5},{8,10},{9,11},{10,... | collective-permute-start | bytes 98312 | tf_op jit(solution)/shard_map/ppermute | solution.py:198
  38.8 1.9 %collective-permute-done.13.refs_3_ = f32[64,128]{1,0:T(8,128)S(1)} collective-permute-done((f32[64,128]{1,0:T(8,128)S(1)}, f32[64,128]{1,0:T(8,128)S(1)}, u32[]{:S(2)}, u32[]{:S(2)}) %collective-permute-start.13) | collective-permute-done | bytes 32800 | tf_op jit(solution)/shard_map/ppermute | solution.py:198
  40.7 2.4 %collective-permute-done.14.refs_4_ = f32[64,128]{1,0:T(8,128)S(1)} collective-permute-done((f32[64,128]{1,0:T(8,128)S(1)}, f32[64,128]{1,0:T(8,128)S(1)}, u32[]{:S(2)}, u32[]{:S(2)}) %collective-permute-start.14) | collective-permute-done | bytes 32800 | tf_op jit(solution)/shard_map/ppermute | solution.py:198
  43.5 3.5 %collective-permute-start.16 = (f32[128,128]{1,0:T(8,128)S(1)}, f32[128,128]{1,0:T(8,128)S(1)}, u32[]{:S(2)}, u32[]{:S(2)}) collective-permute-start(f32[128,128]{1,0:T(8,128)S(1)} %get-tuple-element.82), channel_id=1, source_target_pairs={{4,0},{8,4},{12,8},{16,12},{20,16},{24,20},{28,24},{0,28},{5,1},{9... | collective-permute-start | bytes 196616 | tf_op jit(solution)/shard_map/ppermute | solution.py:195
  47.1 0.5 collective-permute-start.17
  47.7 2.9 %collective-permute-start.19 = (f32[64,128]{1,0:T(8,128)S(1)}, f32[64,128]{1,0:T(8,128)S(1)}, u32[]{:S(2)}, u32[]{:S(2)}) collective-permute-start(f32[64,128]{1,0:T(8,128)S(1)} %get-tuple-element.85), channel_id=1, source_target_pairs={{0,3},{1,2},{2,1},{3,0},{4,7},{5,6},{6,5},{7,4},{8,11},{9,10},{10,... | collective-permute-start | bytes 98312 | tf_op jit(solution)/shard_map/ppermute | solution.py:198
  51.0 0.5 collective-permute-done.18.refs_3_
  51.5 1.0 %collective-permute-done.19.refs_4_ = f32[64,128]{1,0:T(8,128)S(1)} collective-permute-done((f32[64,128]{1,0:T(8,128)S(1)}, f32[64,128]{1,0:T(8,128)S(1)}, u32[]{:S(2)}, u32[]{:S(2)}) %collective-permute-start.19) | collective-permute-done | bytes 32800 | tf_op jit(solution)/shard_map/ppermute | solution.py:198
  52.9 3.5 %collective-permute-start.21 = (f32[128,128]{1,0:T(8,128)S(1)}, f32[128,128]{1,0:T(8,128)S(1)}, u32[]{:S(2)}, u32[]{:S(2)}) collective-permute-start(f32[128,128]{1,0:T(8,128)S(1)} %get-tuple-element.89), channel_id=1, source_target_pairs={{4,0},{8,4},{12,8},{16,12},{20,16},{24,20},{28,24},{0,28},{5,1},{9... | collective-permute-start | bytes 196616 | tf_op jit(solution)/shard_map/ppermute | solution.py:195
  56.4 1.9 %collective-permute-start.22 = (f32[64,128]{1,0:T(8,128)S(1)}, f32[64,128]{1,0:T(8,128)S(1)}, u32[]{:S(2)}, u32[]{:S(2)}) collective-permute-start(f32[64,128]{1,0:T(8,128)S(1)} %get-tuple-element.90), channel_id=1, source_target_pairs={{0,1},{1,0},{2,3},{3,2},{4,5},{5,4},{6,7},{7,6},{8,9},{9,8},{10,11... | collective-permute-start | bytes 98312 | tf_op jit(solution)/shard_map/ppermute | solution.py:198
  58.3 1.5 %collective-permute-start.23 = (f32[64,128]{1,0:T(8,128)S(1)}, f32[64,128]{1,0:T(8,128)S(1)}, u32[]{:S(2)}, u32[]{:S(2)}) collective-permute-start(f32[64,128]{1,0:T(8,128)S(1)} %get-tuple-element.91), channel_id=1, source_target_pairs={{0,2},{1,3},{2,0},{3,1},{4,6},{5,7},{6,4},{7,5},{8,10},{9,11},{10,... | collective-permute-start | bytes 98312 | tf_op jit(solution)/shard_map/ppermute | solution.py:198
  60.3 1.9 %collective-permute-done.23.refs_3_ = f32[64,128]{1,0:T(8,128)S(1)} collective-permute-done((f32[64,128]{1,0:T(8,128)S(1)}, f32[64,128]{1,0:T(8,128)S(1)}, u32[]{:S(2)}, u32[]{:S(2)}) %collective-permute-start.23) | collective-permute-done | bytes 32800 | tf_op jit(solution)/shard_map/ppermute | solution.py:198
  62.2 2.4 %collective-permute-done.24.refs_4_ = f32[64,128]{1,0:T(8,128)S(1)} collective-permute-done((f32[64,128]{1,0:T(8,128)S(1)}, f32[64,128]{1,0:T(8,128)S(1)}, u32[]{:S(2)}, u32[]{:S(2)}) %collective-permute-start.24) | collective-permute-done | bytes 32800 | tf_op jit(solution)/shard_map/ppermute | solution.py:198
  65.0 3.5 %collective-permute-start.26 = (f32[128,128]{1,0:T(8,128)S(1)}, f32[128,128]{1,0:T(8,128)S(1)}, u32[]{:S(2)}, u32[]{:S(2)}) collective-permute-start(f32[128,128]{1,0:T(8,128)S(1)} %get-tuple-element.96), channel_id=1, source_target_pairs={{4,0},{8,4},{12,8},{16,12},{20,16},{24,20},{28,24},{0,28},{5,1},{9... | collective-permute-start | bytes 196616 | tf_op jit(solution)/shard_map/ppermute | solution.py:195
  69.2 2.9 %collective-permute-start.29 = (f32[64,128]{1,0:T(8,128)S(1)}, f32[64,128]{1,0:T(8,128)S(1)}, u32[]{:S(2)}, u32[]{:S(2)}) collective-permute-start(f32[64,128]{1,0:T(8,128)S(1)} %get-tuple-element.99), channel_id=1, source_target_pairs={{0,3},{1,2},{2,1},{3,0},{4,7},{5,6},{6,5},{7,4},{8,11},{9,10},{10,... | collective-permute-start | bytes 98312 | tf_op jit(solution)/shard_map/ppermute | solution.py:198
  73.0 1.0 %collective-permute-done.29.refs_4_ = f32[64,128]{1,0:T(8,128)S(1)} collective-permute-done((f32[64,128]{1,0:T(8,128)S(1)}, f32[64,128]{1,0:T(8,128)S(1)}, u32[]{:S(2)}, u32[]{:S(2)}) %collective-permute-start.29) | collective-permute-done | bytes 32800 | tf_op jit(solution)/shard_map/ppermute | solution.py:198
  74.4 3.5 %collective-permute-start.31 = (f32[128,128]{1,0:T(8,128)S(1)}, f32[128,128]{1,0:T(8,128)S(1)}, u32[]{:S(2)}, u32[]{:S(2)}) collective-permute-start(f32[128,128]{1,0:T(8,128)S(1)} %get-tuple-element.103), channel_id=1, source_target_pairs={{4,0},{8,4},{12,8},{16,12},{20,16},{24,20},{28,24},{0,28},{5,1},{9... | collective-permute-start | bytes 196616 | tf_op jit(solution)/shard_map/ppermute | solution.py:195
  77.9 1.9 %collective-permute-start.32 = (f32[64,128]{1,0:T(8,128)S(1)}, f32[64,128]{1,0:T(8,128)S(1)}, u32[]{:S(2)}, u32[]{:S(2)}) collective-permute-start(f32[64,128]{1,0:T(8,128)S(1)} %get-tuple-element.104), channel_id=1, source_target_pairs={{0,1},{1,0},{2,3},{3,2},{4,5},{5,4},{6,7},{7,6},{8,9},{9,8},{10,11... | collective-permute-start | bytes 98312 | tf_op jit(solution)/shard_map/ppermute | solution.py:198
  79.8 1.5 %collective-permute-start.33 = (f32[64,128]{1,0:T(8,128)S(1)}, f32[64,128]{1,0:T(8,128)S(1)}, u32[]{:S(2)}, u32[]{:S(2)}) collective-permute-start(f32[64,128]{1,0:T(8,128)S(1)} %get-tuple-element.105), channel_id=1, source_target_pairs={{0,2},{1,3},{2,0},{3,1},{4,6},{5,7},{6,4},{7,5},{8,10},{9,11},{10,... | collective-permute-start | bytes 98312 | tf_op jit(solution)/shard_map/ppermute | solution.py:198
  81.8 1.9 %collective-permute-done.33.refs_3_ = f32[64,128]{1,0:T(8,128)S(1)} collective-permute-done((f32[64,128]{1,0:T(8,128)S(1)}, f32[64,128]{1,0:T(8,128)S(1)}, u32[]{:S(2)}, u32[]{:S(2)}) %collective-permute-start.33) | collective-permute-done | bytes 32800 | tf_op jit(solution)/shard_map/ppermute | solution.py:198
  83.7 2.4 %collective-permute-done.34.refs_4_ = f32[64,128]{1,0:T(8,128)S(1)} collective-permute-done((f32[64,128]{1,0:T(8,128)S(1)}, f32[64,128]{1,0:T(8,128)S(1)}, u32[]{:S(2)}, u32[]{:S(2)}) %collective-permute-start.34) | collective-permute-done | bytes 32800 | tf_op jit(solution)/shard_map/ppermute | solution.py:198
  86.5 3.5 %collective-permute-start.36 = (f32[128,128]{1,0:T(8,128)S(1)}, f32[128,128]{1,0:T(8,128)S(1)}, u32[]{:S(2)}, u32[]{:S(2)}) collective-permute-start(f32[128,128]{1,0:T(8,128)S(1)} %get-tuple-element.116), channel_id=1, source_target_pairs={{4,0},{8,4},{12,8},{16,12},{20,16},{24,20},{28,24},{0,28},{5,1},{9... | collective-permute-start | bytes 196616 | tf_op jit(solution)/shard_map/ppermute | solution.py:195
  90.7 2.9 %collective-permute-start.39 = (f32[64,128]{1,0:T(8,128)S(1)}, f32[64,128]{1,0:T(8,128)S(1)}, u32[]{:S(2)}, u32[]{:S(2)}) collective-permute-start(f32[64,128]{1,0:T(8,128)S(1)} %get-tuple-element.119), channel_id=1, source_target_pairs={{0,3},{1,2},{2,1},{3,0},{4,7},{5,6},{6,5},{7,4},{8,11},{9,10},{10,... | collective-permute-start | bytes 98312 | tf_op jit(solution)/shard_map/ppermute | solution.py:198
  93.6 0.9 local7.1
  94.5 1.0 %collective-permute-done.39.refs_4_ = f32[64,128]{1,0:T(8,128)S(1)} collective-permute-done((f32[64,128]{1,0:T(8,128)S(1)}, f32[64,128]{1,0:T(8,128)S(1)}, u32[]{:S(2)}, u32[]{:S(2)}) %collective-permute-start.39) | collective-permute-done | bytes 32800 | tf_op jit(solution)/shard_map/ppermute | solution.py:198
  95.5 0.9 final.1
  (68 shorter events, 7.9 us)
Async XLA Ops:
  2.9 1.4 %copy-start = (bf16[8,6,128,128]{3,2,1,0:T(8,128)(2,1)S(1)}, bf16[8,6,128,128]{3,2,1,0:T(8,128)(2,1)}, u32[]{:S(2)}) copy-start(bf16[8,6,128,128]{3,2,1,0:T(8,128)(2,1)} %coupling.31) | copy-start | bytes 4718596
  4.3 0.9 copy-start.2
  5.2 0.9 copy-start.4
  6.2 0.7 copy-start.6
  6.9 0.7 copy-start.7
  7.5 9.3 %copy-start.1 = (bf16[8,6,128,128]{3,2,1,0:T(8,128)(2,1)S(1)}, bf16[8,6,128,128]{3,2,1,0:T(8,128)(2,1)}, u32[]{:S(2)}) copy-start(bf16[8,6,128,128]{3,2,1,0:T(8,128)(2,1)} %coupling.31) | copy-start | bytes 4718596
  7.5 9.3 %copy-start.5 = (f32[8,64,128]{2,1,0:T(8,128)S(1)}, f32[8,64,128]{2,1,0:T(8,128)}, u32[]{:S(2)}) copy-start(f32[8,64,128]{2,1,0:T(8,128)} %resid.1) | copy-start | bytes 786436
  8.7 12.9 %copy-start.3 = (bf16[8,128,128]{2,1,0:T(8,128)(2,1)S(1)}, bf16[8,128,128]{2,1,0:T(8,128)(2,1)}, u32[]{:S(2)}) copy-start(bf16[8,128,128]{2,1,0:T(8,128)(2,1)} %diag.15) | copy-start | bytes 786436
  8.7 12.9 %collective-permute-start = (f32[136,128]{1,0:T(8,128)S(1)}, f32[136,128]{1,0:T(8,128)S(1)}, u32[]{:S(2)}, u32[]{:S(2)}) collective-permute-start(f32[136,128]{1,0:T(8,128)S(1)} %get-tuple-element.63), channel_id=1, source_target_pairs={{0,4},{4,8},{8,12},{12,16},{16,20},{20,24},{24,28},{28,0},{1,5},{5... | collective-permute-start | bytes 208904 | tf_op jit(solution)/shard_map/ppermute | solution.py:195
  9.2 12.4 %collective-permute-start.1 = (f32[136,128]{1,0:T(8,128)S(1)}, f32[136,128]{1,0:T(8,128)S(1)}, u32[]{:S(2)}, u32[]{:S(2)}) collective-permute-start(f32[136,128]{1,0:T(8,128)S(1)} %get-tuple-element.64), channel_id=1, source_target_pairs={{4,0},{8,4},{12,8},{16,12},{20,16},{24,20},{28,24},{0,28},{5,1},{9... | collective-permute-start | bytes 208904 | tf_op jit(solution)/shard_map/ppermute | solution.py:195
  13.3 4.3 %collective-permute-start.2 = (f32[72,128]{1,0:T(8,128)S(1)}, f32[72,128]{1,0:T(8,128)S(1)}, u32[]{:S(2)}, u32[]{:S(2)}) collective-permute-start(f32[72,128]{1,0:T(8,128)S(1)} %get-tuple-element.65), channel_id=1, source_target_pairs={{0,1},{1,0},{2,3},{3,2},{4,5},{5,4},{6,7},{7,6},{8,9},{9,8},{10,11... | collective-permute-start | bytes 110600 | tf_op jit(solution)/shard_map/ppermute | solution.py:198
  15.3 4.0 %collective-permute-start.3 = (f32[72,128]{1,0:T(8,128)S(1)}, f32[72,128]{1,0:T(8,128)S(1)}, u32[]{:S(2)}, u32[]{:S(2)}) collective-permute-start(f32[72,128]{1,0:T(8,128)S(1)} %get-tuple-element.66), channel_id=1, source_target_pairs={{0,2},{1,3},{2,0},{3,1},{4,6},{5,7},{6,4},{7,5},{8,10},{9,11},{10,... | collective-permute-start | bytes 110600 | tf_op jit(solution)/shard_map/ppermute | solution.py:198
  16.8 4.9 %collective-permute-start.4 = (f32[72,128]{1,0:T(8,128)S(1)}, f32[72,128]{1,0:T(8,128)S(1)}, u32[]{:S(2)}, u32[]{:S(2)}) collective-permute-start(f32[72,128]{1,0:T(8,128)S(1)} %get-tuple-element.67), channel_id=1, source_target_pairs={{0,3},{1,2},{2,1},{3,0},{4,7},{5,6},{6,5},{7,4},{8,11},{9,10},{10,... | collective-permute-start | bytes 110600 | tf_op jit(solution)/shard_map/ppermute | solution.py:198
  22.0 9.0 %collective-permute-start.5 = (f32[128,128]{1,0:T(8,128)S(1)}, f32[128,128]{1,0:T(8,128)S(1)}, u32[]{:S(2)}, u32[]{:S(2)}) collective-permute-start(f32[128,128]{1,0:T(8,128)S(1)} %get-tuple-element.69), channel_id=1, source_target_pairs={{0,4},{4,8},{8,12},{12,16},{16,20},{20,24},{24,28},{28,0},{1,5},{5... | collective-permute-start | bytes 196616 | tf_op jit(solution)/shard_map/ppermute | solution.py:195
  22.0 9.0 %collective-permute-start.6 = (f32[128,128]{1,0:T(8,128)S(1)}, f32[128,128]{1,0:T(8,128)S(1)}, u32[]{:S(2)}, u32[]{:S(2)}) collective-permute-start(f32[128,128]{1,0:T(8,128)S(1)} %get-tuple-element.70), channel_id=1, source_target_pairs={{4,0},{8,4},{12,8},{16,12},{20,16},{24,20},{28,24},{0,28},{5,1},{9... | collective-permute-start | bytes 196616 | tf_op jit(solution)/shard_map/ppermute | solution.py:195
  25.6 3.9 %collective-permute-start.7 = (f32[64,128]{1,0:T(8,128)S(1)}, f32[64,128]{1,0:T(8,128)S(1)}, u32[]{:S(2)}, u32[]{:S(2)}) collective-permute-start(f32[64,128]{1,0:T(8,128)S(1)} %get-tuple-element.71), channel_id=1, source_target_pairs={{0,1},{1,0},{2,3},{3,2},{4,5},{5,4},{6,7},{7,6},{8,9},{9,8},{10,11... | collective-permute-start | bytes 98312 | tf_op jit(solution)/shard_map/ppermute | solution.py:198
  26.1 3.9 %collective-permute-start.8 = (f32[64,128]{1,0:T(8,128)S(1)}, f32[64,128]{1,0:T(8,128)S(1)}, u32[]{:S(2)}, u32[]{:S(2)}) collective-permute-start(f32[64,128]{1,0:T(8,128)S(1)} %get-tuple-element.72), channel_id=1, source_target_pairs={{0,2},{1,3},{2,0},{3,1},{4,6},{5,7},{6,4},{7,5},{8,10},{9,11},{10,... | collective-permute-start | bytes 98312 | tf_op jit(solution)/shard_map/ppermute | solution.py:198
  26.2 4.8 %collective-permute-start.9 = (f32[64,128]{1,0:T(8,128)S(1)}, f32[64,128]{1,0:T(8,128)S(1)}, u32[]{:S(2)}, u32[]{:S(2)}) collective-permute-start(f32[64,128]{1,0:T(8,128)S(1)} %get-tuple-element.73), channel_id=1, source_target_pairs={{0,3},{1,2},{2,1},{3,0},{4,7},{5,6},{6,5},{7,4},{8,11},{9,10},{10,... | collective-permute-start | bytes 98312 | tf_op jit(solution)/shard_map/ppermute | solution.py:198
  31.3 11.9 %collective-permute-start.10 = (f32[128,128]{1,0:T(8,128)S(1)}, f32[128,128]{1,0:T(8,128)S(1)}, u32[]{:S(2)}, u32[]{:S(2)}) collective-permute-start(f32[128,128]{1,0:T(8,128)S(1)} %get-tuple-element.75), channel_id=1, source_target_pairs={{0,4},{4,8},{8,12},{12,16},{16,20},{20,24},{24,28},{28,0},{1,5},{5... | collective-permute-start | bytes 196616 | tf_op jit(solution)/shard_map/ppermute | solution.py:195
  31.4 11.8 %collective-permute-start.11 = (f32[128,128]{1,0:T(8,128)S(1)}, f32[128,128]{1,0:T(8,128)S(1)}, u32[]{:S(2)}, u32[]{:S(2)}) collective-permute-start(f32[128,128]{1,0:T(8,128)S(1)} %get-tuple-element.76), channel_id=1, source_target_pairs={{4,0},{8,4},{12,8},{16,12},{20,16},{24,20},{28,24},{0,28},{5,1},{9... | collective-permute-start | bytes 196616 | tf_op jit(solution)/shard_map/ppermute | solution.py:195
  34.9 3.9 %collective-permute-start.12 = (f32[64,128]{1,0:T(8,128)S(1)}, f32[64,128]{1,0:T(8,128)S(1)}, u32[]{:S(2)}, u32[]{:S(2)}) collective-permute-start(f32[64,128]{1,0:T(8,128)S(1)} %get-tuple-element.77), channel_id=1, source_target_pairs={{0,1},{1,0},{2,3},{3,2},{4,5},{5,4},{6,7},{7,6},{8,9},{9,8},{10,11... | collective-permute-start | bytes 98312 | tf_op jit(solution)/shard_map/ppermute | solution.py:198
  36.8 3.9 %collective-permute-start.13 = (f32[64,128]{1,0:T(8,128)S(1)}, f32[64,128]{1,0:T(8,128)S(1)}, u32[]{:S(2)}, u32[]{:S(2)}) collective-permute-start(f32[64,128]{1,0:T(8,128)S(1)} %get-tuple-element.78), channel_id=1, source_target_pairs={{0,2},{1,3},{2,0},{3,1},{4,6},{5,7},{6,4},{7,5},{8,10},{9,11},{10,... | collective-permute-start | bytes 98312 | tf_op jit(solution)/shard_map/ppermute | solution.py:198
  38.3 4.8 %collective-permute-start.14 = (f32[64,128]{1,0:T(8,128)S(1)}, f32[64,128]{1,0:T(8,128)S(1)}, u32[]{:S(2)}, u32[]{:S(2)}) collective-permute-start(f32[64,128]{1,0:T(8,128)S(1)} %get-tuple-element.79), channel_id=1, source_target_pairs={{0,3},{1,2},{2,1},{3,0},{4,7},{5,6},{6,5},{7,4},{8,11},{9,10},{10,... | collective-permute-start | bytes 98312 | tf_op jit(solution)/shard_map/ppermute | solution.py:198
  43.5 9.0 %collective-permute-start.15 = (f32[128,128]{1,0:T(8,128)S(1)}, f32[128,128]{1,0:T(8,128)S(1)}, u32[]{:S(2)}, u32[]{:S(2)}) collective-permute-start(f32[128,128]{1,0:T(8,128)S(1)} %get-tuple-element.81), channel_id=1, source_target_pairs={{0,4},{4,8},{8,12},{12,16},{16,20},{20,24},{24,28},{28,0},{1,5},{5... | collective-permute-start | bytes 196616 | tf_op jit(solution)/shard_map/ppermute | solution.py:195
  43.5 9.0 %collective-permute-start.16 = (f32[128,128]{1,0:T(8,128)S(1)}, f32[128,128]{1,0:T(8,128)S(1)}, u32[]{:S(2)}, u32[]{:S(2)}) collective-permute-start(f32[128,128]{1,0:T(8,128)S(1)} %get-tuple-element.82), channel_id=1, source_target_pairs={{4,0},{8,4},{12,8},{16,12},{20,16},{24,20},{28,24},{0,28},{5,1},{9... | collective-permute-start | bytes 196616 | tf_op jit(solution)/shard_map/ppermute | solution.py:195
  47.1 3.9 %collective-permute-start.17 = (f32[64,128]{1,0:T(8,128)S(1)}, f32[64,128]{1,0:T(8,128)S(1)}, u32[]{:S(2)}, u32[]{:S(2)}) collective-permute-start(f32[64,128]{1,0:T(8,128)S(1)} %get-tuple-element.83), channel_id=1, source_target_pairs={{0,1},{1,0},{2,3},{3,2},{4,5},{5,4},{6,7},{7,6},{8,9},{9,8},{10,11... | collective-permute-start | bytes 98312 | tf_op jit(solution)/shard_map/ppermute | solution.py:198
  47.6 3.9 %collective-permute-start.18 = (f32[64,128]{1,0:T(8,128)S(1)}, f32[64,128]{1,0:T(8,128)S(1)}, u32[]{:S(2)}, u32[]{:S(2)}) collective-permute-start(f32[64,128]{1,0:T(8,128)S(1)} %get-tuple-element.84), channel_id=1, source_target_pairs={{0,2},{1,3},{2,0},{3,1},{4,6},{5,7},{6,4},{7,5},{8,10},{9,11},{10,... | collective-permute-start | bytes 98312 | tf_op jit(solution)/shard_map/ppermute | solution.py:198
  47.7 4.8 %collective-permute-start.19 = (f32[64,128]{1,0:T(8,128)S(1)}, f32[64,128]{1,0:T(8,128)S(1)}, u32[]{:S(2)}, u32[]{:S(2)}) collective-permute-start(f32[64,128]{1,0:T(8,128)S(1)} %get-tuple-element.85), channel_id=1, source_target_pairs={{0,3},{1,2},{2,1},{3,0},{4,7},{5,6},{6,5},{7,4},{8,11},{9,10},{10,... | collective-permute-start | bytes 98312 | tf_op jit(solution)/shard_map/ppermute | solution.py:198
  52.8 11.9 %collective-permute-start.20 = (f32[128,128]{1,0:T(8,128)S(1)}, f32[128,128]{1,0:T(8,128)S(1)}, u32[]{:S(2)}, u32[]{:S(2)}) collective-permute-start(f32[128,128]{1,0:T(8,128)S(1)} %get-tuple-element.88), channel_id=1, source_target_pairs={{0,4},{4,8},{8,12},{12,16},{16,20},{20,24},{24,28},{28,0},{1,5},{5... | collective-permute-start | bytes 196616 | tf_op jit(solution)/shard_map/ppermute | solution.py:195
  52.9 11.8 %collective-permute-start.21 = (f32[128,128]{1,0:T(8,128)S(1)}, f32[128,128]{1,0:T(8,128)S(1)}, u32[]{:S(2)}, u32[]{:S(2)}) collective-permute-start(f32[128,128]{1,0:T(8,128)S(1)} %get-tuple-element.89), channel_id=1, source_target_pairs={{4,0},{8,4},{12,8},{16,12},{20,16},{24,20},{28,24},{0,28},{5,1},{9... | collective-permute-start | bytes 196616 | tf_op jit(solution)/shard_map/ppermute | solution.py:195
  56.4 3.9 %collective-permute-start.22 = (f32[64,128]{1,0:T(8,128)S(1)}, f32[64,128]{1,0:T(8,128)S(1)}, u32[]{:S(2)}, u32[]{:S(2)}) collective-permute-start(f32[64,128]{1,0:T(8,128)S(1)} %get-tuple-element.90), channel_id=1, source_target_pairs={{0,1},{1,0},{2,3},{3,2},{4,5},{5,4},{6,7},{7,6},{8,9},{9,8},{10,11... | collective-permute-start | bytes 98312 | tf_op jit(solution)/shard_map/ppermute | solution.py:198
  58.3 3.9 %collective-permute-start.23 = (f32[64,128]{1,0:T(8,128)S(1)}, f32[64,128]{1,0:T(8,128)S(1)}, u32[]{:S(2)}, u32[]{:S(2)}) collective-permute-start(f32[64,128]{1,0:T(8,128)S(1)} %get-tuple-element.91), channel_id=1, source_target_pairs={{0,2},{1,3},{2,0},{3,1},{4,6},{5,7},{6,4},{7,5},{8,10},{9,11},{10,... | collective-permute-start | bytes 98312 | tf_op jit(solution)/shard_map/ppermute | solution.py:198
  59.8 4.8 %collective-permute-start.24 = (f32[64,128]{1,0:T(8,128)S(1)}, f32[64,128]{1,0:T(8,128)S(1)}, u32[]{:S(2)}, u32[]{:S(2)}) collective-permute-start(f32[64,128]{1,0:T(8,128)S(1)} %get-tuple-element.92), channel_id=1, source_target_pairs={{0,3},{1,2},{2,1},{3,0},{4,7},{5,6},{6,5},{7,4},{8,11},{9,10},{10,... | collective-permute-start | bytes 98312 | tf_op jit(solution)/shard_map/ppermute | solution.py:198
  65.0 9.0 %collective-permute-start.25 = (f32[128,128]{1,0:T(8,128)S(1)}, f32[128,128]{1,0:T(8,128)S(1)}, u32[]{:S(2)}, u32[]{:S(2)}) collective-permute-start(f32[128,128]{1,0:T(8,128)S(1)} %get-tuple-element.95), channel_id=1, source_target_pairs={{0,4},{4,8},{8,12},{12,16},{16,20},{20,24},{24,28},{28,0},{1,5},{5... | collective-permute-start | bytes 196616 | tf_op jit(solution)/shard_map/ppermute | solution.py:195
  65.0 9.0 %collective-permute-start.26 = (f32[128,128]{1,0:T(8,128)S(1)}, f32[128,128]{1,0:T(8,128)S(1)}, u32[]{:S(2)}, u32[]{:S(2)}) collective-permute-start(f32[128,128]{1,0:T(8,128)S(1)} %get-tuple-element.96), channel_id=1, source_target_pairs={{4,0},{8,4},{12,8},{16,12},{20,16},{24,20},{28,24},{0,28},{5,1},{9... | collective-permute-start | bytes 196616 | tf_op jit(solution)/shard_map/ppermute | solution.py:195
  68.6 3.9 %collective-permute-start.27 = (f32[64,128]{1,0:T(8,128)S(1)}, f32[64,128]{1,0:T(8,128)S(1)}, u32[]{:S(2)}, u32[]{:S(2)}) collective-permute-start(f32[64,128]{1,0:T(8,128)S(1)} %get-tuple-element.97), channel_id=1, source_target_pairs={{0,1},{1,0},{2,3},{3,2},{4,5},{5,4},{6,7},{7,6},{8,9},{9,8},{10,11... | collective-permute-start | bytes 98312 | tf_op jit(solution)/shard_map/ppermute | solution.py:198
  69.1 3.9 %collective-permute-start.28 = (f32[64,128]{1,0:T(8,128)S(1)}, f32[64,128]{1,0:T(8,128)S(1)}, u32[]{:S(2)}, u32[]{:S(2)}) collective-permute-start(f32[64,128]{1,0:T(8,128)S(1)} %get-tuple-element.98), channel_id=1, source_target_pairs={{0,2},{1,3},{2,0},{3,1},{4,6},{5,7},{6,4},{7,5},{8,10},{9,11},{10,... | collective-permute-start | bytes 98312 | tf_op jit(solution)/shard_map/ppermute | solution.py:198
  69.2 4.8 %collective-permute-start.29 = (f32[64,128]{1,0:T(8,128)S(1)}, f32[64,128]{1,0:T(8,128)S(1)}, u32[]{:S(2)}, u32[]{:S(2)}) collective-permute-start(f32[64,128]{1,0:T(8,128)S(1)} %get-tuple-element.99), channel_id=1, source_target_pairs={{0,3},{1,2},{2,1},{3,0},{4,7},{5,6},{6,5},{7,4},{8,11},{9,10},{10,... | collective-permute-start | bytes 98312 | tf_op jit(solution)/shard_map/ppermute | solution.py:198
  74.3 11.9 %collective-permute-start.30 = (f32[128,128]{1,0:T(8,128)S(1)}, f32[128,128]{1,0:T(8,128)S(1)}, u32[]{:S(2)}, u32[]{:S(2)}) collective-permute-start(f32[128,128]{1,0:T(8,128)S(1)} %get-tuple-element.102), channel_id=1, source_target_pairs={{0,4},{4,8},{8,12},{12,16},{16,20},{20,24},{24,28},{28,0},{1,5},{5... | collective-permute-start | bytes 196616 | tf_op jit(solution)/shard_map/ppermute | solution.py:195
  74.4 11.8 %collective-permute-start.31 = (f32[128,128]{1,0:T(8,128)S(1)}, f32[128,128]{1,0:T(8,128)S(1)}, u32[]{:S(2)}, u32[]{:S(2)}) collective-permute-start(f32[128,128]{1,0:T(8,128)S(1)} %get-tuple-element.103), channel_id=1, source_target_pairs={{4,0},{8,4},{12,8},{16,12},{20,16},{24,20},{28,24},{0,28},{5,1},{9... | collective-permute-start | bytes 196616 | tf_op jit(solution)/shard_map/ppermute | solution.py:195
  77.9 3.9 %collective-permute-start.32 = (f32[64,128]{1,0:T(8,128)S(1)}, f32[64,128]{1,0:T(8,128)S(1)}, u32[]{:S(2)}, u32[]{:S(2)}) collective-permute-start(f32[64,128]{1,0:T(8,128)S(1)} %get-tuple-element.104), channel_id=1, source_target_pairs={{0,1},{1,0},{2,3},{3,2},{4,5},{5,4},{6,7},{7,6},{8,9},{9,8},{10,11... | collective-permute-start | bytes 98312 | tf_op jit(solution)/shard_map/ppermute | solution.py:198
  79.8 3.9 %collective-permute-start.33 = (f32[64,128]{1,0:T(8,128)S(1)}, f32[64,128]{1,0:T(8,128)S(1)}, u32[]{:S(2)}, u32[]{:S(2)}) collective-permute-start(f32[64,128]{1,0:T(8,128)S(1)} %get-tuple-element.105), channel_id=1, source_target_pairs={{0,2},{1,3},{2,0},{3,1},{4,6},{5,7},{6,4},{7,5},{8,10},{9,11},{10,... | collective-permute-start | bytes 98312 | tf_op jit(solution)/shard_map/ppermute | solution.py:198
  81.4 4.8 %collective-permute-start.34 = (f32[64,128]{1,0:T(8,128)S(1)}, f32[64,128]{1,0:T(8,128)S(1)}, u32[]{:S(2)}, u32[]{:S(2)}) collective-permute-start(f32[64,128]{1,0:T(8,128)S(1)} %get-tuple-element.106), channel_id=1, source_target_pairs={{0,3},{1,2},{2,1},{3,0},{4,7},{5,6},{6,5},{7,4},{8,11},{9,10},{10,... | collective-permute-start | bytes 98312 | tf_op jit(solution)/shard_map/ppermute | solution.py:198
  86.5 9.0 %collective-permute-start.35 = (f32[128,128]{1,0:T(8,128)S(1)}, f32[128,128]{1,0:T(8,128)S(1)}, u32[]{:S(2)}, u32[]{:S(2)}) collective-permute-start(f32[128,128]{1,0:T(8,128)S(1)} %get-tuple-element.115), channel_id=1, source_target_pairs={{0,4},{4,8},{8,12},{12,16},{16,20},{20,24},{24,28},{28,0},{1,5},{5... | collective-permute-start | bytes 196616 | tf_op jit(solution)/shard_map/ppermute | solution.py:195
  86.5 9.0 %collective-permute-start.36 = (f32[128,128]{1,0:T(8,128)S(1)}, f32[128,128]{1,0:T(8,128)S(1)}, u32[]{:S(2)}, u32[]{:S(2)}) collective-permute-start(f32[128,128]{1,0:T(8,128)S(1)} %get-tuple-element.116), channel_id=1, source_target_pairs={{4,0},{8,4},{12,8},{16,12},{20,16},{24,20},{28,24},{0,28},{5,1},{9... | collective-permute-start | bytes 196616 | tf_op jit(solution)/shard_map/ppermute | solution.py:195
  90.1 4.3 %collective-permute-start.37 = (f32[64,128]{1,0:T(8,128)S(1)}, f32[64,128]{1,0:T(8,128)S(1)}, u32[]{:S(2)}, u32[]{:S(2)}) collective-permute-start(f32[64,128]{1,0:T(8,128)S(1)} %get-tuple-element.117), channel_id=1, source_target_pairs={{0,1},{1,0},{2,3},{3,2},{4,5},{5,4},{6,7},{7,6},{8,9},{9,8},{10,11... | collective-permute-start | bytes 98312 | tf_op jit(solution)/shard_map/ppermute | solution.py:198
  90.6 3.9 %collective-permute-start.38 = (f32[64,128]{1,0:T(8,128)S(1)}, f32[64,128]{1,0:T(8,128)S(1)}, u32[]{:S(2)}, u32[]{:S(2)}) collective-permute-start(f32[64,128]{1,0:T(8,128)S(1)} %get-tuple-element.118), channel_id=1, source_target_pairs={{0,2},{1,3},{2,0},{3,1},{4,6},{5,7},{6,4},{7,5},{8,10},{9,11},{10,... | collective-permute-start | bytes 98312 | tf_op jit(solution)/shard_map/ppermute | solution.py:198
  90.7 4.8 %collective-permute-start.39 = (f32[64,128]{1,0:T(8,128)S(1)}, f32[64,128]{1,0:T(8,128)S(1)}, u32[]{:S(2)}, u32[]{:S(2)}) collective-permute-start(f32[64,128]{1,0:T(8,128)S(1)} %get-tuple-element.119), channel_id=1, source_target_pairs={{0,3},{1,2},{2,1},{3,0},{4,7},{5,6},{6,5},{7,4},{8,11},{9,10},{10,... | collective-permute-start | bytes 98312 | tf_op jit(solution)/shard_map/ppermute | solution.py:198

commit v2 on v0

v2 whole, which is shorter than its diff:
```python
import functools

import jax
import jax.numpy as jnp
from jax import lax
from jax.experimental import pallas as pl
from jax.experimental.pallas import tpu as pltpu
from jax.sharding import PartitionSpec as P

COLORS = 4
SWEEPS = 2
META = 8

VMEM = pl.BlockSpec(memory_space=pltpu.VMEM)
SMEM = pl.BlockSpec(memory_space=pltpu.SMEM)
HBM = pl.BlockSpec(memory_space=pltpu.HBM)


def dot(a, b):
    return jnp.dot(a, b, preferred_element_type=jnp.float32)


class Plan:
    def __init__(self, rows, rhs_count, width, group):
        self.rows, self.n, self.w, self.group = rows, rhs_count, width, group
        self.quarter = rows // COLORS
        self.phases = group.bit_length() - 1
        self.lanes = 2 + self.phases
        self.carried = [[s for s in range(1, group) if s >> d & 1] for d in range(self.phases)]
        self.order, self.local, self.slot = 0, rows, 3 * rows
        self.table = 5 * rows
        self.dom_meta = -(-rows // 8) * 8

    def stride(self, step):
        return self.n + (META if step == 0 else 0)

    def at(self, s, phase, step):
        return self.carried[phase].index(s) * self.stride(step)

    def types(self, step):
        dom = self.quarter * self.n + (self.dom_meta if step == 0 else 0)
        shapes = [dom, dom] + [len(c) * self.stride(step) for c in self.carried]
        return [pltpu.VMEM((length, self.w), jnp.float32) for length in shapes]


def items_of(plan, step, got, meta):
    color = step % COLORS
    out = []
    for s in range(1, plan.group):
        d = s.bit_length() - 1
        line = plan.at(s, d, 0) + plan.n + color
        out.append((meta[2 + d], line, got[2 + d], plan.at(s, d, step)))
    for lane in range(2):
        for p in range(plan.quarter):
            line = plan.quarter * plan.n + color * plan.quarter + p
            out.append((meta[lane], line, got[lane], p * plan.n))
    return out


def subtract(plan, value, row, items):
    for meta, line, got, start in items:
        here = meta[pl.ds(line, 1), :] == row
        value = value - jnp.where(here, got[pl.ds(start, plan.n), :], 0.0)
    return value


def products(plan, step, table, changes, coupling, sends):
    parity = lax.rem(lax.axis_index("dom"), 2)
    far, near = sends[:2]
    terms = []
    for p in range(plan.quarter):
        at = step % COLORS * plan.quarter + p
        j = table[plan.order + at]
        both = dot(changes[p], jnp.concatenate([coupling[j, 2], coupling[j, 3]], axis=1))
        for k in range(2):
            terms.append((table[plan.slot + 2 * at + k], both[:, k * plan.w : (k + 1) * plan.w]))
        both = dot(
            changes[p],
            jnp.concatenate([coupling[j, 5 - parity], coupling[j, 4 + parity]], axis=1),
        )
        far[pl.ds(p * plan.n, plan.n), :] = both[:, : plan.w]
        near[pl.ds(p * plan.n, plan.n), :] = both[:, plan.w :]
    for s in range(1, plan.group):
        total = jnp.zeros((plan.n, plan.w), jnp.float32)
        for slot, term in terms:
            total = total + jnp.where(slot == s, term, 0.0)
        d = (s & -s).bit_length() - 1
        sends[2 + d][pl.ds(plan.at(s, d, step), plan.n), :] = total


def first_kernel(plan, *refs):
    hbm, outs, scratch = refs[:8], refs[8 : 14 + plan.lanes], refs[14 + plan.lanes :]
    table, coupling, diag, rhs, sol, change = outs[:6]
    sends = outs[6:]
    color, local_target, group_peer, group_list, dom_target = scratch[:5]
    sems = scratch[5]
    targets = (color, group_peer, group_list, dom_target, local_target, rhs, diag, coupling)
    copies = [
        pltpu.make_async_copy(src, dst, sems.at[i]) for i, (src, dst) in enumerate(zip(hbm, targets))
    ]
    for copy in copies:
        copy.start()
    for copy in copies[:5]:
        copy.wait()
    me = lax.axis_index("sub")
    parity = lax.rem(lax.axis_index("dom"), 2)
    colors = [color[i] for i in range(plan.rows)]
    for i in range(plan.rows):
        before = jnp.int32(0)
        for e in range(i):
            before = before + (colors[e] == colors[i]).astype(jnp.int32)
        at = colors[i] * plan.quarter + before
        table[plan.order + at] = i
        for k in range(2):
            table[plan.local + 2 * at + k] = local_target[k, i]
            table[plan.slot + 2 * at + k] = me ^ group_peer[k, i]
    line = lax.broadcasted_iota(jnp.int32, (META, plan.w), 0)
    for s in range(1, plan.group):
        meta = jnp.full((META, plan.w), -1, jnp.int32)
        for c in range(COLORS):
            meta = jnp.where(line == c, group_list[0, c, me ^ s], meta)
        d = (s & -s).bit_length() - 1
        sends[2 + d][pl.ds(plan.at(s, d, 0) + plan.n, META), :] = meta.astype(jnp.float32)
    line = lax.broadcasted_iota(jnp.int32, (plan.dom_meta, plan.w), 0)
    for send, k in zip(sends[:2], (1 - parity, parity)):
        meta = jnp.full((plan.dom_meta, plan.w), -1, jnp.int32)
        for at in range(plan.rows):
            meta = jnp.where(line == at, dom_target[k, table[plan.order + at]], meta)
        send[pl.ds(plan.quarter * plan.n, plan.dom_meta), :] = meta.astype(jnp.float32)
    copies[5].wait()
    copies[6].wait()
    changes = []
    for p in range(plan.quarter):
        j = table[plan.order + p]
        new = dot(rhs[j].astype(jnp.bfloat16), diag[j])
        sol[p] = new
        changes.append(new.astype(jnp.bfloat16))
        change[p] = changes[p]
    copies[7].wait()
    products(plan, 0, table, changes, coupling, sends)


def step_kernel(plan, step, table, resid, diag, coupling, *refs):
    got, meta, refs = refs[: plan.lanes], refs[plan.lanes : 2 * plan.lanes], refs[2 * plan.lanes :]
    has_old = step >= COLORS
    if has_old:
        old, refs = refs[0], refs[1:]
    sol, change = refs[:2]
    items = items_of(plan, step - 1, got, meta)
    changes = []
    for p in range(plan.quarter):
        j = table[plan.order + step % COLORS * plan.quarter + p]
        value = subtract(plan, resid[j], j.astype(jnp.float32), items)
        new = dot(value.astype(jnp.bfloat16), diag[j])
        sol[p] = new
        if has_old:
            new = new - old[p]
        changes.append(new.astype(jnp.bfloat16))
        change[p] = changes[p]
    products(plan, step, table, changes, coupling, refs[2:])


def forward_kernel(plan, step, phase, *refs):
    got, out = refs[1:-1], refs[-1]
    for s in plan.carried[phase]:
        lower = s & ((1 << phase) - 1)
        if lower:
            d = lower.bit_length() - 1
            length = plan.stride(step)
            out[pl.ds(plan.at(s, phase, step), length), :] = got[d][
                pl.ds(plan.at(s, d, step), length), :
            ]


def local_kernel(plan, step, last, table, resid, coupling, change, *refs):
    items = []
    if step > 0:
        items = items_of(plan, step - 1, refs[: plan.lanes], refs[plan.lanes : 2 * plan.lanes])
        refs = refs[2 * plan.lanes :]
    if last:
        sols, refs = refs[:COLORS], refs[COLORS:]
    out = refs[0]
    for r in range(plan.rows):
        out[r] = subtract(plan, resid[r], jnp.float32(r), items)
    for p in range(plan.quarter):
        at = step % COLORS * plan.quarter + p
        j = table[plan.order + at]
        both = dot(change[p], jnp.concatenate([coupling[j, 0], coupling[j, 1]], axis=1))
        for k in range(2):
            t = table[plan.local + 2 * at + k]
            out[t] = out[t] - both[:, k * plan.w : (k + 1) * plan.w]
    if last:
        for c in range(COLORS):
            for p in range(plan.quarter):
                refs[1][table[plan.order + c * plan.quarter + p]] = sols[c][p]


def final_kernel(plan, step, resid, *refs):
    items = items_of(plan, step, refs[: plan.lanes], refs[plan.lanes : 2 * plan.lanes])
    out = refs[-1]
    for r in range(plan.rows):
        out[r] = subtract(plan, resid[r], jnp.float32(r), items)


def on_device(coupling, diag_inv, rhs, color, local_target, group_peer, group_list, dom_target):
    rows, rhs_count, width = rhs.shape
    doms, group = lax.axis_size("dom"), lax.axis_size("sub")
    assert group & (group - 1) == 0 and doms % 2 == 0
    plan = Plan(rows, rhs_count, width, group)
    f32 = jnp.float32
    near_pairs = [(i, i ^ 1) for i in range(doms)]
    far_pairs = [(i, (i + 1 if i % 2 else i - 1) % doms) for i in range(doms)]
    params = pltpu.CompilerParams(vmem_limit_bytes=16 * 1024 * 1024)

    def call(body, name, ins, in_specs, outs, **kw):
        smem = [getattr(o, "memory_space", None) == pltpu.SMEM for o in outs]
        return pl.pallas_call(
            body,
            name=name,
            in_specs=in_specs + [VMEM] * (len(ins) - len(in_specs)),
            out_specs=[SMEM if s else VMEM for s in smem],
            out_shape=outs,
            compiler_params=params,
            **kw,
        )(*ins)

    def exchange(step, sends):
        got = [None] * plan.lanes
        arrived = []
        for d in range(plan.phases):
            send = sends[2 + d]
            if d:
                (send,) = call(
                    functools.partial(forward_kernel, plan, step, d),
                    f"forward{step}",
                    [send, *arrived],
                    [VMEM],
                    [plan.types(step)[2 + d]],
                    input_output_aliases={0: 0},
                )
            arrived.append(lax.ppermute(send, "sub", [(i, i ^ (1 << d)) for i in range(group)]))
            if d == 0:
                got[0] = lax.ppermute(sends[0], "dom", far_pairs)
        got[1] = lax.ppermute(sends[1], "dom", near_pairs)
        got[2:] = arrived
        return got

    sol_t = pltpu.VMEM((plan.quarter, plan.n, plan.w), f32)
    change_t = pltpu.VMEM((plan.quarter, plan.n, plan.w), jnp.bfloat16)
    resid_t = pltpu.VMEM(rhs.shape, f32)
    tables = [color, group_peer.T, group_list, dom_target.T, local_target.T]
    hbm = [pltpu.with_memory_space_constraint(a, pltpu.HBM) for a in tables + [rhs, diag_inv, coupling]]
    table_scratch = [tables[i].shape for i in (0, 4, 1, 2, 3)]
    table, tiles, diags, resid, sol, change, *sends = call(
        functools.partial(first_kernel, plan),
        "first",
        hbm,
        [HBM] * len(hbm),
        [
            pltpu.SMEM((plan.table,), jnp.int32),
            pltpu.VMEM(coupling.shape, coupling.dtype),
            pltpu.VMEM(diag_inv.shape, diag_inv.dtype),
            resid_t,
            sol_t,
            change_t,
        ]
        + plan.types(0),
        scratch_shapes=[pltpu.SMEM(shape, jnp.int32) for shape in table_scratch]
        + [pltpu.SemaphoreType.DMA((len(hbm),))],
    )
    sols = [sol]
    got = meta = None
    steps = SWEEPS * COLORS
    for step in range(steps):
        c = step % COLORS
        if step > 0:
            ins = [table, resid, diags, tiles, *got, *meta]
            if step >= COLORS:
                ins.append(sols[c])
            sol, change, *sends = call(
                functools.partial(step_kernel, plan, step),
                f"step{step}",
                ins,
                [SMEM],
                [sol_t, change_t] + plan.types(step),
            )
            sols[c:] = [sol] + sols[c + 1 :]
        last = step == steps - 1
        ins = [table, resid, tiles, change]
        if step > 0:
            ins += [*got, *meta]
        if last:
            ins += sols
        resid, *rest = call(
            functools.partial(local_kernel, plan, step, last),
            f"local{step}",
            ins,
            [SMEM],
            [resid_t] + ([jax.ShapeDtypeStruct(rhs.shape, f32)] if last else []),
            input_output_aliases={1: 0},
        )
        got = exchange(step, sends)
        if step == 0:
            meta = got
    (defect,) = call(
        functools.partial(final_kernel, plan, steps - 1),
        "final",
        [resid, *got, *meta],
        [],
        [jax.ShapeDtypeStruct(rhs.shape, f32)],
    )
    return rest[0], defect


def solution(mesh):
    placed = (
        P(("dom", "sub"), None, None, None),
        P(("dom", "sub"), None, None),
        P(("dom", "sub"), None, None),
        P(("dom", "sub")),
        P(("dom", "sub"), None),
        P(("dom", "sub"), None),
        P(("dom", "sub"), None, None),
        P(("dom", "sub"), None),
    )
    return jax.shard_map(
        on_device,
        mesh=mesh,
        in_specs=placed,
        out_specs=(P(("dom", "sub"), None, None), P(("dom", "sub"), None, None)),
        check_vma=False,
    )
```

time: 156 us -> 79.3 us (0.51)
  blocking collectives: 96.6 us -> 0 us
  waiting for transfers between devices: 0.05 us -> 52.5 us
  local copies, waits for them, and re-layouts: 22.4 us -> 0 us
  matrix products: 12 us -> 0 us
  Pallas kernels: 0 us -> 7.13 us
  other arithmetic: 5.23 us -> 0 us
    all_gather x10 -> x0, blocking collectives: 96.6 us -> none  [the longest x8 79.9 us: on_device(): lax.all_gather(group_terms.reshape(2 * quarter, rhs_count, block_width),...]
    ppermute x18 -> x32, waiting for transfers between devices: 0.05 us -> 52.5 us  [the longest x16 31.5 us: exchange(): lax.ppermute(send, 'sub', [(i, i ^ 1 << d) for i in range(group)])]
    dot_general x40 -> x0, matrix products: 12 us -> none  [the longest x8 5.01 us: on_device(): added = jnp.dot(selector, arrived_items, precision=lax.Precision.HIGHEST)]
    gather x9 -> x0, local copies, waits for them, and re-layouts: 9.86 us -> none  [the longest x1 2.24 us: on_device(): diag_inv[order_flat].reshape(COLORS, quarter, block_width, block_width)]
    unnamed x80 -> x0, local copies, waits for them, and re-layouts: 7.92 us -> none
    pallas_call x0 -> x25, Pallas kernels: none -> 7.13 us  [call(): pl.pallas_call(body, name=name, in_specs=in_specs + [VMEM] * (len(ins) -...]
    sort x2 -> x0, other arithmetic: 2.69 us -> none  [the longest x1 1.73 us: on_device(): order_flat = jnp.argsort(color, stable=True)]
    eq x16 -> x0, local copies, waits for them, and re-layouts: 2.02 us -> none  [the longest x8 0.86 us: on_device(): matches = gathered_peers[:, color_now].reshape(-1) == own_member]
  transfers between devices with their start and end apart: 18 -> 32, of which waited for: 0 -> 23; matrix products, arithmetic and copies ran while one was open for 15% -> 0% of each run, Pallas kernels for 0% -> 3%
where the time goes in v2:
time: 79.3 us; the launch traced here: 79.1 us
  waiting for transfers between devices  52.5 us (66%)
  starting transfers between devices  18.7 us (24%)
  Pallas kernels  7.13 us (9%)
    ppermute x16, waiting for transfers between devices, exchange(): lax.ppermute(send, 'sub', [(i, i ^ 1 << d) for i in range(group)])  31.5 us
    ppermute x8, waiting for transfers between devices, exchange(): got[0] = lax.ppermute(sends[0], 'dom', far_pairs)  20.9 us
    ppermute x16, starting transfers between devices, exchange(): lax.ppermute(send, 'sub', [(i, i ^ 1 << d) for i in range(group)])  16 us
    pallas_call x25, Pallas kernels, call(): pl.pallas_call(body, name=name, in_specs=in_specs + [VMEM] * (len(ins) -...  7.13 us
    ppermute x8, starting transfers between devices, exchange(): got[0] = lax.ppermute(sends[0], 'dom', far_pairs)  2.68 us
  transfers between devices with their start and end apart: 32, of which 23 were waited for; matrix products, arithmetic and copies ran while one was open for 0% of the time, Pallas kernels for 3%

profile of v2, /device:TPU:0, one launch (start us, length us, event | category | flops | bytes accessed | tf_op | source)
XLA Modules:
  0.0 79.1 jit_solution(6626209696676273580)
XLA Ops:
  0.6 1.8 %first.1 = (s32[40]{0:T(128)S(4)}, bf16[8,6,128,128]{3,2,1,0:T(8,128)(2,1)S(1)}, bf16[8,128,128]{2,1,0:T(8,128)(2,1)S(1)}, f32[8,64,128]{2,1,0:T(8,128)S(1)}, f3...) custom-call(s32[8]{0:T(128)} %refs_0_.1, ...), custom_call_target="tpu_custom_call" | custom-call | tf_op jit(solution)/shard_map/first/pallas_call | solution.py:217
  2.5 3.0 %collective-permute-start.2 = (f32[144,128]{1,0:T(8,128)S(1)}, f32[144,128]{1,0:T(8,128)S(1)}, u32[]{:S(2)}, u32[]{:S(2)}) collective-permute-start(f32[144,128]{1,0:T(8,128)S(1)} %get-tuple-element.63), channel_id=1, source_target_pairs={{0,1},{1,0},{2,3},{3,2},{4,5},{5,4},{6,7},{7,6},{8,9},{9,8},{10,11... | collective-permute-start | bytes 221192 | tf_op jit(solution)/shard_map/ppermute | solution.py:241
  5.5 2.3 %collective-permute-done.2.refs_1_.refs_2_.refs_6_ = f32[144,128]{1,0:T(8,128)S(1)} collective-permute-done((f32[144,128]{1,0:T(8,128)S(1)}, f32[144,128]{1,0:T(8,128)S(1)}, u32[]{:S(2)}, u32[]{:S(2)}) %collective-permute-start.2) | collective-permute-done | bytes 73760 | tf_op jit(solution)/shard_map/ppermute | solution.py:241
  7.8 2.0 %collective-permute-start.3 = (f32[144,128]{1,0:T(8,128)S(1)}, f32[144,128]{1,0:T(8,128)S(1)}, u32[]{:S(2)}, u32[]{:S(2)}) collective-permute-start(f32[144,128]{1,0:T(8,128)S(1)} %forward0.1), channel_id=1, source_target_pairs={{0,2},{1,3},{2,0},{3,1},{4,6},{5,7},{6,4},{7,5},{8,10},{9,11},{10,... | collective-permute-start | bytes 221192 | tf_op jit(solution)/shard_map/ppermute | solution.py:241
  9.9 1.6 %collective-permute-start = (f32[136,128]{1,0:T(8,128)S(1)}, f32[136,128]{1,0:T(8,128)S(1)}, u32[]{:S(2)}, u32[]{:S(2)}) collective-permute-start(f32[136,128]{1,0:T(8,128)S(1)} %get-tuple-element.61), channel_id=1, source_target_pairs={{0,28},{4,8},{8,4},{12,16},{16,12},{20,24},{24,20},{28,0},{1,29},{... | collective-permute-start | bytes 208904 | tf_op jit(solution)/shard_map/ppermute | solution.py:243
  11.7 4.2 %collective-permute-done.refs_0_.refs_4_ = f32[136,128]{1,0:T(8,128)S(1)} collective-permute-done((f32[136,128]{1,0:T(8,128)S(1)}, f32[136,128]{1,0:T(8,128)S(1)}, u32[]{:S(2)}, u32[]{:S(2)}) %collective-permute-start) | collective-permute-done | bytes 69664 | tf_op jit(solution)/shard_map/ppermute | solution.py:243
  15.9 0.3 step1.1
  16.2 1.6 %collective-permute-start.6 = (f32[128,128]{1,0:T(8,128)S(1)}, f32[128,128]{1,0:T(8,128)S(1)}, u32[]{:S(2)}, u32[]{:S(2)}) collective-permute-start(f32[128,128]{1,0:T(8,128)S(1)} %get-tuple-element.68), channel_id=1, source_target_pairs={{0,1},{1,0},{2,3},{3,2},{4,5},{5,4},{6,7},{7,6},{8,9},{9,8},{10,11... | collective-permute-start | bytes 196616 | tf_op jit(solution)/shard_map/ppermute | solution.py:241
  17.8 1.1 %collective-permute-start.4 = (f32[128,128]{1,0:T(8,128)S(1)}, f32[128,128]{1,0:T(8,128)S(1)}, u32[]{:S(2)}, u32[]{:S(2)}) collective-permute-start(f32[128,128]{1,0:T(8,128)S(1)} %get-tuple-element.66), channel_id=1, source_target_pairs={{0,28},{4,8},{8,4},{12,16},{16,12},{20,24},{24,20},{28,0},{1,29},{... | collective-permute-start | bytes 196616 | tf_op jit(solution)/shard_map/ppermute | solution.py:243
  18.8 1.7 %collective-permute-done.6.refs_1_.refs_2_ = f32[128,128]{1,0:T(8,128)S(1)} collective-permute-done((f32[128,128]{1,0:T(8,128)S(1)}, f32[128,128]{1,0:T(8,128)S(1)}, u32[]{:S(2)}, u32[]{:S(2)}) %collective-permute-start.6) | collective-permute-done | bytes 65568 | tf_op jit(solution)/shard_map/ppermute | solution.py:241
  20.8 2.5 %collective-permute-done.4.refs_0_ = f32[128,128]{1,0:T(8,128)S(1)} collective-permute-done((f32[128,128]{1,0:T(8,128)S(1)}, f32[128,128]{1,0:T(8,128)S(1)}, u32[]{:S(2)}, u32[]{:S(2)}) %collective-permute-start.4) | collective-permute-done | bytes 65568 | tf_op jit(solution)/shard_map/ppermute | solution.py:243
  23.3 1.6 %collective-permute-done.7.refs_3_ = f32[128,128]{1,0:T(8,128)S(1)} collective-permute-done((f32[128,128]{1,0:T(8,128)S(1)}, f32[128,128]{1,0:T(8,128)S(1)}, u32[]{:S(2)}, u32[]{:S(2)}) %collective-permute-start.7) | collective-permute-done | bytes 65568 | tf_op jit(solution)/shard_map/ppermute | solution.py:241
  24.8 0.3 step2.1
  25.1 1.6 %collective-permute-start.10 = (f32[128,128]{1,0:T(8,128)S(1)}, f32[128,128]{1,0:T(8,128)S(1)}, u32[]{:S(2)}, u32[]{:S(2)}) collective-permute-start(f32[128,128]{1,0:T(8,128)S(1)} %get-tuple-element.73), channel_id=1, source_target_pairs={{0,1},{1,0},{2,3},{3,2},{4,5},{5,4},{6,7},{7,6},{8,9},{9,8},{10,11... | collective-permute-start | bytes 196616 | tf_op jit(solution)/shard_map/ppermute | solution.py:241
  26.7 2.8 %collective-permute-done.10.refs_1_.refs_2_ = f32[128,128]{1,0:T(8,128)S(1)} collective-permute-done((f32[128,128]{1,0:T(8,128)S(1)}, f32[128,128]{1,0:T(8,128)S(1)}, u32[]{:S(2)}, u32[]{:S(2)}) %collective-permute-start.10) | collective-permute-done | bytes 65568 | tf_op jit(solution)/shard_map/ppermute | solution.py:241
  29.5 0.2 local2.1.resid
  29.7 2.5 %collective-permute-done.8.refs_0_ = f32[128,128]{1,0:T(8,128)S(1)} collective-permute-done((f32[128,128]{1,0:T(8,128)S(1)}, f32[128,128]{1,0:T(8,128)S(1)}, u32[]{:S(2)}, u32[]{:S(2)}) %collective-permute-start.8) | collective-permute-done | bytes 65568 | tf_op jit(solution)/shard_map/ppermute | solution.py:243
  32.2 1.6 %collective-permute-done.11.refs_3_ = f32[128,128]{1,0:T(8,128)S(1)} collective-permute-done((f32[128,128]{1,0:T(8,128)S(1)}, f32[128,128]{1,0:T(8,128)S(1)}, u32[]{:S(2)}, u32[]{:S(2)}) %collective-permute-start.11) | collective-permute-done | bytes 65568 | tf_op jit(solution)/shard_map/ppermute | solution.py:241
  33.7 0.3 step3.1
  34.0 1.6 %collective-permute-start.14 = (f32[128,128]{1,0:T(8,128)S(1)}, f32[128,128]{1,0:T(8,128)S(1)}, u32[]{:S(2)}, u32[]{:S(2)}) collective-permute-start(f32[128,128]{1,0:T(8,128)S(1)} %get-tuple-element.78), channel_id=1, source_target_pairs={{0,1},{1,0},{2,3},{3,2},{4,5},{5,4},{6,7},{7,6},{8,9},{9,8},{10,11... | collective-permute-start | bytes 196616 | tf_op jit(solution)/shard_map/ppermute | solution.py:241
  35.6 2.8 %collective-permute-done.14.refs_1_.refs_2_ = f32[128,128]{1,0:T(8,128)S(1)} collective-permute-done((f32[128,128]{1,0:T(8,128)S(1)}, f32[128,128]{1,0:T(8,128)S(1)}, u32[]{:S(2)}, u32[]{:S(2)}) %collective-permute-start.14) | collective-permute-done | bytes 65568 | tf_op jit(solution)/shard_map/ppermute | solution.py:241
  38.4 0.2 local3.1.resid
  38.6 2.5 %collective-permute-done.12.refs_0_ = f32[128,128]{1,0:T(8,128)S(1)} collective-permute-done((f32[128,128]{1,0:T(8,128)S(1)}, f32[128,128]{1,0:T(8,128)S(1)}, u32[]{:S(2)}, u32[]{:S(2)}) %collective-permute-start.12) | collective-permute-done | bytes 65568 | tf_op jit(solution)/shard_map/ppermute | solution.py:243
  41.1 1.6 %collective-permute-done.15.refs_3_ = f32[128,128]{1,0:T(8,128)S(1)} collective-permute-done((f32[128,128]{1,0:T(8,128)S(1)}, f32[128,128]{1,0:T(8,128)S(1)}, u32[]{:S(2)}, u32[]{:S(2)}) %collective-permute-start.15) | collective-permute-done | bytes 65568 | tf_op jit(solution)/shard_map/ppermute | solution.py:241
  42.6 0.3 step4.1
  42.9 1.6 %collective-permute-start.18 = (f32[128,128]{1,0:T(8,128)S(1)}, f32[128,128]{1,0:T(8,128)S(1)}, u32[]{:S(2)}, u32[]{:S(2)}) collective-permute-start(f32[128,128]{1,0:T(8,128)S(1)} %get-tuple-element.84), channel_id=1, source_target_pairs={{0,1},{1,0},{2,3},{3,2},{4,5},{5,4},{6,7},{7,6},{8,9},{9,8},{10,11... | collective-permute-start | bytes 196616 | tf_op jit(solution)/shard_map/ppermute | solution.py:241
  44.5 2.8 %collective-permute-done.18.refs_1_.refs_2_ = f32[128,128]{1,0:T(8,128)S(1)} collective-permute-done((f32[128,128]{1,0:T(8,128)S(1)}, f32[128,128]{1,0:T(8,128)S(1)}, u32[]{:S(2)}, u32[]{:S(2)}) %collective-permute-start.18) | collective-permute-done | bytes 65568 | tf_op jit(solution)/shard_map/ppermute | solution.py:241
  47.3 0.2 local4.1.resid
  47.5 2.5 %collective-permute-done.16.refs_0_ = f32[128,128]{1,0:T(8,128)S(1)} collective-permute-done((f32[128,128]{1,0:T(8,128)S(1)}, f32[128,128]{1,0:T(8,128)S(1)}, u32[]{:S(2)}, u32[]{:S(2)}) %collective-permute-start.16) | collective-permute-done | bytes 65568 | tf_op jit(solution)/shard_map/ppermute | solution.py:243
  50.0 1.6 %collective-permute-done.19.refs_3_ = f32[128,128]{1,0:T(8,128)S(1)} collective-permute-done((f32[128,128]{1,0:T(8,128)S(1)}, f32[128,128]{1,0:T(8,128)S(1)}, u32[]{:S(2)}, u32[]{:S(2)}) %collective-permute-start.19) | collective-permute-done | bytes 65568 | tf_op jit(solution)/shard_map/ppermute | solution.py:241
  51.5 0.3 step5.1
  51.8 1.6 %collective-permute-start.22 = (f32[128,128]{1,0:T(8,128)S(1)}, f32[128,128]{1,0:T(8,128)S(1)}, u32[]{:S(2)}, u32[]{:S(2)}) collective-permute-start(f32[128,128]{1,0:T(8,128)S(1)} %get-tuple-element.90), channel_id=1, source_target_pairs={{0,1},{1,0},{2,3},{3,2},{4,5},{5,4},{6,7},{7,6},{8,9},{9,8},{10,11... | collective-permute-start | bytes 196616 | tf_op jit(solution)/shard_map/ppermute | solution.py:241
  53.4 2.8 %collective-permute-done.22.refs_1_.refs_2_ = f32[128,128]{1,0:T(8,128)S(1)} collective-permute-done((f32[128,128]{1,0:T(8,128)S(1)}, f32[128,128]{1,0:T(8,128)S(1)}, u32[]{:S(2)}, u32[]{:S(2)}) %collective-permute-start.22) | collective-permute-done | bytes 65568 | tf_op jit(solution)/shard_map/ppermute | solution.py:241
  56.4 2.5 %collective-permute-done.20.refs_0_ = f32[128,128]{1,0:T(8,128)S(1)} collective-permute-done((f32[128,128]{1,0:T(8,128)S(1)}, f32[128,128]{1,0:T(8,128)S(1)}, u32[]{:S(2)}, u32[]{:S(2)}) %collective-permute-start.20) | collective-permute-done | bytes 65568 | tf_op jit(solution)/shard_map/ppermute | solution.py:243
  58.9 1.6 %collective-permute-done.23.refs_3_ = f32[128,128]{1,0:T(8,128)S(1)} collective-permute-done((f32[128,128]{1,0:T(8,128)S(1)}, f32[128,128]{1,0:T(8,128)S(1)}, u32[]{:S(2)}, u32[]{:S(2)}) %collective-permute-start.23) | collective-permute-done | bytes 65568 | tf_op jit(solution)/shard_map/ppermute | solution.py:241
  60.4 0.3 step6.1
  60.7 1.6 %collective-permute-start.26 = (f32[128,128]{1,0:T(8,128)S(1)}, f32[128,128]{1,0:T(8,128)S(1)}, u32[]{:S(2)}, u32[]{:S(2)}) collective-permute-start(f32[128,128]{1,0:T(8,128)S(1)} %get-tuple-element.96), channel_id=1, source_target_pairs={{0,1},{1,0},{2,3},{3,2},{4,5},{5,4},{6,7},{7,6},{8,9},{9,8},{10,11... | collective-permute-start | bytes 196616 | tf_op jit(solution)/shard_map/ppermute | solution.py:241
  62.3 2.8 %collective-permute-done.26.refs_1_.refs_2_ = f32[128,128]{1,0:T(8,128)S(1)} collective-permute-done((f32[128,128]{1,0:T(8,128)S(1)}, f32[128,128]{1,0:T(8,128)S(1)}, u32[]{:S(2)}, u32[]{:S(2)}) %collective-permute-start.26) | collective-permute-done | bytes 65568 | tf_op jit(solution)/shard_map/ppermute | solution.py:241
  65.1 0.2 local6.1.resid
  65.3 2.5 %collective-permute-done.24.refs_0_ = f32[128,128]{1,0:T(8,128)S(1)} collective-permute-done((f32[128,128]{1,0:T(8,128)S(1)}, f32[128,128]{1,0:T(8,128)S(1)}, u32[]{:S(2)}, u32[]{:S(2)}) %collective-permute-start.24) | collective-permute-done | bytes 65568 | tf_op jit(solution)/shard_map/ppermute | solution.py:243
  67.8 1.6 %collective-permute-done.27.refs_3_ = f32[128,128]{1,0:T(8,128)S(1)} collective-permute-done((f32[128,128]{1,0:T(8,128)S(1)}, f32[128,128]{1,0:T(8,128)S(1)}, u32[]{:S(2)}, u32[]{:S(2)}) %collective-permute-start.27) | collective-permute-done | bytes 65568 | tf_op jit(solution)/shard_map/ppermute | solution.py:241
  69.3 0.3 step7.1
  69.7 1.6 %collective-permute-start.30 = (f32[128,128]{1,0:T(8,128)S(1)}, f32[128,128]{1,0:T(8,128)S(1)}, u32[]{:S(2)}, u32[]{:S(2)}) collective-permute-start(f32[128,128]{1,0:T(8,128)S(1)} %get-tuple-element.108), channel_id=1, source_target_pairs={{0,1},{1,0},{2,3},{3,2},{4,5},{5,4},{6,7},{7,6},{8,9},{9,8},{10,11... | collective-permute-start | bytes 196616 | tf_op jit(solution)/shard_map/ppermute | solution.py:241
  71.2 2.8 %collective-permute-done.30.refs_1_.refs_2_ = f32[128,128]{1,0:T(8,128)S(1)} collective-permute-done((f32[128,128]{1,0:T(8,128)S(1)}, f32[128,128]{1,0:T(8,128)S(1)}, u32[]{:S(2)}, u32[]{:S(2)}) %collective-permute-start.30) | collective-permute-done | bytes 65568 | tf_op jit(solution)/shard_map/ppermute | solution.py:241
  74.0 0.9 %local7.1 = (f32[8,64,128]{2,1,0:T(8,128)S(1)}, f32[8,64,128]{2,1,0:T(8,128)}) custom-call(s32[40]{0:T(128)S(4)} %get-tuple-element.56.table, f32[8,64,128]{2,1,0:T(8,128)S(1)} %local6.1.resid, bf16[8,6,128,128]{3,2,1,0:T(8,128)(2,1)S(1)} %get-tuple-element.58.coupling, ...), custom_call_target="tpu_custom_call", output_to_operand_aliasing={{0}: (1, {})} | custom-call | tf_op jit(solution)/shard_map/local7/pallas_call | solution.py:217
  74.9 1.8 %collective-permute-done.28.refs_0_ = f32[128,128]{1,0:T(8,128)S(1)} collective-permute-done((f32[128,128]{1,0:T(8,128)S(1)}, f32[128,128]{1,0:T(8,128)S(1)}, u32[]{:S(2)}, u32[]{:S(2)}) %collective-permute-start.28) | collective-permute-done | bytes 65568 | tf_op jit(solution)/shard_map/ppermute | solution.py:243
  76.7 1.6 %collective-permute-done.31.refs_3_ = f32[128,128]{1,0:T(8,128)S(1)} collective-permute-done((f32[128,128]{1,0:T(8,128)S(1)}, f32[128,128]{1,0:T(8,128)S(1)}, u32[]{:S(2)}, u32[]{:S(2)}) %collective-permute-start.31) | collective-permute-done | bytes 65568 | tf_op jit(solution)/shard_map/ppermute | solution.py:241
  78.3 0.9 %final.1 = f32[8,64,128]{2,1,0:T(8,128)} custom-call(f32[8,64,128]{2,1,0:T(8,128)S(1)} %get-tuple-element.105.resid, f32[128,128]{1,0:T(8,128)S(1)} %collective-permute-done.28.refs_0_, f32[128,128]{1,0:T(8,128)S(1)} %collective-permute-done.29.refs_1_, f32[128,128]{1,0:T(8,128)S(1)} %collective-permute-done.30.refs_1_.refs_2_, ...), custom_call_target="tpu_custom_call" | custom-call | tf_op jit(solution)/shard_map/final/pallas_call | solution.py:217
  (41 shorter events, 0.8 us)
Async XLA Ops:
  2.5 5.3 %collective-permute-start.2 = (f32[144,128]{1,0:T(8,128)S(1)}, f32[144,128]{1,0:T(8,128)S(1)}, u32[]{:S(2)}, u32[]{:S(2)}) collective-permute-start(f32[144,128]{1,0:T(8,128)S(1)} %get-tuple-element.63), channel_id=1, source_target_pairs={{0,1},{1,0},{2,3},{3,2},{4,5},{5,4},{6,7},{7,6},{8,9},{9,8},{10,11... | collective-permute-start | bytes 221192 | tf_op jit(solution)/shard_map/ppermute | solution.py:241
  7.8 8.1 %collective-permute-start.3 = (f32[144,128]{1,0:T(8,128)S(1)}, f32[144,128]{1,0:T(8,128)S(1)}, u32[]{:S(2)}, u32[]{:S(2)}) collective-permute-start(f32[144,128]{1,0:T(8,128)S(1)} %forward0.1), channel_id=1, source_target_pairs={{0,2},{1,3},{2,0},{3,1},{4,6},{5,7},{6,4},{7,5},{8,10},{9,11},{10,... | collective-permute-start | bytes 221192 | tf_op jit(solution)/shard_map/ppermute | solution.py:241
  9.9 6.0 %collective-permute-start = (f32[136,128]{1,0:T(8,128)S(1)}, f32[136,128]{1,0:T(8,128)S(1)}, u32[]{:S(2)}, u32[]{:S(2)}) collective-permute-start(f32[136,128]{1,0:T(8,128)S(1)} %get-tuple-element.61), channel_id=1, source_target_pairs={{0,28},{4,8},{8,4},{12,16},{16,12},{20,24},{24,20},{28,0},{1,29},{... | collective-permute-start | bytes 208904 | tf_op jit(solution)/shard_map/ppermute | solution.py:243
  11.5 4.4 %collective-permute-start.1 = (f32[136,128]{1,0:T(8,128)S(1)}, f32[136,128]{1,0:T(8,128)S(1)}, u32[]{:S(2)}, u32[]{:S(2)}) collective-permute-start(f32[136,128]{1,0:T(8,128)S(1)} %get-tuple-element.62), channel_id=1, source_target_pairs={{0,4},{4,0},{8,12},{12,8},{16,20},{20,16},{24,28},{28,24},{1,5},{5... | collective-permute-start | bytes 208904 | tf_op jit(solution)/shard_map/ppermute | solution.py:244
  16.2 4.3 %collective-permute-start.6 = (f32[128,128]{1,0:T(8,128)S(1)}, f32[128,128]{1,0:T(8,128)S(1)}, u32[]{:S(2)}, u32[]{:S(2)}) collective-permute-start(f32[128,128]{1,0:T(8,128)S(1)} %get-tuple-element.68), channel_id=1, source_target_pairs={{0,1},{1,0},{2,3},{3,2},{4,5},{5,4},{6,7},{7,6},{8,9},{9,8},{10,11... | collective-permute-start | bytes 196616 | tf_op jit(solution)/shard_map/ppermute | solution.py:241
  17.8 5.5 %collective-permute-start.4 = (f32[128,128]{1,0:T(8,128)S(1)}, f32[128,128]{1,0:T(8,128)S(1)}, u32[]{:S(2)}, u32[]{:S(2)}) collective-permute-start(f32[128,128]{1,0:T(8,128)S(1)} %get-tuple-element.66), channel_id=1, source_target_pairs={{0,28},{4,8},{8,4},{12,16},{16,12},{20,24},{24,20},{28,0},{1,29},{... | collective-permute-start | bytes 196616 | tf_op jit(solution)/shard_map/ppermute | solution.py:243
  18.8 4.4 %collective-permute-start.5 = (f32[128,128]{1,0:T(8,128)S(1)}, f32[128,128]{1,0:T(8,128)S(1)}, u32[]{:S(2)}, u32[]{:S(2)}) collective-permute-start(f32[128,128]{1,0:T(8,128)S(1)} %get-tuple-element.67), channel_id=1, source_target_pairs={{0,4},{4,0},{8,12},{12,8},{16,20},{20,16},{24,28},{28,24},{1,5},{5... | collective-permute-start | bytes 196616 | tf_op jit(solution)/shard_map/ppermute | solution.py:244
  20.5 4.3 %collective-permute-start.7 = (f32[128,128]{1,0:T(8,128)S(1)}, f32[128,128]{1,0:T(8,128)S(1)}, u32[]{:S(2)}, u32[]{:S(2)}) collective-permute-start(f32[128,128]{1,0:T(8,128)S(1)} %forward1.1), channel_id=1, source_target_pairs={{0,2},{1,3},{2,0},{3,1},{4,6},{5,7},{6,4},{7,5},{8,10},{9,11},{10,... | collective-permute-start | bytes 196616 | tf_op jit(solution)/shard_map/ppermute | solution.py:241
  25.1 4.3 %collective-permute-start.10 = (f32[128,128]{1,0:T(8,128)S(1)}, f32[128,128]{1,0:T(8,128)S(1)}, u32[]{:S(2)}, u32[]{:S(2)}) collective-permute-start(f32[128,128]{1,0:T(8,128)S(1)} %get-tuple-element.73), channel_id=1, source_target_pairs={{0,1},{1,0},{2,3},{3,2},{4,5},{5,4},{6,7},{7,6},{8,9},{9,8},{10,11... | collective-permute-start | bytes 196616 | tf_op jit(solution)/shard_map/ppermute | solution.py:241
  26.7 5.5 %collective-permute-start.8 = (f32[128,128]{1,0:T(8,128)S(1)}, f32[128,128]{1,0:T(8,128)S(1)}, u32[]{:S(2)}, u32[]{:S(2)}) collective-permute-start(f32[128,128]{1,0:T(8,128)S(1)} %get-tuple-element.71), channel_id=1, source_target_pairs={{0,28},{4,8},{8,4},{12,16},{16,12},{20,24},{24,20},{28,0},{1,29},{... | collective-permute-start | bytes 196616 | tf_op jit(solution)/shard_map/ppermute | solution.py:243
  26.7 5.5 %collective-permute-start.9 = (f32[128,128]{1,0:T(8,128)S(1)}, f32[128,128]{1,0:T(8,128)S(1)}, u32[]{:S(2)}, u32[]{:S(2)}) collective-permute-start(f32[128,128]{1,0:T(8,128)S(1)} %get-tuple-element.72), channel_id=1, source_target_pairs={{0,4},{4,0},{8,12},{12,8},{16,20},{20,16},{24,28},{28,24},{1,5},{5... | collective-permute-start | bytes 196616 | tf_op jit(solution)/shard_map/ppermute | solution.py:244
  29.4 4.3 %collective-permute-start.11 = (f32[128,128]{1,0:T(8,128)S(1)}, f32[128,128]{1,0:T(8,128)S(1)}, u32[]{:S(2)}, u32[]{:S(2)}) collective-permute-start(f32[128,128]{1,0:T(8,128)S(1)} %forward2.1), channel_id=1, source_target_pairs={{0,2},{1,3},{2,0},{3,1},{4,6},{5,7},{6,4},{7,5},{8,10},{9,11},{10,... | collective-permute-start | bytes 196616 | tf_op jit(solution)/shard_map/ppermute | solution.py:241
  34.0 4.3 %collective-permute-start.14 = (f32[128,128]{1,0:T(8,128)S(1)}, f32[128,128]{1,0:T(8,128)S(1)}, u32[]{:S(2)}, u32[]{:S(2)}) collective-permute-start(f32[128,128]{1,0:T(8,128)S(1)} %get-tuple-element.78), channel_id=1, source_target_pairs={{0,1},{1,0},{2,3},{3,2},{4,5},{5,4},{6,7},{7,6},{8,9},{9,8},{10,11... | collective-permute-start | bytes 196616 | tf_op jit(solution)/shard_map/ppermute | solution.py:241
  35.6 5.5 %collective-permute-start.12 = (f32[128,128]{1,0:T(8,128)S(1)}, f32[128,128]{1,0:T(8,128)S(1)}, u32[]{:S(2)}, u32[]{:S(2)}) collective-permute-start(f32[128,128]{1,0:T(8,128)S(1)} %get-tuple-element.76), channel_id=1, source_target_pairs={{0,28},{4,8},{8,4},{12,16},{16,12},{20,24},{24,20},{28,0},{1,29},{... | collective-permute-start | bytes 196616 | tf_op jit(solution)/shard_map/ppermute | solution.py:243
  35.6 5.5 %collective-permute-start.13 = (f32[128,128]{1,0:T(8,128)S(1)}, f32[128,128]{1,0:T(8,128)S(1)}, u32[]{:S(2)}, u32[]{:S(2)}) collective-permute-start(f32[128,128]{1,0:T(8,128)S(1)} %get-tuple-element.77), channel_id=1, source_target_pairs={{0,4},{4,0},{8,12},{12,8},{16,20},{20,16},{24,28},{28,24},{1,5},{5... | collective-permute-start | bytes 196616 | tf_op jit(solution)/shard_map/ppermute | solution.py:244
  38.4 4.3 %collective-permute-start.15 = (f32[128,128]{1,0:T(8,128)S(1)}, f32[128,128]{1,0:T(8,128)S(1)}, u32[]{:S(2)}, u32[]{:S(2)}) collective-permute-start(f32[128,128]{1,0:T(8,128)S(1)} %forward3.1), channel_id=1, source_target_pairs={{0,2},{1,3},{2,0},{3,1},{4,6},{5,7},{6,4},{7,5},{8,10},{9,11},{10,... | collective-permute-start | bytes 196616 | tf_op jit(solution)/shard_map/ppermute | solution.py:241
  42.9 4.3 %collective-permute-start.18 = (f32[128,128]{1,0:T(8,128)S(1)}, f32[128,128]{1,0:T(8,128)S(1)}, u32[]{:S(2)}, u32[]{:S(2)}) collective-permute-start(f32[128,128]{1,0:T(8,128)S(1)} %get-tuple-element.84), channel_id=1, source_target_pairs={{0,1},{1,0},{2,3},{3,2},{4,5},{5,4},{6,7},{7,6},{8,9},{9,8},{10,11... | collective-permute-start | bytes 196616 | tf_op jit(solution)/shard_map/ppermute | solution.py:241
  44.5 5.5 %collective-permute-start.16 = (f32[128,128]{1,0:T(8,128)S(1)}, f32[128,128]{1,0:T(8,128)S(1)}, u32[]{:S(2)}, u32[]{:S(2)}) collective-permute-start(f32[128,128]{1,0:T(8,128)S(1)} %get-tuple-element.82), channel_id=1, source_target_pairs={{0,28},{4,8},{8,4},{12,16},{16,12},{20,24},{24,20},{28,0},{1,29},{... | collective-permute-start | bytes 196616 | tf_op jit(solution)/shard_map/ppermute | solution.py:243
  44.5 5.5 %collective-permute-start.17 = (f32[128,128]{1,0:T(8,128)S(1)}, f32[128,128]{1,0:T(8,128)S(1)}, u32[]{:S(2)}, u32[]{:S(2)}) collective-permute-start(f32[128,128]{1,0:T(8,128)S(1)} %get-tuple-element.83), channel_id=1, source_target_pairs={{0,4},{4,0},{8,12},{12,8},{16,20},{20,16},{24,28},{28,24},{1,5},{5... | collective-permute-start | bytes 196616 | tf_op jit(solution)/shard_map/ppermute | solution.py:244
  47.3 4.3 %collective-permute-start.19 = (f32[128,128]{1,0:T(8,128)S(1)}, f32[128,128]{1,0:T(8,128)S(1)}, u32[]{:S(2)}, u32[]{:S(2)}) collective-permute-start(f32[128,128]{1,0:T(8,128)S(1)} %forward4.1), channel_id=1, source_target_pairs={{0,2},{1,3},{2,0},{3,1},{4,6},{5,7},{6,4},{7,5},{8,10},{9,11},{10,... | collective-permute-start | bytes 196616 | tf_op jit(solution)/shard_map/ppermute | solution.py:241
  51.8 4.3 %collective-permute-start.22 = (f32[128,128]{1,0:T(8,128)S(1)}, f32[128,128]{1,0:T(8,128)S(1)}, u32[]{:S(2)}, u32[]{:S(2)}) collective-permute-start(f32[128,128]{1,0:T(8,128)S(1)} %get-tuple-element.90), channel_id=1, source_target_pairs={{0,1},{1,0},{2,3},{3,2},{4,5},{5,4},{6,7},{7,6},{8,9},{9,8},{10,11... | collective-permute-start | bytes 196616 | tf_op jit(solution)/shard_map/ppermute | solution.py:241
  53.4 5.5 %collective-permute-start.20 = (f32[128,128]{1,0:T(8,128)S(1)}, f32[128,128]{1,0:T(8,128)S(1)}, u32[]{:S(2)}, u32[]{:S(2)}) collective-permute-start(f32[128,128]{1,0:T(8,128)S(1)} %get-tuple-element.88), channel_id=1, source_target_pairs={{0,28},{4,8},{8,4},{12,16},{16,12},{20,24},{24,20},{28,0},{1,29},{... | collective-permute-start | bytes 196616 | tf_op jit(solution)/shard_map/ppermute | solution.py:243
  53.4 5.5 %collective-permute-start.21 = (f32[128,128]{1,0:T(8,128)S(1)}, f32[128,128]{1,0:T(8,128)S(1)}, u32[]{:S(2)}, u32[]{:S(2)}) collective-permute-start(f32[128,128]{1,0:T(8,128)S(1)} %get-tuple-element.89), channel_id=1, source_target_pairs={{0,4},{4,0},{8,12},{12,8},{16,20},{20,16},{24,28},{28,24},{1,5},{5... | collective-permute-start | bytes 196616 | tf_op jit(solution)/shard_map/ppermute | solution.py:244
  56.2 4.3 %collective-permute-start.23 = (f32[128,128]{1,0:T(8,128)S(1)}, f32[128,128]{1,0:T(8,128)S(1)}, u32[]{:S(2)}, u32[]{:S(2)}) collective-permute-start(f32[128,128]{1,0:T(8,128)S(1)} %forward5.1), channel_id=1, source_target_pairs={{0,2},{1,3},{2,0},{3,1},{4,6},{5,7},{6,4},{7,5},{8,10},{9,11},{10,... | collective-permute-start | bytes 196616 | tf_op jit(solution)/shard_map/ppermute | solution.py:241
  60.7 4.3 %collective-permute-start.26 = (f32[128,128]{1,0:T(8,128)S(1)}, f32[128,128]{1,0:T(8,128)S(1)}, u32[]{:S(2)}, u32[]{:S(2)}) collective-permute-start(f32[128,128]{1,0:T(8,128)S(1)} %get-tuple-element.96), channel_id=1, source_target_pairs={{0,1},{1,0},{2,3},{3,2},{4,5},{5,4},{6,7},{7,6},{8,9},{9,8},{10,11... | collective-permute-start | bytes 196616 | tf_op jit(solution)/shard_map/ppermute | solution.py:241
  62.3 5.5 %collective-permute-start.24 = (f32[128,128]{1,0:T(8,128)S(1)}, f32[128,128]{1,0:T(8,128)S(1)}, u32[]{:S(2)}, u32[]{:S(2)}) collective-permute-start(f32[128,128]{1,0:T(8,128)S(1)} %get-tuple-element.94), channel_id=1, source_target_pairs={{0,28},{4,8},{8,4},{12,16},{16,12},{20,24},{24,20},{28,0},{1,29},{... | collective-permute-start | bytes 196616 | tf_op jit(solution)/shard_map/ppermute | solution.py:243
  62.3 5.5 %collective-permute-start.25 = (f32[128,128]{1,0:T(8,128)S(1)}, f32[128,128]{1,0:T(8,128)S(1)}, u32[]{:S(2)}, u32[]{:S(2)}) collective-permute-start(f32[128,128]{1,0:T(8,128)S(1)} %get-tuple-element.95), channel_id=1, source_target_pairs={{0,4},{4,0},{8,12},{12,8},{16,20},{20,16},{24,28},{28,24},{1,5},{5... | collective-permute-start | bytes 196616 | tf_op jit(solution)/shard_map/ppermute | solution.py:244
  65.1 4.3 %collective-permute-start.27 = (f32[128,128]{1,0:T(8,128)S(1)}, f32[128,128]{1,0:T(8,128)S(1)}, u32[]{:S(2)}, u32[]{:S(2)}) collective-permute-start(f32[128,128]{1,0:T(8,128)S(1)} %forward6.1), channel_id=1, source_target_pairs={{0,2},{1,3},{2,0},{3,1},{4,6},{5,7},{6,4},{7,5},{8,10},{9,11},{10,... | collective-permute-start | bytes 196616 | tf_op jit(solution)/shard_map/ppermute | solution.py:241
  69.7 4.3 %collective-permute-start.30 = (f32[128,128]{1,0:T(8,128)S(1)}, f32[128,128]{1,0:T(8,128)S(1)}, u32[]{:S(2)}, u32[]{:S(2)}) collective-permute-start(f32[128,128]{1,0:T(8,128)S(1)} %get-tuple-element.108), channel_id=1, source_target_pairs={{0,1},{1,0},{2,3},{3,2},{4,5},{5,4},{6,7},{7,6},{8,9},{9,8},{10,11... | collective-permute-start | bytes 196616 | tf_op jit(solution)/shard_map/ppermute | solution.py:241
  71.2 5.5 %collective-permute-start.28 = (f32[128,128]{1,0:T(8,128)S(1)}, f32[128,128]{1,0:T(8,128)S(1)}, u32[]{:S(2)}, u32[]{:S(2)}) collective-permute-start(f32[128,128]{1,0:T(8,128)S(1)} %get-tuple-element.106), channel_id=1, source_target_pairs={{0,28},{4,8},{8,4},{12,16},{16,12},{20,24},{24,20},{28,0},{1,29},{... | collective-permute-start | bytes 196616 | tf_op jit(solution)/shard_map/ppermute | solution.py:243
  71.2 5.5 %collective-permute-start.29 = (f32[128,128]{1,0:T(8,128)S(1)}, f32[128,128]{1,0:T(8,128)S(1)}, u32[]{:S(2)}, u32[]{:S(2)}) collective-permute-start(f32[128,128]{1,0:T(8,128)S(1)} %get-tuple-element.107), channel_id=1, source_target_pairs={{0,4},{4,0},{8,12},{12,8},{16,20},{20,16},{24,28},{28,24},{1,5},{5... | collective-permute-start | bytes 196616 | tf_op jit(solution)/shard_map/ppermute | solution.py:244
  74.0 4.3 %collective-permute-start.31 = (f32[128,128]{1,0:T(8,128)S(1)}, f32[128,128]{1,0:T(8,128)S(1)}, u32[]{:S(2)}, u32[]{:S(2)}) collective-permute-start(f32[128,128]{1,0:T(8,128)S(1)} %forward7.1), channel_id=1, source_target_pairs={{0,2},{1,3},{2,0},{3,1},{4,6},{5,7},{6,4},{7,5},{8,10},{9,11},{10,... | collective-permute-start | bytes 196616 | tf_op jit(solution)/shard_map/ppermute | solution.py:241

commit v3 on v2

--- a/solution.py
+++ b/solution.py
@@ -24,9 +24,7 @@
     def __init__(self, rows, rhs_count, width, group):
         self.rows, self.n, self.w, self.group = rows, rhs_count, width, group
         self.quarter = rows // COLORS
-        self.phases = group.bit_length() - 1
-        self.lanes = 2 + self.phases
-        self.carried = [[s for s in range(1, group) if s >> d & 1] for d in range(self.phases)]
+        self.lanes = 3
         self.order, self.local, self.slot = 0, rows, 3 * rows
         self.table = 5 * rows
         self.dom_meta = -(-rows // 8) * 8
@@ -34,22 +32,20 @@
     def stride(self, step):
         return self.n + (META if step == 0 else 0)
 
-    def at(self, s, phase, step):
-        return self.carried[phase].index(s) * self.stride(step)
+    def at(self, member, step):
+        return member * self.stride(step)
 
     def types(self, step):
         dom = self.quarter * self.n + (self.dom_meta if step == 0 else 0)
-        shapes = [dom, dom] + [len(c) * self.stride(step) for c in self.carried]
+        shapes = [dom, dom] + [self.group * self.stride(step)]
         return [pltpu.VMEM((length, self.w), jnp.float32) for length in shapes]
 
 
 def items_of(plan, step, got, meta):
     color = step % COLORS
     out = []
-    for s in range(1, plan.group):
-        d = s.bit_length() - 1
-        line = plan.at(s, d, 0) + plan.n + color
-        out.append((meta[2 + d], line, got[2 + d], plan.at(s, d, step)))
+    for q in range(plan.group):
+        out.append((meta[2], plan.at(q, 0) + plan.n + color, got[2], plan.at(q, step)))
     for lane in range(2):
         for p in range(plan.quarter):
             line = plan.quarter * plan.n + color * plan.quarter + p
@@ -80,12 +76,11 @@
         )
         far[pl.ds(p * plan.n, plan.n), :] = both[:, : plan.w]
         near[pl.ds(p * plan.n, plan.n), :] = both[:, plan.w :]
-    for s in range(1, plan.group):
+    for q in range(plan.group):
         total = jnp.zeros((plan.n, plan.w), jnp.float32)
         for slot, term in terms:
-            total = total + jnp.where(slot == s, term, 0.0)
-        d = (s & -s).bit_length() - 1
-        sends[2 + d][pl.ds(plan.at(s, d, step), plan.n), :] = total
+            total = total + jnp.where(slot == q, term, 0.0)
+        sends[2][pl.ds(plan.at(q, step), plan.n), :] = total
 
 
 def first_kernel(plan, *refs):
@@ -102,7 +97,6 @@
         copy.start()
     for copy in copies[:5]:
         copy.wait()
-    me = lax.axis_index("sub")
     parity = lax.rem(lax.axis_index("dom"), 2)
     colors = [color[i] for i in range(plan.rows)]
     for i in range(plan.rows):
@@ -113,14 +107,13 @@
         table[plan.order + at] = i
         for k in range(2):
             table[plan.local + 2 * at + k] = local_target[k, i]
-            table[plan.slot + 2 * at + k] = me ^ group_peer[k, i]
+            table[plan.slot + 2 * at + k] = group_peer[k, i]
     line = lax.broadcasted_iota(jnp.int32, (META, plan.w), 0)
-    for s in range(1, plan.group):
+    for q in range(plan.group):
         meta = jnp.full((META, plan.w), -1, jnp.int32)
         for c in range(COLORS):
-            meta = jnp.where(line == c, group_list[0, c, me ^ s], meta)
-        d = (s & -s).bit_length() - 1
-        sends[2 + d][pl.ds(plan.at(s, d, 0) + plan.n, META), :] = meta.astype(jnp.float32)
+            meta = jnp.where(line == c, group_list[0, c, q], meta)
+        sends[2][pl.ds(plan.at(q, 0) + plan.n, META), :] = meta.astype(jnp.float32)
     line = lax.broadcasted_iota(jnp.int32, (plan.dom_meta, plan.w), 0)
     for send, k in zip(sends[:2], (1 - parity, parity)):
         meta = jnp.full((plan.dom_meta, plan.w), -1, jnp.int32)
@@ -158,18 +151,6 @@
         changes.append(new.astype(jnp.bfloat16))
         change[p] = changes[p]
     products(plan, step, table, changes, coupling, refs[2:])
-
-
-def forward_kernel(plan, step, phase, *refs):
-    got, out = refs[1:-1], refs[-1]
-    for s in plan.carried[phase]:
-        lower = s & ((1 << phase) - 1)
-        if lower:
-            d = lower.bit_length() - 1
-            length = plan.stride(step)
-            out[pl.ds(plan.at(s, phase, step), length), :] = got[d][
-                pl.ds(plan.at(s, d, step), length), :
-            ]
 
 
 def local_kernel(plan, step, last, table, resid, coupling, change, *refs):
@@ -205,7 +186,7 @@
 def on_device(coupling, diag_inv, rhs, color, local_target, group_peer, group_list, dom_target):
     rows, rhs_count, width = rhs.shape
     doms, group = lax.axis_size("dom"), lax.axis_size("sub")
-    assert group & (group - 1) == 0 and doms % 2 == 0
+    assert doms % 2 == 0
     plan = Plan(rows, rhs_count, width, group)
     f32 = jnp.float32
     near_pairs = [(i, i ^ 1) for i in range(doms)]
@@ -225,25 +206,9 @@
         )(*ins)
 
     def exchange(step, sends):
-        got = [None] * plan.lanes
-        arrived = []
-        for d in range(plan.phases):
-            send = sends[2 + d]
-            if d:
-                (send,) = call(
-                    functools.partial(forward_kernel, plan, step, d),
-                    f"forward{step}",
-                    [send, *arrived],
-                    [VMEM],
-                    [plan.types(step)[2 + d]],
-                    input_output_aliases={0: 0},
-                )
-            arrived.append(lax.ppermute(send, "sub", [(i, i ^ (1 << d)) for i in range(group)]))
-            if d == 0:
-                got[0] = lax.ppermute(sends[0], "dom", far_pairs)
-        got[1] = lax.ppermute(sends[1], "dom", near_pairs)
-        got[2:] = arrived
-        return got
+        far = lax.ppermute(sends[0], "dom", far_pairs)
+        near = lax.ppermute(sends[1], "dom", near_pairs)
+        return [far, near, lax.all_to_all(sends[2], "sub", 0, 0, tiled=True)]
 
     sol_t = pltpu.VMEM((plan.quarter, plan.n, plan.w), f32)
     change_t = pltpu.VMEM((plan.quarter, plan.n, plan.w), jnp.bfloat16)

time: 79.3 us -> 90.8 us (1.15)
  starting transfers between devices: 18.7 us -> 40.8 us
  waiting for transfers between devices: 52.5 us -> 35.7 us
  Pallas kernels: 7.13 us -> 12.5 us
    all_to_all x0 -> x8, starting transfers between devices: none -> 34.5 us  [exchange(): return [far, near, lax.all_to_all(sends[2], 'sub', 0, 0, tiled=True)]]
    ppermute x32 -> x16, waiting for transfers between devices: 52.5 us -> 35.7 us  [the longest x8 35.7 us: exchange(): far = lax.ppermute(sends[0], 'dom', far_pairs)]
    ppermute x32 -> x16, starting transfers between devices: 18.7 us -> 6.31 us  [the longest x8 6.28 us: exchange(): far = lax.ppermute(sends[0], 'dom', far_pairs)]
    pallas_call x25 -> x17, Pallas kernels: 7.13 us -> 12.5 us  [call(): pl.pallas_call(body, name=name, in_specs=in_specs + [VMEM] * (len(ins) -...]
  transfers between devices with their start and end apart: 32 -> 24, of which waited for: 23 -> 8; matrix products, arithmetic and copies ran while one was open for 0% -> 0% of each run, Pallas kernels for 3% -> 3%
where the time goes in v3:
time: 90.8 us; the launch traced here: 89.8 us
  starting transfers between devices  40.8 us (45%)
  waiting for transfers between devices  35.7 us (39%)
  Pallas kernels  12.5 us (14%)
    ppermute x8, waiting for transfers between devices, exchange(): far = lax.ppermute(sends[0], 'dom', far_pairs)  35.7 us
    all_to_all x8, starting transfers between devices, exchange(): return [far, near, lax.all_to_all(sends[2], 'sub', 0, 0, tiled=True)]  34.5 us
    pallas_call x17, Pallas kernels, call(): pl.pallas_call(body, name=name, in_specs=in_specs + [VMEM] * (len(ins) -...  12.5 us
    ppermute x8, starting transfers between devices, exchange(): far = lax.ppermute(sends[0], 'dom', far_pairs)  6.28 us
  transfers between devices with their start and end apart: 24, of which 8 were waited for; matrix products, arithmetic and copies ran while one was open for 0% of the time, Pallas kernels for 3%

profile of v3, /device:TPU:0, one launch (start us, length us, event | category | flops | bytes accessed | tf_op | source)
XLA Modules:
  0.0 89.8 jit_solution(7860262453329909711)
XLA Ops:
  0.6 2.5 %first.1 = (s32[40]{0:T(128)S(4)}, bf16[8,6,128,128]{3,2,1,0:T(8,128)(2,1)S(1)}, bf16[8,128,128]{2,1,0:T(8,128)(2,1)S(1)}, f32[8,64,128]{2,1,0:T(8,128)S(1)}, f3...) custom-call(s32[8]{0:T(128)} %refs_0_.1, ...), custom_call_target="tpu_custom_call" | custom-call | tf_op jit(solution)/shard_map/first/pallas_call | solution.py:198
  3.1 5.2 %all-to-all-start = ((f32[4,72,128]{2,1,0:T(8,128)}), f32[4,72,128]{2,1,0:T(8,128)S(1)}, u32[]{:S(2)}, u32[]{:S(2)}) async-start(f32[4,72,128]{2,1,0:T(8,128)} %bitcast.3), calls=%async_computation | async-start | bytes 294912 | tf_op jit(solution)/shard_map/all_to_all | solution.py:211
  8.3 2.8 %collective-permute-start = (f32[136,128]{1,0:T(8,128)S(1)}, f32[136,128]{1,0:T(8,128)S(1)}, u32[]{:S(2)}, u32[]{:S(2)}) collective-permute-start(f32[136,128]{1,0:T(8,128)S(1)} %get-tuple-element.53), channel_id=1, source_target_pairs={{0,28},{4,8},{8,4},{12,16},{16,12},{20,24},{24,20},{28,0},{1,29},{... | collective-permute-start | bytes 208904 | tf_op jit(solution)/shard_map/ppermute | solution.py:209
  11.1 0.2 local0.1.resid
  11.3 3.1 %collective-permute-done.refs_0_.refs_3_ = f32[136,128]{1,0:T(8,128)S(1)} collective-permute-done((f32[136,128]{1,0:T(8,128)S(1)}, f32[136,128]{1,0:T(8,128)S(1)}, u32[]{:S(2)}, u32[]{:S(2)}) %collective-permute-start) | collective-permute-done | bytes 69664 | tf_op jit(solution)/shard_map/ppermute | solution.py:209
  14.3 0.0 collective-permute-done.1.refs_1_.refs_4_
  14.3 0.0 all-to-all-done
  14.3 1.0 %step1.1 = (f32[2,64,128]{2,1,0:T(8,128)S(1)}, bf16[2,64,128]{2,1,0:T(8,128)(2,1)S(1)}, f32[128,128]{1,0:T(8,128)S(1)}, f32[128,128]{1,0:T(8,128)S(1)}, f32[256,128]{1,0:T(8,128)}) custom-call(s32[40]{0:T(128)S(4)} %get-tuple-element.48.table, f32[8,64,128]{2,1,0:T(8,128)S(1)} %local0.1.resid, bf16[8,128,128]{2,1,0:T(8,128)(2,1)S(1)} %get-tuple-element.52.diag, ...), custom_call_target="tpu_custom_call" | custom-call | tf_op jit(solution)/shard_map/step1/pallas_call | solution.py:198
  15.3 4.2 %all-to-all-start.1 = ((f32[4,64,128]{2,1,0:T(8,128)}), f32[4,64,128]{2,1,0:T(8,128)S(1)}, u32[]{:S(2)}, u32[]{:S(2)}) async-start(f32[4,64,128]{2,1,0:T(8,128)} %bitcast.5), calls=%async_computation.1 | async-start | bytes 262144 | tf_op jit(solution)/shard_map/all_to_all | solution.py:211
  19.5 1.7 %collective-permute-start.2 = (f32[128,128]{1,0:T(8,128)S(1)}, f32[128,128]{1,0:T(8,128)S(1)}, u32[]{:S(2)}, u32[]{:S(2)}) collective-permute-start(f32[128,128]{1,0:T(8,128)S(1)} %get-tuple-element.57), channel_id=1, source_target_pairs={{0,28},{4,8},{8,4},{12,16},{16,12},{20,24},{24,20},{28,0},{1,29},{... | collective-permute-start | bytes 196616 | tf_op jit(solution)/shard_map/ppermute | solution.py:209
  21.2 0.0 collective-permute-start.3
  21.2 0.2 local1.1.resid
  21.5 3.5 %collective-permute-done.2.refs_0_ = f32[128,128]{1,0:T(8,128)S(1)} collective-permute-done((f32[128,128]{1,0:T(8,128)S(1)}, f32[128,128]{1,0:T(8,128)S(1)}, u32[]{:S(2)}, u32[]{:S(2)}) %collective-permute-start.2) | collective-permute-done | bytes 65568 | tf_op jit(solution)/shard_map/ppermute | solution.py:209
  25.0 0.0 collective-permute-done.3.refs_1_
  25.0 0.0 all-to-all-done.1
  25.0 1.0 %step2.1 = (f32[2,64,128]{2,1,0:T(8,128)S(1)}, bf16[2,64,128]{2,1,0:T(8,128)(2,1)S(1)}, f32[128,128]{1,0:T(8,128)S(1)}, f32[128,128]{1,0:T(8,128)S(1)}, f32[256,128]{1,0:T(8,128)}) custom-call(s32[40]{0:T(128)S(4)} %get-tuple-element.48.table, f32[8,64,128]{2,1,0:T(8,128)S(1)} %local1.1.resid, bf16[8,128,128]{2,1,0:T(8,128)(2,1)S(1)} %get-tuple-element.52.diag, ...), custom_call_target="tpu_custom_call" | custom-call | tf_op jit(solution)/shard_map/step2/pallas_call | solution.py:198
  26.0 4.2 %all-to-all-start.2 = ((f32[4,64,128]{2,1,0:T(8,128)}), f32[4,64,128]{2,1,0:T(8,128)S(1)}, u32[]{:S(2)}, u32[]{:S(2)}) async-start(f32[4,64,128]{2,1,0:T(8,128)} %bitcast.7), calls=%async_computation.2 | async-start | bytes 262144 | tf_op jit(solution)/shard_map/all_to_all | solution.py:211
  30.1 1.2 %collective-permute-start.4 = (f32[128,128]{1,0:T(8,128)S(1)}, f32[128,128]{1,0:T(8,128)S(1)}, u32[]{:S(2)}, u32[]{:S(2)}) collective-permute-start(f32[128,128]{1,0:T(8,128)S(1)} %get-tuple-element.61), channel_id=1, source_target_pairs={{0,28},{4,8},{8,4},{12,16},{16,12},{20,24},{24,20},{28,0},{1,29},{... | collective-permute-start | bytes 196616 | tf_op jit(solution)/shard_map/ppermute | solution.py:209
  31.3 0.0 collective-permute-start.5
  31.3 0.2 local2.1.resid
  31.6 4.1 %collective-permute-done.4.refs_0_ = f32[128,128]{1,0:T(8,128)S(1)} collective-permute-done((f32[128,128]{1,0:T(8,128)S(1)}, f32[128,128]{1,0:T(8,128)S(1)}, u32[]{:S(2)}, u32[]{:S(2)}) %collective-permute-start.4) | collective-permute-done | bytes 65568 | tf_op jit(solution)/shard_map/ppermute | solution.py:209
  35.6 0.0 collective-permute-done.5.refs_1_
  35.6 1.0 %step3.1 = (f32[2,64,128]{2,1,0:T(8,128)S(1)}, bf16[2,64,128]{2,1,0:T(8,128)(2,1)S(1)}, f32[128,128]{1,0:T(8,128)S(1)}, f32[128,128]{1,0:T(8,128)S(1)}, f32[256,128]{1,0:T(8,128)}) custom-call(s32[40]{0:T(128)S(4)} %get-tuple-element.48.table, f32[8,64,128]{2,1,0:T(8,128)S(1)} %local2.1.resid, bf16[8,128,128]{2,1,0:T(8,128)(2,1)S(1)} %get-tuple-element.52.diag, ...), custom_call_target="tpu_custom_call" | custom-call | tf_op jit(solution)/shard_map/step3/pallas_call | solution.py:198
  36.6 4.2 %all-to-all-start.3 = ((f32[4,64,128]{2,1,0:T(8,128)}), f32[4,64,128]{2,1,0:T(8,128)S(1)}, u32[]{:S(2)}, u32[]{:S(2)}) async-start(f32[4,64,128]{2,1,0:T(8,128)} %bitcast.9), calls=%async_computation.3 | async-start | bytes 262144 | tf_op jit(solution)/shard_map/all_to_all | solution.py:211
  40.8 0.6 collective-permute-start.6
  41.4 0.0 collective-permute-start.7
  41.4 0.2 local3.1.resid
  41.6 4.6 %collective-permute-done.6.refs_0_ = f32[128,128]{1,0:T(8,128)S(1)} collective-permute-done((f32[128,128]{1,0:T(8,128)S(1)}, f32[128,128]{1,0:T(8,128)S(1)}, u32[]{:S(2)}, u32[]{:S(2)}) %collective-permute-start.6) | collective-permute-done | bytes 65568 | tf_op jit(solution)/shard_map/ppermute | solution.py:209
  46.3 0.0 all-to-all-done.3
  46.3 1.0 %step4.1 = (f32[2,64,128]{2,1,0:T(8,128)S(1)}, bf16[2,64,128]{2,1,0:T(8,128)(2,1)S(1)}, f32[128,128]{1,0:T(8,128)S(1)}, f32[128,128]{1,0:T(8,128)S(1)}, f32[256,128]{1,0:T(8,128)}) custom-call(s32[40]{0:T(128)S(4)} %get-tuple-element.48.table, f32[8,64,128]{2,1,0:T(8,128)S(1)} %local3.1.resid, bf16[8,128,128]{2,1,0:T(8,128)(2,1)S(1)} %get-tuple-element.52.diag, ...), custom_call_target="tpu_custom_call" | custom-call | tf_op jit(solution)/shard_map/step4/pallas_call | solution.py:198
  47.3 4.2 %all-to-all-start.4 = ((f32[4,64,128]{2,1,0:T(8,128)}), f32[4,64,128]{2,1,0:T(8,128)S(1)}, u32[]{:S(2)}, u32[]{:S(2)}) async-start(f32[4,64,128]{2,1,0:T(8,128)} %bitcast.11), calls=%async_computation.4 | async-start | bytes 262144 | tf_op jit(solution)/shard_map/all_to_all | solution.py:211
  51.5 0.0 collective-permute-start.8
  51.5 0.2 local4.1.resid
  51.7 5.2 %collective-permute-done.8.refs_0_ = f32[128,128]{1,0:T(8,128)S(1)} collective-permute-done((f32[128,128]{1,0:T(8,128)S(1)}, f32[128,128]{1,0:T(8,128)S(1)}, u32[]{:S(2)}, u32[]{:S(2)}) %collective-permute-start.8) | collective-permute-done | bytes 65568 | tf_op jit(solution)/shard_map/ppermute | solution.py:209
  56.9 0.0 collective-permute-done.9.refs_1_
  56.9 1.0 %step5.1 = (f32[2,64,128]{2,1,0:T(8,128)S(1)}, bf16[2,64,128]{2,1,0:T(8,128)(2,1)S(1)}, f32[128,128]{1,0:T(8,128)S(1)}, f32[128,128]{1,0:T(8,128)S(1)}, f32[256,128]{1,0:T(8,128)}) custom-call(s32[40]{0:T(128)S(4)} %get-tuple-element.48.table, f32[8,64,128]{2,1,0:T(8,128)S(1)} %local4.1.resid, bf16[8,128,128]{2,1,0:T(8,128)(2,1)S(1)} %get-tuple-element.52.diag, ...), custom_call_target="tpu_custom_call" | custom-call | tf_op jit(solution)/shard_map/step5/pallas_call | solution.py:198
  57.9 4.2 %all-to-all-start.5 = ((f32[4,64,128]{2,1,0:T(8,128)}), f32[4,64,128]{2,1,0:T(8,128)S(1)}, u32[]{:S(2)}, u32[]{:S(2)}) async-start(f32[4,64,128]{2,1,0:T(8,128)} %bitcast.13), calls=%async_computation.5 | async-start | bytes 262144 | tf_op jit(solution)/shard_map/all_to_all | solution.py:211
  62.1 0.2 local5.1.resid
  62.4 5.2 %collective-permute-done.10.refs_0_ = f32[128,128]{1,0:T(8,128)S(1)} collective-permute-done((f32[128,128]{1,0:T(8,128)S(1)}, f32[128,128]{1,0:T(8,128)S(1)}, u32[]{:S(2)}, u32[]{:S(2)}) %collective-permute-start.10) | collective-permute-done | bytes 65568 | tf_op jit(solution)/shard_map/ppermute | solution.py:209
  67.6 1.0 %step6.1 = (f32[2,64,128]{2,1,0:T(8,128)S(1)}, bf16[2,64,128]{2,1,0:T(8,128)(2,1)S(1)}, f32[128,128]{1,0:T(8,128)S(1)}, f32[128,128]{1,0:T(8,128)S(1)}, f32[256,128]{1,0:T(8,128)}) custom-call(s32[40]{0:T(128)S(4)} %get-tuple-element.48.table, f32[8,64,128]{2,1,0:T(8,128)S(1)} %local5.1.resid, bf16[8,128,128]{2,1,0:T(8,128)(2,1)S(1)} %get-tuple-element.52.diag, ...), custom_call_target="tpu_custom_call" | custom-call | tf_op jit(solution)/shard_map/step6/pallas_call | solution.py:198
  68.6 4.2 %all-to-all-start.6 = ((f32[4,64,128]{2,1,0:T(8,128)}), f32[4,64,128]{2,1,0:T(8,128)S(1)}, u32[]{:S(2)}, u32[]{:S(2)}) async-start(f32[4,64,128]{2,1,0:T(8,128)} %bitcast.15), calls=%async_computation.6 | async-start | bytes 262144 | tf_op jit(solution)/shard_map/all_to_all | solution.py:211
  72.8 0.2 local6.1.resid
  73.0 5.2 %collective-permute-done.12.refs_0_ = f32[128,128]{1,0:T(8,128)S(1)} collective-permute-done((f32[128,128]{1,0:T(8,128)S(1)}, f32[128,128]{1,0:T(8,128)S(1)}, u32[]{:S(2)}, u32[]{:S(2)}) %collective-permute-start.12) | collective-permute-done | bytes 65568 | tf_op jit(solution)/shard_map/ppermute | solution.py:209
  78.3 1.0 %step7.1 = (f32[2,64,128]{2,1,0:T(8,128)S(1)}, bf16[2,64,128]{2,1,0:T(8,128)(2,1)S(1)}, f32[128,128]{1,0:T(8,128)S(1)}, f32[128,128]{1,0:T(8,128)S(1)}, f32[256,128]{1,0:T(8,128)}) custom-call(s32[40]{0:T(128)S(4)} %get-tuple-element.48.table, f32[8,64,128]{2,1,0:T(8,128)S(1)} %local6.1.resid, bf16[8,128,128]{2,1,0:T(8,128)(2,1)S(1)} %get-tuple-element.52.diag, ...), custom_call_target="tpu_custom_call" | custom-call | tf_op jit(solution)/shard_map/step7/pallas_call | solution.py:198
  79.2 4.2 %all-to-all-start.7 = ((f32[4,64,128]{2,1,0:T(8,128)}), f32[4,64,128]{2,1,0:T(8,128)S(1)}, u32[]{:S(2)}, u32[]{:S(2)}) async-start(f32[4,64,128]{2,1,0:T(8,128)} %bitcast.17), calls=%async_computation.7 | async-start | bytes 262144 | tf_op jit(solution)/shard_map/all_to_all | solution.py:211
  83.4 0.8 local7.1
  84.2 4.7 %collective-permute-done.14.refs_0_ = f32[128,128]{1,0:T(8,128)S(1)} collective-permute-done((f32[128,128]{1,0:T(8,128)S(1)}, f32[128,128]{1,0:T(8,128)S(1)}, u32[]{:S(2)}, u32[]{:S(2)}) %collective-permute-start.14) | collective-permute-done | bytes 65568 | tf_op jit(solution)/shard_map/ppermute | solution.py:209
  88.9 0.9 final.1
  (17 shorter events, 0.0 us)
Async XLA Ops:
  3.1 11.2 %all-to-all-start = ((f32[4,72,128]{2,1,0:T(8,128)}), f32[4,72,128]{2,1,0:T(8,128)S(1)}, u32[]{:S(2)}, u32[]{:S(2)}) async-start(f32[4,72,128]{2,1,0:T(8,128)} %bitcast.3), calls=%async_computation | async-start | bytes 294912 | tf_op jit(solution)/shard_map/all_to_all | solution.py:211
  8.3 6.0 %collective-permute-start = (f32[136,128]{1,0:T(8,128)S(1)}, f32[136,128]{1,0:T(8,128)S(1)}, u32[]{:S(2)}, u32[]{:S(2)}) collective-permute-start(f32[136,128]{1,0:T(8,128)S(1)} %get-tuple-element.53), channel_id=1, source_target_pairs={{0,28},{4,8},{8,4},{12,16},{16,12},{20,24},{24,20},{28,0},{1,29},{... | collective-permute-start | bytes 208904 | tf_op jit(solution)/shard_map/ppermute | solution.py:209
  11.1 3.3 %collective-permute-start.1 = (f32[136,128]{1,0:T(8,128)S(1)}, f32[136,128]{1,0:T(8,128)S(1)}, u32[]{:S(2)}, u32[]{:S(2)}) collective-permute-start(f32[136,128]{1,0:T(8,128)S(1)} %get-tuple-element.54), channel_id=1, source_target_pairs={{0,4},{4,0},{8,12},{12,8},{16,20},{20,16},{24,28},{28,24},{1,5},{5... | collective-permute-start | bytes 208904 | tf_op jit(solution)/shard_map/ppermute | solution.py:210
  15.3 9.7 %all-to-all-start.1 = ((f32[4,64,128]{2,1,0:T(8,128)}), f32[4,64,128]{2,1,0:T(8,128)S(1)}, u32[]{:S(2)}, u32[]{:S(2)}) async-start(f32[4,64,128]{2,1,0:T(8,128)} %bitcast.5), calls=%async_computation.1 | async-start | bytes 262144 | tf_op jit(solution)/shard_map/all_to_all | solution.py:211
  19.5 5.5 %collective-permute-start.2 = (f32[128,128]{1,0:T(8,128)S(1)}, f32[128,128]{1,0:T(8,128)S(1)}, u32[]{:S(2)}, u32[]{:S(2)}) collective-permute-start(f32[128,128]{1,0:T(8,128)S(1)} %get-tuple-element.57), channel_id=1, source_target_pairs={{0,28},{4,8},{8,4},{12,16},{16,12},{20,24},{24,20},{28,0},{1,29},{... | collective-permute-start | bytes 196616 | tf_op jit(solution)/shard_map/ppermute | solution.py:209
  21.2 3.8 %collective-permute-start.3 = (f32[128,128]{1,0:T(8,128)S(1)}, f32[128,128]{1,0:T(8,128)S(1)}, u32[]{:S(2)}, u32[]{:S(2)}) collective-permute-start(f32[128,128]{1,0:T(8,128)S(1)} %get-tuple-element.58), channel_id=1, source_target_pairs={{0,4},{4,0},{8,12},{12,8},{16,20},{20,16},{24,28},{28,24},{1,5},{5... | collective-permute-start | bytes 196616 | tf_op jit(solution)/shard_map/ppermute | solution.py:210
  26.0 9.7 %all-to-all-start.2 = ((f32[4,64,128]{2,1,0:T(8,128)}), f32[4,64,128]{2,1,0:T(8,128)S(1)}, u32[]{:S(2)}, u32[]{:S(2)}) async-start(f32[4,64,128]{2,1,0:T(8,128)} %bitcast.7), calls=%async_computation.2 | async-start | bytes 262144 | tf_op jit(solution)/shard_map/all_to_all | solution.py:211
  30.1 5.5 %collective-permute-start.4 = (f32[128,128]{1,0:T(8,128)S(1)}, f32[128,128]{1,0:T(8,128)S(1)}, u32[]{:S(2)}, u32[]{:S(2)}) collective-permute-start(f32[128,128]{1,0:T(8,128)S(1)} %get-tuple-element.61), channel_id=1, source_target_pairs={{0,28},{4,8},{8,4},{12,16},{16,12},{20,24},{24,20},{28,0},{1,29},{... | collective-permute-start | bytes 196616 | tf_op jit(solution)/shard_map/ppermute | solution.py:209
  31.3 4.3 %collective-permute-start.5 = (f32[128,128]{1,0:T(8,128)S(1)}, f32[128,128]{1,0:T(8,128)S(1)}, u32[]{:S(2)}, u32[]{:S(2)}) collective-permute-start(f32[128,128]{1,0:T(8,128)S(1)} %get-tuple-element.62), channel_id=1, source_target_pairs={{0,4},{4,0},{8,12},{12,8},{16,20},{20,16},{24,28},{28,24},{1,5},{5... | collective-permute-start | bytes 196616 | tf_op jit(solution)/shard_map/ppermute | solution.py:210
  36.6 9.7 %all-to-all-start.3 = ((f32[4,64,128]{2,1,0:T(8,128)}), f32[4,64,128]{2,1,0:T(8,128)S(1)}, u32[]{:S(2)}, u32[]{:S(2)}) async-start(f32[4,64,128]{2,1,0:T(8,128)} %bitcast.9), calls=%async_computation.3 | async-start | bytes 262144 | tf_op jit(solution)/shard_map/all_to_all | solution.py:211
  40.8 5.5 %collective-permute-start.6 = (f32[128,128]{1,0:T(8,128)S(1)}, f32[128,128]{1,0:T(8,128)S(1)}, u32[]{:S(2)}, u32[]{:S(2)}) collective-permute-start(f32[128,128]{1,0:T(8,128)S(1)} %get-tuple-element.65), channel_id=1, source_target_pairs={{0,28},{4,8},{8,4},{12,16},{16,12},{20,24},{24,20},{28,0},{1,29},{... | collective-permute-start | bytes 196616 | tf_op jit(solution)/shard_map/ppermute | solution.py:209
  41.4 4.9 %collective-permute-start.7 = (f32[128,128]{1,0:T(8,128)S(1)}, f32[128,128]{1,0:T(8,128)S(1)}, u32[]{:S(2)}, u32[]{:S(2)}) collective-permute-start(f32[128,128]{1,0:T(8,128)S(1)} %get-tuple-element.66), channel_id=1, source_target_pairs={{0,4},{4,0},{8,12},{12,8},{16,20},{20,16},{24,28},{28,24},{1,5},{5... | collective-permute-start | bytes 196616 | tf_op jit(solution)/shard_map/ppermute | solution.py:210
  47.3 9.7 %all-to-all-start.4 = ((f32[4,64,128]{2,1,0:T(8,128)}), f32[4,64,128]{2,1,0:T(8,128)S(1)}, u32[]{:S(2)}, u32[]{:S(2)}) async-start(f32[4,64,128]{2,1,0:T(8,128)} %bitcast.11), calls=%async_computation.4 | async-start | bytes 262144 | tf_op jit(solution)/shard_map/all_to_all | solution.py:211
  51.5 5.5 %collective-permute-start.8 = (f32[128,128]{1,0:T(8,128)S(1)}, f32[128,128]{1,0:T(8,128)S(1)}, u32[]{:S(2)}, u32[]{:S(2)}) collective-permute-start(f32[128,128]{1,0:T(8,128)S(1)} %get-tuple-element.70), channel_id=1, source_target_pairs={{0,28},{4,8},{8,4},{12,16},{16,12},{20,24},{24,20},{28,0},{1,29},{... | collective-permute-start | bytes 196616 | tf_op jit(solution)/shard_map/ppermute | solution.py:209
  51.5 5.5 %collective-permute-start.9 = (f32[128,128]{1,0:T(8,128)S(1)}, f32[128,128]{1,0:T(8,128)S(1)}, u32[]{:S(2)}, u32[]{:S(2)}) collective-permute-start(f32[128,128]{1,0:T(8,128)S(1)} %get-tuple-element.71), channel_id=1, source_target_pairs={{0,4},{4,0},{8,12},{12,8},{16,20},{20,16},{24,28},{28,24},{1,5},{5... | collective-permute-start | bytes 196616 | tf_op jit(solution)/shard_map/ppermute | solution.py:210
  57.9 9.7 %all-to-all-start.5 = ((f32[4,64,128]{2,1,0:T(8,128)}), f32[4,64,128]{2,1,0:T(8,128)S(1)}, u32[]{:S(2)}, u32[]{:S(2)}) async-start(f32[4,64,128]{2,1,0:T(8,128)} %bitcast.13), calls=%async_computation.5 | async-start | bytes 262144 | tf_op jit(solution)/shard_map/all_to_all | solution.py:211
  62.1 5.5 %collective-permute-start.10 = (f32[128,128]{1,0:T(8,128)S(1)}, f32[128,128]{1,0:T(8,128)S(1)}, u32[]{:S(2)}, u32[]{:S(2)}) collective-permute-start(f32[128,128]{1,0:T(8,128)S(1)} %get-tuple-element.75), channel_id=1, source_target_pairs={{0,28},{4,8},{8,4},{12,16},{16,12},{20,24},{24,20},{28,0},{1,29},{... | collective-permute-start | bytes 196616 | tf_op jit(solution)/shard_map/ppermute | solution.py:209
  62.1 5.5 %collective-permute-start.11 = (f32[128,128]{1,0:T(8,128)S(1)}, f32[128,128]{1,0:T(8,128)S(1)}, u32[]{:S(2)}, u32[]{:S(2)}) collective-permute-start(f32[128,128]{1,0:T(8,128)S(1)} %get-tuple-element.76), channel_id=1, source_target_pairs={{0,4},{4,0},{8,12},{12,8},{16,20},{20,16},{24,28},{28,24},{1,5},{5... | collective-permute-start | bytes 196616 | tf_op jit(solution)/shard_map/ppermute | solution.py:210
  68.6 9.7 %all-to-all-start.6 = ((f32[4,64,128]{2,1,0:T(8,128)}), f32[4,64,128]{2,1,0:T(8,128)S(1)}, u32[]{:S(2)}, u32[]{:S(2)}) async-start(f32[4,64,128]{2,1,0:T(8,128)} %bitcast.15), calls=%async_computation.6 | async-start | bytes 262144 | tf_op jit(solution)/shard_map/all_to_all | solution.py:211
  72.8 5.5 %collective-permute-start.12 = (f32[128,128]{1,0:T(8,128)S(1)}, f32[128,128]{1,0:T(8,128)S(1)}, u32[]{:S(2)}, u32[]{:S(2)}) collective-permute-start(f32[128,128]{1,0:T(8,128)S(1)} %get-tuple-element.80), channel_id=1, source_target_pairs={{0,28},{4,8},{8,4},{12,16},{16,12},{20,24},{24,20},{28,0},{1,29},{... | collective-permute-start | bytes 196616 | tf_op jit(solution)/shard_map/ppermute | solution.py:209
  72.8 5.5 %collective-permute-start.13 = (f32[128,128]{1,0:T(8,128)S(1)}, f32[128,128]{1,0:T(8,128)S(1)}, u32[]{:S(2)}, u32[]{:S(2)}) collective-permute-start(f32[128,128]{1,0:T(8,128)S(1)} %get-tuple-element.81), channel_id=1, source_target_pairs={{0,4},{4,0},{8,12},{12,8},{16,20},{20,16},{24,28},{28,24},{1,5},{5... | collective-permute-start | bytes 196616 | tf_op jit(solution)/shard_map/ppermute | solution.py:210
  79.2 9.7 %all-to-all-start.7 = ((f32[4,64,128]{2,1,0:T(8,128)}), f32[4,64,128]{2,1,0:T(8,128)S(1)}, u32[]{:S(2)}, u32[]{:S(2)}) async-start(f32[4,64,128]{2,1,0:T(8,128)} %bitcast.17), calls=%async_computation.7 | async-start | bytes 262144 | tf_op jit(solution)/shard_map/all_to_all | solution.py:211
  83.4 5.5 %collective-permute-start.14 = (f32[128,128]{1,0:T(8,128)S(1)}, f32[128,128]{1,0:T(8,128)S(1)}, u32[]{:S(2)}, u32[]{:S(2)}) collective-permute-start(f32[128,128]{1,0:T(8,128)S(1)} %get-tuple-element.91), channel_id=1, source_target_pairs={{0,28},{4,8},{8,4},{12,16},{16,12},{20,24},{24,20},{28,0},{1,29},{... | collective-permute-start | bytes 196616 | tf_op jit(solution)/shard_map/ppermute | solution.py:209
  83.4 5.5 %collective-permute-start.15 = (f32[128,128]{1,0:T(8,128)S(1)}, f32[128,128]{1,0:T(8,128)S(1)}, u32[]{:S(2)}, u32[]{:S(2)}) collective-permute-start(f32[128,128]{1,0:T(8,128)S(1)} %get-tuple-element.92), channel_id=1, source_target_pairs={{0,4},{4,0},{8,12},{12,8},{16,20},{20,16},{24,28},{28,24},{1,5},{5... | collective-permute-start | bytes 196616 | tf_op jit(solution)/shard_map/ppermute | solution.py:210

commit v4 on v2

--- a/solution.py
+++ b/solution.py
@@ -30,6 +30,12 @@
         self.order, self.local, self.slot = 0, rows, 3 * rows
         self.table = 5 * rows
         self.dom_meta = -(-rows // 8) * 8
+
+    def turned(self, distance, back=False):
+        half = self.phases // 2
+        if back:
+            half = self.phases - half
+        return (distance >> half | distance << (self.phases - half)) & (self.group - 1)
 
     def stride(self, step):
         return self.n + (META if step == 0 else 0)
@@ -104,6 +110,7 @@
         copy.wait()
     me = lax.axis_index("sub")
     parity = lax.rem(lax.axis_index("dom"), 2)
+    odd = parity == 1
     colors = [color[i] for i in range(plan.rows)]
     for i in range(plan.rows):
         before = jnp.int32(0)
@@ -113,12 +120,14 @@
         table[plan.order + at] = i
         for k in range(2):
             table[plan.local + 2 * at + k] = local_target[k, i]
-            table[plan.slot + 2 * at + k] = me ^ group_peer[k, i]
+            distance = me ^ group_peer[k, i]
+            table[plan.slot + 2 * at + k] = jnp.where(odd, plan.turned(distance), distance)
     line = lax.broadcasted_iota(jnp.int32, (META, plan.w), 0)
     for s in range(1, plan.group):
         meta = jnp.full((META, plan.w), -1, jnp.int32)
+        q = me ^ jnp.where(odd, plan.turned(s, back=True), s)
         for c in range(COLORS):
-            meta = jnp.where(line == c, group_list[0, c, me ^ s], meta)
+            meta = jnp.where(line == c, group_list[0, c, q], meta)
         d = (s & -s).bit_length() - 1
         sends[2 + d][pl.ds(plan.at(s, d, 0) + plan.n, META), :] = meta.astype(jnp.float32)
     line = lax.broadcasted_iota(jnp.int32, (plan.dom_meta, plan.w), 0)
@@ -161,7 +170,7 @@
 
 
 def forward_kernel(plan, step, phase, *refs):
-    got, out = refs[1:-1], refs[-1]
+    got, out = refs[2:-2], refs[-2]
     for s in plan.carried[phase]:
         lower = s & ((1 << phase) - 1)
         if lower:
@@ -210,6 +219,11 @@
     f32 = jnp.float32
     near_pairs = [(i, i ^ 1) for i in range(doms)]
     far_pairs = [(i, (i + 1 if i % 2 else i - 1) % doms) for i in range(doms)]
+    flips = [(1 << d, plan.turned(1 << d, back=True)) for d in range(plan.phases)]
+    group_pairs = [
+        [(i * group + m, i * group + (m ^ flip[i % 2])) for i in range(doms) for m in range(group)]
+        for flip in flips
+    ]
     params = pltpu.CompilerParams(vmem_limit_bytes=16 * 1024 * 1024)
 
     def call(body, name, ins, in_specs, outs, **kw):
@@ -226,22 +240,23 @@
 
     def exchange(step, sends):
         got = [None] * plan.lanes
+        near = sends[1]
         arrived = []
         for d in range(plan.phases):
             send = sends[2 + d]
             if d:
-                (send,) = call(
+                send, near = call(
                     functools.partial(forward_kernel, plan, step, d),
                     f"forward{step}",
-                    [send, *arrived],
-                    [VMEM],
-                    [plan.types(step)[2 + d]],
-                    input_output_aliases={0: 0},
+                    [send, near, *arrived],
+                    [],
+                    [plan.types(step)[2 + d], plan.types(step)[1]],
+                    input_output_aliases={0: 0, 1: 1},
                 )
-            arrived.append(lax.ppermute(send, "sub", [(i, i ^ (1 << d)) for i in range(group)]))
+            arrived.append(lax.ppermute(send, ("dom", "sub"), group_pairs[d]))
             if d == 0:
                 got[0] = lax.ppermute(sends[0], "dom", far_pairs)
-        got[1] = lax.ppermute(sends[1], "dom", near_pairs)
+        got[1] = lax.ppermute(near, "dom", near_pairs)
         got[2:] = arrived
         return got
 

time: 79.3 us -> 79.3 us (level)
  no operation moved by 1% of the time
where the time goes in v4:
time: 79.3 us; the launch traced here: 79.1 us
  waiting for transfers between devices  52.6 us (66%)
  starting transfers between devices  18.5 us (23%)
  Pallas kernels  7.15 us (9%)
  between operations  0.8 us (1%)
    ppermute x16, waiting for transfers between devices, exchange(): arrived.append(lax.ppermute(send, ('dom', 'sub'), group_pairs[d]))  31.8 us
    ppermute x8, waiting for transfers between devices, exchange(): got[0] = lax.ppermute(sends[0], 'dom', far_pairs)  20.9 us
    ppermute x16, starting transfers between devices, exchange(): arrived.append(lax.ppermute(send, ('dom', 'sub'), group_pairs[d]))  16 us
    pallas_call x25, Pallas kernels, call(): pl.pallas_call(body, name=name, in_specs=in_specs + [VMEM] * (len(ins) -...  7.15 us
    ppermute x8, starting transfers between devices, exchange(): got[0] = lax.ppermute(sends[0], 'dom', far_pairs)  2.45 us
  transfers between devices with their start and end apart: 32, of which 23 were waited for; matrix products, arithmetic and copies ran while one was open for 0% of the time, Pallas kernels for 3%

profile of v4, /device:TPU:0, one launch (start us, length us, event | category | flops | bytes accessed | tf_op | source)
XLA Modules:
  0.0 79.1 jit_solution(5494392995269729418)
XLA Ops:
  0.6 1.8 %first.1 = (s32[40]{0:T(128)S(4)}, bf16[8,6,128,128]{3,2,1,0:T(8,128)(2,1)S(1)}, bf16[8,128,128]{2,1,0:T(8,128)(2,1)S(1)}, f32[8,64,128]{2,1,0:T(8,128)S(1)}, f3...) custom-call(s32[8]{0:T(128)} %refs_0_.1, ...), custom_call_target="tpu_custom_call" | custom-call | tf_op jit(solution)/shard_map/first/pallas_call | solution.py:231
  2.5 3.0 %collective-permute-start.1 = (f32[144,128]{1,0:T(8,128)S(1)}, f32[144,128]{1,0:T(8,128)S(1)}, u32[]{:S(2)}, u32[]{:S(2)}) collective-permute-start(f32[144,128]{1,0:T(8,128)S(1)} %get-tuple-element.80), channel_id=1, source_target_pairs={{0,1},{1,0},{2,3},{3,2},{4,6},{5,7},{6,4},{7,5},{8,9},{9,8},{10,11... | collective-permute-start | bytes 221192 | tf_op jit(solution)/shard_map/ppermute | solution.py:256
  5.5 2.3 %collective-permute-done.1.refs_2_.refs_6_ = f32[144,128]{1,0:T(8,128)S(1)} collective-permute-done((f32[144,128]{1,0:T(8,128)S(1)}, f32[144,128]{1,0:T(8,128)S(1)}, u32[]{:S(2)}, u32[]{:S(2)}) %collective-permute-start.1) | collective-permute-done | bytes 73760 | tf_op jit(solution)/shard_map/ppermute | solution.py:256
  7.8 2.0 %collective-permute-start.3 = (f32[144,128]{1,0:T(8,128)S(1)}, f32[144,128]{1,0:T(8,128)S(1)}, u32[]{:S(2)}, u32[]{:S(2)}) collective-permute-start(f32[144,128]{1,0:T(8,128)S(1)} %get-tuple-element.82), channel_id=1, source_target_pairs={{0,2},{1,3},{2,0},{3,1},{4,5},{5,4},{6,7},{7,6},{8,10},{9,11},{10,... | collective-permute-start | bytes 221192 | tf_op jit(solution)/shard_map/ppermute | solution.py:256
  9.9 1.6 %collective-permute-start = (f32[136,128]{1,0:T(8,128)S(1)}, f32[136,128]{1,0:T(8,128)S(1)}, u32[]{:S(2)}, u32[]{:S(2)}) collective-permute-start(f32[136,128]{1,0:T(8,128)S(1)} %get-tuple-element.77), channel_id=1, source_target_pairs={{0,28},{4,8},{8,4},{12,16},{16,12},{20,24},{24,20},{28,0},{1,29},{... | collective-permute-start | bytes 208904 | tf_op jit(solution)/shard_map/ppermute | solution.py:258
  11.7 4.2 %collective-permute-done.refs_0_.refs_4_ = f32[136,128]{1,0:T(8,128)S(1)} collective-permute-done((f32[136,128]{1,0:T(8,128)S(1)}, f32[136,128]{1,0:T(8,128)S(1)}, u32[]{:S(2)}, u32[]{:S(2)}) %collective-permute-start) | collective-permute-done | bytes 69664 | tf_op jit(solution)/shard_map/ppermute | solution.py:258
  15.9 0.3 step1.1
  16.2 1.6 %collective-permute-start.5 = (f32[128,128]{1,0:T(8,128)S(1)}, f32[128,128]{1,0:T(8,128)S(1)}, u32[]{:S(2)}, u32[]{:S(2)}) collective-permute-start(f32[128,128]{1,0:T(8,128)S(1)} %get-tuple-element.87), channel_id=1, source_target_pairs={{0,1},{1,0},{2,3},{3,2},{4,6},{5,7},{6,4},{7,5},{8,9},{9,8},{10,11... | collective-permute-start | bytes 196616 | tf_op jit(solution)/shard_map/ppermute | solution.py:256
  17.8 0.8 %collective-permute-start.4 = (f32[128,128]{1,0:T(8,128)S(1)}, f32[128,128]{1,0:T(8,128)S(1)}, u32[]{:S(2)}, u32[]{:S(2)}) collective-permute-start(f32[128,128]{1,0:T(8,128)S(1)} %get-tuple-element.84), channel_id=1, source_target_pairs={{0,28},{4,8},{8,4},{12,16},{16,12},{20,24},{24,20},{28,0},{1,29},{... | collective-permute-start | bytes 196616 | tf_op jit(solution)/shard_map/ppermute | solution.py:258
  18.6 1.9 %collective-permute-done.5.refs_2_ = f32[128,128]{1,0:T(8,128)S(1)} collective-permute-done((f32[128,128]{1,0:T(8,128)S(1)}, f32[128,128]{1,0:T(8,128)S(1)}, u32[]{:S(2)}, u32[]{:S(2)}) %collective-permute-start.5) | collective-permute-done | bytes 65568 | tf_op jit(solution)/shard_map/ppermute | solution.py:256
  20.6 0.2 local1.1.resid
  20.8 2.5 %collective-permute-done.4.refs_0_ = f32[128,128]{1,0:T(8,128)S(1)} collective-permute-done((f32[128,128]{1,0:T(8,128)S(1)}, f32[128,128]{1,0:T(8,128)S(1)}, u32[]{:S(2)}, u32[]{:S(2)}) %collective-permute-start.4) | collective-permute-done | bytes 65568 | tf_op jit(solution)/shard_map/ppermute | solution.py:258
  23.3 1.6 %collective-permute-done.7.refs_3_ = f32[128,128]{1,0:T(8,128)S(1)} collective-permute-done((f32[128,128]{1,0:T(8,128)S(1)}, f32[128,128]{1,0:T(8,128)S(1)}, u32[]{:S(2)}, u32[]{:S(2)}) %collective-permute-start.7) | collective-permute-done | bytes 65568 | tf_op jit(solution)/shard_map/ppermute | solution.py:256
  24.8 0.3 step2.1
  25.1 1.6 %collective-permute-start.9 = (f32[128,128]{1,0:T(8,128)S(1)}, f32[128,128]{1,0:T(8,128)S(1)}, u32[]{:S(2)}, u32[]{:S(2)}) collective-permute-start(f32[128,128]{1,0:T(8,128)S(1)} %get-tuple-element.94), channel_id=1, source_target_pairs={{0,1},{1,0},{2,3},{3,2},{4,6},{5,7},{6,4},{7,5},{8,9},{9,8},{10,11... | collective-permute-start | bytes 196616 | tf_op jit(solution)/shard_map/ppermute | solution.py:256
  26.7 2.8 %collective-permute-done.9.refs_2_ = f32[128,128]{1,0:T(8,128)S(1)} collective-permute-done((f32[128,128]{1,0:T(8,128)S(1)}, f32[128,128]{1,0:T(8,128)S(1)}, u32[]{:S(2)}, u32[]{:S(2)}) %collective-permute-start.9) | collective-permute-done | bytes 65568 | tf_op jit(solution)/shard_map/ppermute | solution.py:256
  29.5 0.2 local2.1.resid
  29.7 2.5 %collective-permute-done.8.refs_0_ = f32[128,128]{1,0:T(8,128)S(1)} collective-permute-done((f32[128,128]{1,0:T(8,128)S(1)}, f32[128,128]{1,0:T(8,128)S(1)}, u32[]{:S(2)}, u32[]{:S(2)}) %collective-permute-start.8) | collective-permute-done | bytes 65568 | tf_op jit(solution)/shard_map/ppermute | solution.py:258
  32.2 1.6 %collective-permute-done.11.refs_3_ = f32[128,128]{1,0:T(8,128)S(1)} collective-permute-done((f32[128,128]{1,0:T(8,128)S(1)}, f32[128,128]{1,0:T(8,128)S(1)}, u32[]{:S(2)}, u32[]{:S(2)}) %collective-permute-start.11) | collective-permute-done | bytes 65568 | tf_op jit(solution)/shard_map/ppermute | solution.py:256
  33.7 0.3 step3.1
  34.0 1.6 %collective-permute-start.13 = (f32[128,128]{1,0:T(8,128)S(1)}, f32[128,128]{1,0:T(8,128)S(1)}, u32[]{:S(2)}, u32[]{:S(2)}) collective-permute-start(f32[128,128]{1,0:T(8,128)S(1)} %get-tuple-element.101), channel_id=1, source_target_pairs={{0,1},{1,0},{2,3},{3,2},{4,6},{5,7},{6,4},{7,5},{8,9},{9,8},{10,11... | collective-permute-start | bytes 196616 | tf_op jit(solution)/shard_map/ppermute | solution.py:256
  35.6 2.8 %collective-permute-done.13.refs_2_ = f32[128,128]{1,0:T(8,128)S(1)} collective-permute-done((f32[128,128]{1,0:T(8,128)S(1)}, f32[128,128]{1,0:T(8,128)S(1)}, u32[]{:S(2)}, u32[]{:S(2)}) %collective-permute-start.13) | collective-permute-done | bytes 65568 | tf_op jit(solution)/shard_map/ppermute | solution.py:256
  38.6 2.5 %collective-permute-done.12.refs_0_ = f32[128,128]{1,0:T(8,128)S(1)} collective-permute-done((f32[128,128]{1,0:T(8,128)S(1)}, f32[128,128]{1,0:T(8,128)S(1)}, u32[]{:S(2)}, u32[]{:S(2)}) %collective-permute-start.12) | collective-permute-done | bytes 65568 | tf_op jit(solution)/shard_map/ppermute | solution.py:258
  41.1 1.6 %collective-permute-done.15.refs_3_ = f32[128,128]{1,0:T(8,128)S(1)} collective-permute-done((f32[128,128]{1,0:T(8,128)S(1)}, f32[128,128]{1,0:T(8,128)S(1)}, u32[]{:S(2)}, u32[]{:S(2)}) %collective-permute-start.15) | collective-permute-done | bytes 65568 | tf_op jit(solution)/shard_map/ppermute | solution.py:256
  42.6 0.3 step4.1
  42.9 1.6 %collective-permute-start.17 = (f32[128,128]{1,0:T(8,128)S(1)}, f32[128,128]{1,0:T(8,128)S(1)}, u32[]{:S(2)}, u32[]{:S(2)}) collective-permute-start(f32[128,128]{1,0:T(8,128)S(1)} %get-tuple-element.109), channel_id=1, source_target_pairs={{0,1},{1,0},{2,3},{3,2},{4,6},{5,7},{6,4},{7,5},{8,9},{9,8},{10,11... | collective-permute-start | bytes 196616 | tf_op jit(solution)/shard_map/ppermute | solution.py:256
  44.5 2.8 %collective-permute-done.17.refs_2_ = f32[128,128]{1,0:T(8,128)S(1)} collective-permute-done((f32[128,128]{1,0:T(8,128)S(1)}, f32[128,128]{1,0:T(8,128)S(1)}, u32[]{:S(2)}, u32[]{:S(2)}) %collective-permute-start.17) | collective-permute-done | bytes 65568 | tf_op jit(solution)/shard_map/ppermute | solution.py:256
  47.5 2.5 %collective-permute-done.16.refs_0_ = f32[128,128]{1,0:T(8,128)S(1)} collective-permute-done((f32[128,128]{1,0:T(8,128)S(1)}, f32[128,128]{1,0:T(8,128)S(1)}, u32[]{:S(2)}, u32[]{:S(2)}) %collective-permute-start.16) | collective-permute-done | bytes 65568 | tf_op jit(solution)/shard_map/ppermute | solution.py:258
  50.0 1.6 %collective-permute-done.19.refs_3_ = f32[128,128]{1,0:T(8,128)S(1)} collective-permute-done((f32[128,128]{1,0:T(8,128)S(1)}, f32[128,128]{1,0:T(8,128)S(1)}, u32[]{:S(2)}, u32[]{:S(2)}) %collective-permute-start.19) | collective-permute-done | bytes 65568 | tf_op jit(solution)/shard_map/ppermute | solution.py:256
  51.5 0.3 step5.1
  51.9 1.6 %collective-permute-start.21 = (f32[128,128]{1,0:T(8,128)S(1)}, f32[128,128]{1,0:T(8,128)S(1)}, u32[]{:S(2)}, u32[]{:S(2)}) collective-permute-start(f32[128,128]{1,0:T(8,128)S(1)} %get-tuple-element.117), channel_id=1, source_target_pairs={{0,1},{1,0},{2,3},{3,2},{4,6},{5,7},{6,4},{7,5},{8,9},{9,8},{10,11... | collective-permute-start | bytes 196616 | tf_op jit(solution)/shard_map/ppermute | solution.py:256
  53.4 2.8 %collective-permute-done.21.refs_2_ = f32[128,128]{1,0:T(8,128)S(1)} collective-permute-done((f32[128,128]{1,0:T(8,128)S(1)}, f32[128,128]{1,0:T(8,128)S(1)}, u32[]{:S(2)}, u32[]{:S(2)}) %collective-permute-start.21) | collective-permute-done | bytes 65568 | tf_op jit(solution)/shard_map/ppermute | solution.py:256
  56.2 0.2 local5.1.resid
  56.4 2.5 %collective-permute-done.20.refs_0_ = f32[128,128]{1,0:T(8,128)S(1)} collective-permute-done((f32[128,128]{1,0:T(8,128)S(1)}, f32[128,128]{1,0:T(8,128)S(1)}, u32[]{:S(2)}, u32[]{:S(2)}) %collective-permute-start.20) | collective-permute-done | bytes 65568 | tf_op jit(solution)/shard_map/ppermute | solution.py:258
  58.9 1.6 %collective-permute-done.23.refs_3_ = f32[128,128]{1,0:T(8,128)S(1)} collective-permute-done((f32[128,128]{1,0:T(8,128)S(1)}, f32[128,128]{1,0:T(8,128)S(1)}, u32[]{:S(2)}, u32[]{:S(2)}) %collective-permute-start.23) | collective-permute-done | bytes 65568 | tf_op jit(solution)/shard_map/ppermute | solution.py:256
  60.5 0.3 step6.1
  60.8 1.6 %collective-permute-start.25 = (f32[128,128]{1,0:T(8,128)S(1)}, f32[128,128]{1,0:T(8,128)S(1)}, u32[]{:S(2)}, u32[]{:S(2)}) collective-permute-start(f32[128,128]{1,0:T(8,128)S(1)} %get-tuple-element.125), channel_id=1, source_target_pairs={{0,1},{1,0},{2,3},{3,2},{4,6},{5,7},{6,4},{7,5},{8,9},{9,8},{10,11... | collective-permute-start | bytes 196616 | tf_op jit(solution)/shard_map/ppermute | solution.py:256
  62.3 2.8 %collective-permute-done.25.refs_2_ = f32[128,128]{1,0:T(8,128)S(1)} collective-permute-done((f32[128,128]{1,0:T(8,128)S(1)}, f32[128,128]{1,0:T(8,128)S(1)}, u32[]{:S(2)}, u32[]{:S(2)}) %collective-permute-start.25) | collective-permute-done | bytes 65568 | tf_op jit(solution)/shard_map/ppermute | solution.py:256
  65.1 0.2 local6.1.resid
  65.3 2.5 %collective-permute-done.24.refs_0_ = f32[128,128]{1,0:T(8,128)S(1)} collective-permute-done((f32[128,128]{1,0:T(8,128)S(1)}, f32[128,128]{1,0:T(8,128)S(1)}, u32[]{:S(2)}, u32[]{:S(2)}) %collective-permute-start.24) | collective-permute-done | bytes 65568 | tf_op jit(solution)/shard_map/ppermute | solution.py:258
  67.8 1.6 %collective-permute-done.27.refs_3_ = f32[128,128]{1,0:T(8,128)S(1)} collective-permute-done((f32[128,128]{1,0:T(8,128)S(1)}, f32[128,128]{1,0:T(8,128)S(1)}, u32[]{:S(2)}, u32[]{:S(2)}) %collective-permute-start.27) | collective-permute-done | bytes 65568 | tf_op jit(solution)/shard_map/ppermute | solution.py:256
  69.4 0.3 step7.1
  69.7 1.6 %collective-permute-start.29 = (f32[128,128]{1,0:T(8,128)S(1)}, f32[128,128]{1,0:T(8,128)S(1)}, u32[]{:S(2)}, u32[]{:S(2)}) collective-permute-start(f32[128,128]{1,0:T(8,128)S(1)} %get-tuple-element.139), channel_id=1, source_target_pairs={{0,1},{1,0},{2,3},{3,2},{4,6},{5,7},{6,4},{7,5},{8,9},{9,8},{10,11... | collective-permute-start | bytes 196616 | tf_op jit(solution)/shard_map/ppermute | solution.py:256
  71.2 2.8 %collective-permute-done.29.refs_2_ = f32[128,128]{1,0:T(8,128)S(1)} collective-permute-done((f32[128,128]{1,0:T(8,128)S(1)}, f32[128,128]{1,0:T(8,128)S(1)}, u32[]{:S(2)}, u32[]{:S(2)}) %collective-permute-start.29) | collective-permute-done | bytes 65568 | tf_op jit(solution)/shard_map/ppermute | solution.py:256
  74.0 0.9 %local7.1 = (f32[8,64,128]{2,1,0:T(8,128)S(1)}, f32[8,64,128]{2,1,0:T(8,128)}) custom-call(s32[40]{0:T(128)S(4)} %get-tuple-element.72.table, f32[8,64,128]{2,1,0:T(8,128)S(1)} %local6.1.resid, bf16[8,6,128,128]{3,2,1,0:T(8,128)(2,1)S(1)} %get-tuple-element.74.coupling, ...), custom_call_target="tpu_custom_call", output_to_operand_aliasing={{0}: (1, {})} | custom-call | tf_op jit(solution)/shard_map/local7/pallas_call | solution.py:231
  74.9 1.8 %collective-permute-done.28.refs_0_ = f32[128,128]{1,0:T(8,128)S(1)} collective-permute-done((f32[128,128]{1,0:T(8,128)S(1)}, f32[128,128]{1,0:T(8,128)S(1)}, u32[]{:S(2)}, u32[]{:S(2)}) %collective-permute-start.28) | collective-permute-done | bytes 65568 | tf_op jit(solution)/shard_map/ppermute | solution.py:258
  76.7 1.6 %collective-permute-done.31.refs_3_ = f32[128,128]{1,0:T(8,128)S(1)} collective-permute-done((f32[128,128]{1,0:T(8,128)S(1)}, f32[128,128]{1,0:T(8,128)S(1)}, u32[]{:S(2)}, u32[]{:S(2)}) %collective-permute-start.31) | collective-permute-done | bytes 65568 | tf_op jit(solution)/shard_map/ppermute | solution.py:256
  78.3 0.9 %final.1 = f32[8,64,128]{2,1,0:T(8,128)} custom-call(f32[8,64,128]{2,1,0:T(8,128)S(1)} %get-tuple-element.135.resid, f32[128,128]{1,0:T(8,128)S(1)} %collective-permute-done.28.refs_0_, f32[128,128]{1,0:T(8,128)S(1)} %collective-permute-done.30.refs_1_, f32[128,128]{1,0:T(8,128)S(1)} %collective-permute-done.29.refs_2_, ...), custom_call_target="tpu_custom_call" | custom-call | tf_op jit(solution)/shard_map/final/pallas_call | solution.py:231
  (41 shorter events, 0.8 us)
Async XLA Ops:
  2.5 5.3 %collective-permute-start.1 = (f32[144,128]{1,0:T(8,128)S(1)}, f32[144,128]{1,0:T(8,128)S(1)}, u32[]{:S(2)}, u32[]{:S(2)}) collective-permute-start(f32[144,128]{1,0:T(8,128)S(1)} %get-tuple-element.80), channel_id=1, source_target_pairs={{0,1},{1,0},{2,3},{3,2},{4,6},{5,7},{6,4},{7,5},{8,9},{9,8},{10,11... | collective-permute-start | bytes 221192 | tf_op jit(solution)/shard_map/ppermute | solution.py:256
  7.8 8.1 %collective-permute-start.3 = (f32[144,128]{1,0:T(8,128)S(1)}, f32[144,128]{1,0:T(8,128)S(1)}, u32[]{:S(2)}, u32[]{:S(2)}) collective-permute-start(f32[144,128]{1,0:T(8,128)S(1)} %get-tuple-element.82), channel_id=1, source_target_pairs={{0,2},{1,3},{2,0},{3,1},{4,5},{5,4},{6,7},{7,6},{8,10},{9,11},{10,... | collective-permute-start | bytes 221192 | tf_op jit(solution)/shard_map/ppermute | solution.py:256
  9.9 6.0 %collective-permute-start = (f32[136,128]{1,0:T(8,128)S(1)}, f32[136,128]{1,0:T(8,128)S(1)}, u32[]{:S(2)}, u32[]{:S(2)}) collective-permute-start(f32[136,128]{1,0:T(8,128)S(1)} %get-tuple-element.77), channel_id=1, source_target_pairs={{0,28},{4,8},{8,4},{12,16},{16,12},{20,24},{24,20},{28,0},{1,29},{... | collective-permute-start | bytes 208904 | tf_op jit(solution)/shard_map/ppermute | solution.py:258
  11.5 4.4 %collective-permute-start.2 = (f32[136,128]{1,0:T(8,128)S(1)}, f32[136,128]{1,0:T(8,128)S(1)}, u32[]{:S(2)}, u32[]{:S(2)}) collective-permute-start(f32[136,128]{1,0:T(8,128)S(1)} %get-tuple-element.81), channel_id=1, source_target_pairs={{0,4},{4,0},{8,12},{12,8},{16,20},{20,16},{24,28},{28,24},{1,5},{5... | collective-permute-start | bytes 208904 | tf_op jit(solution)/shard_map/ppermute | solution.py:259
  16.2 4.3 %collective-permute-start.5 = (f32[128,128]{1,0:T(8,128)S(1)}, f32[128,128]{1,0:T(8,128)S(1)}, u32[]{:S(2)}, u32[]{:S(2)}) collective-permute-start(f32[128,128]{1,0:T(8,128)S(1)} %get-tuple-element.87), channel_id=1, source_target_pairs={{0,1},{1,0},{2,3},{3,2},{4,6},{5,7},{6,4},{7,5},{8,9},{9,8},{10,11... | collective-permute-start | bytes 196616 | tf_op jit(solution)/shard_map/ppermute | solution.py:256
  17.8 5.5 %collective-permute-start.4 = (f32[128,128]{1,0:T(8,128)S(1)}, f32[128,128]{1,0:T(8,128)S(1)}, u32[]{:S(2)}, u32[]{:S(2)}) collective-permute-start(f32[128,128]{1,0:T(8,128)S(1)} %get-tuple-element.84), channel_id=1, source_target_pairs={{0,28},{4,8},{8,4},{12,16},{16,12},{20,24},{24,20},{28,0},{1,29},{... | collective-permute-start | bytes 196616 | tf_op jit(solution)/shard_map/ppermute | solution.py:258
  20.5 2.7 %collective-permute-start.6 = (f32[128,128]{1,0:T(8,128)S(1)}, f32[128,128]{1,0:T(8,128)S(1)}, u32[]{:S(2)}, u32[]{:S(2)}) collective-permute-start(f32[128,128]{1,0:T(8,128)S(1)} %get-tuple-element.88), channel_id=1, source_target_pairs={{0,4},{4,0},{8,12},{12,8},{16,20},{20,16},{24,28},{28,24},{1,5},{5... | collective-permute-start | bytes 196616 | tf_op jit(solution)/shard_map/ppermute | solution.py:259
  20.5 4.3 %collective-permute-start.7 = (f32[128,128]{1,0:T(8,128)S(1)}, f32[128,128]{1,0:T(8,128)S(1)}, u32[]{:S(2)}, u32[]{:S(2)}) collective-permute-start(f32[128,128]{1,0:T(8,128)S(1)} %get-tuple-element.89), channel_id=1, source_target_pairs={{0,2},{1,3},{2,0},{3,1},{4,5},{5,4},{6,7},{7,6},{8,10},{9,11},{10,... | collective-permute-start | bytes 196616 | tf_op jit(solution)/shard_map/ppermute | solution.py:256
  25.1 4.3 %collective-permute-start.9 = (f32[128,128]{1,0:T(8,128)S(1)}, f32[128,128]{1,0:T(8,128)S(1)}, u32[]{:S(2)}, u32[]{:S(2)}) collective-permute-start(f32[128,128]{1,0:T(8,128)S(1)} %get-tuple-element.94), channel_id=1, source_target_pairs={{0,1},{1,0},{2,3},{3,2},{4,6},{5,7},{6,4},{7,5},{8,9},{9,8},{10,11... | collective-permute-start | bytes 196616 | tf_op jit(solution)/shard_map/ppermute | solution.py:256
  26.7 5.5 %collective-permute-start.8 = (f32[128,128]{1,0:T(8,128)S(1)}, f32[128,128]{1,0:T(8,128)S(1)}, u32[]{:S(2)}, u32[]{:S(2)}) collective-permute-start(f32[128,128]{1,0:T(8,128)S(1)} %get-tuple-element.91), channel_id=1, source_target_pairs={{0,28},{4,8},{8,4},{12,16},{16,12},{20,24},{24,20},{28,0},{1,29},{... | collective-permute-start | bytes 196616 | tf_op jit(solution)/shard_map/ppermute | solution.py:258
  29.5 2.7 %collective-permute-start.10 = (f32[128,128]{1,0:T(8,128)S(1)}, f32[128,128]{1,0:T(8,128)S(1)}, u32[]{:S(2)}, u32[]{:S(2)}) collective-permute-start(f32[128,128]{1,0:T(8,128)S(1)} %get-tuple-element.95), channel_id=1, source_target_pairs={{0,4},{4,0},{8,12},{12,8},{16,20},{20,16},{24,28},{28,24},{1,5},{5... | collective-permute-start | bytes 196616 | tf_op jit(solution)/shard_map/ppermute | solution.py:259
  29.5 4.3 %collective-permute-start.11 = (f32[128,128]{1,0:T(8,128)S(1)}, f32[128,128]{1,0:T(8,128)S(1)}, u32[]{:S(2)}, u32[]{:S(2)}) collective-permute-start(f32[128,128]{1,0:T(8,128)S(1)} %get-tuple-element.96), channel_id=1, source_target_pairs={{0,2},{1,3},{2,0},{3,1},{4,5},{5,4},{6,7},{7,6},{8,10},{9,11},{10,... | collective-permute-start | bytes 196616 | tf_op jit(solution)/shard_map/ppermute | solution.py:256
  34.0 4.3 %collective-permute-start.13 = (f32[128,128]{1,0:T(8,128)S(1)}, f32[128,128]{1,0:T(8,128)S(1)}, u32[]{:S(2)}, u32[]{:S(2)}) collective-permute-start(f32[128,128]{1,0:T(8,128)S(1)} %get-tuple-element.101), channel_id=1, source_target_pairs={{0,1},{1,0},{2,3},{3,2},{4,6},{5,7},{6,4},{7,5},{8,9},{9,8},{10,11... | collective-permute-start | bytes 196616 | tf_op jit(solution)/shard_map/ppermute | solution.py:256
  35.6 5.5 %collective-permute-start.12 = (f32[128,128]{1,0:T(8,128)S(1)}, f32[128,128]{1,0:T(8,128)S(1)}, u32[]{:S(2)}, u32[]{:S(2)}) collective-permute-start(f32[128,128]{1,0:T(8,128)S(1)} %get-tuple-element.98), channel_id=1, source_target_pairs={{0,28},{4,8},{8,4},{12,16},{16,12},{20,24},{24,20},{28,0},{1,29},{... | collective-permute-start | bytes 196616 | tf_op jit(solution)/shard_map/ppermute | solution.py:258
  38.4 2.7 %collective-permute-start.14 = (f32[128,128]{1,0:T(8,128)S(1)}, f32[128,128]{1,0:T(8,128)S(1)}, u32[]{:S(2)}, u32[]{:S(2)}) collective-permute-start(f32[128,128]{1,0:T(8,128)S(1)} %get-tuple-element.102), channel_id=1, source_target_pairs={{0,4},{4,0},{8,12},{12,8},{16,20},{20,16},{24,28},{28,24},{1,5},{5... | collective-permute-start | bytes 196616 | tf_op jit(solution)/shard_map/ppermute | solution.py:259
  38.4 4.3 %collective-permute-start.15 = (f32[128,128]{1,0:T(8,128)S(1)}, f32[128,128]{1,0:T(8,128)S(1)}, u32[]{:S(2)}, u32[]{:S(2)}) collective-permute-start(f32[128,128]{1,0:T(8,128)S(1)} %get-tuple-element.103), channel_id=1, source_target_pairs={{0,2},{1,3},{2,0},{3,1},{4,5},{5,4},{6,7},{7,6},{8,10},{9,11},{10,... | collective-permute-start | bytes 196616 | tf_op jit(solution)/shard_map/ppermute | solution.py:256
  42.9 4.3 %collective-permute-start.17 = (f32[128,128]{1,0:T(8,128)S(1)}, f32[128,128]{1,0:T(8,128)S(1)}, u32[]{:S(2)}, u32[]{:S(2)}) collective-permute-start(f32[128,128]{1,0:T(8,128)S(1)} %get-tuple-element.109), channel_id=1, source_target_pairs={{0,1},{1,0},{2,3},{3,2},{4,6},{5,7},{6,4},{7,5},{8,9},{9,8},{10,11... | collective-permute-start | bytes 196616 | tf_op jit(solution)/shard_map/ppermute | solution.py:256
  44.5 5.5 %collective-permute-start.16 = (f32[128,128]{1,0:T(8,128)S(1)}, f32[128,128]{1,0:T(8,128)S(1)}, u32[]{:S(2)}, u32[]{:S(2)}) collective-permute-start(f32[128,128]{1,0:T(8,128)S(1)} %get-tuple-element.106), channel_id=1, source_target_pairs={{0,28},{4,8},{8,4},{12,16},{16,12},{20,24},{24,20},{28,0},{1,29},{... | collective-permute-start | bytes 196616 | tf_op jit(solution)/shard_map/ppermute | solution.py:258
  47.3 2.7 %collective-permute-start.18 = (f32[128,128]{1,0:T(8,128)S(1)}, f32[128,128]{1,0:T(8,128)S(1)}, u32[]{:S(2)}, u32[]{:S(2)}) collective-permute-start(f32[128,128]{1,0:T(8,128)S(1)} %get-tuple-element.110), channel_id=1, source_target_pairs={{0,4},{4,0},{8,12},{12,8},{16,20},{20,16},{24,28},{28,24},{1,5},{5... | collective-permute-start | bytes 196616 | tf_op jit(solution)/shard_map/ppermute | solution.py:259
  47.3 4.3 %collective-permute-start.19 = (f32[128,128]{1,0:T(8,128)S(1)}, f32[128,128]{1,0:T(8,128)S(1)}, u32[]{:S(2)}, u32[]{:S(2)}) collective-permute-start(f32[128,128]{1,0:T(8,128)S(1)} %get-tuple-element.111), channel_id=1, source_target_pairs={{0,2},{1,3},{2,0},{3,1},{4,5},{5,4},{6,7},{7,6},{8,10},{9,11},{10,... | collective-permute-start | bytes 196616 | tf_op jit(solution)/shard_map/ppermute | solution.py:256
  51.9 4.3 %collective-permute-start.21 = (f32[128,128]{1,0:T(8,128)S(1)}, f32[128,128]{1,0:T(8,128)S(1)}, u32[]{:S(2)}, u32[]{:S(2)}) collective-permute-start(f32[128,128]{1,0:T(8,128)S(1)} %get-tuple-element.117), channel_id=1, source_target_pairs={{0,1},{1,0},{2,3},{3,2},{4,6},{5,7},{6,4},{7,5},{8,9},{9,8},{10,11... | collective-permute-start | bytes 196616 | tf_op jit(solution)/shard_map/ppermute | solution.py:256
  53.4 5.5 %collective-permute-start.20 = (f32[128,128]{1,0:T(8,128)S(1)}, f32[128,128]{1,0:T(8,128)S(1)}, u32[]{:S(2)}, u32[]{:S(2)}) collective-permute-start(f32[128,128]{1,0:T(8,128)S(1)} %get-tuple-element.114), channel_id=1, source_target_pairs={{0,28},{4,8},{8,4},{12,16},{16,12},{20,24},{24,20},{28,0},{1,29},{... | collective-permute-start | bytes 196616 | tf_op jit(solution)/shard_map/ppermute | solution.py:258
  56.2 2.7 %collective-permute-start.22 = (f32[128,128]{1,0:T(8,128)S(1)}, f32[128,128]{1,0:T(8,128)S(1)}, u32[]{:S(2)}, u32[]{:S(2)}) collective-permute-start(f32[128,128]{1,0:T(8,128)S(1)} %get-tuple-element.118), channel_id=1, source_target_pairs={{0,4},{4,0},{8,12},{12,8},{16,20},{20,16},{24,28},{28,24},{1,5},{5... | collective-permute-start | bytes 196616 | tf_op jit(solution)/shard_map/ppermute | solution.py:259
  56.2 4.3 %collective-permute-start.23 = (f32[128,128]{1,0:T(8,128)S(1)}, f32[128,128]{1,0:T(8,128)S(1)}, u32[]{:S(2)}, u32[]{:S(2)}) collective-permute-start(f32[128,128]{1,0:T(8,128)S(1)} %get-tuple-element.119), channel_id=1, source_target_pairs={{0,2},{1,3},{2,0},{3,1},{4,5},{5,4},{6,7},{7,6},{8,10},{9,11},{10,... | collective-permute-start | bytes 196616 | tf_op jit(solution)/shard_map/ppermute | solution.py:256
  60.8 4.3 %collective-permute-start.25 = (f32[128,128]{1,0:T(8,128)S(1)}, f32[128,128]{1,0:T(8,128)S(1)}, u32[]{:S(2)}, u32[]{:S(2)}) collective-permute-start(f32[128,128]{1,0:T(8,128)S(1)} %get-tuple-element.125), channel_id=1, source_target_pairs={{0,1},{1,0},{2,3},{3,2},{4,6},{5,7},{6,4},{7,5},{8,9},{9,8},{10,11... | collective-permute-start | bytes 196616 | tf_op jit(solution)/shard_map/ppermute | solution.py:256
  62.3 5.5 %collective-permute-start.24 = (f32[128,128]{1,0:T(8,128)S(1)}, f32[128,128]{1,0:T(8,128)S(1)}, u32[]{:S(2)}, u32[]{:S(2)}) collective-permute-start(f32[128,128]{1,0:T(8,128)S(1)} %get-tuple-element.122), channel_id=1, source_target_pairs={{0,28},{4,8},{8,4},{12,16},{16,12},{20,24},{24,20},{28,0},{1,29},{... | collective-permute-start | bytes 196616 | tf_op jit(solution)/shard_map/ppermute | solution.py:258
  65.1 2.7 %collective-permute-start.26 = (f32[128,128]{1,0:T(8,128)S(1)}, f32[128,128]{1,0:T(8,128)S(1)}, u32[]{:S(2)}, u32[]{:S(2)}) collective-permute-start(f32[128,128]{1,0:T(8,128)S(1)} %get-tuple-element.126), channel_id=1, source_target_pairs={{0,4},{4,0},{8,12},{12,8},{16,20},{20,16},{24,28},{28,24},{1,5},{5... | collective-permute-start | bytes 196616 | tf_op jit(solution)/shard_map/ppermute | solution.py:259
  65.1 4.3 %collective-permute-start.27 = (f32[128,128]{1,0:T(8,128)S(1)}, f32[128,128]{1,0:T(8,128)S(1)}, u32[]{:S(2)}, u32[]{:S(2)}) collective-permute-start(f32[128,128]{1,0:T(8,128)S(1)} %get-tuple-element.127), channel_id=1, source_target_pairs={{0,2},{1,3},{2,0},{3,1},{4,5},{5,4},{6,7},{7,6},{8,10},{9,11},{10,... | collective-permute-start | bytes 196616 | tf_op jit(solution)/shard_map/ppermute | solution.py:256
  69.7 4.3 %collective-permute-start.29 = (f32[128,128]{1,0:T(8,128)S(1)}, f32[128,128]{1,0:T(8,128)S(1)}, u32[]{:S(2)}, u32[]{:S(2)}) collective-permute-start(f32[128,128]{1,0:T(8,128)S(1)} %get-tuple-element.139), channel_id=1, source_target_pairs={{0,1},{1,0},{2,3},{3,2},{4,6},{5,7},{6,4},{7,5},{8,9},{9,8},{10,11... | collective-permute-start | bytes 196616 | tf_op jit(solution)/shard_map/ppermute | solution.py:256
  71.2 5.5 %collective-permute-start.28 = (f32[128,128]{1,0:T(8,128)S(1)}, f32[128,128]{1,0:T(8,128)S(1)}, u32[]{:S(2)}, u32[]{:S(2)}) collective-permute-start(f32[128,128]{1,0:T(8,128)S(1)} %get-tuple-element.136), channel_id=1, source_target_pairs={{0,28},{4,8},{8,4},{12,16},{16,12},{20,24},{24,20},{28,0},{1,29},{... | collective-permute-start | bytes 196616 | tf_op jit(solution)/shard_map/ppermute | solution.py:258
  74.0 2.7 %collective-permute-start.30 = (f32[128,128]{1,0:T(8,128)S(1)}, f32[128,128]{1,0:T(8,128)S(1)}, u32[]{:S(2)}, u32[]{:S(2)}) collective-permute-start(f32[128,128]{1,0:T(8,128)S(1)} %get-tuple-element.140), channel_id=1, source_target_pairs={{0,4},{4,0},{8,12},{12,8},{16,20},{20,16},{24,28},{28,24},{1,5},{5... | collective-permute-start | bytes 196616 | tf_op jit(solution)/shard_map/ppermute | solution.py:259
  74.0 4.3 %collective-permute-start.31 = (f32[128,128]{1,0:T(8,128)S(1)}, f32[128,128]{1,0:T(8,128)S(1)}, u32[]{:S(2)}, u32[]{:S(2)}) collective-permute-start(f32[128,128]{1,0:T(8,128)S(1)} %get-tuple-element.141), channel_id=1, source_target_pairs={{0,2},{1,3},{2,0},{3,1},{4,5},{5,4},{6,7},{7,6},{8,10},{9,11},{10,... | collective-permute-start | bytes 196616 | tf_op jit(solution)/shard_map/ppermute | solution.py:256

commit v5 on v3

--- a/solution.py
+++ b/solution.py
@@ -24,29 +24,25 @@
     def __init__(self, rows, rhs_count, width, group):
         self.rows, self.n, self.w, self.group = rows, rhs_count, width, group
         self.quarter = rows // COLORS
-        self.lanes = 3
+        self.lanes = group + 1
         self.order, self.local, self.slot = 0, rows, 3 * rows
         self.table = 5 * rows
         self.dom_meta = -(-rows // 8) * 8
 
-    def stride(self, step):
-        return self.n + (META if step == 0 else 0)
-
-    def at(self, member, step):
-        return member * self.stride(step)
-
     def types(self, step):
-        dom = self.quarter * self.n + (self.dom_meta if step == 0 else 0)
-        shapes = [dom, dom] + [self.group * self.stride(step)]
+        extra = (self.dom_meta, META) if step == 0 else (0, 0)
+        dom, one = self.quarter * self.n + extra[0], self.n + extra[1]
+        shapes = [dom] + [one] * (self.group - 1) + [dom]
         return [pltpu.VMEM((length, self.w), jnp.float32) for length in shapes]
 
 
 def items_of(plan, step, got, meta):
     color = step % COLORS
     out = []
-    for q in range(plan.group):
-        out.append((meta[2], plan.at(q, 0) + plan.n + color, got[2], plan.at(q, step)))
-    for lane in range(2):
+    for lane in range(plan.lanes):
+        if 0 < lane < plan.group:
+            out.append((meta[lane], plan.n + color, got[lane], 0))
+            continue
         for p in range(plan.quarter):
             line = plan.quarter * plan.n + color * plan.quarter + p
             out.append((meta[lane], line, got[lane], p * plan.n))
@@ -60,27 +56,31 @@
     return value
 
 
+def lanes_of(plan, refs):
+    return refs[: plan.lanes], refs[plan.lanes :]
+
+
 def products(plan, step, table, changes, coupling, sends):
     parity = lax.rem(lax.axis_index("dom"), 2)
-    far, near = sends[:2]
+    far, near = sends[0], sends[-1]
     terms = []
     for p in range(plan.quarter):
         at = step % COLORS * plan.quarter + p
         j = table[plan.order + at]
-        both = dot(changes[p], jnp.concatenate([coupling[j, 2], coupling[j, 3]], axis=1))
-        for k in range(2):
-            terms.append((table[plan.slot + 2 * at + k], both[:, k * plan.w : (k + 1) * plan.w]))
         both = dot(
             changes[p],
             jnp.concatenate([coupling[j, 5 - parity], coupling[j, 4 + parity]], axis=1),
         )
         far[pl.ds(p * plan.n, plan.n), :] = both[:, : plan.w]
         near[pl.ds(p * plan.n, plan.n), :] = both[:, plan.w :]
-    for q in range(plan.group):
+        both = dot(changes[p], jnp.concatenate([coupling[j, 2], coupling[j, 3]], axis=1))
+        for k in range(2):
+            terms.append((table[plan.slot + 2 * at + k], both[:, k * plan.w : (k + 1) * plan.w]))
+    for s in range(1, plan.group):
         total = jnp.zeros((plan.n, plan.w), jnp.float32)
         for slot, term in terms:
-            total = total + jnp.where(slot == q, term, 0.0)
-        sends[2][pl.ds(plan.at(q, step), plan.n), :] = total
+            total = total + jnp.where(slot == s, term, 0.0)
+        sends[s][pl.ds(0, plan.n), :] = total
 
 
 def first_kernel(plan, *refs):
@@ -97,6 +97,7 @@
         copy.start()
     for copy in copies[:5]:
         copy.wait()
+    me = lax.axis_index("sub")
     parity = lax.rem(lax.axis_index("dom"), 2)
     colors = [color[i] for i in range(plan.rows)]
     for i in range(plan.rows):
@@ -107,15 +108,15 @@
         table[plan.order + at] = i
         for k in range(2):
             table[plan.local + 2 * at + k] = local_target[k, i]
-            table[plan.slot + 2 * at + k] = group_peer[k, i]
+            table[plan.slot + 2 * at + k] = me ^ group_peer[k, i]
     line = lax.broadcasted_iota(jnp.int32, (META, plan.w), 0)
-    for q in range(plan.group):
+    for s in range(1, plan.group):
         meta = jnp.full((META, plan.w), -1, jnp.int32)
         for c in range(COLORS):
-            meta = jnp.where(line == c, group_list[0, c, q], meta)
-        sends[2][pl.ds(plan.at(q, 0) + plan.n, META), :] = meta.astype(jnp.float32)
+            meta = jnp.where(line == c, group_list[0, c, me ^ s], meta)
+        sends[s][pl.ds(plan.n, META), :] = meta.astype(jnp.float32)
     line = lax.broadcasted_iota(jnp.int32, (plan.dom_meta, plan.w), 0)
-    for send, k in zip(sends[:2], (1 - parity, parity)):
+    for send, k in ((sends[0], 1 - parity), (sends[-1], parity)):
         meta = jnp.full((plan.dom_meta, plan.w), -1, jnp.int32)
         for at in range(plan.rows):
             meta = jnp.where(line == at, dom_target[k, table[plan.order + at]], meta)
@@ -134,7 +135,8 @@
 
 
 def step_kernel(plan, step, table, resid, diag, coupling, *refs):
-    got, meta, refs = refs[: plan.lanes], refs[plan.lanes : 2 * plan.lanes], refs[2 * plan.lanes :]
+    got, refs = lanes_of(plan, refs)
+    meta, refs = lanes_of(plan, refs)
     has_old = step >= COLORS
     if has_old:
         old, refs = refs[0], refs[1:]
@@ -153,11 +155,12 @@
     products(plan, step, table, changes, coupling, refs[2:])
 
 
-def local_kernel(plan, step, last, table, resid, coupling, change, *refs):
+def local_kernel(plan, step, last, table, resid, coupling, change, near, *refs):
     items = []
     if step > 0:
-        items = items_of(plan, step - 1, refs[: plan.lanes], refs[plan.lanes : 2 * plan.lanes])
-        refs = refs[2 * plan.lanes :]
+        got, refs = lanes_of(plan, refs)
+        meta, refs = lanes_of(plan, refs)
+        items = items_of(plan, step - 1, got, meta)
     if last:
         sols, refs = refs[:COLORS], refs[COLORS:]
     out = refs[0]
@@ -173,11 +176,13 @@
     if last:
         for c in range(COLORS):
             for p in range(plan.quarter):
-                refs[1][table[plan.order + c * plan.quarter + p]] = sols[c][p]
+                refs[2][table[plan.order + c * plan.quarter + p]] = sols[c][p]
 
 
 def final_kernel(plan, step, resid, *refs):
-    items = items_of(plan, step, refs[: plan.lanes], refs[plan.lanes : 2 * plan.lanes])
+    got, refs = lanes_of(plan, refs)
+    meta, refs = lanes_of(plan, refs)
+    items = items_of(plan, step, got, meta)
     out = refs[-1]
     for r in range(plan.rows):
         out[r] = subtract(plan, resid[r], jnp.float32(r), items)
@@ -186,7 +191,7 @@
 def on_device(coupling, diag_inv, rhs, color, local_target, group_peer, group_list, dom_target):
     rows, rhs_count, width = rhs.shape
     doms, group = lax.axis_size("dom"), lax.axis_size("sub")
-    assert doms % 2 == 0
+    assert group & (group - 1) == 0 and doms % 2 == 0
     plan = Plan(rows, rhs_count, width, group)
     f32 = jnp.float32
     near_pairs = [(i, i ^ 1) for i in range(doms)]
@@ -205,10 +210,11 @@
             **kw,
         )(*ins)
 
-    def exchange(step, sends):
-        far = lax.ppermute(sends[0], "dom", far_pairs)
-        near = lax.ppermute(sends[1], "dom", near_pairs)
-        return [far, near, lax.all_to_all(sends[2], "sub", 0, 0, tiled=True)]
+    def exchange(sends):
+        got = [lax.ppermute(sends[0], "dom", far_pairs)]
+        for s in reversed(range(1, group)):
+            got.insert(1, lax.ppermute(sends[s], "sub", [(i, i ^ s) for i in range(group)]))
+        return got + [lax.ppermute(sends[-1], "dom", near_pairs)]
 
     sol_t = pltpu.VMEM((plan.quarter, plan.n, plan.w), f32)
     change_t = pltpu.VMEM((plan.quarter, plan.n, plan.w), jnp.bfloat16)
@@ -251,20 +257,20 @@
             )
             sols[c:] = [sol] + sols[c + 1 :]
         last = step == steps - 1
-        ins = [table, resid, tiles, change]
+        ins = [table, resid, tiles, change, sends[-1]]
         if step > 0:
             ins += [*got, *meta]
         if last:
             ins += sols
-        resid, *rest = call(
+        resid, sends[-1], *rest = call(
             functools.partial(local_kernel, plan, step, last),
             f"local{step}",
             ins,
             [SMEM],
-            [resid_t] + ([jax.ShapeDtypeStruct(rhs.shape, f32)] if last else []),
-            input_output_aliases={1: 0},
+            [resid_t, plan.types(step)[-1]] + ([jax.ShapeDtypeStruct(rhs.shape, f32)] if last else []),
+            input_output_aliases={1: 0, 4: 1},
         )
-        got = exchange(step, sends)
+        got = exchange(sends)
         if step == 0:
             meta = got
     (defect,) = call(

time: 90.8 us -> 76.5 us (0.84)
  waiting for transfers between devices: 35.7 us -> 26.9 us
  Pallas kernels: 12.5 us -> 7.16 us
    ppermute x16 -> x40, starting transfers between devices: 6.31 us -> 41.4 us  [the longest x24 27.9 us: exchange(): lax.ppermute(sends[s], 'sub', [(i, i ^ s) for i in range(group)])]
    all_to_all x8 -> x0, starting transfers between devices: 34.5 us -> none  [exchange(): return [far, near, lax.all_to_all(sends[2], 'sub', 0, 0, tiled=True)]]
    ppermute x16 -> x40, waiting for transfers between devices: 35.7 us -> 26.9 us  [the longest x24 26.9 us: exchange(): lax.ppermute(sends[s], 'sub', [(i, i ^ s) for i in range(group)])]
    pallas_call x17, Pallas kernels: 12.5 us -> 7.16 us  [call(): pl.pallas_call(body, name=name, in_specs=in_specs + [VMEM] * (len(ins) -...]
  transfers between devices with their start and end apart: 24 -> 40, of which waited for: 8 -> 24; matrix products, arithmetic and copies ran while one was open for 0% -> 0% of each run, Pallas kernels for 3% -> 0%
where the time goes in v5:
time: 76.5 us; the launch traced here: 76.3 us
  starting transfers between devices  41.4 us (54%)
  waiting for transfers between devices  26.9 us (35%)
  Pallas kernels  7.16 us (9%)
  between operations  0.83 us (1%)
    ppermute x24, starting transfers between devices, exchange(): lax.ppermute(sends[s], 'sub', [(i, i ^ s) for i in range(group)])  27.9 us
    ppermute x24, waiting for transfers between devices, exchange(): lax.ppermute(sends[s], 'sub', [(i, i ^ s) for i in range(group)])  26.9 us
    ppermute x8, starting transfers between devices, exchange(): got = [lax.ppermute(sends[0], 'dom', far_pairs)]  12.6 us
    pallas_call x17, Pallas kernels, call(): pl.pallas_call(body, name=name, in_specs=in_specs + [VMEM] * (len(ins) -...  7.16 us
  transfers between devices with their start and end apart: 40, of which 24 were waited for; matrix products, arithmetic and copies ran while one was open for 0% of the time, Pallas kernels for 0%

profile of v5, /device:TPU:0, one launch (start us, length us, event | category | flops | bytes accessed | tf_op | source)
XLA Modules:
  0.0 76.3 jit_solution(16045567931714534777)
XLA Ops:
  0.6 1.8 %first.1 = (s32[40]{0:T(128)S(4)}, bf16[8,6,128,128]{3,2,1,0:T(8,128)(2,1)S(1)}, bf16[8,128,128]{2,1,0:T(8,128)(2,1)S(1)}, f32[8,64,128]{2,1,0:T(8,128)S(1)}, f3...) custom-call(s32[8]{0:T(128)} %refs_0_.1, ...), custom_call_target="tpu_custom_call" | custom-call | tf_op jit(solution)/shard_map/first/pallas_call | solution.py:203
  2.7 0.5 collective-permute-start.4
  3.2 4.7 %collective-permute-start = (f32[136,128]{1,0:T(8,128)S(1)}, f32[136,128]{1,0:T(8,128)S(1)}, u32[]{:S(2)}, u32[]{:S(2)}) collective-permute-start(f32[136,128]{1,0:T(8,128)S(1)} %get-tuple-element.86), channel_id=1, source_target_pairs={{0,28},{4,8},{8,4},{12,16},{16,12},{20,24},{24,20},{28,0},{1,29},{... | collective-permute-start | bytes 208904 | tf_op jit(solution)/shard_map/ppermute | solution.py:214
  7.9 1.5 %collective-permute-start.1 = (f32[72,128]{1,0:T(8,128)S(1)}, f32[72,128]{1,0:T(8,128)S(1)}, u32[]{:S(2)}, u32[]{:S(2)}) collective-permute-start(f32[72,128]{1,0:T(8,128)S(1)} %get-tuple-element.87), channel_id=1, source_target_pairs={{0,1},{1,0},{2,3},{3,2},{4,5},{5,4},{6,7},{7,6},{8,9},{9,8},{10,11... | collective-permute-start | bytes 110600 | tf_op jit(solution)/shard_map/ppermute | solution.py:216
  9.4 1.5 %collective-permute-start.2 = (f32[72,128]{1,0:T(8,128)S(1)}, f32[72,128]{1,0:T(8,128)S(1)}, u32[]{:S(2)}, u32[]{:S(2)}) collective-permute-start(f32[72,128]{1,0:T(8,128)S(1)} %get-tuple-element.88), channel_id=1, source_target_pairs={{0,2},{1,3},{2,0},{3,1},{4,6},{5,7},{6,4},{7,5},{8,10},{9,11},{10,... | collective-permute-start | bytes 110600 | tf_op jit(solution)/shard_map/ppermute | solution.py:216
  11.8 1.5 %collective-permute-done.2.refs_2_.refs_7_ = f32[72,128]{1,0:T(8,128)S(1)} collective-permute-done((f32[72,128]{1,0:T(8,128)S(1)}, f32[72,128]{1,0:T(8,128)S(1)}, u32[]{:S(2)}, u32[]{:S(2)}) %collective-permute-start.2) | collective-permute-done | bytes 36896 | tf_op jit(solution)/shard_map/ppermute | solution.py:216
  13.3 2.4 %collective-permute-done.3.refs_3_.refs_8_ = f32[72,128]{1,0:T(8,128)S(1)} collective-permute-done((f32[72,128]{1,0:T(8,128)S(1)}, f32[72,128]{1,0:T(8,128)S(1)}, u32[]{:S(2)}, u32[]{:S(2)}) %collective-permute-start.3) | collective-permute-done | bytes 36896 | tf_op jit(solution)/shard_map/ppermute | solution.py:216
  16.4 0.5 collective-permute-start.5
  16.9 0.5 collective-permute-start.6
  17.5 0.5 collective-permute-start.7
  18.0 2.4 %collective-permute-start.8 = (f32[64,128]{1,0:T(8,128)S(1)}, f32[64,128]{1,0:T(8,128)S(1)}, u32[]{:S(2)}, u32[]{:S(2)}) collective-permute-start(f32[64,128]{1,0:T(8,128)S(1)} %get-tuple-element.97), channel_id=1, source_target_pairs={{0,3},{1,2},{2,1},{3,0},{4,7},{5,6},{6,5},{7,4},{8,11},{9,10},{10,... | collective-permute-start | bytes 98312 | tf_op jit(solution)/shard_map/ppermute | solution.py:216
  20.8 0.7 collective-permute-done.7.refs_2_
  21.6 1.2 %collective-permute-done.8.refs_3_ = f32[64,128]{1,0:T(8,128)S(1)} collective-permute-done((f32[64,128]{1,0:T(8,128)S(1)}, f32[64,128]{1,0:T(8,128)S(1)}, u32[]{:S(2)}, u32[]{:S(2)}) %collective-permute-start.8) | collective-permute-done | bytes 32800 | tf_op jit(solution)/shard_map/ppermute | solution.py:216
  23.4 1.4 %collective-permute-start.10 = (f32[128,128]{1,0:T(8,128)S(1)}, f32[128,128]{1,0:T(8,128)S(1)}, u32[]{:S(2)}, u32[]{:S(2)}) collective-permute-start(f32[128,128]{1,0:T(8,128)S(1)} %get-tuple-element.102), channel_id=1, source_target_pairs={{0,28},{4,8},{8,4},{12,16},{16,12},{20,24},{24,20},{28,0},{1,29},{... | collective-permute-start | bytes 196616 | tf_op jit(solution)/shard_map/ppermute | solution.py:214
  24.8 1.5 %collective-permute-start.11 = (f32[64,128]{1,0:T(8,128)S(1)}, f32[64,128]{1,0:T(8,128)S(1)}, u32[]{:S(2)}, u32[]{:S(2)}) collective-permute-start(f32[64,128]{1,0:T(8,128)S(1)} %get-tuple-element.103), channel_id=1, source_target_pairs={{0,1},{1,0},{2,3},{3,2},{4,5},{5,4},{6,7},{7,6},{8,9},{9,8},{10,11... | collective-permute-start | bytes 98312 | tf_op jit(solution)/shard_map/ppermute | solution.py:216
  26.3 1.5 %collective-permute-start.12 = (f32[64,128]{1,0:T(8,128)S(1)}, f32[64,128]{1,0:T(8,128)S(1)}, u32[]{:S(2)}, u32[]{:S(2)}) collective-permute-start(f32[64,128]{1,0:T(8,128)S(1)} %get-tuple-element.104), channel_id=1, source_target_pairs={{0,2},{1,3},{2,0},{3,1},{4,6},{5,7},{6,4},{7,5},{8,10},{9,11},{10,... | collective-permute-start | bytes 98312 | tf_op jit(solution)/shard_map/ppermute | solution.py:216
  28.7 1.5 %collective-permute-done.12.refs_2_ = f32[64,128]{1,0:T(8,128)S(1)} collective-permute-done((f32[64,128]{1,0:T(8,128)S(1)}, f32[64,128]{1,0:T(8,128)S(1)}, u32[]{:S(2)}, u32[]{:S(2)}) %collective-permute-start.12) | collective-permute-done | bytes 32800 | tf_op jit(solution)/shard_map/ppermute | solution.py:216
  30.2 2.4 %collective-permute-done.13.refs_3_ = f32[64,128]{1,0:T(8,128)S(1)} collective-permute-done((f32[64,128]{1,0:T(8,128)S(1)}, f32[64,128]{1,0:T(8,128)S(1)}, u32[]{:S(2)}, u32[]{:S(2)}) %collective-permute-start.13) | collective-permute-done | bytes 32800 | tf_op jit(solution)/shard_map/ppermute | solution.py:216
  33.3 0.6 collective-permute-start.15
  33.8 0.5 collective-permute-start.16
  34.3 0.5 collective-permute-start.17
  34.9 2.4 %collective-permute-start.18 = (f32[64,128]{1,0:T(8,128)S(1)}, f32[64,128]{1,0:T(8,128)S(1)}, u32[]{:S(2)}, u32[]{:S(2)}) collective-permute-start(f32[64,128]{1,0:T(8,128)S(1)} %get-tuple-element.113), channel_id=1, source_target_pairs={{0,3},{1,2},{2,1},{3,0},{4,7},{5,6},{6,5},{7,4},{8,11},{9,10},{10,... | collective-permute-start | bytes 98312 | tf_op jit(solution)/shard_map/ppermute | solution.py:216
  37.7 0.9 %collective-permute-done.17.refs_2_ = f32[64,128]{1,0:T(8,128)S(1)} collective-permute-done((f32[64,128]{1,0:T(8,128)S(1)}, f32[64,128]{1,0:T(8,128)S(1)}, u32[]{:S(2)}, u32[]{:S(2)}) %collective-permute-start.17) | collective-permute-done | bytes 32800 | tf_op jit(solution)/shard_map/ppermute | solution.py:216
  38.6 1.1 %collective-permute-done.18.refs_3_ = f32[64,128]{1,0:T(8,128)S(1)} collective-permute-done((f32[64,128]{1,0:T(8,128)S(1)}, f32[64,128]{1,0:T(8,128)S(1)}, u32[]{:S(2)}, u32[]{:S(2)}) %collective-permute-start.18) | collective-permute-done | bytes 32800 | tf_op jit(solution)/shard_map/ppermute | solution.py:216
  40.3 2.8 %collective-permute-start.20 = (f32[128,128]{1,0:T(8,128)S(1)}, f32[128,128]{1,0:T(8,128)S(1)}, u32[]{:S(2)}, u32[]{:S(2)}) collective-permute-start(f32[128,128]{1,0:T(8,128)S(1)} %get-tuple-element.119), channel_id=1, source_target_pairs={{0,28},{4,8},{8,4},{12,16},{16,12},{20,24},{24,20},{28,0},{1,29},{... | collective-permute-start | bytes 196616 | tf_op jit(solution)/shard_map/ppermute | solution.py:214
  43.1 1.5 %collective-permute-start.21 = (f32[64,128]{1,0:T(8,128)S(1)}, f32[64,128]{1,0:T(8,128)S(1)}, u32[]{:S(2)}, u32[]{:S(2)}) collective-permute-start(f32[64,128]{1,0:T(8,128)S(1)} %get-tuple-element.120), channel_id=1, source_target_pairs={{0,1},{1,0},{2,3},{3,2},{4,5},{5,4},{6,7},{7,6},{8,9},{9,8},{10,11... | collective-permute-start | bytes 98312 | tf_op jit(solution)/shard_map/ppermute | solution.py:216
  44.6 1.5 %collective-permute-start.22 = (f32[64,128]{1,0:T(8,128)S(1)}, f32[64,128]{1,0:T(8,128)S(1)}, u32[]{:S(2)}, u32[]{:S(2)}) collective-permute-start(f32[64,128]{1,0:T(8,128)S(1)} %get-tuple-element.121), channel_id=1, source_target_pairs={{0,2},{1,3},{2,0},{3,1},{4,6},{5,7},{6,4},{7,5},{8,10},{9,11},{10,... | collective-permute-start | bytes 98312 | tf_op jit(solution)/shard_map/ppermute | solution.py:216
  47.0 1.7 %collective-permute-done.22.refs_2_ = f32[64,128]{1,0:T(8,128)S(1)} collective-permute-done((f32[64,128]{1,0:T(8,128)S(1)}, f32[64,128]{1,0:T(8,128)S(1)}, u32[]{:S(2)}, u32[]{:S(2)}) %collective-permute-start.22) | collective-permute-done | bytes 32800 | tf_op jit(solution)/shard_map/ppermute | solution.py:216
  48.7 2.3 %collective-permute-done.23.refs_3_ = f32[64,128]{1,0:T(8,128)S(1)} collective-permute-done((f32[64,128]{1,0:T(8,128)S(1)}, f32[64,128]{1,0:T(8,128)S(1)}, u32[]{:S(2)}, u32[]{:S(2)}) %collective-permute-start.23) | collective-permute-done | bytes 32800 | tf_op jit(solution)/shard_map/ppermute | solution.py:216
  51.6 0.5 collective-permute-start.25
  52.1 0.5 collective-permute-start.26
  52.7 0.5 collective-permute-start.27
  53.2 2.4 %collective-permute-start.28 = (f32[64,128]{1,0:T(8,128)S(1)}, f32[64,128]{1,0:T(8,128)S(1)}, u32[]{:S(2)}, u32[]{:S(2)}) collective-permute-start(f32[64,128]{1,0:T(8,128)S(1)} %get-tuple-element.131), channel_id=1, source_target_pairs={{0,3},{1,2},{2,1},{3,0},{4,7},{5,6},{6,5},{7,4},{8,11},{9,10},{10,... | collective-permute-start | bytes 98312 | tf_op jit(solution)/shard_map/ppermute | solution.py:216
  56.0 0.7 collective-permute-done.27.refs_2_
  56.7 1.2 %collective-permute-done.28.refs_3_ = f32[64,128]{1,0:T(8,128)S(1)} collective-permute-done((f32[64,128]{1,0:T(8,128)S(1)}, f32[64,128]{1,0:T(8,128)S(1)}, u32[]{:S(2)}, u32[]{:S(2)}) %collective-permute-start.28) | collective-permute-done | bytes 32800 | tf_op jit(solution)/shard_map/ppermute | solution.py:216
  58.6 1.4 %collective-permute-start.30 = (f32[128,128]{1,0:T(8,128)S(1)}, f32[128,128]{1,0:T(8,128)S(1)}, u32[]{:S(2)}, u32[]{:S(2)}) collective-permute-start(f32[128,128]{1,0:T(8,128)S(1)} %get-tuple-element.137), channel_id=1, source_target_pairs={{0,28},{4,8},{8,4},{12,16},{16,12},{20,24},{24,20},{28,0},{1,29},{... | collective-permute-start | bytes 196616 | tf_op jit(solution)/shard_map/ppermute | solution.py:214
  60.0 1.5 %collective-permute-start.31 = (f32[64,128]{1,0:T(8,128)S(1)}, f32[64,128]{1,0:T(8,128)S(1)}, u32[]{:S(2)}, u32[]{:S(2)}) collective-permute-start(f32[64,128]{1,0:T(8,128)S(1)} %get-tuple-element.138), channel_id=1, source_target_pairs={{0,1},{1,0},{2,3},{3,2},{4,5},{5,4},{6,7},{7,6},{8,9},{9,8},{10,11... | collective-permute-start | bytes 98312 | tf_op jit(solution)/shard_map/ppermute | solution.py:216
  61.5 1.5 %collective-permute-start.32 = (f32[64,128]{1,0:T(8,128)S(1)}, f32[64,128]{1,0:T(8,128)S(1)}, u32[]{:S(2)}, u32[]{:S(2)}) collective-permute-start(f32[64,128]{1,0:T(8,128)S(1)} %get-tuple-element.139), channel_id=1, source_target_pairs={{0,2},{1,3},{2,0},{3,1},{4,6},{5,7},{6,4},{7,5},{8,10},{9,11},{10,... | collective-permute-start | bytes 98312 | tf_op jit(solution)/shard_map/ppermute | solution.py:216
  63.9 1.5 %collective-permute-done.32.refs_2_ = f32[64,128]{1,0:T(8,128)S(1)} collective-permute-done((f32[64,128]{1,0:T(8,128)S(1)}, f32[64,128]{1,0:T(8,128)S(1)}, u32[]{:S(2)}, u32[]{:S(2)}) %collective-permute-start.32) | collective-permute-done | bytes 32800 | tf_op jit(solution)/shard_map/ppermute | solution.py:216
  65.4 2.4 %collective-permute-done.33.refs_3_ = f32[64,128]{1,0:T(8,128)S(1)} collective-permute-done((f32[64,128]{1,0:T(8,128)S(1)}, f32[64,128]{1,0:T(8,128)S(1)}, u32[]{:S(2)}, u32[]{:S(2)}) %collective-permute-start.33) | collective-permute-done | bytes 32800 | tf_op jit(solution)/shard_map/ppermute | solution.py:216
  68.2 0.9 %local7.1 = (f32[8,64,128]{2,1,0:T(8,128)S(1)}, f32[128,128]{1,0:T(8,128)S(1)}, f32[8,64,128]{2,1,0:T(8,128)}) custom-call(s32[40]{0:T(128)S(4)} %get-tuple-element.79.table, f32[8,64,128]{2,1,0:T(8,128)S(1)} %get-tuple-element.136.resid, bf16[8,6,128,128]{3,2,1,0:T(8,128)(2,1)S(1)} %get-tuple-element.81.coupling, ...), custom_call_target="tpu_custom_call", output_to_operand_aliasing={{0}: (1, {}), {1}: (4, {})} | custom-call | tf_op jit(solution)/shard_map/local7/pallas_call | solution.py:203
  69.0 0.6 collective-permute-start.35
  69.6 0.5 collective-permute-start.36
  70.1 0.5 collective-permute-start.37
  70.6 2.4 %collective-permute-start.38 = (f32[64,128]{1,0:T(8,128)S(1)}, f32[64,128]{1,0:T(8,128)S(1)}, u32[]{:S(2)}, u32[]{:S(2)}) collective-permute-start(f32[64,128]{1,0:T(8,128)S(1)} %get-tuple-element.154), channel_id=1, source_target_pairs={{0,3},{1,2},{2,1},{3,0},{4,7},{5,6},{6,5},{7,4},{8,11},{9,10},{10,... | collective-permute-start | bytes 98312 | tf_op jit(solution)/shard_map/ppermute | solution.py:216
  73.5 0.9 %collective-permute-done.37.refs_2_ = f32[64,128]{1,0:T(8,128)S(1)} collective-permute-done((f32[64,128]{1,0:T(8,128)S(1)}, f32[64,128]{1,0:T(8,128)S(1)}, u32[]{:S(2)}, u32[]{:S(2)}) %collective-permute-start.37) | collective-permute-done | bytes 32800 | tf_op jit(solution)/shard_map/ppermute | solution.py:216
  74.4 1.1 %collective-permute-done.38.refs_3_ = f32[64,128]{1,0:T(8,128)S(1)} collective-permute-done((f32[64,128]{1,0:T(8,128)S(1)}, f32[64,128]{1,0:T(8,128)S(1)}, u32[]{:S(2)}, u32[]{:S(2)}) %collective-permute-start.38) | collective-permute-done | bytes 32800 | tf_op jit(solution)/shard_map/ppermute | solution.py:216
  75.4 0.9 %final.1 = f32[8,64,128]{2,1,0:T(8,128)} custom-call(f32[8,64,128]{2,1,0:T(8,128)S(1)} %get-tuple-element.150.resid, f32[128,128]{1,0:T(8,128)S(1)} %collective-permute-done.35.refs_0_, f32[64,128]{1,0:T(8,128)S(1)} %collective-permute-done.36.refs_1_, f32[64,128]{1,0:T(8,128)S(1)} %collective-permute-done.37.refs_2_, ...), custom_call_target="tpu_custom_call" | custom-call | tf_op jit(solution)/shard_map/final/pallas_call | solution.py:203
  (49 shorter events, 9.4 us)
Async XLA Ops:
  2.7 13.1 %collective-permute-start.4 = (f32[136,128]{1,0:T(8,128)S(1)}, f32[136,128]{1,0:T(8,128)S(1)}, u32[]{:S(2)}, u32[]{:S(2)}) collective-permute-start(f32[136,128]{1,0:T(8,128)S(1)} %get-tuple-element.90), channel_id=1, source_target_pairs={{0,4},{4,0},{8,12},{12,8},{16,20},{20,16},{24,28},{28,24},{1,5},{5... | collective-permute-start | bytes 208904 | tf_op jit(solution)/shard_map/ppermute | solution.py:217
  3.2 12.6 %collective-permute-start = (f32[136,128]{1,0:T(8,128)S(1)}, f32[136,128]{1,0:T(8,128)S(1)}, u32[]{:S(2)}, u32[]{:S(2)}) collective-permute-start(f32[136,128]{1,0:T(8,128)S(1)} %get-tuple-element.86), channel_id=1, source_target_pairs={{0,28},{4,8},{8,4},{12,16},{16,12},{20,24},{24,20},{28,0},{1,29},{... | collective-permute-start | bytes 208904 | tf_op jit(solution)/shard_map/ppermute | solution.py:214
  7.9 4.0 %collective-permute-start.1 = (f32[72,128]{1,0:T(8,128)S(1)}, f32[72,128]{1,0:T(8,128)S(1)}, u32[]{:S(2)}, u32[]{:S(2)}) collective-permute-start(f32[72,128]{1,0:T(8,128)S(1)} %get-tuple-element.87), channel_id=1, source_target_pairs={{0,1},{1,0},{2,3},{3,2},{4,5},{5,4},{6,7},{7,6},{8,9},{9,8},{10,11... | collective-permute-start | bytes 110600 | tf_op jit(solution)/shard_map/ppermute | solution.py:216
  9.4 4.0 %collective-permute-start.2 = (f32[72,128]{1,0:T(8,128)S(1)}, f32[72,128]{1,0:T(8,128)S(1)}, u32[]{:S(2)}, u32[]{:S(2)}) collective-permute-start(f32[72,128]{1,0:T(8,128)S(1)} %get-tuple-element.88), channel_id=1, source_target_pairs={{0,2},{1,3},{2,0},{3,1},{4,6},{5,7},{6,4},{7,5},{8,10},{9,11},{10,... | collective-permute-start | bytes 110600 | tf_op jit(solution)/shard_map/ppermute | solution.py:216
  10.9 4.9 %collective-permute-start.3 = (f32[72,128]{1,0:T(8,128)S(1)}, f32[72,128]{1,0:T(8,128)S(1)}, u32[]{:S(2)}, u32[]{:S(2)}) collective-permute-start(f32[72,128]{1,0:T(8,128)S(1)} %get-tuple-element.89), channel_id=1, source_target_pairs={{0,3},{1,2},{2,1},{3,0},{4,7},{5,6},{6,5},{7,4},{8,11},{9,10},{10,... | collective-permute-start | bytes 110600 | tf_op jit(solution)/shard_map/ppermute | solution.py:216
  16.3 6.5 %collective-permute-start.9 = (f32[128,128]{1,0:T(8,128)S(1)}, f32[128,128]{1,0:T(8,128)S(1)}, u32[]{:S(2)}, u32[]{:S(2)}) collective-permute-start(f32[128,128]{1,0:T(8,128)S(1)} %get-tuple-element.98), channel_id=1, source_target_pairs={{0,4},{4,0},{8,12},{12,8},{16,20},{20,16},{24,28},{28,24},{1,5},{5... | collective-permute-start | bytes 196616 | tf_op jit(solution)/shard_map/ppermute | solution.py:217
  16.4 6.4 %collective-permute-start.5 = (f32[128,128]{1,0:T(8,128)S(1)}, f32[128,128]{1,0:T(8,128)S(1)}, u32[]{:S(2)}, u32[]{:S(2)}) collective-permute-start(f32[128,128]{1,0:T(8,128)S(1)} %get-tuple-element.94), channel_id=1, source_target_pairs={{0,28},{4,8},{8,4},{12,16},{16,12},{20,24},{24,20},{28,0},{1,29},{... | collective-permute-start | bytes 196616 | tf_op jit(solution)/shard_map/ppermute | solution.py:214
  16.9 3.9 %collective-permute-start.6 = (f32[64,128]{1,0:T(8,128)S(1)}, f32[64,128]{1,0:T(8,128)S(1)}, u32[]{:S(2)}, u32[]{:S(2)}) collective-permute-start(f32[64,128]{1,0:T(8,128)S(1)} %get-tuple-element.95), channel_id=1, source_target_pairs={{0,1},{1,0},{2,3},{3,2},{4,5},{5,4},{6,7},{7,6},{8,9},{9,8},{10,11... | collective-permute-start | bytes 98312 | tf_op jit(solution)/shard_map/ppermute | solution.py:216
  17.5 4.1 %collective-permute-start.7 = (f32[64,128]{1,0:T(8,128)S(1)}, f32[64,128]{1,0:T(8,128)S(1)}, u32[]{:S(2)}, u32[]{:S(2)}) collective-permute-start(f32[64,128]{1,0:T(8,128)S(1)} %get-tuple-element.96), channel_id=1, source_target_pairs={{0,2},{1,3},{2,0},{3,1},{4,6},{5,7},{6,4},{7,5},{8,10},{9,11},{10,... | collective-permute-start | bytes 98312 | tf_op jit(solution)/shard_map/ppermute | solution.py:216
  18.0 4.8 %collective-permute-start.8 = (f32[64,128]{1,0:T(8,128)S(1)}, f32[64,128]{1,0:T(8,128)S(1)}, u32[]{:S(2)}, u32[]{:S(2)}) collective-permute-start(f32[64,128]{1,0:T(8,128)S(1)} %get-tuple-element.97), channel_id=1, source_target_pairs={{0,3},{1,2},{2,1},{3,0},{4,7},{5,6},{6,5},{7,4},{8,11},{9,10},{10,... | collective-permute-start | bytes 98312 | tf_op jit(solution)/shard_map/ppermute | solution.py:216
  23.3 9.3 %collective-permute-start.14 = (f32[128,128]{1,0:T(8,128)S(1)}, f32[128,128]{1,0:T(8,128)S(1)}, u32[]{:S(2)}, u32[]{:S(2)}) collective-permute-start(f32[128,128]{1,0:T(8,128)S(1)} %get-tuple-element.106), channel_id=1, source_target_pairs={{0,4},{4,0},{8,12},{12,8},{16,20},{20,16},{24,28},{28,24},{1,5},{5... | collective-permute-start | bytes 196616 | tf_op jit(solution)/shard_map/ppermute | solution.py:217
  23.4 9.2 %collective-permute-start.10 = (f32[128,128]{1,0:T(8,128)S(1)}, f32[128,128]{1,0:T(8,128)S(1)}, u32[]{:S(2)}, u32[]{:S(2)}) collective-permute-start(f32[128,128]{1,0:T(8,128)S(1)} %get-tuple-element.102), channel_id=1, source_target_pairs={{0,28},{4,8},{8,4},{12,16},{16,12},{20,24},{24,20},{28,0},{1,29},{... | collective-permute-start | bytes 196616 | tf_op jit(solution)/shard_map/ppermute | solution.py:214
  24.8 3.9 %collective-permute-start.11 = (f32[64,128]{1,0:T(8,128)S(1)}, f32[64,128]{1,0:T(8,128)S(1)}, u32[]{:S(2)}, u32[]{:S(2)}) collective-permute-start(f32[64,128]{1,0:T(8,128)S(1)} %get-tuple-element.103), channel_id=1, source_target_pairs={{0,1},{1,0},{2,3},{3,2},{4,5},{5,4},{6,7},{7,6},{8,9},{9,8},{10,11... | collective-permute-start | bytes 98312 | tf_op jit(solution)/shard_map/ppermute | solution.py:216
  26.3 3.9 %collective-permute-start.12 = (f32[64,128]{1,0:T(8,128)S(1)}, f32[64,128]{1,0:T(8,128)S(1)}, u32[]{:S(2)}, u32[]{:S(2)}) collective-permute-start(f32[64,128]{1,0:T(8,128)S(1)} %get-tuple-element.104), channel_id=1, source_target_pairs={{0,2},{1,3},{2,0},{3,1},{4,6},{5,7},{6,4},{7,5},{8,10},{9,11},{10,... | collective-permute-start | bytes 98312 | tf_op jit(solution)/shard_map/ppermute | solution.py:216
  27.8 4.8 %collective-permute-start.13 = (f32[64,128]{1,0:T(8,128)S(1)}, f32[64,128]{1,0:T(8,128)S(1)}, u32[]{:S(2)}, u32[]{:S(2)}) collective-permute-start(f32[64,128]{1,0:T(8,128)S(1)} %get-tuple-element.105), channel_id=1, source_target_pairs={{0,3},{1,2},{2,1},{3,0},{4,7},{5,6},{6,5},{7,4},{8,11},{9,10},{10,... | collective-permute-start | bytes 98312 | tf_op jit(solution)/shard_map/ppermute | solution.py:216
  33.2 6.5 %collective-permute-start.19 = (f32[128,128]{1,0:T(8,128)S(1)}, f32[128,128]{1,0:T(8,128)S(1)}, u32[]{:S(2)}, u32[]{:S(2)}) collective-permute-start(f32[128,128]{1,0:T(8,128)S(1)} %get-tuple-element.114), channel_id=1, source_target_pairs={{0,4},{4,0},{8,12},{12,8},{16,20},{20,16},{24,28},{28,24},{1,5},{5... | collective-permute-start | bytes 196616 | tf_op jit(solution)/shard_map/ppermute | solution.py:217
  33.3 6.4 %collective-permute-start.15 = (f32[128,128]{1,0:T(8,128)S(1)}, f32[128,128]{1,0:T(8,128)S(1)}, u32[]{:S(2)}, u32[]{:S(2)}) collective-permute-start(f32[128,128]{1,0:T(8,128)S(1)} %get-tuple-element.110), channel_id=1, source_target_pairs={{0,28},{4,8},{8,4},{12,16},{16,12},{20,24},{24,20},{28,0},{1,29},{... | collective-permute-start | bytes 196616 | tf_op jit(solution)/shard_map/ppermute | solution.py:214
  33.8 3.9 %collective-permute-start.16 = (f32[64,128]{1,0:T(8,128)S(1)}, f32[64,128]{1,0:T(8,128)S(1)}, u32[]{:S(2)}, u32[]{:S(2)}) collective-permute-start(f32[64,128]{1,0:T(8,128)S(1)} %get-tuple-element.111), channel_id=1, source_target_pairs={{0,1},{1,0},{2,3},{3,2},{4,5},{5,4},{6,7},{7,6},{8,9},{9,8},{10,11... | collective-permute-start | bytes 98312 | tf_op jit(solution)/shard_map/ppermute | solution.py:216
  34.3 4.3 %collective-permute-start.17 = (f32[64,128]{1,0:T(8,128)S(1)}, f32[64,128]{1,0:T(8,128)S(1)}, u32[]{:S(2)}, u32[]{:S(2)}) collective-permute-start(f32[64,128]{1,0:T(8,128)S(1)} %get-tuple-element.112), channel_id=1, source_target_pairs={{0,2},{1,3},{2,0},{3,1},{4,6},{5,7},{6,4},{7,5},{8,10},{9,11},{10,... | collective-permute-start | bytes 98312 | tf_op jit(solution)/shard_map/ppermute | solution.py:216
  34.9 4.8 %collective-permute-start.18 = (f32[64,128]{1,0:T(8,128)S(1)}, f32[64,128]{1,0:T(8,128)S(1)}, u32[]{:S(2)}, u32[]{:S(2)}) collective-permute-start(f32[64,128]{1,0:T(8,128)S(1)} %get-tuple-element.113), channel_id=1, source_target_pairs={{0,3},{1,2},{2,1},{3,0},{4,7},{5,6},{6,5},{7,4},{8,11},{9,10},{10,... | collective-permute-start | bytes 98312 | tf_op jit(solution)/shard_map/ppermute | solution.py:216
  40.2 10.8 %collective-permute-start.24 = (f32[128,128]{1,0:T(8,128)S(1)}, f32[128,128]{1,0:T(8,128)S(1)}, u32[]{:S(2)}, u32[]{:S(2)}) collective-permute-start(f32[128,128]{1,0:T(8,128)S(1)} %get-tuple-element.123), channel_id=1, source_target_pairs={{0,4},{4,0},{8,12},{12,8},{16,20},{20,16},{24,28},{28,24},{1,5},{5... | collective-permute-start | bytes 196616 | tf_op jit(solution)/shard_map/ppermute | solution.py:217
  40.3 10.7 %collective-permute-start.20 = (f32[128,128]{1,0:T(8,128)S(1)}, f32[128,128]{1,0:T(8,128)S(1)}, u32[]{:S(2)}, u32[]{:S(2)}) collective-permute-start(f32[128,128]{1,0:T(8,128)S(1)} %get-tuple-element.119), channel_id=1, source_target_pairs={{0,28},{4,8},{8,4},{12,16},{16,12},{20,24},{24,20},{28,0},{1,29},{... | collective-permute-start | bytes 196616 | tf_op jit(solution)/shard_map/ppermute | solution.py:214
  43.1 3.9 %collective-permute-start.21 = (f32[64,128]{1,0:T(8,128)S(1)}, f32[64,128]{1,0:T(8,128)S(1)}, u32[]{:S(2)}, u32[]{:S(2)}) collective-permute-start(f32[64,128]{1,0:T(8,128)S(1)} %get-tuple-element.120), channel_id=1, source_target_pairs={{0,1},{1,0},{2,3},{3,2},{4,5},{5,4},{6,7},{7,6},{8,9},{9,8},{10,11... | collective-permute-start | bytes 98312 | tf_op jit(solution)/shard_map/ppermute | solution.py:216
  44.6 4.1 %collective-permute-start.22 = (f32[64,128]{1,0:T(8,128)S(1)}, f32[64,128]{1,0:T(8,128)S(1)}, u32[]{:S(2)}, u32[]{:S(2)}) collective-permute-start(f32[64,128]{1,0:T(8,128)S(1)} %get-tuple-element.121), channel_id=1, source_target_pairs={{0,2},{1,3},{2,0},{3,1},{4,6},{5,7},{6,4},{7,5},{8,10},{9,11},{10,... | collective-permute-start | bytes 98312 | tf_op jit(solution)/shard_map/ppermute | solution.py:216
  46.1 4.8 %collective-permute-start.23 = (f32[64,128]{1,0:T(8,128)S(1)}, f32[64,128]{1,0:T(8,128)S(1)}, u32[]{:S(2)}, u32[]{:S(2)}) collective-permute-start(f32[64,128]{1,0:T(8,128)S(1)} %get-tuple-element.122), channel_id=1, source_target_pairs={{0,3},{1,2},{2,1},{3,0},{4,7},{5,6},{6,5},{7,4},{8,11},{9,10},{10,... | collective-permute-start | bytes 98312 | tf_op jit(solution)/shard_map/ppermute | solution.py:216
  51.5 6.5 %collective-permute-start.29 = (f32[128,128]{1,0:T(8,128)S(1)}, f32[128,128]{1,0:T(8,128)S(1)}, u32[]{:S(2)}, u32[]{:S(2)}) collective-permute-start(f32[128,128]{1,0:T(8,128)S(1)} %get-tuple-element.132), channel_id=1, source_target_pairs={{0,4},{4,0},{8,12},{12,8},{16,20},{20,16},{24,28},{28,24},{1,5},{5... | collective-permute-start | bytes 196616 | tf_op jit(solution)/shard_map/ppermute | solution.py:217
  51.6 6.4 %collective-permute-start.25 = (f32[128,128]{1,0:T(8,128)S(1)}, f32[128,128]{1,0:T(8,128)S(1)}, u32[]{:S(2)}, u32[]{:S(2)}) collective-permute-start(f32[128,128]{1,0:T(8,128)S(1)} %get-tuple-element.128), channel_id=1, source_target_pairs={{0,28},{4,8},{8,4},{12,16},{16,12},{20,24},{24,20},{28,0},{1,29},{... | collective-permute-start | bytes 196616 | tf_op jit(solution)/shard_map/ppermute | solution.py:214
  52.1 3.9 %collective-permute-start.26 = (f32[64,128]{1,0:T(8,128)S(1)}, f32[64,128]{1,0:T(8,128)S(1)}, u32[]{:S(2)}, u32[]{:S(2)}) collective-permute-start(f32[64,128]{1,0:T(8,128)S(1)} %get-tuple-element.129), channel_id=1, source_target_pairs={{0,1},{1,0},{2,3},{3,2},{4,5},{5,4},{6,7},{7,6},{8,9},{9,8},{10,11... | collective-permute-start | bytes 98312 | tf_op jit(solution)/shard_map/ppermute | solution.py:216
  52.7 4.1 %collective-permute-start.27 = (f32[64,128]{1,0:T(8,128)S(1)}, f32[64,128]{1,0:T(8,128)S(1)}, u32[]{:S(2)}, u32[]{:S(2)}) collective-permute-start(f32[64,128]{1,0:T(8,128)S(1)} %get-tuple-element.130), channel_id=1, source_target_pairs={{0,2},{1,3},{2,0},{3,1},{4,6},{5,7},{6,4},{7,5},{8,10},{9,11},{10,... | collective-permute-start | bytes 98312 | tf_op jit(solution)/shard_map/ppermute | solution.py:216
  53.2 4.8 %collective-permute-start.28 = (f32[64,128]{1,0:T(8,128)S(1)}, f32[64,128]{1,0:T(8,128)S(1)}, u32[]{:S(2)}, u32[]{:S(2)}) collective-permute-start(f32[64,128]{1,0:T(8,128)S(1)} %get-tuple-element.131), channel_id=1, source_target_pairs={{0,3},{1,2},{2,1},{3,0},{4,7},{5,6},{6,5},{7,4},{8,11},{9,10},{10,... | collective-permute-start | bytes 98312 | tf_op jit(solution)/shard_map/ppermute | solution.py:216
  58.5 9.3 %collective-permute-start.34 = (f32[128,128]{1,0:T(8,128)S(1)}, f32[128,128]{1,0:T(8,128)S(1)}, u32[]{:S(2)}, u32[]{:S(2)}) collective-permute-start(f32[128,128]{1,0:T(8,128)S(1)} %get-tuple-element.141), channel_id=1, source_target_pairs={{0,4},{4,0},{8,12},{12,8},{16,20},{20,16},{24,28},{28,24},{1,5},{5... | collective-permute-start | bytes 196616 | tf_op jit(solution)/shard_map/ppermute | solution.py:217
  58.6 9.3 %collective-permute-start.30 = (f32[128,128]{1,0:T(8,128)S(1)}, f32[128,128]{1,0:T(8,128)S(1)}, u32[]{:S(2)}, u32[]{:S(2)}) collective-permute-start(f32[128,128]{1,0:T(8,128)S(1)} %get-tuple-element.137), channel_id=1, source_target_pairs={{0,28},{4,8},{8,4},{12,16},{16,12},{20,24},{24,20},{28,0},{1,29},{... | collective-permute-start | bytes 196616 | tf_op jit(solution)/shard_map/ppermute | solution.py:214
  60.0 3.9 %collective-permute-start.31 = (f32[64,128]{1,0:T(8,128)S(1)}, f32[64,128]{1,0:T(8,128)S(1)}, u32[]{:S(2)}, u32[]{:S(2)}) collective-permute-start(f32[64,128]{1,0:T(8,128)S(1)} %get-tuple-element.138), channel_id=1, source_target_pairs={{0,1},{1,0},{2,3},{3,2},{4,5},{5,4},{6,7},{7,6},{8,9},{9,8},{10,11... | collective-permute-start | bytes 98312 | tf_op jit(solution)/shard_map/ppermute | solution.py:216
  61.5 3.9 %collective-permute-start.32 = (f32[64,128]{1,0:T(8,128)S(1)}, f32[64,128]{1,0:T(8,128)S(1)}, u32[]{:S(2)}, u32[]{:S(2)}) collective-permute-start(f32[64,128]{1,0:T(8,128)S(1)} %get-tuple-element.139), channel_id=1, source_target_pairs={{0,2},{1,3},{2,0},{3,1},{4,6},{5,7},{6,4},{7,5},{8,10},{9,11},{10,... | collective-permute-start | bytes 98312 | tf_op jit(solution)/shard_map/ppermute | solution.py:216
  63.0 4.8 %collective-permute-start.33 = (f32[64,128]{1,0:T(8,128)S(1)}, f32[64,128]{1,0:T(8,128)S(1)}, u32[]{:S(2)}, u32[]{:S(2)}) collective-permute-start(f32[64,128]{1,0:T(8,128)S(1)} %get-tuple-element.140), channel_id=1, source_target_pairs={{0,3},{1,2},{2,1},{3,0},{4,7},{5,6},{6,5},{7,4},{8,11},{9,10},{10,... | collective-permute-start | bytes 98312 | tf_op jit(solution)/shard_map/ppermute | solution.py:216
  69.0 6.4 %collective-permute-start.39 = (f32[128,128]{1,0:T(8,128)S(1)}, f32[128,128]{1,0:T(8,128)S(1)}, u32[]{:S(2)}, u32[]{:S(2)}) collective-permute-start(f32[128,128]{1,0:T(8,128)S(1)} %get-tuple-element.155), channel_id=1, source_target_pairs={{0,4},{4,0},{8,12},{12,8},{16,20},{20,16},{24,28},{28,24},{1,5},{5... | collective-permute-start | bytes 196616 | tf_op jit(solution)/shard_map/ppermute | solution.py:217
  69.0 6.4 %collective-permute-start.35 = (f32[128,128]{1,0:T(8,128)S(1)}, f32[128,128]{1,0:T(8,128)S(1)}, u32[]{:S(2)}, u32[]{:S(2)}) collective-permute-start(f32[128,128]{1,0:T(8,128)S(1)} %get-tuple-element.151), channel_id=1, source_target_pairs={{0,28},{4,8},{8,4},{12,16},{16,12},{20,24},{24,20},{28,0},{1,29},{... | collective-permute-start | bytes 196616 | tf_op jit(solution)/shard_map/ppermute | solution.py:214
  69.6 3.9 %collective-permute-start.36 = (f32[64,128]{1,0:T(8,128)S(1)}, f32[64,128]{1,0:T(8,128)S(1)}, u32[]{:S(2)}, u32[]{:S(2)}) collective-permute-start(f32[64,128]{1,0:T(8,128)S(1)} %get-tuple-element.152), channel_id=1, source_target_pairs={{0,1},{1,0},{2,3},{3,2},{4,5},{5,4},{6,7},{7,6},{8,9},{9,8},{10,11... | collective-permute-start | bytes 98312 | tf_op jit(solution)/shard_map/ppermute | solution.py:216
  70.1 4.3 %collective-permute-start.37 = (f32[64,128]{1,0:T(8,128)S(1)}, f32[64,128]{1,0:T(8,128)S(1)}, u32[]{:S(2)}, u32[]{:S(2)}) collective-permute-start(f32[64,128]{1,0:T(8,128)S(1)} %get-tuple-element.153), channel_id=1, source_target_pairs={{0,2},{1,3},{2,0},{3,1},{4,6},{5,7},{6,4},{7,5},{8,10},{9,11},{10,... | collective-permute-start | bytes 98312 | tf_op jit(solution)/shard_map/ppermute | solution.py:216
  70.6 4.8 %collective-permute-start.38 = (f32[64,128]{1,0:T(8,128)S(1)}, f32[64,128]{1,0:T(8,128)S(1)}, u32[]{:S(2)}, u32[]{:S(2)}) collective-permute-start(f32[64,128]{1,0:T(8,128)S(1)} %get-tuple-element.154), channel_id=1, source_target_pairs={{0,3},{1,2},{2,1},{3,0},{4,7},{5,6},{6,5},{7,4},{8,11},{9,10},{10,... | collective-permute-start | bytes 98312 | tf_op jit(solution)/shard_map/ppermute | solution.py:216

commit v6 on v5

--- a/solution.py
+++ b/solution.py
@@ -24,28 +24,27 @@
     def __init__(self, rows, rhs_count, width, group):
         self.rows, self.n, self.w, self.group = rows, rhs_count, width, group
         self.quarter = rows // COLORS
-        self.lanes = group + 1
+        self.lanes = group + self.quarter
+        self.distances = [1] + list(reversed(range(2, group)))
         self.order, self.local, self.slot = 0, rows, 3 * rows
         self.table = 5 * rows
         self.dom_meta = -(-rows // 8) * 8
 
     def types(self, step):
         extra = (self.dom_meta, META) if step == 0 else (0, 0)
-        dom, one = self.quarter * self.n + extra[0], self.n + extra[1]
-        shapes = [dom] + [one] * (self.group - 1) + [dom]
+        far, one = self.quarter * self.n + extra[0], self.n + extra[1]
+        shapes = [far] + [one] * (self.lanes - 1)
         return [pltpu.VMEM((length, self.w), jnp.float32) for length in shapes]
 
 
 def items_of(plan, step, got, meta):
     color = step % COLORS
     out = []
-    for lane in range(plan.lanes):
-        if 0 < lane < plan.group:
-            out.append((meta[lane], plan.n + color, got[lane], 0))
-            continue
-        for p in range(plan.quarter):
-            line = plan.quarter * plan.n + color * plan.quarter + p
-            out.append((meta[lane], line, got[lane], p * plan.n))
+    for p in range(plan.quarter):
+        line = plan.quarter * plan.n + color * plan.quarter + p
+        out.append((meta[0], line, got[0], p * plan.n))
+    for lane in range(1, plan.lanes):
+        out.append((meta[lane], plan.n + color, got[lane], 0))
     return out
 
 
@@ -62,7 +61,7 @@
 
 def products(plan, step, table, changes, coupling, sends):
     parity = lax.rem(lax.axis_index("dom"), 2)
-    far, near = sends[0], sends[-1]
+    far, near = sends[0], sends[plan.group :]
     terms = []
     for p in range(plan.quarter):
         at = step % COLORS * plan.quarter + p
@@ -72,15 +71,15 @@
             jnp.concatenate([coupling[j, 5 - parity], coupling[j, 4 + parity]], axis=1),
         )
         far[pl.ds(p * plan.n, plan.n), :] = both[:, : plan.w]
-        near[pl.ds(p * plan.n, plan.n), :] = both[:, plan.w :]
+        near[p][pl.ds(0, plan.n), :] = both[:, plan.w :]
         both = dot(changes[p], jnp.concatenate([coupling[j, 2], coupling[j, 3]], axis=1))
         for k in range(2):
             terms.append((table[plan.slot + 2 * at + k], both[:, k * plan.w : (k + 1) * plan.w]))
-    for s in range(1, plan.group):
+    for lane, s in enumerate(plan.distances):
         total = jnp.zeros((plan.n, plan.w), jnp.float32)
         for slot, term in terms:
             total = total + jnp.where(slot == s, term, 0.0)
-        sends[s][pl.ds(0, plan.n), :] = total
+        sends[1 + lane][pl.ds(0, plan.n), :] = total
 
 
 def first_kernel(plan, *refs):
@@ -110,17 +109,22 @@
             table[plan.local + 2 * at + k] = local_target[k, i]
             table[plan.slot + 2 * at + k] = me ^ group_peer[k, i]
     line = lax.broadcasted_iota(jnp.int32, (META, plan.w), 0)
-    for s in range(1, plan.group):
+    for lane, s in enumerate(plan.distances):
         meta = jnp.full((META, plan.w), -1, jnp.int32)
         for c in range(COLORS):
             meta = jnp.where(line == c, group_list[0, c, me ^ s], meta)
-        sends[s][pl.ds(plan.n, META), :] = meta.astype(jnp.float32)
+        sends[1 + lane][pl.ds(plan.n, META), :] = meta.astype(jnp.float32)
+    for p in range(plan.quarter):
+        meta = jnp.full((META, plan.w), -1, jnp.int32)
+        for c in range(COLORS):
+            at = c * plan.quarter + p
+            meta = jnp.where(line == c, dom_target[parity, table[plan.order + at]], meta)
+        sends[plan.group + p][pl.ds(plan.n, META), :] = meta.astype(jnp.float32)
     line = lax.broadcasted_iota(jnp.int32, (plan.dom_meta, plan.w), 0)
-    for send, k in ((sends[0], 1 - parity), (sends[-1], parity)):
-        meta = jnp.full((plan.dom_meta, plan.w), -1, jnp.int32)
-        for at in range(plan.rows):
-            meta = jnp.where(line == at, dom_target[k, table[plan.order + at]], meta)
-        send[pl.ds(plan.quarter * plan.n, plan.dom_meta), :] = meta.astype(jnp.float32)
+    meta = jnp.full((plan.dom_meta, plan.w), -1, jnp.int32)
+    for at in range(plan.rows):
+        meta = jnp.where(line == at, dom_target[1 - parity, table[plan.order + at]], meta)
+    sends[0][pl.ds(plan.quarter * plan.n, plan.dom_meta), :] = meta.astype(jnp.float32)
     copies[5].wait()
     copies[6].wait()
     changes = []
@@ -155,7 +159,7 @@
     products(plan, step, table, changes, coupling, refs[2:])
 
 
-def local_kernel(plan, step, last, table, resid, coupling, change, near, *refs):
+def local_kernel(plan, step, last, table, resid, coupling, change, *refs):
     items = []
     if step > 0:
         got, refs = lanes_of(plan, refs)
@@ -176,7 +180,7 @@
     if last:
         for c in range(COLORS):
             for p in range(plan.quarter):
-                refs[2][table[plan.order + c * plan.quarter + p]] = sols[c][p]
+                refs[1][table[plan.order + c * plan.quarter + p]] = sols[c][p]
 
 
 def final_kernel(plan, step, resid, *refs):
@@ -212,9 +216,9 @@
 
     def exchange(sends):
         got = [lax.ppermute(sends[0], "dom", far_pairs)]
-        for s in reversed(range(1, group)):
-            got.insert(1, lax.ppermute(sends[s], "sub", [(i, i ^ s) for i in range(group)]))
-        return got + [lax.ppermute(sends[-1], "dom", near_pairs)]
+        for send, s in zip(sends[1:group], plan.distances):
+            got.append(lax.ppermute(send, "sub", [(i, i ^ s) for i in range(group)]))
+        return got + [lax.ppermute(send, "dom", near_pairs) for send in sends[group:]]
 
     sol_t = pltpu.VMEM((plan.quarter, plan.n, plan.w), f32)
     change_t = pltpu.VMEM((plan.quarter, plan.n, plan.w), jnp.bfloat16)
@@ -257,18 +261,18 @@
             )
             sols[c:] = [sol] + sols[c + 1 :]
         last = step == steps - 1
-        ins = [table, resid, tiles, change, sends[-1]]
+        ins = [table, resid, tiles, change]
         if step > 0:
             ins += [*got, *meta]
         if last:
             ins += sols
-        resid, sends[-1], *rest = call(
+        resid, *rest = call(
             functools.partial(local_kernel, plan, step, last),
             f"local{step}",
             ins,
             [SMEM],
-            [resid_t, plan.types(step)[-1]] + ([jax.ShapeDtypeStruct(rhs.shape, f32)] if last else []),
-            input_output_aliases={1: 0, 4: 1},
+            [resid_t] + ([jax.ShapeDtypeStruct(rhs.shape, f32)] if last else []),
+            input_output_aliases={1: 0},
         )
         got = exchange(sends)
         if step == 0:

time: 76.5 us -> 68.5 us (0.90)
  waiting for transfers between devices: 26.9 us -> 19.7 us
  starting transfers between devices: 41.4 us -> 40.6 us
    ppermute x32 -> x40, waiting for transfers between devices: 26.9 us -> 19.4 us  [the longest x24 19.3 us: exchange(): got.append(lax.ppermute(send, 'sub', [(i, i ^ s) for i in range(group)]))]
    ppermute x8, starting transfers between devices: 12.6 us -> 8.64 us  [exchange(): got = [lax.ppermute(sends[0], 'dom', far_pairs)]]
    ppermute x32 -> x40, starting transfers between devices: 28.8 us -> 32 us  [the longest x24 29.4 us: exchange(): got.append(lax.ppermute(send, 'sub', [(i, i ^ s) for i in range(group)]))]
  transfers between devices with their start and end apart: 40 -> 48, of which waited for: 24 -> 21; matrix products, arithmetic and copies ran while one was open for 0% -> 0% of each run, Pallas kernels for 0% -> 3%
where the time goes in v6:
time: 68.5 us; the launch traced here: 68.3 us
  starting transfers between devices  40.6 us (59%)
  waiting for transfers between devices  19.7 us (29%)
  Pallas kernels  7.17 us (10%)
  between operations  0.79 us (1%)
    ppermute x24, starting transfers between devices, exchange(): got.append(lax.ppermute(send, 'sub', [(i, i ^ s) for i in range(group)]))  29.4 us
    ppermute x24, waiting for transfers between devices, exchange(): got.append(lax.ppermute(send, 'sub', [(i, i ^ s) for i in range(group)]))  19.3 us
    ppermute x8, starting transfers between devices, exchange(): got = [lax.ppermute(sends[0], 'dom', far_pairs)]  8.64 us
    pallas_call x17, Pallas kernels, call(): pl.pallas_call(body, name=name, in_specs=in_specs + [VMEM] * (len(ins) -...  7.17 us
    ppermute x16, starting transfers between devices, exchange(): lax.ppermute(send, 'dom', near_pairs)  2.61 us
  transfers between devices with their start and end apart: 48, of which 21 were waited for; matrix products, arithmetic and copies ran while one was open for 0% of the time, Pallas kernels for 3%

profile of v6, /device:TPU:0, one launch (start us, length us, event | category | flops | bytes accessed | tf_op | source)
XLA Modules:
  0.0 68.3 jit_solution(11604972639050748116)
XLA Ops:
  0.6 1.8 %first.1 = (s32[40]{0:T(128)S(4)}, bf16[8,6,128,128]{3,2,1,0:T(8,128)(2,1)S(1)}, bf16[8,128,128]{2,1,0:T(8,128)(2,1)S(1)}, f32[8,64,128]{2,1,0:T(8,128)S(1)}, f3...) custom-call(s32[8]{0:T(128)} %refs_0_.1, ...), custom_call_target="tpu_custom_call" | custom-call | tf_op jit(solution)/shard_map/first/pallas_call | solution.py:207
  2.5 3.0 %collective-permute-start.1 = (f32[72,128]{1,0:T(8,128)S(1)}, f32[72,128]{1,0:T(8,128)S(1)}, u32[]{:S(2)}, u32[]{:S(2)}) collective-permute-start(f32[72,128]{1,0:T(8,128)S(1)} %get-tuple-element.78), channel_id=1, source_target_pairs={{0,1},{1,0},{2,3},{3,2},{4,5},{5,4},{6,7},{7,6},{8,9},{9,8},{10,11... | collective-permute-start | bytes 110600 | tf_op jit(solution)/shard_map/ppermute | solution.py:220
  5.5 2.8 %collective-permute-start = (f32[136,128]{1,0:T(8,128)S(1)}, f32[136,128]{1,0:T(8,128)S(1)}, u32[]{:S(2)}, u32[]{:S(2)}) collective-permute-start(f32[136,128]{1,0:T(8,128)S(1)} %get-tuple-element.77), channel_id=1, source_target_pairs={{0,28},{4,8},{8,4},{12,16},{16,12},{20,24},{24,20},{28,0},{1,29},{... | collective-permute-start | bytes 208904 | tf_op jit(solution)/shard_map/ppermute | solution.py:218
  8.2 1.5 %collective-permute-start.2 = (f32[72,128]{1,0:T(8,128)S(1)}, f32[72,128]{1,0:T(8,128)S(1)}, u32[]{:S(2)}, u32[]{:S(2)}) collective-permute-start(f32[72,128]{1,0:T(8,128)S(1)} %get-tuple-element.79), channel_id=1, source_target_pairs={{0,3},{1,2},{2,1},{3,0},{4,7},{5,6},{6,5},{7,4},{8,11},{9,10},{10,... | collective-permute-start | bytes 110600 | tf_op jit(solution)/shard_map/ppermute | solution.py:220
  10.3 0.5 collective-permute-start.5
  10.9 2.2 %collective-permute-done.2.refs_2_.refs_8_ = f32[72,128]{1,0:T(8,128)S(1)} collective-permute-done((f32[72,128]{1,0:T(8,128)S(1)}, f32[72,128]{1,0:T(8,128)S(1)}, u32[]{:S(2)}, u32[]{:S(2)}) %collective-permute-start.2) | collective-permute-done | bytes 36896 | tf_op jit(solution)/shard_map/ppermute | solution.py:220
  13.1 0.6 collective-permute-done.3.refs_3_.refs_9_
  14.0 1.6 %collective-permute-start.7 = (f32[64,128]{1,0:T(8,128)S(1)}, f32[64,128]{1,0:T(8,128)S(1)}, u32[]{:S(2)}, u32[]{:S(2)}) collective-permute-start(f32[64,128]{1,0:T(8,128)S(1)} %get-tuple-element.85), channel_id=1, source_target_pairs={{0,1},{1,0},{2,3},{3,2},{4,5},{5,4},{6,7},{7,6},{8,9},{9,8},{10,11... | collective-permute-start | bytes 98312 | tf_op jit(solution)/shard_map/ppermute | solution.py:220
  15.6 1.3 %collective-permute-start.8 = (f32[64,128]{1,0:T(8,128)S(1)}, f32[64,128]{1,0:T(8,128)S(1)}, u32[]{:S(2)}, u32[]{:S(2)}) collective-permute-start(f32[64,128]{1,0:T(8,128)S(1)} %get-tuple-element.86), channel_id=1, source_target_pairs={{0,3},{1,2},{2,1},{3,0},{4,7},{5,6},{6,5},{7,4},{8,11},{9,10},{10,... | collective-permute-start | bytes 98312 | tf_op jit(solution)/shard_map/ppermute | solution.py:220
  16.9 0.7 %collective-permute-start.9 = (f32[64,128]{1,0:T(8,128)S(1)}, f32[64,128]{1,0:T(8,128)S(1)}, u32[]{:S(2)}, u32[]{:S(2)}) collective-permute-start(f32[64,128]{1,0:T(8,128)S(1)} %get-tuple-element.87), channel_id=1, source_target_pairs={{0,2},{1,3},{2,0},{3,1},{4,6},{5,7},{6,4},{7,5},{8,10},{9,11},{10,... | collective-permute-start | bytes 98312 | tf_op jit(solution)/shard_map/ppermute | solution.py:220
  17.6 0.7 collective-permute-done.7.refs_1_
  18.5 1.9 %collective-permute-done.8.refs_2_ = f32[64,128]{1,0:T(8,128)S(1)} collective-permute-done((f32[64,128]{1,0:T(8,128)S(1)}, f32[64,128]{1,0:T(8,128)S(1)}, u32[]{:S(2)}, u32[]{:S(2)}) %collective-permute-start.8) | collective-permute-done | bytes 32800 | tf_op jit(solution)/shard_map/ppermute | solution.py:220
  21.4 0.6 collective-permute-start.13
  22.0 1.8 %collective-permute-start.12 = (f32[128,128]{1,0:T(8,128)S(1)}, f32[128,128]{1,0:T(8,128)S(1)}, u32[]{:S(2)}, u32[]{:S(2)}) collective-permute-start(f32[128,128]{1,0:T(8,128)S(1)} %get-tuple-element.91), channel_id=1, source_target_pairs={{0,28},{4,8},{8,4},{12,16},{16,12},{20,24},{24,20},{28,0},{1,29},{... | collective-permute-start | bytes 196616 | tf_op jit(solution)/shard_map/ppermute | solution.py:218
  23.8 1.4 %collective-permute-start.14 = (f32[64,128]{1,0:T(8,128)S(1)}, f32[64,128]{1,0:T(8,128)S(1)}, u32[]{:S(2)}, u32[]{:S(2)}) collective-permute-start(f32[64,128]{1,0:T(8,128)S(1)} %get-tuple-element.93), channel_id=1, source_target_pairs={{0,3},{1,2},{2,1},{3,0},{4,7},{5,6},{6,5},{7,4},{8,11},{9,10},{10,... | collective-permute-start | bytes 98312 | tf_op jit(solution)/shard_map/ppermute | solution.py:220
  25.2 1.3 %collective-permute-start.15 = (f32[64,128]{1,0:T(8,128)S(1)}, f32[64,128]{1,0:T(8,128)S(1)}, u32[]{:S(2)}, u32[]{:S(2)}) collective-permute-start(f32[64,128]{1,0:T(8,128)S(1)} %get-tuple-element.94), channel_id=1, source_target_pairs={{0,2},{1,3},{2,0},{3,1},{4,6},{5,7},{6,4},{7,5},{8,10},{9,11},{10,... | collective-permute-start | bytes 98312 | tf_op jit(solution)/shard_map/ppermute | solution.py:220
  26.5 0.5 collective-permute-start.17
  27.2 1.4 %collective-permute-done.14.refs_2_ = f32[64,128]{1,0:T(8,128)S(1)} collective-permute-done((f32[64,128]{1,0:T(8,128)S(1)}, f32[64,128]{1,0:T(8,128)S(1)}, u32[]{:S(2)}, u32[]{:S(2)}) %collective-permute-start.14) | collective-permute-done | bytes 32800 | tf_op jit(solution)/shard_map/ppermute | solution.py:220
  28.6 0.5 collective-permute-done.15.refs_3_
  29.5 1.5 %collective-permute-start.19 = (f32[64,128]{1,0:T(8,128)S(1)}, f32[64,128]{1,0:T(8,128)S(1)}, u32[]{:S(2)}, u32[]{:S(2)}) collective-permute-start(f32[64,128]{1,0:T(8,128)S(1)} %get-tuple-element.99), channel_id=1, source_target_pairs={{0,1},{1,0},{2,3},{3,2},{4,5},{5,4},{6,7},{7,6},{8,9},{9,8},{10,11... | collective-permute-start | bytes 98312 | tf_op jit(solution)/shard_map/ppermute | solution.py:220
  31.2 1.4 %collective-permute-start.20 = (f32[64,128]{1,0:T(8,128)S(1)}, f32[64,128]{1,0:T(8,128)S(1)}, u32[]{:S(2)}, u32[]{:S(2)}) collective-permute-start(f32[64,128]{1,0:T(8,128)S(1)} %get-tuple-element.100), channel_id=1, source_target_pairs={{0,3},{1,2},{2,1},{3,0},{4,7},{5,6},{6,5},{7,4},{8,11},{9,10},{10,... | collective-permute-start | bytes 98312 | tf_op jit(solution)/shard_map/ppermute | solution.py:220
  32.6 0.6 collective-permute-start.21
  33.9 2.1 %collective-permute-done.20.refs_2_ = f32[64,128]{1,0:T(8,128)S(1)} collective-permute-done((f32[64,128]{1,0:T(8,128)S(1)}, f32[64,128]{1,0:T(8,128)S(1)}, u32[]{:S(2)}, u32[]{:S(2)}) %collective-permute-start.20) | collective-permute-done | bytes 32800 | tf_op jit(solution)/shard_map/ppermute | solution.py:220
  36.8 0.7 collective-permute-start.25
  37.5 1.8 %collective-permute-start.24 = (f32[128,128]{1,0:T(8,128)S(1)}, f32[128,128]{1,0:T(8,128)S(1)}, u32[]{:S(2)}, u32[]{:S(2)}) collective-permute-start(f32[128,128]{1,0:T(8,128)S(1)} %get-tuple-element.106), channel_id=1, source_target_pairs={{0,28},{4,8},{8,4},{12,16},{16,12},{20,24},{24,20},{28,0},{1,29},{... | collective-permute-start | bytes 196616 | tf_op jit(solution)/shard_map/ppermute | solution.py:218
  39.3 1.5 %collective-permute-start.26 = (f32[64,128]{1,0:T(8,128)S(1)}, f32[64,128]{1,0:T(8,128)S(1)}, u32[]{:S(2)}, u32[]{:S(2)}) collective-permute-start(f32[64,128]{1,0:T(8,128)S(1)} %get-tuple-element.108), channel_id=1, source_target_pairs={{0,3},{1,2},{2,1},{3,0},{4,7},{5,6},{6,5},{7,4},{8,11},{9,10},{10,... | collective-permute-start | bytes 98312 | tf_op jit(solution)/shard_map/ppermute | solution.py:220
  40.8 1.4 %collective-permute-start.27 = (f32[64,128]{1,0:T(8,128)S(1)}, f32[64,128]{1,0:T(8,128)S(1)}, u32[]{:S(2)}, u32[]{:S(2)}) collective-permute-start(f32[64,128]{1,0:T(8,128)S(1)} %get-tuple-element.109), channel_id=1, source_target_pairs={{0,2},{1,3},{2,0},{3,1},{4,6},{5,7},{6,4},{7,5},{8,10},{9,11},{10,... | collective-permute-start | bytes 98312 | tf_op jit(solution)/shard_map/ppermute | solution.py:220
  42.2 0.5 collective-permute-start.29
  42.9 1.2 %collective-permute-done.26.refs_2_ = f32[64,128]{1,0:T(8,128)S(1)} collective-permute-done((f32[64,128]{1,0:T(8,128)S(1)}, f32[64,128]{1,0:T(8,128)S(1)}, u32[]{:S(2)}, u32[]{:S(2)}) %collective-permute-start.26) | collective-permute-done | bytes 32800 | tf_op jit(solution)/shard_map/ppermute | solution.py:220
  44.1 0.6 collective-permute-done.27.refs_3_
  45.0 1.4 %collective-permute-start.31 = (f32[64,128]{1,0:T(8,128)S(1)}, f32[64,128]{1,0:T(8,128)S(1)}, u32[]{:S(2)}, u32[]{:S(2)}) collective-permute-start(f32[64,128]{1,0:T(8,128)S(1)} %get-tuple-element.115), channel_id=1, source_target_pairs={{0,1},{1,0},{2,3},{3,2},{4,5},{5,4},{6,7},{7,6},{8,9},{9,8},{10,11... | collective-permute-start | bytes 98312 | tf_op jit(solution)/shard_map/ppermute | solution.py:220
  46.6 1.5 %collective-permute-start.32 = (f32[64,128]{1,0:T(8,128)S(1)}, f32[64,128]{1,0:T(8,128)S(1)}, u32[]{:S(2)}, u32[]{:S(2)}) collective-permute-start(f32[64,128]{1,0:T(8,128)S(1)} %get-tuple-element.116), channel_id=1, source_target_pairs={{0,3},{1,2},{2,1},{3,0},{4,7},{5,6},{6,5},{7,4},{8,11},{9,10},{10,... | collective-permute-start | bytes 98312 | tf_op jit(solution)/shard_map/ppermute | solution.py:220
  48.1 0.5 collective-permute-start.33
  49.4 2.0 %collective-permute-done.32.refs_2_ = f32[64,128]{1,0:T(8,128)S(1)} collective-permute-done((f32[64,128]{1,0:T(8,128)S(1)}, f32[64,128]{1,0:T(8,128)S(1)}, u32[]{:S(2)}, u32[]{:S(2)}) %collective-permute-start.32) | collective-permute-done | bytes 32800 | tf_op jit(solution)/shard_map/ppermute | solution.py:220
  51.4 0.6 collective-permute-done.33.refs_3_
  52.4 0.6 collective-permute-start.37
  53.0 1.8 %collective-permute-start.36 = (f32[128,128]{1,0:T(8,128)S(1)}, f32[128,128]{1,0:T(8,128)S(1)}, u32[]{:S(2)}, u32[]{:S(2)}) collective-permute-start(f32[128,128]{1,0:T(8,128)S(1)} %get-tuple-element.122), channel_id=1, source_target_pairs={{0,28},{4,8},{8,4},{12,16},{16,12},{20,24},{24,20},{28,0},{1,29},{... | collective-permute-start | bytes 196616 | tf_op jit(solution)/shard_map/ppermute | solution.py:218
  54.8 1.4 %collective-permute-start.38 = (f32[64,128]{1,0:T(8,128)S(1)}, f32[64,128]{1,0:T(8,128)S(1)}, u32[]{:S(2)}, u32[]{:S(2)}) collective-permute-start(f32[64,128]{1,0:T(8,128)S(1)} %get-tuple-element.124), channel_id=1, source_target_pairs={{0,3},{1,2},{2,1},{3,0},{4,7},{5,6},{6,5},{7,4},{8,11},{9,10},{10,... | collective-permute-start | bytes 98312 | tf_op jit(solution)/shard_map/ppermute | solution.py:220
  56.2 1.4 %collective-permute-start.39 = (f32[64,128]{1,0:T(8,128)S(1)}, f32[64,128]{1,0:T(8,128)S(1)}, u32[]{:S(2)}, u32[]{:S(2)}) collective-permute-start(f32[64,128]{1,0:T(8,128)S(1)} %get-tuple-element.125), channel_id=1, source_target_pairs={{0,2},{1,3},{2,0},{3,1},{4,6},{5,7},{6,4},{7,5},{8,10},{9,11},{10,... | collective-permute-start | bytes 98312 | tf_op jit(solution)/shard_map/ppermute | solution.py:220
  57.6 0.5 collective-permute-start.41
  58.3 1.3 %collective-permute-done.38.refs_2_ = f32[64,128]{1,0:T(8,128)S(1)} collective-permute-done((f32[64,128]{1,0:T(8,128)S(1)}, f32[64,128]{1,0:T(8,128)S(1)}, u32[]{:S(2)}, u32[]{:S(2)}) %collective-permute-start.38) | collective-permute-done | bytes 32800 | tf_op jit(solution)/shard_map/ppermute | solution.py:220
  59.6 0.5 collective-permute-done.39.refs_3_
  60.4 1.5 %collective-permute-start.43 = (f32[64,128]{1,0:T(8,128)S(1)}, f32[64,128]{1,0:T(8,128)S(1)}, u32[]{:S(2)}, u32[]{:S(2)}) collective-permute-start(f32[64,128]{1,0:T(8,128)S(1)} %get-tuple-element.137), channel_id=1, source_target_pairs={{0,1},{1,0},{2,3},{3,2},{4,5},{5,4},{6,7},{7,6},{8,9},{9,8},{10,11... | collective-permute-start | bytes 98312 | tf_op jit(solution)/shard_map/ppermute | solution.py:220
  62.1 1.4 %collective-permute-start.44 = (f32[64,128]{1,0:T(8,128)S(1)}, f32[64,128]{1,0:T(8,128)S(1)}, u32[]{:S(2)}, u32[]{:S(2)}) collective-permute-start(f32[64,128]{1,0:T(8,128)S(1)} %get-tuple-element.138), channel_id=1, source_target_pairs={{0,3},{1,2},{2,1},{3,0},{4,7},{5,6},{6,5},{7,4},{8,11},{9,10},{10,... | collective-permute-start | bytes 98312 | tf_op jit(solution)/shard_map/ppermute | solution.py:220
  63.5 0.6 collective-permute-start.45
  64.6 0.9 %local7.1 = (f32[8,64,128]{2,1,0:T(8,128)S(1)}, f32[8,64,128]{2,1,0:T(8,128)}) custom-call(s32[40]{0:T(128)S(4)} %get-tuple-element.72.table, f32[8,64,128]{2,1,0:T(8,128)S(1)} %local6.1.resid, bf16[8,6,128,128]{3,2,1,0:T(8,128)(2,1)S(1)} %get-tuple-element.74.coupling, ...), custom_call_target="tpu_custom_call", output_to_operand_aliasing={{0}: (1, {})} | custom-call | tf_op jit(solution)/shard_map/local7/pallas_call | solution.py:207
  65.5 1.4 %collective-permute-done.44.refs_2_ = f32[64,128]{1,0:T(8,128)S(1)} collective-permute-done((f32[64,128]{1,0:T(8,128)S(1)}, f32[64,128]{1,0:T(8,128)S(1)}, u32[]{:S(2)}, u32[]{:S(2)}) %collective-permute-start.44) | collective-permute-done | bytes 32800 | tf_op jit(solution)/shard_map/ppermute | solution.py:220
  67.5 0.9 %final.1 = f32[8,64,128]{2,1,0:T(8,128)} custom-call(f32[8,64,128]{2,1,0:T(8,128)S(1)} %get-tuple-element.135.resid, f32[128,128]{1,0:T(8,128)S(1)} %collective-permute-done.42.refs_0_, f32[64,128]{1,0:T(8,128)S(1)} %collective-permute-done.43.refs_1_, f32[64,128]{1,0:T(8,128)S(1)} %collective-permute-done.44.refs_2_, ...), custom_call_target="tpu_custom_call" | custom-call | tf_op jit(solution)/shard_map/final/pallas_call | solution.py:207
  (65 shorter events, 7.9 us)
Async XLA Ops:
  2.5 7.8 %collective-permute-start.1 = (f32[72,128]{1,0:T(8,128)S(1)}, f32[72,128]{1,0:T(8,128)S(1)}, u32[]{:S(2)}, u32[]{:S(2)}) collective-permute-start(f32[72,128]{1,0:T(8,128)S(1)} %get-tuple-element.78), channel_id=1, source_target_pairs={{0,1},{1,0},{2,3},{3,2},{4,5},{5,4},{6,7},{7,6},{8,9},{9,8},{10,11... | collective-permute-start | bytes 110600 | tf_op jit(solution)/shard_map/ppermute | solution.py:220
  5.5 8.2 %collective-permute-start = (f32[136,128]{1,0:T(8,128)S(1)}, f32[136,128]{1,0:T(8,128)S(1)}, u32[]{:S(2)}, u32[]{:S(2)}) collective-permute-start(f32[136,128]{1,0:T(8,128)S(1)} %get-tuple-element.77), channel_id=1, source_target_pairs={{0,28},{4,8},{8,4},{12,16},{16,12},{20,24},{24,20},{28,0},{1,29},{... | collective-permute-start | bytes 208904 | tf_op jit(solution)/shard_map/ppermute | solution.py:218
  8.2 4.9 %collective-permute-start.2 = (f32[72,128]{1,0:T(8,128)S(1)}, f32[72,128]{1,0:T(8,128)S(1)}, u32[]{:S(2)}, u32[]{:S(2)}) collective-permute-start(f32[72,128]{1,0:T(8,128)S(1)} %get-tuple-element.79), channel_id=1, source_target_pairs={{0,3},{1,2},{2,1},{3,0},{4,7},{5,6},{6,5},{7,4},{8,11},{9,10},{10,... | collective-permute-start | bytes 110600 | tf_op jit(solution)/shard_map/ppermute | solution.py:220
  9.7 4.0 %collective-permute-start.3 = (f32[72,128]{1,0:T(8,128)S(1)}, f32[72,128]{1,0:T(8,128)S(1)}, u32[]{:S(2)}, u32[]{:S(2)}) collective-permute-start(f32[72,128]{1,0:T(8,128)S(1)} %get-tuple-element.80), channel_id=1, source_target_pairs={{0,2},{1,3},{2,0},{3,1},{4,6},{5,7},{6,4},{7,5},{8,10},{9,11},{10,... | collective-permute-start | bytes 110600 | tf_op jit(solution)/shard_map/ppermute | solution.py:220
  10.2 3.5 %collective-permute-start.4 = (f32[72,128]{1,0:T(8,128)S(1)}, f32[72,128]{1,0:T(8,128)S(1)}, u32[]{:S(2)}, u32[]{:S(2)}) collective-permute-start(f32[72,128]{1,0:T(8,128)S(1)} %get-tuple-element.81), channel_id=1, source_target_pairs={{0,4},{4,0},{8,12},{12,8},{16,20},{20,16},{24,28},{28,24},{1,5},{5... | collective-permute-start | bytes 110600 | tf_op jit(solution)/shard_map/ppermute | solution.py:221
  10.3 3.5 %collective-permute-start.5 = (f32[72,128]{1,0:T(8,128)S(1)}, f32[72,128]{1,0:T(8,128)S(1)}, u32[]{:S(2)}, u32[]{:S(2)}) collective-permute-start(f32[72,128]{1,0:T(8,128)S(1)} %get-tuple-element.82), channel_id=1, source_target_pairs={{0,4},{4,0},{8,12},{12,8},{16,20},{20,16},{24,28},{28,24},{1,5},{5... | collective-permute-start | bytes 110600 | tf_op jit(solution)/shard_map/ppermute | solution.py:221
  14.0 4.2 %collective-permute-start.7 = (f32[64,128]{1,0:T(8,128)S(1)}, f32[64,128]{1,0:T(8,128)S(1)}, u32[]{:S(2)}, u32[]{:S(2)}) collective-permute-start(f32[64,128]{1,0:T(8,128)S(1)} %get-tuple-element.85), channel_id=1, source_target_pairs={{0,1},{1,0},{2,3},{3,2},{4,5},{5,4},{6,7},{7,6},{8,9},{9,8},{10,11... | collective-permute-start | bytes 98312 | tf_op jit(solution)/shard_map/ppermute | solution.py:220
  15.6 5.5 %collective-permute-start.6 = (f32[128,128]{1,0:T(8,128)S(1)}, f32[128,128]{1,0:T(8,128)S(1)}, u32[]{:S(2)}, u32[]{:S(2)}) collective-permute-start(f32[128,128]{1,0:T(8,128)S(1)} %get-tuple-element.84), channel_id=1, source_target_pairs={{0,28},{4,8},{8,4},{12,16},{16,12},{20,24},{24,20},{28,0},{1,29},{... | collective-permute-start | bytes 196616 | tf_op jit(solution)/shard_map/ppermute | solution.py:218
  15.6 4.8 %collective-permute-start.8 = (f32[64,128]{1,0:T(8,128)S(1)}, f32[64,128]{1,0:T(8,128)S(1)}, u32[]{:S(2)}, u32[]{:S(2)}) collective-permute-start(f32[64,128]{1,0:T(8,128)S(1)} %get-tuple-element.86), channel_id=1, source_target_pairs={{0,3},{1,2},{2,1},{3,0},{4,7},{5,6},{6,5},{7,4},{8,11},{9,10},{10,... | collective-permute-start | bytes 98312 | tf_op jit(solution)/shard_map/ppermute | solution.py:220
  16.9 3.9 %collective-permute-start.9 = (f32[64,128]{1,0:T(8,128)S(1)}, f32[64,128]{1,0:T(8,128)S(1)}, u32[]{:S(2)}, u32[]{:S(2)}) collective-permute-start(f32[64,128]{1,0:T(8,128)S(1)} %get-tuple-element.87), channel_id=1, source_target_pairs={{0,2},{1,3},{2,0},{3,1},{4,6},{5,7},{6,4},{7,5},{8,10},{9,11},{10,... | collective-permute-start | bytes 98312 | tf_op jit(solution)/shard_map/ppermute | solution.py:220
  17.6 3.2 %collective-permute-start.10 = (f32[64,128]{1,0:T(8,128)S(1)}, f32[64,128]{1,0:T(8,128)S(1)}, u32[]{:S(2)}, u32[]{:S(2)}) collective-permute-start(f32[64,128]{1,0:T(8,128)S(1)} %get-tuple-element.88), channel_id=1, source_target_pairs={{0,4},{4,0},{8,12},{12,8},{16,20},{20,16},{24,28},{28,24},{1,5},{5... | collective-permute-start | bytes 98312 | tf_op jit(solution)/shard_map/ppermute | solution.py:221
  18.3 2.5 %collective-permute-start.11 = (f32[64,128]{1,0:T(8,128)S(1)}, f32[64,128]{1,0:T(8,128)S(1)}, u32[]{:S(2)}, u32[]{:S(2)}) collective-permute-start(f32[64,128]{1,0:T(8,128)S(1)} %get-tuple-element.89), channel_id=1, source_target_pairs={{0,4},{4,0},{8,12},{12,8},{16,20},{20,16},{24,28},{28,24},{1,5},{5... | collective-permute-start | bytes 98312 | tf_op jit(solution)/shard_map/ppermute | solution.py:221
  21.4 5.1 %collective-permute-start.13 = (f32[64,128]{1,0:T(8,128)S(1)}, f32[64,128]{1,0:T(8,128)S(1)}, u32[]{:S(2)}, u32[]{:S(2)}) collective-permute-start(f32[64,128]{1,0:T(8,128)S(1)} %get-tuple-element.92), channel_id=1, source_target_pairs={{0,1},{1,0},{2,3},{3,2},{4,5},{5,4},{6,7},{7,6},{8,9},{9,8},{10,11... | collective-permute-start | bytes 98312 | tf_op jit(solution)/shard_map/ppermute | solution.py:220
  22.0 7.2 %collective-permute-start.12 = (f32[128,128]{1,0:T(8,128)S(1)}, f32[128,128]{1,0:T(8,128)S(1)}, u32[]{:S(2)}, u32[]{:S(2)}) collective-permute-start(f32[128,128]{1,0:T(8,128)S(1)} %get-tuple-element.91), channel_id=1, source_target_pairs={{0,28},{4,8},{8,4},{12,16},{16,12},{20,24},{24,20},{28,0},{1,29},{... | collective-permute-start | bytes 196616 | tf_op jit(solution)/shard_map/ppermute | solution.py:218
  23.8 4.8 %collective-permute-start.14 = (f32[64,128]{1,0:T(8,128)S(1)}, f32[64,128]{1,0:T(8,128)S(1)}, u32[]{:S(2)}, u32[]{:S(2)}) collective-permute-start(f32[64,128]{1,0:T(8,128)S(1)} %get-tuple-element.93), channel_id=1, source_target_pairs={{0,3},{1,2},{2,1},{3,0},{4,7},{5,6},{6,5},{7,4},{8,11},{9,10},{10,... | collective-permute-start | bytes 98312 | tf_op jit(solution)/shard_map/ppermute | solution.py:220
  25.2 3.9 %collective-permute-start.15 = (f32[64,128]{1,0:T(8,128)S(1)}, f32[64,128]{1,0:T(8,128)S(1)}, u32[]{:S(2)}, u32[]{:S(2)}) collective-permute-start(f32[64,128]{1,0:T(8,128)S(1)} %get-tuple-element.94), channel_id=1, source_target_pairs={{0,2},{1,3},{2,0},{3,1},{4,6},{5,7},{6,4},{7,5},{8,10},{9,11},{10,... | collective-permute-start | bytes 98312 | tf_op jit(solution)/shard_map/ppermute | solution.py:220
  26.5 2.7 %collective-permute-start.16 = (f32[64,128]{1,0:T(8,128)S(1)}, f32[64,128]{1,0:T(8,128)S(1)}, u32[]{:S(2)}, u32[]{:S(2)}) collective-permute-start(f32[64,128]{1,0:T(8,128)S(1)} %get-tuple-element.95), channel_id=1, source_target_pairs={{0,4},{4,0},{8,12},{12,8},{16,20},{20,16},{24,28},{28,24},{1,5},{5... | collective-permute-start | bytes 98312 | tf_op jit(solution)/shard_map/ppermute | solution.py:221
  26.5 2.7 %collective-permute-start.17 = (f32[64,128]{1,0:T(8,128)S(1)}, f32[64,128]{1,0:T(8,128)S(1)}, u32[]{:S(2)}, u32[]{:S(2)}) collective-permute-start(f32[64,128]{1,0:T(8,128)S(1)} %get-tuple-element.96), channel_id=1, source_target_pairs={{0,4},{4,0},{8,12},{12,8},{16,20},{20,16},{24,28},{28,24},{1,5},{5... | collective-permute-start | bytes 98312 | tf_op jit(solution)/shard_map/ppermute | solution.py:221
  29.5 4.0 %collective-permute-start.19 = (f32[64,128]{1,0:T(8,128)S(1)}, f32[64,128]{1,0:T(8,128)S(1)}, u32[]{:S(2)}, u32[]{:S(2)}) collective-permute-start(f32[64,128]{1,0:T(8,128)S(1)} %get-tuple-element.99), channel_id=1, source_target_pairs={{0,1},{1,0},{2,3},{3,2},{4,5},{5,4},{6,7},{7,6},{8,9},{9,8},{10,11... | collective-permute-start | bytes 98312 | tf_op jit(solution)/shard_map/ppermute | solution.py:220
  31.0 5.5 %collective-permute-start.18 = (f32[128,128]{1,0:T(8,128)S(1)}, f32[128,128]{1,0:T(8,128)S(1)}, u32[]{:S(2)}, u32[]{:S(2)}) collective-permute-start(f32[128,128]{1,0:T(8,128)S(1)} %get-tuple-element.98), channel_id=1, source_target_pairs={{0,28},{4,8},{8,4},{12,16},{16,12},{20,24},{24,20},{28,0},{1,29},{... | collective-permute-start | bytes 196616 | tf_op jit(solution)/shard_map/ppermute | solution.py:218
  31.2 4.8 %collective-permute-start.20 = (f32[64,128]{1,0:T(8,128)S(1)}, f32[64,128]{1,0:T(8,128)S(1)}, u32[]{:S(2)}, u32[]{:S(2)}) collective-permute-start(f32[64,128]{1,0:T(8,128)S(1)} %get-tuple-element.100), channel_id=1, source_target_pairs={{0,3},{1,2},{2,1},{3,0},{4,7},{5,6},{6,5},{7,4},{8,11},{9,10},{10,... | collective-permute-start | bytes 98312 | tf_op jit(solution)/shard_map/ppermute | solution.py:220
  32.6 3.9 %collective-permute-start.21 = (f32[64,128]{1,0:T(8,128)S(1)}, f32[64,128]{1,0:T(8,128)S(1)}, u32[]{:S(2)}, u32[]{:S(2)}) collective-permute-start(f32[64,128]{1,0:T(8,128)S(1)} %get-tuple-element.101), channel_id=1, source_target_pairs={{0,2},{1,3},{2,0},{3,1},{4,6},{5,7},{6,4},{7,5},{8,10},{9,11},{10,... | collective-permute-start | bytes 98312 | tf_op jit(solution)/shard_map/ppermute | solution.py:220
  33.2 3.3 %collective-permute-start.22 = (f32[64,128]{1,0:T(8,128)S(1)}, f32[64,128]{1,0:T(8,128)S(1)}, u32[]{:S(2)}, u32[]{:S(2)}) collective-permute-start(f32[64,128]{1,0:T(8,128)S(1)} %get-tuple-element.102), channel_id=1, source_target_pairs={{0,4},{4,0},{8,12},{12,8},{16,20},{20,16},{24,28},{28,24},{1,5},{5... | collective-permute-start | bytes 98312 | tf_op jit(solution)/shard_map/ppermute | solution.py:221
  33.5 3.0 %collective-permute-start.23 = (f32[64,128]{1,0:T(8,128)S(1)}, f32[64,128]{1,0:T(8,128)S(1)}, u32[]{:S(2)}, u32[]{:S(2)}) collective-permute-start(f32[64,128]{1,0:T(8,128)S(1)} %get-tuple-element.103), channel_id=1, source_target_pairs={{0,4},{4,0},{8,12},{12,8},{16,20},{20,16},{24,28},{28,24},{1,5},{5... | collective-permute-start | bytes 98312 | tf_op jit(solution)/shard_map/ppermute | solution.py:221
  36.8 5.4 %collective-permute-start.25 = (f32[64,128]{1,0:T(8,128)S(1)}, f32[64,128]{1,0:T(8,128)S(1)}, u32[]{:S(2)}, u32[]{:S(2)}) collective-permute-start(f32[64,128]{1,0:T(8,128)S(1)} %get-tuple-element.107), channel_id=1, source_target_pairs={{0,1},{1,0},{2,3},{3,2},{4,5},{5,4},{6,7},{7,6},{8,9},{9,8},{10,11... | collective-permute-start | bytes 98312 | tf_op jit(solution)/shard_map/ppermute | solution.py:220
  37.5 7.2 %collective-permute-start.24 = (f32[128,128]{1,0:T(8,128)S(1)}, f32[128,128]{1,0:T(8,128)S(1)}, u32[]{:S(2)}, u32[]{:S(2)}) collective-permute-start(f32[128,128]{1,0:T(8,128)S(1)} %get-tuple-element.106), channel_id=1, source_target_pairs={{0,28},{4,8},{8,4},{12,16},{16,12},{20,24},{24,20},{28,0},{1,29},{... | collective-permute-start | bytes 196616 | tf_op jit(solution)/shard_map/ppermute | solution.py:218
  39.3 4.8 %collective-permute-start.26 = (f32[64,128]{1,0:T(8,128)S(1)}, f32[64,128]{1,0:T(8,128)S(1)}, u32[]{:S(2)}, u32[]{:S(2)}) collective-permute-start(f32[64,128]{1,0:T(8,128)S(1)} %get-tuple-element.108), channel_id=1, source_target_pairs={{0,3},{1,2},{2,1},{3,0},{4,7},{5,6},{6,5},{7,4},{8,11},{9,10},{10,... | collective-permute-start | bytes 98312 | tf_op jit(solution)/shard_map/ppermute | solution.py:220
  40.8 3.9 %collective-permute-start.27 = (f32[64,128]{1,0:T(8,128)S(1)}, f32[64,128]{1,0:T(8,128)S(1)}, u32[]{:S(2)}, u32[]{:S(2)}) collective-permute-start(f32[64,128]{1,0:T(8,128)S(1)} %get-tuple-element.109), channel_id=1, source_target_pairs={{0,2},{1,3},{2,0},{3,1},{4,6},{5,7},{6,4},{7,5},{8,10},{9,11},{10,... | collective-permute-start | bytes 98312 | tf_op jit(solution)/shard_map/ppermute | solution.py:220
  42.2 2.5 %collective-permute-start.28 = (f32[64,128]{1,0:T(8,128)S(1)}, f32[64,128]{1,0:T(8,128)S(1)}, u32[]{:S(2)}, u32[]{:S(2)}) collective-permute-start(f32[64,128]{1,0:T(8,128)S(1)} %get-tuple-element.110), channel_id=1, source_target_pairs={{0,4},{4,0},{8,12},{12,8},{16,20},{20,16},{24,28},{28,24},{1,5},{5... | collective-permute-start | bytes 98312 | tf_op jit(solution)/shard_map/ppermute | solution.py:221
  42.2 2.5 %collective-permute-start.29 = (f32[64,128]{1,0:T(8,128)S(1)}, f32[64,128]{1,0:T(8,128)S(1)}, u32[]{:S(2)}, u32[]{:S(2)}) collective-permute-start(f32[64,128]{1,0:T(8,128)S(1)} %get-tuple-element.111), channel_id=1, source_target_pairs={{0,4},{4,0},{8,12},{12,8},{16,20},{20,16},{24,28},{28,24},{1,5},{5... | collective-permute-start | bytes 98312 | tf_op jit(solution)/shard_map/ppermute | solution.py:221
  45.0 4.0 %collective-permute-start.31 = (f32[64,128]{1,0:T(8,128)S(1)}, f32[64,128]{1,0:T(8,128)S(1)}, u32[]{:S(2)}, u32[]{:S(2)}) collective-permute-start(f32[64,128]{1,0:T(8,128)S(1)} %get-tuple-element.115), channel_id=1, source_target_pairs={{0,1},{1,0},{2,3},{3,2},{4,5},{5,4},{6,7},{7,6},{8,9},{9,8},{10,11... | collective-permute-start | bytes 98312 | tf_op jit(solution)/shard_map/ppermute | solution.py:220
  46.4 5.6 %collective-permute-start.30 = (f32[128,128]{1,0:T(8,128)S(1)}, f32[128,128]{1,0:T(8,128)S(1)}, u32[]{:S(2)}, u32[]{:S(2)}) collective-permute-start(f32[128,128]{1,0:T(8,128)S(1)} %get-tuple-element.114), channel_id=1, source_target_pairs={{0,28},{4,8},{8,4},{12,16},{16,12},{20,24},{24,20},{28,0},{1,29},{... | collective-permute-start | bytes 196616 | tf_op jit(solution)/shard_map/ppermute | solution.py:218
  46.6 4.8 %collective-permute-start.32 = (f32[64,128]{1,0:T(8,128)S(1)}, f32[64,128]{1,0:T(8,128)S(1)}, u32[]{:S(2)}, u32[]{:S(2)}) collective-permute-start(f32[64,128]{1,0:T(8,128)S(1)} %get-tuple-element.116), channel_id=1, source_target_pairs={{0,3},{1,2},{2,1},{3,0},{4,7},{5,6},{6,5},{7,4},{8,11},{9,10},{10,... | collective-permute-start | bytes 98312 | tf_op jit(solution)/shard_map/ppermute | solution.py:220
  48.1 3.9 %collective-permute-start.33 = (f32[64,128]{1,0:T(8,128)S(1)}, f32[64,128]{1,0:T(8,128)S(1)}, u32[]{:S(2)}, u32[]{:S(2)}) collective-permute-start(f32[64,128]{1,0:T(8,128)S(1)} %get-tuple-element.117), channel_id=1, source_target_pairs={{0,2},{1,3},{2,0},{3,1},{4,6},{5,7},{6,4},{7,5},{8,10},{9,11},{10,... | collective-permute-start | bytes 98312 | tf_op jit(solution)/shard_map/ppermute | solution.py:220
  48.6 3.4 %collective-permute-start.34 = (f32[64,128]{1,0:T(8,128)S(1)}, f32[64,128]{1,0:T(8,128)S(1)}, u32[]{:S(2)}, u32[]{:S(2)}) collective-permute-start(f32[64,128]{1,0:T(8,128)S(1)} %get-tuple-element.118), channel_id=1, source_target_pairs={{0,4},{4,0},{8,12},{12,8},{16,20},{20,16},{24,28},{28,24},{1,5},{5... | collective-permute-start | bytes 98312 | tf_op jit(solution)/shard_map/ppermute | solution.py:221
  49.0 3.0 %collective-permute-start.35 = (f32[64,128]{1,0:T(8,128)S(1)}, f32[64,128]{1,0:T(8,128)S(1)}, u32[]{:S(2)}, u32[]{:S(2)}) collective-permute-start(f32[64,128]{1,0:T(8,128)S(1)} %get-tuple-element.119), channel_id=1, source_target_pairs={{0,4},{4,0},{8,12},{12,8},{16,20},{20,16},{24,28},{28,24},{1,5},{5... | collective-permute-start | bytes 98312 | tf_op jit(solution)/shard_map/ppermute | solution.py:221
  52.4 5.2 %collective-permute-start.37 = (f32[64,128]{1,0:T(8,128)S(1)}, f32[64,128]{1,0:T(8,128)S(1)}, u32[]{:S(2)}, u32[]{:S(2)}) collective-permute-start(f32[64,128]{1,0:T(8,128)S(1)} %get-tuple-element.123), channel_id=1, source_target_pairs={{0,1},{1,0},{2,3},{3,2},{4,5},{5,4},{6,7},{7,6},{8,9},{9,8},{10,11... | collective-permute-start | bytes 98312 | tf_op jit(solution)/shard_map/ppermute | solution.py:220
  53.0 7.2 %collective-permute-start.36 = (f32[128,128]{1,0:T(8,128)S(1)}, f32[128,128]{1,0:T(8,128)S(1)}, u32[]{:S(2)}, u32[]{:S(2)}) collective-permute-start(f32[128,128]{1,0:T(8,128)S(1)} %get-tuple-element.122), channel_id=1, source_target_pairs={{0,28},{4,8},{8,4},{12,16},{16,12},{20,24},{24,20},{28,0},{1,29},{... | collective-permute-start | bytes 196616 | tf_op jit(solution)/shard_map/ppermute | solution.py:218
  54.8 4.8 %collective-permute-start.38 = (f32[64,128]{1,0:T(8,128)S(1)}, f32[64,128]{1,0:T(8,128)S(1)}, u32[]{:S(2)}, u32[]{:S(2)}) collective-permute-start(f32[64,128]{1,0:T(8,128)S(1)} %get-tuple-element.124), channel_id=1, source_target_pairs={{0,3},{1,2},{2,1},{3,0},{4,7},{5,6},{6,5},{7,4},{8,11},{9,10},{10,... | collective-permute-start | bytes 98312 | tf_op jit(solution)/shard_map/ppermute | solution.py:220
  56.2 3.9 %collective-permute-start.39 = (f32[64,128]{1,0:T(8,128)S(1)}, f32[64,128]{1,0:T(8,128)S(1)}, u32[]{:S(2)}, u32[]{:S(2)}) collective-permute-start(f32[64,128]{1,0:T(8,128)S(1)} %get-tuple-element.125), channel_id=1, source_target_pairs={{0,2},{1,3},{2,0},{3,1},{4,6},{5,7},{6,4},{7,5},{8,10},{9,11},{10,... | collective-permute-start | bytes 98312 | tf_op jit(solution)/shard_map/ppermute | solution.py:220
  57.6 2.5 %collective-permute-start.40 = (f32[64,128]{1,0:T(8,128)S(1)}, f32[64,128]{1,0:T(8,128)S(1)}, u32[]{:S(2)}, u32[]{:S(2)}) collective-permute-start(f32[64,128]{1,0:T(8,128)S(1)} %get-tuple-element.126), channel_id=1, source_target_pairs={{0,4},{4,0},{8,12},{12,8},{16,20},{20,16},{24,28},{28,24},{1,5},{5... | collective-permute-start | bytes 98312 | tf_op jit(solution)/shard_map/ppermute | solution.py:221
  57.6 2.5 %collective-permute-start.41 = (f32[64,128]{1,0:T(8,128)S(1)}, f32[64,128]{1,0:T(8,128)S(1)}, u32[]{:S(2)}, u32[]{:S(2)}) collective-permute-start(f32[64,128]{1,0:T(8,128)S(1)} %get-tuple-element.127), channel_id=1, source_target_pairs={{0,4},{4,0},{8,12},{12,8},{16,20},{20,16},{24,28},{28,24},{1,5},{5... | collective-permute-start | bytes 98312 | tf_op jit(solution)/shard_map/ppermute | solution.py:221
  60.4 4.0 %collective-permute-start.43 = (f32[64,128]{1,0:T(8,128)S(1)}, f32[64,128]{1,0:T(8,128)S(1)}, u32[]{:S(2)}, u32[]{:S(2)}) collective-permute-start(f32[64,128]{1,0:T(8,128)S(1)} %get-tuple-element.137), channel_id=1, source_target_pairs={{0,1},{1,0},{2,3},{3,2},{4,5},{5,4},{6,7},{7,6},{8,9},{9,8},{10,11... | collective-permute-start | bytes 98312 | tf_op jit(solution)/shard_map/ppermute | solution.py:220
  62.0 5.5 %collective-permute-start.42 = (f32[128,128]{1,0:T(8,128)S(1)}, f32[128,128]{1,0:T(8,128)S(1)}, u32[]{:S(2)}, u32[]{:S(2)}) collective-permute-start(f32[128,128]{1,0:T(8,128)S(1)} %get-tuple-element.136), channel_id=1, source_target_pairs={{0,28},{4,8},{8,4},{12,16},{16,12},{20,24},{24,20},{28,0},{1,29},{... | collective-permute-start | bytes 196616 | tf_op jit(solution)/shard_map/ppermute | solution.py:218
  62.1 4.8 %collective-permute-start.44 = (f32[64,128]{1,0:T(8,128)S(1)}, f32[64,128]{1,0:T(8,128)S(1)}, u32[]{:S(2)}, u32[]{:S(2)}) collective-permute-start(f32[64,128]{1,0:T(8,128)S(1)} %get-tuple-element.138), channel_id=1, source_target_pairs={{0,3},{1,2},{2,1},{3,0},{4,7},{5,6},{6,5},{7,4},{8,11},{9,10},{10,... | collective-permute-start | bytes 98312 | tf_op jit(solution)/shard_map/ppermute | solution.py:220
  63.5 3.9 %collective-permute-start.45 = (f32[64,128]{1,0:T(8,128)S(1)}, f32[64,128]{1,0:T(8,128)S(1)}, u32[]{:S(2)}, u32[]{:S(2)}) collective-permute-start(f32[64,128]{1,0:T(8,128)S(1)} %get-tuple-element.139), channel_id=1, source_target_pairs={{0,2},{1,3},{2,0},{3,1},{4,6},{5,7},{6,4},{7,5},{8,10},{9,11},{10,... | collective-permute-start | bytes 98312 | tf_op jit(solution)/shard_map/ppermute | solution.py:220
  64.1 3.3 %collective-permute-start.46 = (f32[64,128]{1,0:T(8,128)S(1)}, f32[64,128]{1,0:T(8,128)S(1)}, u32[]{:S(2)}, u32[]{:S(2)}) collective-permute-start(f32[64,128]{1,0:T(8,128)S(1)} %get-tuple-element.140), channel_id=1, source_target_pairs={{0,4},{4,0},{8,12},{12,8},{16,20},{20,16},{24,28},{28,24},{1,5},{5... | collective-permute-start | bytes 98312 | tf_op jit(solution)/shard_map/ppermute | solution.py:221
  64.4 3.0 %collective-permute-start.47 = (f32[64,128]{1,0:T(8,128)S(1)}, f32[64,128]{1,0:T(8,128)S(1)}, u32[]{:S(2)}, u32[]{:S(2)}) collective-permute-start(f32[64,128]{1,0:T(8,128)S(1)} %get-tuple-element.141), channel_id=1, source_target_pairs={{0,4},{4,0},{8,12},{12,8},{16,20},{20,16},{24,28},{28,24},{1,5},{5... | collective-permute-start | bytes 98312 | tf_op jit(solution)/shard_map/ppermute | solution.py:221

commit v7 on v6

--- a/solution.py
+++ b/solution.py
@@ -108,6 +108,17 @@
         for k in range(2):
             table[plan.local + 2 * at + k] = local_target[k, i]
             table[plan.slot + 2 * at + k] = me ^ group_peer[k, i]
+    copies[5].wait()
+    copies[6].wait()
+    changes = []
+    for p in range(plan.quarter):
+        j = table[plan.order + p]
+        new = dot(rhs[j].astype(jnp.bfloat16), diag[j])
+        sol[p] = new
+        changes.append(new.astype(jnp.bfloat16))
+        change[p] = changes[p]
+    copies[7].wait()
+    products(plan, 0, table, changes, coupling, sends)
     line = lax.broadcasted_iota(jnp.int32, (META, plan.w), 0)
     for lane, s in enumerate(plan.distances):
         meta = jnp.full((META, plan.w), -1, jnp.int32)
@@ -125,17 +136,6 @@
     for at in range(plan.rows):
         meta = jnp.where(line == at, dom_target[1 - parity, table[plan.order + at]], meta)
     sends[0][pl.ds(plan.quarter * plan.n, plan.dom_meta), :] = meta.astype(jnp.float32)
-    copies[5].wait()
-    copies[6].wait()
-    changes = []
-    for p in range(plan.quarter):
-        j = table[plan.order + p]
-        new = dot(rhs[j].astype(jnp.bfloat16), diag[j])
-        sol[p] = new
-        changes.append(new.astype(jnp.bfloat16))
-        change[p] = changes[p]
-    copies[7].wait()
-    products(plan, 0, table, changes, coupling, sends)
 
 
 def step_kernel(plan, step, table, resid, diag, coupling, *refs):
@@ -187,9 +187,14 @@
     got, refs = lanes_of(plan, refs)
     meta, refs = lanes_of(plan, refs)
     items = items_of(plan, step, got, meta)
-    out = refs[-1]
+    out, rows, sems = refs
+    copies = []
     for r in range(plan.rows):
-        out[r] = subtract(plan, resid[r], jnp.float32(r), items)
+        rows[r] = subtract(plan, resid[r], jnp.float32(r), items)
+        copies.append(pltpu.make_async_copy(rows.at[r], out.at[r], sems.at[r]))
+        copies[r].start()
+    for copy in copies:
+        copy.wait()
 
 
 def on_device(coupling, diag_inv, rhs, color, local_target, group_peer, group_list, dom_target):
@@ -204,11 +209,12 @@
 
     def call(body, name, ins, in_specs, outs, **kw):
         smem = [getattr(o, "memory_space", None) == pltpu.SMEM for o in outs]
+        out_specs = kw.pop("out_specs", [SMEM if s else VMEM for s in smem])
         return pl.pallas_call(
             body,
             name=name,
             in_specs=in_specs + [VMEM] * (len(ins) - len(in_specs)),
-            out_specs=[SMEM if s else VMEM for s in smem],
+            out_specs=out_specs,
             out_shape=outs,
             compiler_params=params,
             **kw,
@@ -283,6 +289,8 @@
         [resid, *got, *meta],
         [],
         [jax.ShapeDtypeStruct(rhs.shape, f32)],
+        out_specs=[HBM],
+        scratch_shapes=[pltpu.VMEM(rhs.shape, f32), pltpu.SemaphoreType.DMA((rows,))],
     )
     return rest[0], defect
 

time: 68.5 us -> 68.5 us (level)
  no operation moved by 1% of the time
where the time goes in v7:
time: 68.5 us; the launch traced here: 68.3 us
  starting transfers between devices  40.6 us (59%)
  waiting for transfers between devices  19.7 us (29%)
  Pallas kernels  7.18 us (10%)
  between operations  0.82 us (1%)
    ppermute x24, starting transfers between devices, exchange(): got.append(lax.ppermute(send, 'sub', [(i, i ^ s) for i in range(group)]))  29.4 us
    ppermute x24, waiting for transfers between devices, exchange(): got.append(lax.ppermute(send, 'sub', [(i, i ^ s) for i in range(group)]))  19.3 us
    ppermute x8, starting transfers between devices, exchange(): got = [lax.ppermute(sends[0], 'dom', far_pairs)]  8.65 us
    pallas_call x17, Pallas kernels, call(): pl.pallas_call(body, name=name, in_specs=in_specs + [VMEM] * (len(ins) -...  7.18 us
    ppermute x16, starting transfers between devices, exchange(): lax.ppermute(send, 'dom', near_pairs)  2.6 us
  transfers between devices with their start and end apart: 48, of which 21 were waited for; matrix products, arithmetic and copies ran while one was open for 0% of the time, Pallas kernels for 3%

profile of v7, /device:TPU:0, one launch (start us, length us, event | category | flops | bytes accessed | tf_op | source)
XLA Modules:
  0.0 68.3 jit_solution(17532368326548866200)
XLA Ops:
  0.6 1.9 %first.1 = (s32[40]{0:T(128)S(4)}, bf16[8,6,128,128]{3,2,1,0:T(8,128)(2,1)S(1)}, bf16[8,128,128]{2,1,0:T(8,128)(2,1)S(1)}, f32[8,64,128]{2,1,0:T(8,128)S(1)}, f3...) custom-call(s32[8]{0:T(128)} %refs_0_.1, ...), custom_call_target="tpu_custom_call" | custom-call | tf_op jit(solution)/shard_map/first/pallas_call | solution.py:213
  2.5 3.0 %collective-permute-start.1 = (f32[72,128]{1,0:T(8,128)S(1)}, f32[72,128]{1,0:T(8,128)S(1)}, u32[]{:S(2)}, u32[]{:S(2)}) collective-permute-start(f32[72,128]{1,0:T(8,128)S(1)} %get-tuple-element.78), channel_id=1, source_target_pairs={{0,1},{1,0},{2,3},{3,2},{4,5},{5,4},{6,7},{7,6},{8,9},{9,8},{10,11... | collective-permute-start | bytes 110600 | tf_op jit(solution)/shard_map/ppermute | solution.py:226
  5.5 2.8 %collective-permute-start = (f32[136,128]{1,0:T(8,128)S(1)}, f32[136,128]{1,0:T(8,128)S(1)}, u32[]{:S(2)}, u32[]{:S(2)}) collective-permute-start(f32[136,128]{1,0:T(8,128)S(1)} %get-tuple-element.77), channel_id=1, source_target_pairs={{0,28},{4,8},{8,4},{12,16},{16,12},{20,24},{24,20},{28,0},{1,29},{... | collective-permute-start | bytes 208904 | tf_op jit(solution)/shard_map/ppermute | solution.py:224
  8.3 1.5 %collective-permute-start.2 = (f32[72,128]{1,0:T(8,128)S(1)}, f32[72,128]{1,0:T(8,128)S(1)}, u32[]{:S(2)}, u32[]{:S(2)}) collective-permute-start(f32[72,128]{1,0:T(8,128)S(1)} %get-tuple-element.79), channel_id=1, source_target_pairs={{0,3},{1,2},{2,1},{3,0},{4,7},{5,6},{6,5},{7,4},{8,11},{9,10},{10,... | collective-permute-start | bytes 110600 | tf_op jit(solution)/shard_map/ppermute | solution.py:226
  10.3 0.5 collective-permute-start.5
  11.0 2.2 %collective-permute-done.2.refs_2_.refs_8_ = f32[72,128]{1,0:T(8,128)S(1)} collective-permute-done((f32[72,128]{1,0:T(8,128)S(1)}, f32[72,128]{1,0:T(8,128)S(1)}, u32[]{:S(2)}, u32[]{:S(2)}) %collective-permute-start.2) | collective-permute-done | bytes 36896 | tf_op jit(solution)/shard_map/ppermute | solution.py:226
  13.1 0.6 collective-permute-done.3.refs_3_.refs_9_
  14.1 1.6 %collective-permute-start.7 = (f32[64,128]{1,0:T(8,128)S(1)}, f32[64,128]{1,0:T(8,128)S(1)}, u32[]{:S(2)}, u32[]{:S(2)}) collective-permute-start(f32[64,128]{1,0:T(8,128)S(1)} %get-tuple-element.85), channel_id=1, source_target_pairs={{0,1},{1,0},{2,3},{3,2},{4,5},{5,4},{6,7},{7,6},{8,9},{9,8},{10,11... | collective-permute-start | bytes 98312 | tf_op jit(solution)/shard_map/ppermute | solution.py:226
  15.6 1.3 %collective-permute-start.8 = (f32[64,128]{1,0:T(8,128)S(1)}, f32[64,128]{1,0:T(8,128)S(1)}, u32[]{:S(2)}, u32[]{:S(2)}) collective-permute-start(f32[64,128]{1,0:T(8,128)S(1)} %get-tuple-element.86), channel_id=1, source_target_pairs={{0,3},{1,2},{2,1},{3,0},{4,7},{5,6},{6,5},{7,4},{8,11},{9,10},{10,... | collective-permute-start | bytes 98312 | tf_op jit(solution)/shard_map/ppermute | solution.py:226
  16.9 0.7 %collective-permute-start.9 = (f32[64,128]{1,0:T(8,128)S(1)}, f32[64,128]{1,0:T(8,128)S(1)}, u32[]{:S(2)}, u32[]{:S(2)}) collective-permute-start(f32[64,128]{1,0:T(8,128)S(1)} %get-tuple-element.87), channel_id=1, source_target_pairs={{0,2},{1,3},{2,0},{3,1},{4,6},{5,7},{6,4},{7,5},{8,10},{9,11},{10,... | collective-permute-start | bytes 98312 | tf_op jit(solution)/shard_map/ppermute | solution.py:226
  17.6 0.7 collective-permute-done.7.refs_1_
  18.5 1.9 %collective-permute-done.8.refs_2_ = f32[64,128]{1,0:T(8,128)S(1)} collective-permute-done((f32[64,128]{1,0:T(8,128)S(1)}, f32[64,128]{1,0:T(8,128)S(1)}, u32[]{:S(2)}, u32[]{:S(2)}) %collective-permute-start.8) | collective-permute-done | bytes 32800 | tf_op jit(solution)/shard_map/ppermute | solution.py:226
  21.4 0.6 collective-permute-start.13
  22.0 1.8 %collective-permute-start.12 = (f32[128,128]{1,0:T(8,128)S(1)}, f32[128,128]{1,0:T(8,128)S(1)}, u32[]{:S(2)}, u32[]{:S(2)}) collective-permute-start(f32[128,128]{1,0:T(8,128)S(1)} %get-tuple-element.91), channel_id=1, source_target_pairs={{0,28},{4,8},{8,4},{12,16},{16,12},{20,24},{24,20},{28,0},{1,29},{... | collective-permute-start | bytes 196616 | tf_op jit(solution)/shard_map/ppermute | solution.py:224
  23.9 1.4 %collective-permute-start.14 = (f32[64,128]{1,0:T(8,128)S(1)}, f32[64,128]{1,0:T(8,128)S(1)}, u32[]{:S(2)}, u32[]{:S(2)}) collective-permute-start(f32[64,128]{1,0:T(8,128)S(1)} %get-tuple-element.93), channel_id=1, source_target_pairs={{0,3},{1,2},{2,1},{3,0},{4,7},{5,6},{6,5},{7,4},{8,11},{9,10},{10,... | collective-permute-start | bytes 98312 | tf_op jit(solution)/shard_map/ppermute | solution.py:226
  25.3 1.3 %collective-permute-start.15 = (f32[64,128]{1,0:T(8,128)S(1)}, f32[64,128]{1,0:T(8,128)S(1)}, u32[]{:S(2)}, u32[]{:S(2)}) collective-permute-start(f32[64,128]{1,0:T(8,128)S(1)} %get-tuple-element.94), channel_id=1, source_target_pairs={{0,2},{1,3},{2,0},{3,1},{4,6},{5,7},{6,4},{7,5},{8,10},{9,11},{10,... | collective-permute-start | bytes 98312 | tf_op jit(solution)/shard_map/ppermute | solution.py:226
  26.5 0.5 collective-permute-start.17
  27.3 1.4 %collective-permute-done.14.refs_2_ = f32[64,128]{1,0:T(8,128)S(1)} collective-permute-done((f32[64,128]{1,0:T(8,128)S(1)}, f32[64,128]{1,0:T(8,128)S(1)}, u32[]{:S(2)}, u32[]{:S(2)}) %collective-permute-start.14) | collective-permute-done | bytes 32800 | tf_op jit(solution)/shard_map/ppermute | solution.py:226
  28.7 0.5 collective-permute-done.15.refs_3_
  29.5 1.5 %collective-permute-start.19 = (f32[64,128]{1,0:T(8,128)S(1)}, f32[64,128]{1,0:T(8,128)S(1)}, u32[]{:S(2)}, u32[]{:S(2)}) collective-permute-start(f32[64,128]{1,0:T(8,128)S(1)} %get-tuple-element.99), channel_id=1, source_target_pairs={{0,1},{1,0},{2,3},{3,2},{4,5},{5,4},{6,7},{7,6},{8,9},{9,8},{10,11... | collective-permute-start | bytes 98312 | tf_op jit(solution)/shard_map/ppermute | solution.py:226
  31.2 1.4 %collective-permute-start.20 = (f32[64,128]{1,0:T(8,128)S(1)}, f32[64,128]{1,0:T(8,128)S(1)}, u32[]{:S(2)}, u32[]{:S(2)}) collective-permute-start(f32[64,128]{1,0:T(8,128)S(1)} %get-tuple-element.100), channel_id=1, source_target_pairs={{0,3},{1,2},{2,1},{3,0},{4,7},{5,6},{6,5},{7,4},{8,11},{9,10},{10,... | collective-permute-start | bytes 98312 | tf_op jit(solution)/shard_map/ppermute | solution.py:226
  32.6 0.6 collective-permute-start.21
  33.9 2.1 %collective-permute-done.20.refs_2_ = f32[64,128]{1,0:T(8,128)S(1)} collective-permute-done((f32[64,128]{1,0:T(8,128)S(1)}, f32[64,128]{1,0:T(8,128)S(1)}, u32[]{:S(2)}, u32[]{:S(2)}) %collective-permute-start.20) | collective-permute-done | bytes 32800 | tf_op jit(solution)/shard_map/ppermute | solution.py:226
  36.8 0.7 collective-permute-start.25
  37.5 1.8 %collective-permute-start.24 = (f32[128,128]{1,0:T(8,128)S(1)}, f32[128,128]{1,0:T(8,128)S(1)}, u32[]{:S(2)}, u32[]{:S(2)}) collective-permute-start(f32[128,128]{1,0:T(8,128)S(1)} %get-tuple-element.106), channel_id=1, source_target_pairs={{0,28},{4,8},{8,4},{12,16},{16,12},{20,24},{24,20},{28,0},{1,29},{... | collective-permute-start | bytes 196616 | tf_op jit(solution)/shard_map/ppermute | solution.py:224
  39.3 1.5 %collective-permute-start.26 = (f32[64,128]{1,0:T(8,128)S(1)}, f32[64,128]{1,0:T(8,128)S(1)}, u32[]{:S(2)}, u32[]{:S(2)}) collective-permute-start(f32[64,128]{1,0:T(8,128)S(1)} %get-tuple-element.108), channel_id=1, source_target_pairs={{0,3},{1,2},{2,1},{3,0},{4,7},{5,6},{6,5},{7,4},{8,11},{9,10},{10,... | collective-permute-start | bytes 98312 | tf_op jit(solution)/shard_map/ppermute | solution.py:226
  40.8 1.4 %collective-permute-start.27 = (f32[64,128]{1,0:T(8,128)S(1)}, f32[64,128]{1,0:T(8,128)S(1)}, u32[]{:S(2)}, u32[]{:S(2)}) collective-permute-start(f32[64,128]{1,0:T(8,128)S(1)} %get-tuple-element.109), channel_id=1, source_target_pairs={{0,2},{1,3},{2,0},{3,1},{4,6},{5,7},{6,4},{7,5},{8,10},{9,11},{10,... | collective-permute-start | bytes 98312 | tf_op jit(solution)/shard_map/ppermute | solution.py:226
  42.2 0.5 collective-permute-start.29
  42.9 1.2 %collective-permute-done.26.refs_2_ = f32[64,128]{1,0:T(8,128)S(1)} collective-permute-done((f32[64,128]{1,0:T(8,128)S(1)}, f32[64,128]{1,0:T(8,128)S(1)}, u32[]{:S(2)}, u32[]{:S(2)}) %collective-permute-start.26) | collective-permute-done | bytes 32800 | tf_op jit(solution)/shard_map/ppermute | solution.py:226
  44.1 0.6 collective-permute-done.27.refs_3_
  45.0 1.4 %collective-permute-start.31 = (f32[64,128]{1,0:T(8,128)S(1)}, f32[64,128]{1,0:T(8,128)S(1)}, u32[]{:S(2)}, u32[]{:S(2)}) collective-permute-start(f32[64,128]{1,0:T(8,128)S(1)} %get-tuple-element.115), channel_id=1, source_target_pairs={{0,1},{1,0},{2,3},{3,2},{4,5},{5,4},{6,7},{7,6},{8,9},{9,8},{10,11... | collective-permute-start | bytes 98312 | tf_op jit(solution)/shard_map/ppermute | solution.py:226
  46.6 1.5 %collective-permute-start.32 = (f32[64,128]{1,0:T(8,128)S(1)}, f32[64,128]{1,0:T(8,128)S(1)}, u32[]{:S(2)}, u32[]{:S(2)}) collective-permute-start(f32[64,128]{1,0:T(8,128)S(1)} %get-tuple-element.116), channel_id=1, source_target_pairs={{0,3},{1,2},{2,1},{3,0},{4,7},{5,6},{6,5},{7,4},{8,11},{9,10},{10,... | collective-permute-start | bytes 98312 | tf_op jit(solution)/shard_map/ppermute | solution.py:226
  48.1 0.5 collective-permute-start.33
  49.4 2.0 %collective-permute-done.32.refs_2_ = f32[64,128]{1,0:T(8,128)S(1)} collective-permute-done((f32[64,128]{1,0:T(8,128)S(1)}, f32[64,128]{1,0:T(8,128)S(1)}, u32[]{:S(2)}, u32[]{:S(2)}) %collective-permute-start.32) | collective-permute-done | bytes 32800 | tf_op jit(solution)/shard_map/ppermute | solution.py:226
  51.4 0.6 collective-permute-done.33.refs_3_
  52.4 0.6 collective-permute-start.37
  53.0 1.8 %collective-permute-start.36 = (f32[128,128]{1,0:T(8,128)S(1)}, f32[128,128]{1,0:T(8,128)S(1)}, u32[]{:S(2)}, u32[]{:S(2)}) collective-permute-start(f32[128,128]{1,0:T(8,128)S(1)} %get-tuple-element.122), channel_id=1, source_target_pairs={{0,28},{4,8},{8,4},{12,16},{16,12},{20,24},{24,20},{28,0},{1,29},{... | collective-permute-start | bytes 196616 | tf_op jit(solution)/shard_map/ppermute | solution.py:224
  54.8 1.4 %collective-permute-start.38 = (f32[64,128]{1,0:T(8,128)S(1)}, f32[64,128]{1,0:T(8,128)S(1)}, u32[]{:S(2)}, u32[]{:S(2)}) collective-permute-start(f32[64,128]{1,0:T(8,128)S(1)} %get-tuple-element.124), channel_id=1, source_target_pairs={{0,3},{1,2},{2,1},{3,0},{4,7},{5,6},{6,5},{7,4},{8,11},{9,10},{10,... | collective-permute-start | bytes 98312 | tf_op jit(solution)/shard_map/ppermute | solution.py:226
  56.2 1.4 %collective-permute-start.39 = (f32[64,128]{1,0:T(8,128)S(1)}, f32[64,128]{1,0:T(8,128)S(1)}, u32[]{:S(2)}, u32[]{:S(2)}) collective-permute-start(f32[64,128]{1,0:T(8,128)S(1)} %get-tuple-element.125), channel_id=1, source_target_pairs={{0,2},{1,3},{2,0},{3,1},{4,6},{5,7},{6,4},{7,5},{8,10},{9,11},{10,... | collective-permute-start | bytes 98312 | tf_op jit(solution)/shard_map/ppermute | solution.py:226
  57.6 0.5 collective-permute-start.41
  58.3 1.3 %collective-permute-done.38.refs_2_ = f32[64,128]{1,0:T(8,128)S(1)} collective-permute-done((f32[64,128]{1,0:T(8,128)S(1)}, f32[64,128]{1,0:T(8,128)S(1)}, u32[]{:S(2)}, u32[]{:S(2)}) %collective-permute-start.38) | collective-permute-done | bytes 32800 | tf_op jit(solution)/shard_map/ppermute | solution.py:226
  59.6 0.5 collective-permute-done.39.refs_3_
  60.5 1.5 %collective-permute-start.43 = (f32[64,128]{1,0:T(8,128)S(1)}, f32[64,128]{1,0:T(8,128)S(1)}, u32[]{:S(2)}, u32[]{:S(2)}) collective-permute-start(f32[64,128]{1,0:T(8,128)S(1)} %get-tuple-element.137), channel_id=1, source_target_pairs={{0,1},{1,0},{2,3},{3,2},{4,5},{5,4},{6,7},{7,6},{8,9},{9,8},{10,11... | collective-permute-start | bytes 98312 | tf_op jit(solution)/shard_map/ppermute | solution.py:226
  62.2 1.4 %collective-permute-start.44 = (f32[64,128]{1,0:T(8,128)S(1)}, f32[64,128]{1,0:T(8,128)S(1)}, u32[]{:S(2)}, u32[]{:S(2)}) collective-permute-start(f32[64,128]{1,0:T(8,128)S(1)} %get-tuple-element.138), channel_id=1, source_target_pairs={{0,3},{1,2},{2,1},{3,0},{4,7},{5,6},{6,5},{7,4},{8,11},{9,10},{10,... | collective-permute-start | bytes 98312 | tf_op jit(solution)/shard_map/ppermute | solution.py:226
  63.5 0.6 collective-permute-start.45
  64.7 0.9 %local7.1 = (f32[8,64,128]{2,1,0:T(8,128)S(1)}, f32[8,64,128]{2,1,0:T(8,128)}) custom-call(s32[40]{0:T(128)S(4)} %get-tuple-element.72.table, f32[8,64,128]{2,1,0:T(8,128)S(1)} %local6.1.resid, bf16[8,6,128,128]{3,2,1,0:T(8,128)(2,1)S(1)} %get-tuple-element.74.coupling, ...), custom_call_target="tpu_custom_call", output_to_operand_aliasing={{0}: (1, {})} | custom-call | tf_op jit(solution)/shard_map/local7/pallas_call | solution.py:213
  65.5 1.4 %collective-permute-done.44.refs_2_ = f32[64,128]{1,0:T(8,128)S(1)} collective-permute-done((f32[64,128]{1,0:T(8,128)S(1)}, f32[64,128]{1,0:T(8,128)S(1)}, u32[]{:S(2)}, u32[]{:S(2)}) %collective-permute-start.44) | collective-permute-done | bytes 32800 | tf_op jit(solution)/shard_map/ppermute | solution.py:226
  67.5 0.8 %final.1 = f32[8,64,128]{2,1,0:T(8,128)} custom-call(f32[8,64,128]{2,1,0:T(8,128)S(1)} %get-tuple-element.135.resid, f32[128,128]{1,0:T(8,128)S(1)} %collective-permute-done.42.refs_0_, f32[64,128]{1,0:T(8,128)S(1)} %collective-permute-done.43.refs_1_, f32[64,128]{1,0:T(8,128)S(1)} %collective-permute-done.44.refs_2_, ...), custom_call_target="tpu_custom_call" | custom-call | tf_op jit(solution)/shard_map/final/pallas_call | solution.py:213
  (65 shorter events, 7.9 us)
Async XLA Ops:
  2.5 7.8 %collective-permute-start.1 = (f32[72,128]{1,0:T(8,128)S(1)}, f32[72,128]{1,0:T(8,128)S(1)}, u32[]{:S(2)}, u32[]{:S(2)}) collective-permute-start(f32[72,128]{1,0:T(8,128)S(1)} %get-tuple-element.78), channel_id=1, source_target_pairs={{0,1},{1,0},{2,3},{3,2},{4,5},{5,4},{6,7},{7,6},{8,9},{9,8},{10,11... | collective-permute-start | bytes 110600 | tf_op jit(solution)/shard_map/ppermute | solution.py:226
  5.5 8.2 %collective-permute-start = (f32[136,128]{1,0:T(8,128)S(1)}, f32[136,128]{1,0:T(8,128)S(1)}, u32[]{:S(2)}, u32[]{:S(2)}) collective-permute-start(f32[136,128]{1,0:T(8,128)S(1)} %get-tuple-element.77), channel_id=1, source_target_pairs={{0,28},{4,8},{8,4},{12,16},{16,12},{20,24},{24,20},{28,0},{1,29},{... | collective-permute-start | bytes 208904 | tf_op jit(solution)/shard_map/ppermute | solution.py:224
  8.3 4.9 %collective-permute-start.2 = (f32[72,128]{1,0:T(8,128)S(1)}, f32[72,128]{1,0:T(8,128)S(1)}, u32[]{:S(2)}, u32[]{:S(2)}) collective-permute-start(f32[72,128]{1,0:T(8,128)S(1)} %get-tuple-element.79), channel_id=1, source_target_pairs={{0,3},{1,2},{2,1},{3,0},{4,7},{5,6},{6,5},{7,4},{8,11},{9,10},{10,... | collective-permute-start | bytes 110600 | tf_op jit(solution)/shard_map/ppermute | solution.py:226
  9.8 4.0 %collective-permute-start.3 = (f32[72,128]{1,0:T(8,128)S(1)}, f32[72,128]{1,0:T(8,128)S(1)}, u32[]{:S(2)}, u32[]{:S(2)}) collective-permute-start(f32[72,128]{1,0:T(8,128)S(1)} %get-tuple-element.80), channel_id=1, source_target_pairs={{0,2},{1,3},{2,0},{3,1},{4,6},{5,7},{6,4},{7,5},{8,10},{9,11},{10,... | collective-permute-start | bytes 110600 | tf_op jit(solution)/shard_map/ppermute | solution.py:226
  10.3 3.5 %collective-permute-start.4 = (f32[72,128]{1,0:T(8,128)S(1)}, f32[72,128]{1,0:T(8,128)S(1)}, u32[]{:S(2)}, u32[]{:S(2)}) collective-permute-start(f32[72,128]{1,0:T(8,128)S(1)} %get-tuple-element.81), channel_id=1, source_target_pairs={{0,4},{4,0},{8,12},{12,8},{16,20},{20,16},{24,28},{28,24},{1,5},{5... | collective-permute-start | bytes 110600 | tf_op jit(solution)/shard_map/ppermute | solution.py:227
  10.3 3.5 %collective-permute-start.5 = (f32[72,128]{1,0:T(8,128)S(1)}, f32[72,128]{1,0:T(8,128)S(1)}, u32[]{:S(2)}, u32[]{:S(2)}) collective-permute-start(f32[72,128]{1,0:T(8,128)S(1)} %get-tuple-element.82), channel_id=1, source_target_pairs={{0,4},{4,0},{8,12},{12,8},{16,20},{20,16},{24,28},{28,24},{1,5},{5... | collective-permute-start | bytes 110600 | tf_op jit(solution)/shard_map/ppermute | solution.py:227
  14.1 4.2 %collective-permute-start.7 = (f32[64,128]{1,0:T(8,128)S(1)}, f32[64,128]{1,0:T(8,128)S(1)}, u32[]{:S(2)}, u32[]{:S(2)}) collective-permute-start(f32[64,128]{1,0:T(8,128)S(1)} %get-tuple-element.85), channel_id=1, source_target_pairs={{0,1},{1,0},{2,3},{3,2},{4,5},{5,4},{6,7},{7,6},{8,9},{9,8},{10,11... | collective-permute-start | bytes 98312 | tf_op jit(solution)/shard_map/ppermute | solution.py:226
  15.6 5.5 %collective-permute-start.6 = (f32[128,128]{1,0:T(8,128)S(1)}, f32[128,128]{1,0:T(8,128)S(1)}, u32[]{:S(2)}, u32[]{:S(2)}) collective-permute-start(f32[128,128]{1,0:T(8,128)S(1)} %get-tuple-element.84), channel_id=1, source_target_pairs={{0,28},{4,8},{8,4},{12,16},{16,12},{20,24},{24,20},{28,0},{1,29},{... | collective-permute-start | bytes 196616 | tf_op jit(solution)/shard_map/ppermute | solution.py:224
  15.6 4.8 %collective-permute-start.8 = (f32[64,128]{1,0:T(8,128)S(1)}, f32[64,128]{1,0:T(8,128)S(1)}, u32[]{:S(2)}, u32[]{:S(2)}) collective-permute-start(f32[64,128]{1,0:T(8,128)S(1)} %get-tuple-element.86), channel_id=1, source_target_pairs={{0,3},{1,2},{2,1},{3,0},{4,7},{5,6},{6,5},{7,4},{8,11},{9,10},{10,... | collective-permute-start | bytes 98312 | tf_op jit(solution)/shard_map/ppermute | solution.py:226
  16.9 3.9 %collective-permute-start.9 = (f32[64,128]{1,0:T(8,128)S(1)}, f32[64,128]{1,0:T(8,128)S(1)}, u32[]{:S(2)}, u32[]{:S(2)}) collective-permute-start(f32[64,128]{1,0:T(8,128)S(1)} %get-tuple-element.87), channel_id=1, source_target_pairs={{0,2},{1,3},{2,0},{3,1},{4,6},{5,7},{6,4},{7,5},{8,10},{9,11},{10,... | collective-permute-start | bytes 98312 | tf_op jit(solution)/shard_map/ppermute | solution.py:226
  17.6 3.2 %collective-permute-start.10 = (f32[64,128]{1,0:T(8,128)S(1)}, f32[64,128]{1,0:T(8,128)S(1)}, u32[]{:S(2)}, u32[]{:S(2)}) collective-permute-start(f32[64,128]{1,0:T(8,128)S(1)} %get-tuple-element.88), channel_id=1, source_target_pairs={{0,4},{4,0},{8,12},{12,8},{16,20},{20,16},{24,28},{28,24},{1,5},{5... | collective-permute-start | bytes 98312 | tf_op jit(solution)/shard_map/ppermute | solution.py:227
  18.3 2.5 %collective-permute-start.11 = (f32[64,128]{1,0:T(8,128)S(1)}, f32[64,128]{1,0:T(8,128)S(1)}, u32[]{:S(2)}, u32[]{:S(2)}) collective-permute-start(f32[64,128]{1,0:T(8,128)S(1)} %get-tuple-element.89), channel_id=1, source_target_pairs={{0,4},{4,0},{8,12},{12,8},{16,20},{20,16},{24,28},{28,24},{1,5},{5... | collective-permute-start | bytes 98312 | tf_op jit(solution)/shard_map/ppermute | solution.py:227
  21.4 5.1 %collective-permute-start.13 = (f32[64,128]{1,0:T(8,128)S(1)}, f32[64,128]{1,0:T(8,128)S(1)}, u32[]{:S(2)}, u32[]{:S(2)}) collective-permute-start(f32[64,128]{1,0:T(8,128)S(1)} %get-tuple-element.92), channel_id=1, source_target_pairs={{0,1},{1,0},{2,3},{3,2},{4,5},{5,4},{6,7},{7,6},{8,9},{9,8},{10,11... | collective-permute-start | bytes 98312 | tf_op jit(solution)/shard_map/ppermute | solution.py:226
  22.0 7.2 %collective-permute-start.12 = (f32[128,128]{1,0:T(8,128)S(1)}, f32[128,128]{1,0:T(8,128)S(1)}, u32[]{:S(2)}, u32[]{:S(2)}) collective-permute-start(f32[128,128]{1,0:T(8,128)S(1)} %get-tuple-element.91), channel_id=1, source_target_pairs={{0,28},{4,8},{8,4},{12,16},{16,12},{20,24},{24,20},{28,0},{1,29},{... | collective-permute-start | bytes 196616 | tf_op jit(solution)/shard_map/ppermute | solution.py:224
  23.9 4.8 %collective-permute-start.14 = (f32[64,128]{1,0:T(8,128)S(1)}, f32[64,128]{1,0:T(8,128)S(1)}, u32[]{:S(2)}, u32[]{:S(2)}) collective-permute-start(f32[64,128]{1,0:T(8,128)S(1)} %get-tuple-element.93), channel_id=1, source_target_pairs={{0,3},{1,2},{2,1},{3,0},{4,7},{5,6},{6,5},{7,4},{8,11},{9,10},{10,... | collective-permute-start | bytes 98312 | tf_op jit(solution)/shard_map/ppermute | solution.py:226
  25.3 3.9 %collective-permute-start.15 = (f32[64,128]{1,0:T(8,128)S(1)}, f32[64,128]{1,0:T(8,128)S(1)}, u32[]{:S(2)}, u32[]{:S(2)}) collective-permute-start(f32[64,128]{1,0:T(8,128)S(1)} %get-tuple-element.94), channel_id=1, source_target_pairs={{0,2},{1,3},{2,0},{3,1},{4,6},{5,7},{6,4},{7,5},{8,10},{9,11},{10,... | collective-permute-start | bytes 98312 | tf_op jit(solution)/shard_map/ppermute | solution.py:226
  26.5 2.7 %collective-permute-start.16 = (f32[64,128]{1,0:T(8,128)S(1)}, f32[64,128]{1,0:T(8,128)S(1)}, u32[]{:S(2)}, u32[]{:S(2)}) collective-permute-start(f32[64,128]{1,0:T(8,128)S(1)} %get-tuple-element.95), channel_id=1, source_target_pairs={{0,4},{4,0},{8,12},{12,8},{16,20},{20,16},{24,28},{28,24},{1,5},{5... | collective-permute-start | bytes 98312 | tf_op jit(solution)/shard_map/ppermute | solution.py:227
  26.5 2.7 %collective-permute-start.17 = (f32[64,128]{1,0:T(8,128)S(1)}, f32[64,128]{1,0:T(8,128)S(1)}, u32[]{:S(2)}, u32[]{:S(2)}) collective-permute-start(f32[64,128]{1,0:T(8,128)S(1)} %get-tuple-element.96), channel_id=1, source_target_pairs={{0,4},{4,0},{8,12},{12,8},{16,20},{20,16},{24,28},{28,24},{1,5},{5... | collective-permute-start | bytes 98312 | tf_op jit(solution)/shard_map/ppermute | solution.py:227
  29.5 4.0 %collective-permute-start.19 = (f32[64,128]{1,0:T(8,128)S(1)}, f32[64,128]{1,0:T(8,128)S(1)}, u32[]{:S(2)}, u32[]{:S(2)}) collective-permute-start(f32[64,128]{1,0:T(8,128)S(1)} %get-tuple-element.99), channel_id=1, source_target_pairs={{0,1},{1,0},{2,3},{3,2},{4,5},{5,4},{6,7},{7,6},{8,9},{9,8},{10,11... | collective-permute-start | bytes 98312 | tf_op jit(solution)/shard_map/ppermute | solution.py:226
  31.0 5.5 %collective-permute-start.18 = (f32[128,128]{1,0:T(8,128)S(1)}, f32[128,128]{1,0:T(8,128)S(1)}, u32[]{:S(2)}, u32[]{:S(2)}) collective-permute-start(f32[128,128]{1,0:T(8,128)S(1)} %get-tuple-element.98), channel_id=1, source_target_pairs={{0,28},{4,8},{8,4},{12,16},{16,12},{20,24},{24,20},{28,0},{1,29},{... | collective-permute-start | bytes 196616 | tf_op jit(solution)/shard_map/ppermute | solution.py:224
  31.2 4.8 %collective-permute-start.20 = (f32[64,128]{1,0:T(8,128)S(1)}, f32[64,128]{1,0:T(8,128)S(1)}, u32[]{:S(2)}, u32[]{:S(2)}) collective-permute-start(f32[64,128]{1,0:T(8,128)S(1)} %get-tuple-element.100), channel_id=1, source_target_pairs={{0,3},{1,2},{2,1},{3,0},{4,7},{5,6},{6,5},{7,4},{8,11},{9,10},{10,... | collective-permute-start | bytes 98312 | tf_op jit(solution)/shard_map/ppermute | solution.py:226
  32.6 3.9 %collective-permute-start.21 = (f32[64,128]{1,0:T(8,128)S(1)}, f32[64,128]{1,0:T(8,128)S(1)}, u32[]{:S(2)}, u32[]{:S(2)}) collective-permute-start(f32[64,128]{1,0:T(8,128)S(1)} %get-tuple-element.101), channel_id=1, source_target_pairs={{0,2},{1,3},{2,0},{3,1},{4,6},{5,7},{6,4},{7,5},{8,10},{9,11},{10,... | collective-permute-start | bytes 98312 | tf_op jit(solution)/shard_map/ppermute | solution.py:226
  33.2 3.3 %collective-permute-start.22 = (f32[64,128]{1,0:T(8,128)S(1)}, f32[64,128]{1,0:T(8,128)S(1)}, u32[]{:S(2)}, u32[]{:S(2)}) collective-permute-start(f32[64,128]{1,0:T(8,128)S(1)} %get-tuple-element.102), channel_id=1, source_target_pairs={{0,4},{4,0},{8,12},{12,8},{16,20},{20,16},{24,28},{28,24},{1,5},{5... | collective-permute-start | bytes 98312 | tf_op jit(solution)/shard_map/ppermute | solution.py:227
  33.6 2.9 %collective-permute-start.23 = (f32[64,128]{1,0:T(8,128)S(1)}, f32[64,128]{1,0:T(8,128)S(1)}, u32[]{:S(2)}, u32[]{:S(2)}) collective-permute-start(f32[64,128]{1,0:T(8,128)S(1)} %get-tuple-element.103), channel_id=1, source_target_pairs={{0,4},{4,0},{8,12},{12,8},{16,20},{20,16},{24,28},{28,24},{1,5},{5... | collective-permute-start | bytes 98312 | tf_op jit(solution)/shard_map/ppermute | solution.py:227
  36.8 5.4 %collective-permute-start.25 = (f32[64,128]{1,0:T(8,128)S(1)}, f32[64,128]{1,0:T(8,128)S(1)}, u32[]{:S(2)}, u32[]{:S(2)}) collective-permute-start(f32[64,128]{1,0:T(8,128)S(1)} %get-tuple-element.107), channel_id=1, source_target_pairs={{0,1},{1,0},{2,3},{3,2},{4,5},{5,4},{6,7},{7,6},{8,9},{9,8},{10,11... | collective-permute-start | bytes 98312 | tf_op jit(solution)/shard_map/ppermute | solution.py:226
  37.5 7.2 %collective-permute-start.24 = (f32[128,128]{1,0:T(8,128)S(1)}, f32[128,128]{1,0:T(8,128)S(1)}, u32[]{:S(2)}, u32[]{:S(2)}) collective-permute-start(f32[128,128]{1,0:T(8,128)S(1)} %get-tuple-element.106), channel_id=1, source_target_pairs={{0,28},{4,8},{8,4},{12,16},{16,12},{20,24},{24,20},{28,0},{1,29},{... | collective-permute-start | bytes 196616 | tf_op jit(solution)/shard_map/ppermute | solution.py:224
  39.3 4.8 %collective-permute-start.26 = (f32[64,128]{1,0:T(8,128)S(1)}, f32[64,128]{1,0:T(8,128)S(1)}, u32[]{:S(2)}, u32[]{:S(2)}) collective-permute-start(f32[64,128]{1,0:T(8,128)S(1)} %get-tuple-element.108), channel_id=1, source_target_pairs={{0,3},{1,2},{2,1},{3,0},{4,7},{5,6},{6,5},{7,4},{8,11},{9,10},{10,... | collective-permute-start | bytes 98312 | tf_op jit(solution)/shard_map/ppermute | solution.py:226
  40.8 3.9 %collective-permute-start.27 = (f32[64,128]{1,0:T(8,128)S(1)}, f32[64,128]{1,0:T(8,128)S(1)}, u32[]{:S(2)}, u32[]{:S(2)}) collective-permute-start(f32[64,128]{1,0:T(8,128)S(1)} %get-tuple-element.109), channel_id=1, source_target_pairs={{0,2},{1,3},{2,0},{3,1},{4,6},{5,7},{6,4},{7,5},{8,10},{9,11},{10,... | collective-permute-start | bytes 98312 | tf_op jit(solution)/shard_map/ppermute | solution.py:226
  42.2 2.5 %collective-permute-start.28 = (f32[64,128]{1,0:T(8,128)S(1)}, f32[64,128]{1,0:T(8,128)S(1)}, u32[]{:S(2)}, u32[]{:S(2)}) collective-permute-start(f32[64,128]{1,0:T(8,128)S(1)} %get-tuple-element.110), channel_id=1, source_target_pairs={{0,4},{4,0},{8,12},{12,8},{16,20},{20,16},{24,28},{28,24},{1,5},{5... | collective-permute-start | bytes 98312 | tf_op jit(solution)/shard_map/ppermute | solution.py:227
  42.2 2.5 %collective-permute-start.29 = (f32[64,128]{1,0:T(8,128)S(1)}, f32[64,128]{1,0:T(8,128)S(1)}, u32[]{:S(2)}, u32[]{:S(2)}) collective-permute-start(f32[64,128]{1,0:T(8,128)S(1)} %get-tuple-element.111), channel_id=1, source_target_pairs={{0,4},{4,0},{8,12},{12,8},{16,20},{20,16},{24,28},{28,24},{1,5},{5... | collective-permute-start | bytes 98312 | tf_op jit(solution)/shard_map/ppermute | solution.py:227
  45.0 4.0 %collective-permute-start.31 = (f32[64,128]{1,0:T(8,128)S(1)}, f32[64,128]{1,0:T(8,128)S(1)}, u32[]{:S(2)}, u32[]{:S(2)}) collective-permute-start(f32[64,128]{1,0:T(8,128)S(1)} %get-tuple-element.115), channel_id=1, source_target_pairs={{0,1},{1,0},{2,3},{3,2},{4,5},{5,4},{6,7},{7,6},{8,9},{9,8},{10,11... | collective-permute-start | bytes 98312 | tf_op jit(solution)/shard_map/ppermute | solution.py:226
  46.5 5.6 %collective-permute-start.30 = (f32[128,128]{1,0:T(8,128)S(1)}, f32[128,128]{1,0:T(8,128)S(1)}, u32[]{:S(2)}, u32[]{:S(2)}) collective-permute-start(f32[128,128]{1,0:T(8,128)S(1)} %get-tuple-element.114), channel_id=1, source_target_pairs={{0,28},{4,8},{8,4},{12,16},{16,12},{20,24},{24,20},{28,0},{1,29},{... | collective-permute-start | bytes 196616 | tf_op jit(solution)/shard_map/ppermute | solution.py:224
  46.6 4.8 %collective-permute-start.32 = (f32[64,128]{1,0:T(8,128)S(1)}, f32[64,128]{1,0:T(8,128)S(1)}, u32[]{:S(2)}, u32[]{:S(2)}) collective-permute-start(f32[64,128]{1,0:T(8,128)S(1)} %get-tuple-element.116), channel_id=1, source_target_pairs={{0,3},{1,2},{2,1},{3,0},{4,7},{5,6},{6,5},{7,4},{8,11},{9,10},{10,... | collective-permute-start | bytes 98312 | tf_op jit(solution)/shard_map/ppermute | solution.py:226
  48.1 3.9 %collective-permute-start.33 = (f32[64,128]{1,0:T(8,128)S(1)}, f32[64,128]{1,0:T(8,128)S(1)}, u32[]{:S(2)}, u32[]{:S(2)}) collective-permute-start(f32[64,128]{1,0:T(8,128)S(1)} %get-tuple-element.117), channel_id=1, source_target_pairs={{0,2},{1,3},{2,0},{3,1},{4,6},{5,7},{6,4},{7,5},{8,10},{9,11},{10,... | collective-permute-start | bytes 98312 | tf_op jit(solution)/shard_map/ppermute | solution.py:226
  48.7 3.4 %collective-permute-start.34 = (f32[64,128]{1,0:T(8,128)S(1)}, f32[64,128]{1,0:T(8,128)S(1)}, u32[]{:S(2)}, u32[]{:S(2)}) collective-permute-start(f32[64,128]{1,0:T(8,128)S(1)} %get-tuple-element.118), channel_id=1, source_target_pairs={{0,4},{4,0},{8,12},{12,8},{16,20},{20,16},{24,28},{28,24},{1,5},{5... | collective-permute-start | bytes 98312 | tf_op jit(solution)/shard_map/ppermute | solution.py:227
  49.0 3.0 %collective-permute-start.35 = (f32[64,128]{1,0:T(8,128)S(1)}, f32[64,128]{1,0:T(8,128)S(1)}, u32[]{:S(2)}, u32[]{:S(2)}) collective-permute-start(f32[64,128]{1,0:T(8,128)S(1)} %get-tuple-element.119), channel_id=1, source_target_pairs={{0,4},{4,0},{8,12},{12,8},{16,20},{20,16},{24,28},{28,24},{1,5},{5... | collective-permute-start | bytes 98312 | tf_op jit(solution)/shard_map/ppermute | solution.py:227
  52.4 5.2 %collective-permute-start.37 = (f32[64,128]{1,0:T(8,128)S(1)}, f32[64,128]{1,0:T(8,128)S(1)}, u32[]{:S(2)}, u32[]{:S(2)}) collective-permute-start(f32[64,128]{1,0:T(8,128)S(1)} %get-tuple-element.123), channel_id=1, source_target_pairs={{0,1},{1,0},{2,3},{3,2},{4,5},{5,4},{6,7},{7,6},{8,9},{9,8},{10,11... | collective-permute-start | bytes 98312 | tf_op jit(solution)/shard_map/ppermute | solution.py:226
  53.0 7.2 %collective-permute-start.36 = (f32[128,128]{1,0:T(8,128)S(1)}, f32[128,128]{1,0:T(8,128)S(1)}, u32[]{:S(2)}, u32[]{:S(2)}) collective-permute-start(f32[128,128]{1,0:T(8,128)S(1)} %get-tuple-element.122), channel_id=1, source_target_pairs={{0,28},{4,8},{8,4},{12,16},{16,12},{20,24},{24,20},{28,0},{1,29},{... | collective-permute-start | bytes 196616 | tf_op jit(solution)/shard_map/ppermute | solution.py:224
  54.8 4.8 %collective-permute-start.38 = (f32[64,128]{1,0:T(8,128)S(1)}, f32[64,128]{1,0:T(8,128)S(1)}, u32[]{:S(2)}, u32[]{:S(2)}) collective-permute-start(f32[64,128]{1,0:T(8,128)S(1)} %get-tuple-element.124), channel_id=1, source_target_pairs={{0,3},{1,2},{2,1},{3,0},{4,7},{5,6},{6,5},{7,4},{8,11},{9,10},{10,... | collective-permute-start | bytes 98312 | tf_op jit(solution)/shard_map/ppermute | solution.py:226
  56.2 3.9 %collective-permute-start.39 = (f32[64,128]{1,0:T(8,128)S(1)}, f32[64,128]{1,0:T(8,128)S(1)}, u32[]{:S(2)}, u32[]{:S(2)}) collective-permute-start(f32[64,128]{1,0:T(8,128)S(1)} %get-tuple-element.125), channel_id=1, source_target_pairs={{0,2},{1,3},{2,0},{3,1},{4,6},{5,7},{6,4},{7,5},{8,10},{9,11},{10,... | collective-permute-start | bytes 98312 | tf_op jit(solution)/shard_map/ppermute | solution.py:226
  57.6 2.5 %collective-permute-start.40 = (f32[64,128]{1,0:T(8,128)S(1)}, f32[64,128]{1,0:T(8,128)S(1)}, u32[]{:S(2)}, u32[]{:S(2)}) collective-permute-start(f32[64,128]{1,0:T(8,128)S(1)} %get-tuple-element.126), channel_id=1, source_target_pairs={{0,4},{4,0},{8,12},{12,8},{16,20},{20,16},{24,28},{28,24},{1,5},{5... | collective-permute-start | bytes 98312 | tf_op jit(solution)/shard_map/ppermute | solution.py:227
  57.6 2.5 %collective-permute-start.41 = (f32[64,128]{1,0:T(8,128)S(1)}, f32[64,128]{1,0:T(8,128)S(1)}, u32[]{:S(2)}, u32[]{:S(2)}) collective-permute-start(f32[64,128]{1,0:T(8,128)S(1)} %get-tuple-element.127), channel_id=1, source_target_pairs={{0,4},{4,0},{8,12},{12,8},{16,20},{20,16},{24,28},{28,24},{1,5},{5... | collective-permute-start | bytes 98312 | tf_op jit(solution)/shard_map/ppermute | solution.py:227
  60.5 4.0 %collective-permute-start.43 = (f32[64,128]{1,0:T(8,128)S(1)}, f32[64,128]{1,0:T(8,128)S(1)}, u32[]{:S(2)}, u32[]{:S(2)}) collective-permute-start(f32[64,128]{1,0:T(8,128)S(1)} %get-tuple-element.137), channel_id=1, source_target_pairs={{0,1},{1,0},{2,3},{3,2},{4,5},{5,4},{6,7},{7,6},{8,9},{9,8},{10,11... | collective-permute-start | bytes 98312 | tf_op jit(solution)/shard_map/ppermute | solution.py:226
  62.0 5.5 %collective-permute-start.42 = (f32[128,128]{1,0:T(8,128)S(1)}, f32[128,128]{1,0:T(8,128)S(1)}, u32[]{:S(2)}, u32[]{:S(2)}) collective-permute-start(f32[128,128]{1,0:T(8,128)S(1)} %get-tuple-element.136), channel_id=1, source_target_pairs={{0,28},{4,8},{8,4},{12,16},{16,12},{20,24},{24,20},{28,0},{1,29},{... | collective-permute-start | bytes 196616 | tf_op jit(solution)/shard_map/ppermute | solution.py:224
  62.2 4.8 %collective-permute-start.44 = (f32[64,128]{1,0:T(8,128)S(1)}, f32[64,128]{1,0:T(8,128)S(1)}, u32[]{:S(2)}, u32[]{:S(2)}) collective-permute-start(f32[64,128]{1,0:T(8,128)S(1)} %get-tuple-element.138), channel_id=1, source_target_pairs={{0,3},{1,2},{2,1},{3,0},{4,7},{5,6},{6,5},{7,4},{8,11},{9,10},{10,... | collective-permute-start | bytes 98312 | tf_op jit(solution)/shard_map/ppermute | solution.py:226
  63.5 3.9 %collective-permute-start.45 = (f32[64,128]{1,0:T(8,128)S(1)}, f32[64,128]{1,0:T(8,128)S(1)}, u32[]{:S(2)}, u32[]{:S(2)}) collective-permute-start(f32[64,128]{1,0:T(8,128)S(1)} %get-tuple-element.139), channel_id=1, source_target_pairs={{0,2},{1,3},{2,0},{3,1},{4,6},{5,7},{6,4},{7,5},{8,10},{9,11},{10,... | collective-permute-start | bytes 98312 | tf_op jit(solution)/shard_map/ppermute | solution.py:226
  64.2 3.3 %collective-permute-start.46 = (f32[64,128]{1,0:T(8,128)S(1)}, f32[64,128]{1,0:T(8,128)S(1)}, u32[]{:S(2)}, u32[]{:S(2)}) collective-permute-start(f32[64,128]{1,0:T(8,128)S(1)} %get-tuple-element.140), channel_id=1, source_target_pairs={{0,4},{4,0},{8,12},{12,8},{16,20},{20,16},{24,28},{28,24},{1,5},{5... | collective-permute-start | bytes 98312 | tf_op jit(solution)/shard_map/ppermute | solution.py:227
  64.5 3.0 %collective-permute-start.47 = (f32[64,128]{1,0:T(8,128)S(1)}, f32[64,128]{1,0:T(8,128)S(1)}, u32[]{:S(2)}, u32[]{:S(2)}) collective-permute-start(f32[64,128]{1,0:T(8,128)S(1)} %get-tuple-element.141), channel_id=1, source_target_pairs={{0,4},{4,0},{8,12},{12,8},{16,20},{20,16},{24,28},{28,24},{1,5},{5... | collective-permute-start | bytes 98312 | tf_op jit(solution)/shard_map/ppermute | solution.py:227

commit v8 on v7

--- a/solution.py
+++ b/solution.py
@@ -89,8 +89,11 @@
     color, local_target, group_peer, group_list, dom_target = scratch[:5]
     sems = scratch[5]
     targets = (color, group_peer, group_list, dom_target, local_target, rhs, diag, coupling)
+    pieces = list(zip(hbm[:5], targets[:5]))
+    for src, dst in zip(hbm[5:], targets[5:]):
+        pieces += [(src.at[r], dst.at[r]) for r in range(plan.rows)]
     copies = [
-        pltpu.make_async_copy(src, dst, sems.at[i]) for i, (src, dst) in enumerate(zip(hbm, targets))
+        pltpu.make_async_copy(src, dst, sems.at[i]) for i, (src, dst) in enumerate(pieces)
     ]
     for copy in copies:
         copy.start()
@@ -108,8 +111,8 @@
         for k in range(2):
             table[plan.local + 2 * at + k] = local_target[k, i]
             table[plan.slot + 2 * at + k] = me ^ group_peer[k, i]
-    copies[5].wait()
-    copies[6].wait()
+    for copy in copies[5 : 5 + 2 * plan.rows]:
+        copy.wait()
     changes = []
     for p in range(plan.quarter):
         j = table[plan.order + p]
@@ -117,7 +120,8 @@
         sol[p] = new
         changes.append(new.astype(jnp.bfloat16))
         change[p] = changes[p]
-    copies[7].wait()
+    for copy in copies[5 + 2 * plan.rows :]:
+        copy.wait()
     products(plan, 0, table, changes, coupling, sends)
     line = lax.broadcasted_iota(jnp.int32, (META, plan.w), 0)
     for lane, s in enumerate(plan.distances):
@@ -247,7 +251,7 @@
         ]
         + plan.types(0),
         scratch_shapes=[pltpu.SMEM(shape, jnp.int32) for shape in table_scratch]
-        + [pltpu.SemaphoreType.DMA((len(hbm),))],
+        + [pltpu.SemaphoreType.DMA((5 + 3 * rows,))],
     )
     sols = [sol]
     got = meta = None

time: 68.5 us -> 68.7 us (level)
  no operation moved by 1% of the time
where the time goes in v8:
time: 68.7 us; the launch traced here: 68.6 us
  starting transfers between devices  40.6 us (59%)
  waiting for transfers between devices  19.7 us (29%)
  Pallas kernels  7.41 us (11%)
  between operations  0.81 us (1%)
    ppermute x24, starting transfers between devices, exchange(): got.append(lax.ppermute(send, 'sub', [(i, i ^ s) for i in range(group)]))  29.4 us
    ppermute x24, waiting for transfers between devices, exchange(): got.append(lax.ppermute(send, 'sub', [(i, i ^ s) for i in range(group)]))  19.3 us
    ppermute x8, starting transfers between devices, exchange(): got = [lax.ppermute(sends[0], 'dom', far_pairs)]  8.64 us
    pallas_call x17, Pallas kernels, call(): pl.pallas_call(body, name=name, in_specs=in_specs + [VMEM] * (len(ins) -...  7.41 us
    ppermute x16, starting transfers between devices, exchange(): lax.ppermute(send, 'dom', near_pairs)  2.6 us
  transfers between devices with their start and end apart: 48, of which 21 were waited for; matrix products, arithmetic and copies ran while one was open for 0% of the time, Pallas kernels for 3%

profile of v8, /device:TPU:0, one launch (start us, length us, event | category | flops | bytes accessed | tf_op | source)
XLA Modules:
  0.0 68.6 jit_solution(17133594238478172832)
XLA Ops:
  0.6 2.1 %first.1 = (s32[40]{0:T(128)S(4)}, bf16[8,6,128,128]{3,2,1,0:T(8,128)(2,1)S(1)}, bf16[8,128,128]{2,1,0:T(8,128)(2,1)S(1)}, f32[8,64,128]{2,1,0:T(8,128)S(1)}, f3...) custom-call(s32[8]{0:T(128)} %refs_0_.1, ...), custom_call_target="tpu_custom_call" | custom-call | tf_op jit(solution)/shard_map/first/pallas_call | solution.py:217
  2.7 3.0 %collective-permute-start.1 = (f32[72,128]{1,0:T(8,128)S(1)}, f32[72,128]{1,0:T(8,128)S(1)}, u32[]{:S(2)}, u32[]{:S(2)}) collective-permute-start(f32[72,128]{1,0:T(8,128)S(1)} %get-tuple-element.78), channel_id=1, source_target_pairs={{0,1},{1,0},{2,3},{3,2},{4,5},{5,4},{6,7},{7,6},{8,9},{9,8},{10,11... | collective-permute-start | bytes 110600 | tf_op jit(solution)/shard_map/ppermute | solution.py:230
  5.8 2.8 %collective-permute-start = (f32[136,128]{1,0:T(8,128)S(1)}, f32[136,128]{1,0:T(8,128)S(1)}, u32[]{:S(2)}, u32[]{:S(2)}) collective-permute-start(f32[136,128]{1,0:T(8,128)S(1)} %get-tuple-element.77), channel_id=1, source_target_pairs={{0,28},{4,8},{8,4},{12,16},{16,12},{20,24},{24,20},{28,0},{1,29},{... | collective-permute-start | bytes 208904 | tf_op jit(solution)/shard_map/ppermute | solution.py:228
  8.5 1.5 %collective-permute-start.2 = (f32[72,128]{1,0:T(8,128)S(1)}, f32[72,128]{1,0:T(8,128)S(1)}, u32[]{:S(2)}, u32[]{:S(2)}) collective-permute-start(f32[72,128]{1,0:T(8,128)S(1)} %get-tuple-element.79), channel_id=1, source_target_pairs={{0,3},{1,2},{2,1},{3,0},{4,7},{5,6},{6,5},{7,4},{8,11},{9,10},{10,... | collective-permute-start | bytes 110600 | tf_op jit(solution)/shard_map/ppermute | solution.py:230
  10.5 0.5 collective-permute-start.5
  11.2 2.2 %collective-permute-done.2.refs_2_.refs_8_ = f32[72,128]{1,0:T(8,128)S(1)} collective-permute-done((f32[72,128]{1,0:T(8,128)S(1)}, f32[72,128]{1,0:T(8,128)S(1)}, u32[]{:S(2)}, u32[]{:S(2)}) %collective-permute-start.2) | collective-permute-done | bytes 36896 | tf_op jit(solution)/shard_map/ppermute | solution.py:230
  13.4 0.6 collective-permute-done.3.refs_3_.refs_9_
  14.3 1.6 %collective-permute-start.7 = (f32[64,128]{1,0:T(8,128)S(1)}, f32[64,128]{1,0:T(8,128)S(1)}, u32[]{:S(2)}, u32[]{:S(2)}) collective-permute-start(f32[64,128]{1,0:T(8,128)S(1)} %get-tuple-element.85), channel_id=1, source_target_pairs={{0,1},{1,0},{2,3},{3,2},{4,5},{5,4},{6,7},{7,6},{8,9},{9,8},{10,11... | collective-permute-start | bytes 98312 | tf_op jit(solution)/shard_map/ppermute | solution.py:230
  15.9 1.3 %collective-permute-start.8 = (f32[64,128]{1,0:T(8,128)S(1)}, f32[64,128]{1,0:T(8,128)S(1)}, u32[]{:S(2)}, u32[]{:S(2)}) collective-permute-start(f32[64,128]{1,0:T(8,128)S(1)} %get-tuple-element.86), channel_id=1, source_target_pairs={{0,3},{1,2},{2,1},{3,0},{4,7},{5,6},{6,5},{7,4},{8,11},{9,10},{10,... | collective-permute-start | bytes 98312 | tf_op jit(solution)/shard_map/ppermute | solution.py:230
  17.1 0.7 %collective-permute-start.9 = (f32[64,128]{1,0:T(8,128)S(1)}, f32[64,128]{1,0:T(8,128)S(1)}, u32[]{:S(2)}, u32[]{:S(2)}) collective-permute-start(f32[64,128]{1,0:T(8,128)S(1)} %get-tuple-element.87), channel_id=1, source_target_pairs={{0,2},{1,3},{2,0},{3,1},{4,6},{5,7},{6,4},{7,5},{8,10},{9,11},{10,... | collective-permute-start | bytes 98312 | tf_op jit(solution)/shard_map/ppermute | solution.py:230
  17.9 0.7 collective-permute-done.7.refs_1_
  18.8 1.9 %collective-permute-done.8.refs_2_ = f32[64,128]{1,0:T(8,128)S(1)} collective-permute-done((f32[64,128]{1,0:T(8,128)S(1)}, f32[64,128]{1,0:T(8,128)S(1)}, u32[]{:S(2)}, u32[]{:S(2)}) %collective-permute-start.8) | collective-permute-done | bytes 32800 | tf_op jit(solution)/shard_map/ppermute | solution.py:230
  21.7 0.6 collective-permute-start.13
  22.3 1.8 %collective-permute-start.12 = (f32[128,128]{1,0:T(8,128)S(1)}, f32[128,128]{1,0:T(8,128)S(1)}, u32[]{:S(2)}, u32[]{:S(2)}) collective-permute-start(f32[128,128]{1,0:T(8,128)S(1)} %get-tuple-element.91), channel_id=1, source_target_pairs={{0,28},{4,8},{8,4},{12,16},{16,12},{20,24},{24,20},{28,0},{1,29},{... | collective-permute-start | bytes 196616 | tf_op jit(solution)/shard_map/ppermute | solution.py:228
  24.1 1.4 %collective-permute-start.14 = (f32[64,128]{1,0:T(8,128)S(1)}, f32[64,128]{1,0:T(8,128)S(1)}, u32[]{:S(2)}, u32[]{:S(2)}) collective-permute-start(f32[64,128]{1,0:T(8,128)S(1)} %get-tuple-element.93), channel_id=1, source_target_pairs={{0,3},{1,2},{2,1},{3,0},{4,7},{5,6},{6,5},{7,4},{8,11},{9,10},{10,... | collective-permute-start | bytes 98312 | tf_op jit(solution)/shard_map/ppermute | solution.py:230
  25.5 1.3 %collective-permute-start.15 = (f32[64,128]{1,0:T(8,128)S(1)}, f32[64,128]{1,0:T(8,128)S(1)}, u32[]{:S(2)}, u32[]{:S(2)}) collective-permute-start(f32[64,128]{1,0:T(8,128)S(1)} %get-tuple-element.94), channel_id=1, source_target_pairs={{0,2},{1,3},{2,0},{3,1},{4,6},{5,7},{6,4},{7,5},{8,10},{9,11},{10,... | collective-permute-start | bytes 98312 | tf_op jit(solution)/shard_map/ppermute | solution.py:230
  26.8 0.5 collective-permute-start.17
  27.5 1.4 %collective-permute-done.14.refs_2_ = f32[64,128]{1,0:T(8,128)S(1)} collective-permute-done((f32[64,128]{1,0:T(8,128)S(1)}, f32[64,128]{1,0:T(8,128)S(1)}, u32[]{:S(2)}, u32[]{:S(2)}) %collective-permute-start.14) | collective-permute-done | bytes 32800 | tf_op jit(solution)/shard_map/ppermute | solution.py:230
  28.9 0.5 collective-permute-done.15.refs_3_
  29.8 1.5 %collective-permute-start.19 = (f32[64,128]{1,0:T(8,128)S(1)}, f32[64,128]{1,0:T(8,128)S(1)}, u32[]{:S(2)}, u32[]{:S(2)}) collective-permute-start(f32[64,128]{1,0:T(8,128)S(1)} %get-tuple-element.99), channel_id=1, source_target_pairs={{0,1},{1,0},{2,3},{3,2},{4,5},{5,4},{6,7},{7,6},{8,9},{9,8},{10,11... | collective-permute-start | bytes 98312 | tf_op jit(solution)/shard_map/ppermute | solution.py:230
  31.4 1.4 %collective-permute-start.20 = (f32[64,128]{1,0:T(8,128)S(1)}, f32[64,128]{1,0:T(8,128)S(1)}, u32[]{:S(2)}, u32[]{:S(2)}) collective-permute-start(f32[64,128]{1,0:T(8,128)S(1)} %get-tuple-element.100), channel_id=1, source_target_pairs={{0,3},{1,2},{2,1},{3,0},{4,7},{5,6},{6,5},{7,4},{8,11},{9,10},{10,... | collective-permute-start | bytes 98312 | tf_op jit(solution)/shard_map/ppermute | solution.py:230
  32.8 0.6 collective-permute-start.21
  34.2 2.1 %collective-permute-done.20.refs_2_ = f32[64,128]{1,0:T(8,128)S(1)} collective-permute-done((f32[64,128]{1,0:T(8,128)S(1)}, f32[64,128]{1,0:T(8,128)S(1)}, u32[]{:S(2)}, u32[]{:S(2)}) %collective-permute-start.20) | collective-permute-done | bytes 32800 | tf_op jit(solution)/shard_map/ppermute | solution.py:230
  37.1 0.7 collective-permute-start.25
  37.7 1.8 %collective-permute-start.24 = (f32[128,128]{1,0:T(8,128)S(1)}, f32[128,128]{1,0:T(8,128)S(1)}, u32[]{:S(2)}, u32[]{:S(2)}) collective-permute-start(f32[128,128]{1,0:T(8,128)S(1)} %get-tuple-element.106), channel_id=1, source_target_pairs={{0,28},{4,8},{8,4},{12,16},{16,12},{20,24},{24,20},{28,0},{1,29},{... | collective-permute-start | bytes 196616 | tf_op jit(solution)/shard_map/ppermute | solution.py:228
  39.5 1.5 %collective-permute-start.26 = (f32[64,128]{1,0:T(8,128)S(1)}, f32[64,128]{1,0:T(8,128)S(1)}, u32[]{:S(2)}, u32[]{:S(2)}) collective-permute-start(f32[64,128]{1,0:T(8,128)S(1)} %get-tuple-element.108), channel_id=1, source_target_pairs={{0,3},{1,2},{2,1},{3,0},{4,7},{5,6},{6,5},{7,4},{8,11},{9,10},{10,... | collective-permute-start | bytes 98312 | tf_op jit(solution)/shard_map/ppermute | solution.py:230
  41.0 1.4 %collective-permute-start.27 = (f32[64,128]{1,0:T(8,128)S(1)}, f32[64,128]{1,0:T(8,128)S(1)}, u32[]{:S(2)}, u32[]{:S(2)}) collective-permute-start(f32[64,128]{1,0:T(8,128)S(1)} %get-tuple-element.109), channel_id=1, source_target_pairs={{0,2},{1,3},{2,0},{3,1},{4,6},{5,7},{6,4},{7,5},{8,10},{9,11},{10,... | collective-permute-start | bytes 98312 | tf_op jit(solution)/shard_map/ppermute | solution.py:230
  42.4 0.5 collective-permute-start.29
  43.2 1.2 %collective-permute-done.26.refs_2_ = f32[64,128]{1,0:T(8,128)S(1)} collective-permute-done((f32[64,128]{1,0:T(8,128)S(1)}, f32[64,128]{1,0:T(8,128)S(1)}, u32[]{:S(2)}, u32[]{:S(2)}) %collective-permute-start.26) | collective-permute-done | bytes 32800 | tf_op jit(solution)/shard_map/ppermute | solution.py:230
  44.3 0.6 collective-permute-done.27.refs_3_
  45.3 1.4 %collective-permute-start.31 = (f32[64,128]{1,0:T(8,128)S(1)}, f32[64,128]{1,0:T(8,128)S(1)}, u32[]{:S(2)}, u32[]{:S(2)}) collective-permute-start(f32[64,128]{1,0:T(8,128)S(1)} %get-tuple-element.115), channel_id=1, source_target_pairs={{0,1},{1,0},{2,3},{3,2},{4,5},{5,4},{6,7},{7,6},{8,9},{9,8},{10,11... | collective-permute-start | bytes 98312 | tf_op jit(solution)/shard_map/ppermute | solution.py:230
  46.8 1.5 %collective-permute-start.32 = (f32[64,128]{1,0:T(8,128)S(1)}, f32[64,128]{1,0:T(8,128)S(1)}, u32[]{:S(2)}, u32[]{:S(2)}) collective-permute-start(f32[64,128]{1,0:T(8,128)S(1)} %get-tuple-element.116), channel_id=1, source_target_pairs={{0,3},{1,2},{2,1},{3,0},{4,7},{5,6},{6,5},{7,4},{8,11},{9,10},{10,... | collective-permute-start | bytes 98312 | tf_op jit(solution)/shard_map/ppermute | solution.py:230
  48.4 0.5 collective-permute-start.33
  49.6 2.0 %collective-permute-done.32.refs_2_ = f32[64,128]{1,0:T(8,128)S(1)} collective-permute-done((f32[64,128]{1,0:T(8,128)S(1)}, f32[64,128]{1,0:T(8,128)S(1)}, u32[]{:S(2)}, u32[]{:S(2)}) %collective-permute-start.32) | collective-permute-done | bytes 32800 | tf_op jit(solution)/shard_map/ppermute | solution.py:230
  51.7 0.6 collective-permute-done.33.refs_3_
  52.6 0.6 collective-permute-start.37
  53.2 1.8 %collective-permute-start.36 = (f32[128,128]{1,0:T(8,128)S(1)}, f32[128,128]{1,0:T(8,128)S(1)}, u32[]{:S(2)}, u32[]{:S(2)}) collective-permute-start(f32[128,128]{1,0:T(8,128)S(1)} %get-tuple-element.122), channel_id=1, source_target_pairs={{0,28},{4,8},{8,4},{12,16},{16,12},{20,24},{24,20},{28,0},{1,29},{... | collective-permute-start | bytes 196616 | tf_op jit(solution)/shard_map/ppermute | solution.py:228
  55.0 1.4 %collective-permute-start.38 = (f32[64,128]{1,0:T(8,128)S(1)}, f32[64,128]{1,0:T(8,128)S(1)}, u32[]{:S(2)}, u32[]{:S(2)}) collective-permute-start(f32[64,128]{1,0:T(8,128)S(1)} %get-tuple-element.124), channel_id=1, source_target_pairs={{0,3},{1,2},{2,1},{3,0},{4,7},{5,6},{6,5},{7,4},{8,11},{9,10},{10,... | collective-permute-start | bytes 98312 | tf_op jit(solution)/shard_map/ppermute | solution.py:230
  56.5 1.4 %collective-permute-start.39 = (f32[64,128]{1,0:T(8,128)S(1)}, f32[64,128]{1,0:T(8,128)S(1)}, u32[]{:S(2)}, u32[]{:S(2)}) collective-permute-start(f32[64,128]{1,0:T(8,128)S(1)} %get-tuple-element.125), channel_id=1, source_target_pairs={{0,2},{1,3},{2,0},{3,1},{4,6},{5,7},{6,4},{7,5},{8,10},{9,11},{10,... | collective-permute-start | bytes 98312 | tf_op jit(solution)/shard_map/ppermute | solution.py:230
  57.9 0.5 collective-permute-start.41
  58.6 1.3 %collective-permute-done.38.refs_2_ = f32[64,128]{1,0:T(8,128)S(1)} collective-permute-done((f32[64,128]{1,0:T(8,128)S(1)}, f32[64,128]{1,0:T(8,128)S(1)}, u32[]{:S(2)}, u32[]{:S(2)}) %collective-permute-start.38) | collective-permute-done | bytes 32800 | tf_op jit(solution)/shard_map/ppermute | solution.py:230
  59.9 0.5 collective-permute-done.39.refs_3_
  60.7 1.5 %collective-permute-start.43 = (f32[64,128]{1,0:T(8,128)S(1)}, f32[64,128]{1,0:T(8,128)S(1)}, u32[]{:S(2)}, u32[]{:S(2)}) collective-permute-start(f32[64,128]{1,0:T(8,128)S(1)} %get-tuple-element.137), channel_id=1, source_target_pairs={{0,1},{1,0},{2,3},{3,2},{4,5},{5,4},{6,7},{7,6},{8,9},{9,8},{10,11... | collective-permute-start | bytes 98312 | tf_op jit(solution)/shard_map/ppermute | solution.py:230
  62.4 1.4 %collective-permute-start.44 = (f32[64,128]{1,0:T(8,128)S(1)}, f32[64,128]{1,0:T(8,128)S(1)}, u32[]{:S(2)}, u32[]{:S(2)}) collective-permute-start(f32[64,128]{1,0:T(8,128)S(1)} %get-tuple-element.138), channel_id=1, source_target_pairs={{0,3},{1,2},{2,1},{3,0},{4,7},{5,6},{6,5},{7,4},{8,11},{9,10},{10,... | collective-permute-start | bytes 98312 | tf_op jit(solution)/shard_map/ppermute | solution.py:230
  63.8 0.6 collective-permute-start.45
  64.9 0.9 %local7.1 = (f32[8,64,128]{2,1,0:T(8,128)S(1)}, f32[8,64,128]{2,1,0:T(8,128)}) custom-call(s32[40]{0:T(128)S(4)} %get-tuple-element.72.table, f32[8,64,128]{2,1,0:T(8,128)S(1)} %local6.1.resid, bf16[8,6,128,128]{3,2,1,0:T(8,128)(2,1)S(1)} %get-tuple-element.74.coupling, ...), custom_call_target="tpu_custom_call", output_to_operand_aliasing={{0}: (1, {})} | custom-call | tf_op jit(solution)/shard_map/local7/pallas_call | solution.py:217
  65.8 1.4 %collective-permute-done.44.refs_2_ = f32[64,128]{1,0:T(8,128)S(1)} collective-permute-done((f32[64,128]{1,0:T(8,128)S(1)}, f32[64,128]{1,0:T(8,128)S(1)}, u32[]{:S(2)}, u32[]{:S(2)}) %collective-permute-start.44) | collective-permute-done | bytes 32800 | tf_op jit(solution)/shard_map/ppermute | solution.py:230
  67.7 0.8 %final.1 = f32[8,64,128]{2,1,0:T(8,128)} custom-call(f32[8,64,128]{2,1,0:T(8,128)S(1)} %get-tuple-element.135.resid, f32[128,128]{1,0:T(8,128)S(1)} %collective-permute-done.42.refs_0_, f32[64,128]{1,0:T(8,128)S(1)} %collective-permute-done.43.refs_1_, f32[64,128]{1,0:T(8,128)S(1)} %collective-permute-done.44.refs_2_, ...), custom_call_target="tpu_custom_call" | custom-call | tf_op jit(solution)/shard_map/final/pallas_call | solution.py:217
  (65 shorter events, 7.9 us)
Async XLA Ops:
  2.7 7.8 %collective-permute-start.1 = (f32[72,128]{1,0:T(8,128)S(1)}, f32[72,128]{1,0:T(8,128)S(1)}, u32[]{:S(2)}, u32[]{:S(2)}) collective-permute-start(f32[72,128]{1,0:T(8,128)S(1)} %get-tuple-element.78), channel_id=1, source_target_pairs={{0,1},{1,0},{2,3},{3,2},{4,5},{5,4},{6,7},{7,6},{8,9},{9,8},{10,11... | collective-permute-start | bytes 110600 | tf_op jit(solution)/shard_map/ppermute | solution.py:230
  5.8 8.2 %collective-permute-start = (f32[136,128]{1,0:T(8,128)S(1)}, f32[136,128]{1,0:T(8,128)S(1)}, u32[]{:S(2)}, u32[]{:S(2)}) collective-permute-start(f32[136,128]{1,0:T(8,128)S(1)} %get-tuple-element.77), channel_id=1, source_target_pairs={{0,28},{4,8},{8,4},{12,16},{16,12},{20,24},{24,20},{28,0},{1,29},{... | collective-permute-start | bytes 208904 | tf_op jit(solution)/shard_map/ppermute | solution.py:228
  8.5 4.9 %collective-permute-start.2 = (f32[72,128]{1,0:T(8,128)S(1)}, f32[72,128]{1,0:T(8,128)S(1)}, u32[]{:S(2)}, u32[]{:S(2)}) collective-permute-start(f32[72,128]{1,0:T(8,128)S(1)} %get-tuple-element.79), channel_id=1, source_target_pairs={{0,3},{1,2},{2,1},{3,0},{4,7},{5,6},{6,5},{7,4},{8,11},{9,10},{10,... | collective-permute-start | bytes 110600 | tf_op jit(solution)/shard_map/ppermute | solution.py:230
  10.0 4.0 %collective-permute-start.3 = (f32[72,128]{1,0:T(8,128)S(1)}, f32[72,128]{1,0:T(8,128)S(1)}, u32[]{:S(2)}, u32[]{:S(2)}) collective-permute-start(f32[72,128]{1,0:T(8,128)S(1)} %get-tuple-element.80), channel_id=1, source_target_pairs={{0,2},{1,3},{2,0},{3,1},{4,6},{5,7},{6,4},{7,5},{8,10},{9,11},{10,... | collective-permute-start | bytes 110600 | tf_op jit(solution)/shard_map/ppermute | solution.py:230
  10.5 3.5 %collective-permute-start.4 = (f32[72,128]{1,0:T(8,128)S(1)}, f32[72,128]{1,0:T(8,128)S(1)}, u32[]{:S(2)}, u32[]{:S(2)}) collective-permute-start(f32[72,128]{1,0:T(8,128)S(1)} %get-tuple-element.81), channel_id=1, source_target_pairs={{0,4},{4,0},{8,12},{12,8},{16,20},{20,16},{24,28},{28,24},{1,5},{5... | collective-permute-start | bytes 110600 | tf_op jit(solution)/shard_map/ppermute | solution.py:231
  10.5 3.5 %collective-permute-start.5 = (f32[72,128]{1,0:T(8,128)S(1)}, f32[72,128]{1,0:T(8,128)S(1)}, u32[]{:S(2)}, u32[]{:S(2)}) collective-permute-start(f32[72,128]{1,0:T(8,128)S(1)} %get-tuple-element.82), channel_id=1, source_target_pairs={{0,4},{4,0},{8,12},{12,8},{16,20},{20,16},{24,28},{28,24},{1,5},{5... | collective-permute-start | bytes 110600 | tf_op jit(solution)/shard_map/ppermute | solution.py:231
  14.3 4.2 %collective-permute-start.7 = (f32[64,128]{1,0:T(8,128)S(1)}, f32[64,128]{1,0:T(8,128)S(1)}, u32[]{:S(2)}, u32[]{:S(2)}) collective-permute-start(f32[64,128]{1,0:T(8,128)S(1)} %get-tuple-element.85), channel_id=1, source_target_pairs={{0,1},{1,0},{2,3},{3,2},{4,5},{5,4},{6,7},{7,6},{8,9},{9,8},{10,11... | collective-permute-start | bytes 98312 | tf_op jit(solution)/shard_map/ppermute | solution.py:230
  15.9 5.5 %collective-permute-start.6 = (f32[128,128]{1,0:T(8,128)S(1)}, f32[128,128]{1,0:T(8,128)S(1)}, u32[]{:S(2)}, u32[]{:S(2)}) collective-permute-start(f32[128,128]{1,0:T(8,128)S(1)} %get-tuple-element.84), channel_id=1, source_target_pairs={{0,28},{4,8},{8,4},{12,16},{16,12},{20,24},{24,20},{28,0},{1,29},{... | collective-permute-start | bytes 196616 | tf_op jit(solution)/shard_map/ppermute | solution.py:228
  15.9 4.8 %collective-permute-start.8 = (f32[64,128]{1,0:T(8,128)S(1)}, f32[64,128]{1,0:T(8,128)S(1)}, u32[]{:S(2)}, u32[]{:S(2)}) collective-permute-start(f32[64,128]{1,0:T(8,128)S(1)} %get-tuple-element.86), channel_id=1, source_target_pairs={{0,3},{1,2},{2,1},{3,0},{4,7},{5,6},{6,5},{7,4},{8,11},{9,10},{10,... | collective-permute-start | bytes 98312 | tf_op jit(solution)/shard_map/ppermute | solution.py:230
  17.1 3.9 %collective-permute-start.9 = (f32[64,128]{1,0:T(8,128)S(1)}, f32[64,128]{1,0:T(8,128)S(1)}, u32[]{:S(2)}, u32[]{:S(2)}) collective-permute-start(f32[64,128]{1,0:T(8,128)S(1)} %get-tuple-element.87), channel_id=1, source_target_pairs={{0,2},{1,3},{2,0},{3,1},{4,6},{5,7},{6,4},{7,5},{8,10},{9,11},{10,... | collective-permute-start | bytes 98312 | tf_op jit(solution)/shard_map/ppermute | solution.py:230
  17.9 3.2 %collective-permute-start.10 = (f32[64,128]{1,0:T(8,128)S(1)}, f32[64,128]{1,0:T(8,128)S(1)}, u32[]{:S(2)}, u32[]{:S(2)}) collective-permute-start(f32[64,128]{1,0:T(8,128)S(1)} %get-tuple-element.88), channel_id=1, source_target_pairs={{0,4},{4,0},{8,12},{12,8},{16,20},{20,16},{24,28},{28,24},{1,5},{5... | collective-permute-start | bytes 98312 | tf_op jit(solution)/shard_map/ppermute | solution.py:231
  18.5 2.5 %collective-permute-start.11 = (f32[64,128]{1,0:T(8,128)S(1)}, f32[64,128]{1,0:T(8,128)S(1)}, u32[]{:S(2)}, u32[]{:S(2)}) collective-permute-start(f32[64,128]{1,0:T(8,128)S(1)} %get-tuple-element.89), channel_id=1, source_target_pairs={{0,4},{4,0},{8,12},{12,8},{16,20},{20,16},{24,28},{28,24},{1,5},{5... | collective-permute-start | bytes 98312 | tf_op jit(solution)/shard_map/ppermute | solution.py:231
  21.7 5.1 %collective-permute-start.13 = (f32[64,128]{1,0:T(8,128)S(1)}, f32[64,128]{1,0:T(8,128)S(1)}, u32[]{:S(2)}, u32[]{:S(2)}) collective-permute-start(f32[64,128]{1,0:T(8,128)S(1)} %get-tuple-element.92), channel_id=1, source_target_pairs={{0,1},{1,0},{2,3},{3,2},{4,5},{5,4},{6,7},{7,6},{8,9},{9,8},{10,11... | collective-permute-start | bytes 98312 | tf_op jit(solution)/shard_map/ppermute | solution.py:230
  22.3 7.2 %collective-permute-start.12 = (f32[128,128]{1,0:T(8,128)S(1)}, f32[128,128]{1,0:T(8,128)S(1)}, u32[]{:S(2)}, u32[]{:S(2)}) collective-permute-start(f32[128,128]{1,0:T(8,128)S(1)} %get-tuple-element.91), channel_id=1, source_target_pairs={{0,28},{4,8},{8,4},{12,16},{16,12},{20,24},{24,20},{28,0},{1,29},{... | collective-permute-start | bytes 196616 | tf_op jit(solution)/shard_map/ppermute | solution.py:228
  24.1 4.8 %collective-permute-start.14 = (f32[64,128]{1,0:T(8,128)S(1)}, f32[64,128]{1,0:T(8,128)S(1)}, u32[]{:S(2)}, u32[]{:S(2)}) collective-permute-start(f32[64,128]{1,0:T(8,128)S(1)} %get-tuple-element.93), channel_id=1, source_target_pairs={{0,3},{1,2},{2,1},{3,0},{4,7},{5,6},{6,5},{7,4},{8,11},{9,10},{10,... | collective-permute-start | bytes 98312 | tf_op jit(solution)/shard_map/ppermute | solution.py:230
  25.5 3.9 %collective-permute-start.15 = (f32[64,128]{1,0:T(8,128)S(1)}, f32[64,128]{1,0:T(8,128)S(1)}, u32[]{:S(2)}, u32[]{:S(2)}) collective-permute-start(f32[64,128]{1,0:T(8,128)S(1)} %get-tuple-element.94), channel_id=1, source_target_pairs={{0,2},{1,3},{2,0},{3,1},{4,6},{5,7},{6,4},{7,5},{8,10},{9,11},{10,... | collective-permute-start | bytes 98312 | tf_op jit(solution)/shard_map/ppermute | solution.py:230
  26.8 2.7 %collective-permute-start.16 = (f32[64,128]{1,0:T(8,128)S(1)}, f32[64,128]{1,0:T(8,128)S(1)}, u32[]{:S(2)}, u32[]{:S(2)}) collective-permute-start(f32[64,128]{1,0:T(8,128)S(1)} %get-tuple-element.95), channel_id=1, source_target_pairs={{0,4},{4,0},{8,12},{12,8},{16,20},{20,16},{24,28},{28,24},{1,5},{5... | collective-permute-start | bytes 98312 | tf_op jit(solution)/shard_map/ppermute | solution.py:231
  26.8 2.7 %collective-permute-start.17 = (f32[64,128]{1,0:T(8,128)S(1)}, f32[64,128]{1,0:T(8,128)S(1)}, u32[]{:S(2)}, u32[]{:S(2)}) collective-permute-start(f32[64,128]{1,0:T(8,128)S(1)} %get-tuple-element.96), channel_id=1, source_target_pairs={{0,4},{4,0},{8,12},{12,8},{16,20},{20,16},{24,28},{28,24},{1,5},{5... | collective-permute-start | bytes 98312 | tf_op jit(solution)/shard_map/ppermute | solution.py:231
  29.8 4.0 %collective-permute-start.19 = (f32[64,128]{1,0:T(8,128)S(1)}, f32[64,128]{1,0:T(8,128)S(1)}, u32[]{:S(2)}, u32[]{:S(2)}) collective-permute-start(f32[64,128]{1,0:T(8,128)S(1)} %get-tuple-element.99), channel_id=1, source_target_pairs={{0,1},{1,0},{2,3},{3,2},{4,5},{5,4},{6,7},{7,6},{8,9},{9,8},{10,11... | collective-permute-start | bytes 98312 | tf_op jit(solution)/shard_map/ppermute | solution.py:230
  31.3 5.5 %collective-permute-start.18 = (f32[128,128]{1,0:T(8,128)S(1)}, f32[128,128]{1,0:T(8,128)S(1)}, u32[]{:S(2)}, u32[]{:S(2)}) collective-permute-start(f32[128,128]{1,0:T(8,128)S(1)} %get-tuple-element.98), channel_id=1, source_target_pairs={{0,28},{4,8},{8,4},{12,16},{16,12},{20,24},{24,20},{28,0},{1,29},{... | collective-permute-start | bytes 196616 | tf_op jit(solution)/shard_map/ppermute | solution.py:228
  31.4 4.8 %collective-permute-start.20 = (f32[64,128]{1,0:T(8,128)S(1)}, f32[64,128]{1,0:T(8,128)S(1)}, u32[]{:S(2)}, u32[]{:S(2)}) collective-permute-start(f32[64,128]{1,0:T(8,128)S(1)} %get-tuple-element.100), channel_id=1, source_target_pairs={{0,3},{1,2},{2,1},{3,0},{4,7},{5,6},{6,5},{7,4},{8,11},{9,10},{10,... | collective-permute-start | bytes 98312 | tf_op jit(solution)/shard_map/ppermute | solution.py:230
  32.8 3.9 %collective-permute-start.21 = (f32[64,128]{1,0:T(8,128)S(1)}, f32[64,128]{1,0:T(8,128)S(1)}, u32[]{:S(2)}, u32[]{:S(2)}) collective-permute-start(f32[64,128]{1,0:T(8,128)S(1)} %get-tuple-element.101), channel_id=1, source_target_pairs={{0,2},{1,3},{2,0},{3,1},{4,6},{5,7},{6,4},{7,5},{8,10},{9,11},{10,... | collective-permute-start | bytes 98312 | tf_op jit(solution)/shard_map/ppermute | solution.py:230
  33.4 3.3 %collective-permute-start.22 = (f32[64,128]{1,0:T(8,128)S(1)}, f32[64,128]{1,0:T(8,128)S(1)}, u32[]{:S(2)}, u32[]{:S(2)}) collective-permute-start(f32[64,128]{1,0:T(8,128)S(1)} %get-tuple-element.102), channel_id=1, source_target_pairs={{0,4},{4,0},{8,12},{12,8},{16,20},{20,16},{24,28},{28,24},{1,5},{5... | collective-permute-start | bytes 98312 | tf_op jit(solution)/shard_map/ppermute | solution.py:231
  33.8 2.9 %collective-permute-start.23 = (f32[64,128]{1,0:T(8,128)S(1)}, f32[64,128]{1,0:T(8,128)S(1)}, u32[]{:S(2)}, u32[]{:S(2)}) collective-permute-start(f32[64,128]{1,0:T(8,128)S(1)} %get-tuple-element.103), channel_id=1, source_target_pairs={{0,4},{4,0},{8,12},{12,8},{16,20},{20,16},{24,28},{28,24},{1,5},{5... | collective-permute-start | bytes 98312 | tf_op jit(solution)/shard_map/ppermute | solution.py:231
  37.1 5.4 %collective-permute-start.25 = (f32[64,128]{1,0:T(8,128)S(1)}, f32[64,128]{1,0:T(8,128)S(1)}, u32[]{:S(2)}, u32[]{:S(2)}) collective-permute-start(f32[64,128]{1,0:T(8,128)S(1)} %get-tuple-element.107), channel_id=1, source_target_pairs={{0,1},{1,0},{2,3},{3,2},{4,5},{5,4},{6,7},{7,6},{8,9},{9,8},{10,11... | collective-permute-start | bytes 98312 | tf_op jit(solution)/shard_map/ppermute | solution.py:230
  37.7 7.2 %collective-permute-start.24 = (f32[128,128]{1,0:T(8,128)S(1)}, f32[128,128]{1,0:T(8,128)S(1)}, u32[]{:S(2)}, u32[]{:S(2)}) collective-permute-start(f32[128,128]{1,0:T(8,128)S(1)} %get-tuple-element.106), channel_id=1, source_target_pairs={{0,28},{4,8},{8,4},{12,16},{16,12},{20,24},{24,20},{28,0},{1,29},{... | collective-permute-start | bytes 196616 | tf_op jit(solution)/shard_map/ppermute | solution.py:228
  39.5 4.8 %collective-permute-start.26 = (f32[64,128]{1,0:T(8,128)S(1)}, f32[64,128]{1,0:T(8,128)S(1)}, u32[]{:S(2)}, u32[]{:S(2)}) collective-permute-start(f32[64,128]{1,0:T(8,128)S(1)} %get-tuple-element.108), channel_id=1, source_target_pairs={{0,3},{1,2},{2,1},{3,0},{4,7},{5,6},{6,5},{7,4},{8,11},{9,10},{10,... | collective-permute-start | bytes 98312 | tf_op jit(solution)/shard_map/ppermute | solution.py:230
  41.0 3.9 %collective-permute-start.27 = (f32[64,128]{1,0:T(8,128)S(1)}, f32[64,128]{1,0:T(8,128)S(1)}, u32[]{:S(2)}, u32[]{:S(2)}) collective-permute-start(f32[64,128]{1,0:T(8,128)S(1)} %get-tuple-element.109), channel_id=1, source_target_pairs={{0,2},{1,3},{2,0},{3,1},{4,6},{5,7},{6,4},{7,5},{8,10},{9,11},{10,... | collective-permute-start | bytes 98312 | tf_op jit(solution)/shard_map/ppermute | solution.py:230
  42.4 2.5 %collective-permute-start.28 = (f32[64,128]{1,0:T(8,128)S(1)}, f32[64,128]{1,0:T(8,128)S(1)}, u32[]{:S(2)}, u32[]{:S(2)}) collective-permute-start(f32[64,128]{1,0:T(8,128)S(1)} %get-tuple-element.110), channel_id=1, source_target_pairs={{0,4},{4,0},{8,12},{12,8},{16,20},{20,16},{24,28},{28,24},{1,5},{5... | collective-permute-start | bytes 98312 | tf_op jit(solution)/shard_map/ppermute | solution.py:231
  42.4 2.5 %collective-permute-start.29 = (f32[64,128]{1,0:T(8,128)S(1)}, f32[64,128]{1,0:T(8,128)S(1)}, u32[]{:S(2)}, u32[]{:S(2)}) collective-permute-start(f32[64,128]{1,0:T(8,128)S(1)} %get-tuple-element.111), channel_id=1, source_target_pairs={{0,4},{4,0},{8,12},{12,8},{16,20},{20,16},{24,28},{28,24},{1,5},{5... | collective-permute-start | bytes 98312 | tf_op jit(solution)/shard_map/ppermute | solution.py:231
  45.3 4.0 %collective-permute-start.31 = (f32[64,128]{1,0:T(8,128)S(1)}, f32[64,128]{1,0:T(8,128)S(1)}, u32[]{:S(2)}, u32[]{:S(2)}) collective-permute-start(f32[64,128]{1,0:T(8,128)S(1)} %get-tuple-element.115), channel_id=1, source_target_pairs={{0,1},{1,0},{2,3},{3,2},{4,5},{5,4},{6,7},{7,6},{8,9},{9,8},{10,11... | collective-permute-start | bytes 98312 | tf_op jit(solution)/shard_map/ppermute | solution.py:230
  46.7 5.6 %collective-permute-start.30 = (f32[128,128]{1,0:T(8,128)S(1)}, f32[128,128]{1,0:T(8,128)S(1)}, u32[]{:S(2)}, u32[]{:S(2)}) collective-permute-start(f32[128,128]{1,0:T(8,128)S(1)} %get-tuple-element.114), channel_id=1, source_target_pairs={{0,28},{4,8},{8,4},{12,16},{16,12},{20,24},{24,20},{28,0},{1,29},{... | collective-permute-start | bytes 196616 | tf_op jit(solution)/shard_map/ppermute | solution.py:228
  46.8 4.8 %collective-permute-start.32 = (f32[64,128]{1,0:T(8,128)S(1)}, f32[64,128]{1,0:T(8,128)S(1)}, u32[]{:S(2)}, u32[]{:S(2)}) collective-permute-start(f32[64,128]{1,0:T(8,128)S(1)} %get-tuple-element.116), channel_id=1, source_target_pairs={{0,3},{1,2},{2,1},{3,0},{4,7},{5,6},{6,5},{7,4},{8,11},{9,10},{10,... | collective-permute-start | bytes 98312 | tf_op jit(solution)/shard_map/ppermute | solution.py:230
  48.4 3.9 %collective-permute-start.33 = (f32[64,128]{1,0:T(8,128)S(1)}, f32[64,128]{1,0:T(8,128)S(1)}, u32[]{:S(2)}, u32[]{:S(2)}) collective-permute-start(f32[64,128]{1,0:T(8,128)S(1)} %get-tuple-element.117), channel_id=1, source_target_pairs={{0,2},{1,3},{2,0},{3,1},{4,6},{5,7},{6,4},{7,5},{8,10},{9,11},{10,... | collective-permute-start | bytes 98312 | tf_op jit(solution)/shard_map/ppermute | solution.py:230
  48.9 3.4 %collective-permute-start.34 = (f32[64,128]{1,0:T(8,128)S(1)}, f32[64,128]{1,0:T(8,128)S(1)}, u32[]{:S(2)}, u32[]{:S(2)}) collective-permute-start(f32[64,128]{1,0:T(8,128)S(1)} %get-tuple-element.118), channel_id=1, source_target_pairs={{0,4},{4,0},{8,12},{12,8},{16,20},{20,16},{24,28},{28,24},{1,5},{5... | collective-permute-start | bytes 98312 | tf_op jit(solution)/shard_map/ppermute | solution.py:231
  49.3 3.0 %collective-permute-start.35 = (f32[64,128]{1,0:T(8,128)S(1)}, f32[64,128]{1,0:T(8,128)S(1)}, u32[]{:S(2)}, u32[]{:S(2)}) collective-permute-start(f32[64,128]{1,0:T(8,128)S(1)} %get-tuple-element.119), channel_id=1, source_target_pairs={{0,4},{4,0},{8,12},{12,8},{16,20},{20,16},{24,28},{28,24},{1,5},{5... | collective-permute-start | bytes 98312 | tf_op jit(solution)/shard_map/ppermute | solution.py:231
  52.6 5.2 %collective-permute-start.37 = (f32[64,128]{1,0:T(8,128)S(1)}, f32[64,128]{1,0:T(8,128)S(1)}, u32[]{:S(2)}, u32[]{:S(2)}) collective-permute-start(f32[64,128]{1,0:T(8,128)S(1)} %get-tuple-element.123), channel_id=1, source_target_pairs={{0,1},{1,0},{2,3},{3,2},{4,5},{5,4},{6,7},{7,6},{8,9},{9,8},{10,11... | collective-permute-start | bytes 98312 | tf_op jit(solution)/shard_map/ppermute | solution.py:230
  53.2 7.2 %collective-permute-start.36 = (f32[128,128]{1,0:T(8,128)S(1)}, f32[128,128]{1,0:T(8,128)S(1)}, u32[]{:S(2)}, u32[]{:S(2)}) collective-permute-start(f32[128,128]{1,0:T(8,128)S(1)} %get-tuple-element.122), channel_id=1, source_target_pairs={{0,28},{4,8},{8,4},{12,16},{16,12},{20,24},{24,20},{28,0},{1,29},{... | collective-permute-start | bytes 196616 | tf_op jit(solution)/shard_map/ppermute | solution.py:228
  55.0 4.8 %collective-permute-start.38 = (f32[64,128]{1,0:T(8,128)S(1)}, f32[64,128]{1,0:T(8,128)S(1)}, u32[]{:S(2)}, u32[]{:S(2)}) collective-permute-start(f32[64,128]{1,0:T(8,128)S(1)} %get-tuple-element.124), channel_id=1, source_target_pairs={{0,3},{1,2},{2,1},{3,0},{4,7},{5,6},{6,5},{7,4},{8,11},{9,10},{10,... | collective-permute-start | bytes 98312 | tf_op jit(solution)/shard_map/ppermute | solution.py:230
  56.5 3.9 %collective-permute-start.39 = (f32[64,128]{1,0:T(8,128)S(1)}, f32[64,128]{1,0:T(8,128)S(1)}, u32[]{:S(2)}, u32[]{:S(2)}) collective-permute-start(f32[64,128]{1,0:T(8,128)S(1)} %get-tuple-element.125), channel_id=1, source_target_pairs={{0,2},{1,3},{2,0},{3,1},{4,6},{5,7},{6,4},{7,5},{8,10},{9,11},{10,... | collective-permute-start | bytes 98312 | tf_op jit(solution)/shard_map/ppermute | solution.py:230
  57.8 2.5 %collective-permute-start.40 = (f32[64,128]{1,0:T(8,128)S(1)}, f32[64,128]{1,0:T(8,128)S(1)}, u32[]{:S(2)}, u32[]{:S(2)}) collective-permute-start(f32[64,128]{1,0:T(8,128)S(1)} %get-tuple-element.126), channel_id=1, source_target_pairs={{0,4},{4,0},{8,12},{12,8},{16,20},{20,16},{24,28},{28,24},{1,5},{5... | collective-permute-start | bytes 98312 | tf_op jit(solution)/shard_map/ppermute | solution.py:231
  57.9 2.5 %collective-permute-start.41 = (f32[64,128]{1,0:T(8,128)S(1)}, f32[64,128]{1,0:T(8,128)S(1)}, u32[]{:S(2)}, u32[]{:S(2)}) collective-permute-start(f32[64,128]{1,0:T(8,128)S(1)} %get-tuple-element.127), channel_id=1, source_target_pairs={{0,4},{4,0},{8,12},{12,8},{16,20},{20,16},{24,28},{28,24},{1,5},{5... | collective-permute-start | bytes 98312 | tf_op jit(solution)/shard_map/ppermute | solution.py:231
  60.7 4.0 %collective-permute-start.43 = (f32[64,128]{1,0:T(8,128)S(1)}, f32[64,128]{1,0:T(8,128)S(1)}, u32[]{:S(2)}, u32[]{:S(2)}) collective-permute-start(f32[64,128]{1,0:T(8,128)S(1)} %get-tuple-element.137), channel_id=1, source_target_pairs={{0,1},{1,0},{2,3},{3,2},{4,5},{5,4},{6,7},{7,6},{8,9},{9,8},{10,11... | collective-permute-start | bytes 98312 | tf_op jit(solution)/shard_map/ppermute | solution.py:230
  62.2 5.5 %collective-permute-start.42 = (f32[128,128]{1,0:T(8,128)S(1)}, f32[128,128]{1,0:T(8,128)S(1)}, u32[]{:S(2)}, u32[]{:S(2)}) collective-permute-start(f32[128,128]{1,0:T(8,128)S(1)} %get-tuple-element.136), channel_id=1, source_target_pairs={{0,28},{4,8},{8,4},{12,16},{16,12},{20,24},{24,20},{28,0},{1,29},{... | collective-permute-start | bytes 196616 | tf_op jit(solution)/shard_map/ppermute | solution.py:228
  62.4 4.8 %collective-permute-start.44 = (f32[64,128]{1,0:T(8,128)S(1)}, f32[64,128]{1,0:T(8,128)S(1)}, u32[]{:S(2)}, u32[]{:S(2)}) collective-permute-start(f32[64,128]{1,0:T(8,128)S(1)} %get-tuple-element.138), channel_id=1, source_target_pairs={{0,3},{1,2},{2,1},{3,0},{4,7},{5,6},{6,5},{7,4},{8,11},{9,10},{10,... | collective-permute-start | bytes 98312 | tf_op jit(solution)/shard_map/ppermute | solution.py:230
  63.8 3.9 %collective-permute-start.45 = (f32[64,128]{1,0:T(8,128)S(1)}, f32[64,128]{1,0:T(8,128)S(1)}, u32[]{:S(2)}, u32[]{:S(2)}) collective-permute-start(f32[64,128]{1,0:T(8,128)S(1)} %get-tuple-element.139), channel_id=1, source_target_pairs={{0,2},{1,3},{2,0},{3,1},{4,6},{5,7},{6,4},{7,5},{8,10},{9,11},{10,... | collective-permute-start | bytes 98312 | tf_op jit(solution)/shard_map/ppermute | solution.py:230
  64.4 3.3 %collective-permute-start.46 = (f32[64,128]{1,0:T(8,128)S(1)}, f32[64,128]{1,0:T(8,128)S(1)}, u32[]{:S(2)}, u32[]{:S(2)}) collective-permute-start(f32[64,128]{1,0:T(8,128)S(1)} %get-tuple-element.140), channel_id=1, source_target_pairs={{0,4},{4,0},{8,12},{12,8},{16,20},{20,16},{24,28},{28,24},{1,5},{5... | collective-permute-start | bytes 98312 | tf_op jit(solution)/shard_map/ppermute | solution.py:231
  64.7 3.0 %collective-permute-start.47 = (f32[64,128]{1,0:T(8,128)S(1)}, f32[64,128]{1,0:T(8,128)S(1)}, u32[]{:S(2)}, u32[]{:S(2)}) collective-permute-start(f32[64,128]{1,0:T(8,128)S(1)} %get-tuple-element.141), channel_id=1, source_target_pairs={{0,4},{4,0},{8,12},{12,8},{16,20},{20,16},{24,28},{28,24},{1,5},{5... | collective-permute-start | bytes 98312 | tf_op jit(solution)/shard_map/ppermute | solution.py:231

commit v9 on v7

--- a/solution.py
+++ b/solution.py
@@ -24,8 +24,10 @@
     def __init__(self, rows, rhs_count, width, group):
         self.rows, self.n, self.w, self.group = rows, rhs_count, width, group
         self.quarter = rows // COLORS
-        self.lanes = group + self.quarter
-        self.distances = [1] + list(reversed(range(2, group)))
+        half = group // 2
+        others = [(s, range(group)) for s in range(1, group) if s != half]
+        self.swaps = [(half, range(half))] + others + [(half, range(half, group))]
+        self.lanes = 1 + len(self.swaps) + self.quarter
         self.order, self.local, self.slot = 0, rows, 3 * rows
         self.table = 5 * rows
         self.dom_meta = -(-rows // 8) * 8
@@ -34,6 +36,9 @@
         extra = (self.dom_meta, META) if step == 0 else (0, 0)
         far, one = self.quarter * self.n + extra[0], self.n + extra[1]
         shapes = [far] + [one] * (self.lanes - 1)
+        count = len(self.swaps)
+        spare = [0, 0, 8] + [32] * (count - 3) + [24] + [16] * self.quarter
+        shapes = [length + more for length, more in zip(shapes, spare)]
         return [pltpu.VMEM((length, self.w), jnp.float32) for length in shapes]
 
 
@@ -61,7 +66,7 @@
 
 def products(plan, step, table, changes, coupling, sends):
     parity = lax.rem(lax.axis_index("dom"), 2)
-    far, near = sends[0], sends[plan.group :]
+    far, near = sends[0], sends[1 + len(plan.swaps) :]
     terms = []
     for p in range(plan.quarter):
         at = step % COLORS * plan.quarter + p
@@ -75,7 +80,7 @@
         both = dot(changes[p], jnp.concatenate([coupling[j, 2], coupling[j, 3]], axis=1))
         for k in range(2):
             terms.append((table[plan.slot + 2 * at + k], both[:, k * plan.w : (k + 1) * plan.w]))
-    for lane, s in enumerate(plan.distances):
+    for lane, (s, _) in enumerate(plan.swaps):
         total = jnp.zeros((plan.n, plan.w), jnp.float32)
         for slot, term in terms:
             total = total + jnp.where(slot == s, term, 0.0)
@@ -83,7 +88,8 @@
 
 
 def first_kernel(plan, *refs):
-    hbm, outs, scratch = refs[:8], refs[8 : 14 + plan.lanes], refs[14 + plan.lanes :]
+    last = 14 + plan.lanes
+    hbm, outs, scratch = refs[:8], refs[8:last], refs[last:]
     table, coupling, diag, rhs, sol, change = outs[:6]
     sends = outs[6:]
     color, local_target, group_peer, group_list, dom_target = scratch[:5]
@@ -120,7 +126,7 @@
     copies[7].wait()
     products(plan, 0, table, changes, coupling, sends)
     line = lax.broadcasted_iota(jnp.int32, (META, plan.w), 0)
-    for lane, s in enumerate(plan.distances):
+    for lane, (s, _) in enumerate(plan.swaps):
         meta = jnp.full((META, plan.w), -1, jnp.int32)
         for c in range(COLORS):
             meta = jnp.where(line == c, group_list[0, c, me ^ s], meta)
@@ -130,7 +136,7 @@
         for c in range(COLORS):
             at = c * plan.quarter + p
             meta = jnp.where(line == c, dom_target[parity, table[plan.order + at]], meta)
-        sends[plan.group + p][pl.ds(plan.n, META), :] = meta.astype(jnp.float32)
+        sends[1 + len(plan.swaps) + p][pl.ds(plan.n, META), :] = meta.astype(jnp.float32)
     line = lax.broadcasted_iota(jnp.int32, (plan.dom_meta, plan.w), 0)
     meta = jnp.full((plan.dom_meta, plan.w), -1, jnp.int32)
     for at in range(plan.rows):
@@ -222,9 +228,9 @@
 
     def exchange(sends):
         got = [lax.ppermute(sends[0], "dom", far_pairs)]
-        for send, s in zip(sends[1:group], plan.distances):
-            got.append(lax.ppermute(send, "sub", [(i, i ^ s) for i in range(group)]))
-        return got + [lax.ppermute(send, "dom", near_pairs) for send in sends[group:]]
+        for send, (s, members) in zip(sends[1:], plan.swaps):
+            got.append(lax.ppermute(send, "sub", [(m, m ^ s) for m in members]))
+        return got + [lax.ppermute(send, "dom", near_pairs) for send in sends[len(got) :]]
 
     sol_t = pltpu.VMEM((plan.quarter, plan.n, plan.w), f32)
     change_t = pltpu.VMEM((plan.quarter, plan.n, plan.w), jnp.bfloat16)

time: 68.5 us -> 90.6 us (1.32)
  starting transfers between devices: 40.6 us -> 51.6 us
  waiting for transfers between devices: 19.7 us -> 30.1 us
    ppermute x24 -> x32, starting transfers between devices: 29.4 us -> 36.7 us  [exchange(): got.append(lax.ppermute(send, 'sub', [(m, m ^ s) for m in members]))]
    ppermute x24 -> x32, waiting for transfers between devices: 19.3 us -> 25.5 us  [exchange(): got.append(lax.ppermute(send, 'sub', [(m, m ^ s) for m in members]))]
    ppermute x16, waiting for transfers between devices: 0.04 us -> 4.53 us  [exchange(): lax.ppermute(send, 'dom', near_pairs)]
    ppermute x16, starting transfers between devices: 2.6 us -> 4.49 us  [exchange(): lax.ppermute(send, 'dom', near_pairs)]
    ppermute x8, starting transfers between devices: 8.65 us -> 10.4 us  [exchange(): got = [lax.ppermute(sends[0], 'dom', far_pairs)]]
  transfers between devices with their start and end apart: 48 -> 56, of which waited for: 21 -> 23; matrix products, arithmetic and copies ran while one was open for 0% -> 0% of each run, Pallas kernels for 3% -> 3%
where the time goes in v9:
time: 90.6 us; the launch traced here: 90.2 us
  starting transfers between devices  51.6 us (57%)
  waiting for transfers between devices  30.1 us (33%)
  Pallas kernels  7.37 us (8%)
  between operations  1.08 us (1%)
    ppermute x32, starting transfers between devices, exchange(): got.append(lax.ppermute(send, 'sub', [(m, m ^ s) for m in members]))  36.7 us
    ppermute x32, waiting for transfers between devices, exchange(): got.append(lax.ppermute(send, 'sub', [(m, m ^ s) for m in members]))  25.5 us
    ppermute x8, starting transfers between devices, exchange(): got = [lax.ppermute(sends[0], 'dom', far_pairs)]  10.4 us
    pallas_call x17, Pallas kernels, call(): pl.pallas_call(body, name=name, in_specs=in_specs + [VMEM] * (len(ins) -...  7.37 us
    ppermute x16, waiting for transfers between devices, exchange(): lax.ppermute(send, 'dom', near_pairs)  4.53 us
    ppermute x16, starting transfers between devices, exchange(): lax.ppermute(send, 'dom', near_pairs)  4.49 us
  transfers between devices with their start and end apart: 56, of which 23 were waited for; matrix products, arithmetic and copies ran while one was open for 0% of the time, Pallas kernels for 3%

profile of v9, /device:TPU:0, one launch (start us, length us, event | category | flops | bytes accessed | tf_op | source)
XLA Modules:
  0.0 90.2 jit_solution(2969653546080970499)
XLA Ops:
  0.6 1.9 %first.1 = (s32[40]{0:T(128)S(4)}, bf16[8,6,128,128]{3,2,1,0:T(8,128)(2,1)S(1)}, bf16[8,128,128]{2,1,0:T(8,128)(2,1)S(1)}, f32[8,64,128]{2,1,0:T(8,128)S(1)}, f3...) custom-call(s32[8]{0:T(128)} %refs_0_.1, ...), custom_call_target="tpu_custom_call" | custom-call | tf_op jit(solution)/shard_map/first/pallas_call | solution.py:219
  2.5 3.0 %collective-permute-start.2 = (f32[80,128]{1,0:T(8,128)S(1)}, f32[80,128]{1,0:T(8,128)S(1)}, u32[]{:S(2)}, u32[]{:S(2)}) collective-permute-start(f32[80,128]{1,0:T(8,128)S(1)} %get-tuple-element.87), channel_id=1, source_target_pairs={{0,1},{1,0},{2,3},{3,2},{4,5},{5,4},{6,7},{7,6},{8,9},{9,8},{10,11... | collective-permute-start | bytes 122888 | tf_op jit(solution)/shard_map/ppermute | solution.py:232
  5.5 3.4 %collective-permute-start.1 = (f32[72,128]{1,0:T(8,128)S(1)}, f32[72,128]{1,0:T(8,128)S(1)}, u32[]{:S(2)}, u32[]{:S(2)}) collective-permute-start(f32[72,128]{1,0:T(8,128)S(1)} %get-tuple-element.86), channel_id=1, source_target_pairs={{0,2},{1,3},{4,6},{5,7},{8,10},{9,11},{12,14},{13,15},{16,18},{17,... | collective-permute-start | bytes 110600 | tf_op jit(solution)/shard_map/ppermute | solution.py:232
  9.0 2.5 %collective-permute-start = (f32[136,128]{1,0:T(8,128)S(1)}, f32[136,128]{1,0:T(8,128)S(1)}, u32[]{:S(2)}, u32[]{:S(2)}) collective-permute-start(f32[136,128]{1,0:T(8,128)S(1)} %get-tuple-element.85), channel_id=1, source_target_pairs={{0,28},{4,8},{8,4},{12,16},{16,12},{20,24},{24,20},{28,0},{1,29},{... | collective-permute-start | bytes 208904 | tf_op jit(solution)/shard_map/ppermute | solution.py:230
  11.5 1.3 %collective-permute-start.4 = (f32[96,128]{1,0:T(8,128)S(1)}, f32[96,128]{1,0:T(8,128)S(1)}, u32[]{:S(2)}, u32[]{:S(2)}) collective-permute-start(f32[96,128]{1,0:T(8,128)S(1)} %get-tuple-element.89), channel_id=1, source_target_pairs={{2,0},{3,1},{6,4},{7,5},{10,8},{11,9},{14,12},{15,13},{18,16},{19,... | collective-permute-start | bytes 147464 | tf_op jit(solution)/shard_map/ppermute | solution.py:232
  12.9 0.5 collective-permute-start.6
  13.6 0.5 collective-permute-done.5.refs_5_.refs_12_
  14.3 3.2 %collective-permute-done.4.refs_4_.refs_11_ = f32[96,128]{1,0:T(8,128)S(1)} collective-permute-done((f32[96,128]{1,0:T(8,128)S(1)}, f32[96,128]{1,0:T(8,128)S(1)}, u32[]{:S(2)}, u32[]{:S(2)}) %collective-permute-start.4) | collective-permute-done | bytes 49184 | tf_op jit(solution)/shard_map/ppermute | solution.py:232
  17.8 1.2 %collective-permute-start.9 = (f32[72,128]{1,0:T(8,128)S(1)}, f32[72,128]{1,0:T(8,128)S(1)}, u32[]{:S(2)}, u32[]{:S(2)}) collective-permute-start(f32[72,128]{1,0:T(8,128)S(1)} %get-tuple-element.95), channel_id=1, source_target_pairs={{0,1},{1,0},{2,3},{3,2},{4,5},{5,4},{6,7},{7,6},{8,9},{9,8},{10,11... | collective-permute-start | bytes 110600 | tf_op jit(solution)/shard_map/ppermute | solution.py:232
  19.0 1.6 %collective-permute-start.8 = (f32[64,128]{1,0:T(8,128)S(1)}, f32[64,128]{1,0:T(8,128)S(1)}, u32[]{:S(2)}, u32[]{:S(2)}) collective-permute-start(f32[64,128]{1,0:T(8,128)S(1)} %get-tuple-element.94), channel_id=1, source_target_pairs={{0,2},{1,3},{4,6},{5,7},{8,10},{9,11},{12,14},{13,15},{16,18},{17,... | collective-permute-start | bytes 98312 | tf_op jit(solution)/shard_map/ppermute | solution.py:232
  20.8 0.8 collective-permute-start.10
  21.7 1.3 %collective-permute-start.11 = (f32[88,128]{1,0:T(8,128)S(1)}, f32[88,128]{1,0:T(8,128)S(1)}, u32[]{:S(2)}, u32[]{:S(2)}) collective-permute-start(f32[88,128]{1,0:T(8,128)S(1)} %get-tuple-element.97), channel_id=1, source_target_pairs={{2,0},{3,1},{6,4},{7,5},{10,8},{11,9},{14,12},{15,13},{18,16},{19,... | collective-permute-start | bytes 135176 | tf_op jit(solution)/shard_map/ppermute | solution.py:232
  23.0 0.5 collective-permute-start.13
  24.4 3.2 %collective-permute-done.11.refs_4_ = f32[88,128]{1,0:T(8,128)S(1)} collective-permute-done((f32[88,128]{1,0:T(8,128)S(1)}, f32[88,128]{1,0:T(8,128)S(1)}, u32[]{:S(2)}, u32[]{:S(2)}) %collective-permute-start.11) | collective-permute-done | bytes 45088 | tf_op jit(solution)/shard_map/ppermute | solution.py:232
  27.9 1.0 %collective-permute-start.16 = (f32[72,128]{1,0:T(8,128)S(1)}, f32[72,128]{1,0:T(8,128)S(1)}, u32[]{:S(2)}, u32[]{:S(2)}) collective-permute-start(f32[72,128]{1,0:T(8,128)S(1)} %get-tuple-element.103), channel_id=1, source_target_pairs={{0,1},{1,0},{2,3},{3,2},{4,5},{5,4},{6,7},{7,6},{8,9},{9,8},{10,11... | collective-permute-start | bytes 110600 | tf_op jit(solution)/shard_map/ppermute | solution.py:232
  28.9 1.6 %collective-permute-start.15 = (f32[64,128]{1,0:T(8,128)S(1)}, f32[64,128]{1,0:T(8,128)S(1)}, u32[]{:S(2)}, u32[]{:S(2)}) collective-permute-start(f32[64,128]{1,0:T(8,128)S(1)} %get-tuple-element.102), channel_id=1, source_target_pairs={{0,2},{1,3},{4,6},{5,7},{8,10},{9,11},{12,14},{13,15},{16,18},{17,... | collective-permute-start | bytes 98312 | tf_op jit(solution)/shard_map/ppermute | solution.py:232
  30.5 1.5 %collective-permute-start.14 = (f32[128,128]{1,0:T(8,128)S(1)}, f32[128,128]{1,0:T(8,128)S(1)}, u32[]{:S(2)}, u32[]{:S(2)}) collective-permute-start(f32[128,128]{1,0:T(8,128)S(1)} %get-tuple-element.101), channel_id=1, source_target_pairs={{0,28},{4,8},{8,4},{12,16},{16,12},{20,24},{24,20},{28,0},{1,29},{... | collective-permute-start | bytes 196616 | tf_op jit(solution)/shard_map/ppermute | solution.py:230
  32.2 1.3 %collective-permute-start.18 = (f32[88,128]{1,0:T(8,128)S(1)}, f32[88,128]{1,0:T(8,128)S(1)}, u32[]{:S(2)}, u32[]{:S(2)}) collective-permute-start(f32[88,128]{1,0:T(8,128)S(1)} %get-tuple-element.105), channel_id=1, source_target_pairs={{2,0},{3,1},{6,4},{7,5},{10,8},{11,9},{14,12},{15,13},{18,16},{19,... | collective-permute-start | bytes 135176 | tf_op jit(solution)/shard_map/ppermute | solution.py:232
  33.6 0.5 collective-permute-start.20
  35.0 3.2 %collective-permute-done.18.refs_4_ = f32[88,128]{1,0:T(8,128)S(1)} collective-permute-done((f32[88,128]{1,0:T(8,128)S(1)}, f32[88,128]{1,0:T(8,128)S(1)}, u32[]{:S(2)}, u32[]{:S(2)}) %collective-permute-start.18) | collective-permute-done | bytes 45088 | tf_op jit(solution)/shard_map/ppermute | solution.py:232
  38.5 1.0 %collective-permute-start.23 = (f32[72,128]{1,0:T(8,128)S(1)}, f32[72,128]{1,0:T(8,128)S(1)}, u32[]{:S(2)}, u32[]{:S(2)}) collective-permute-start(f32[72,128]{1,0:T(8,128)S(1)} %get-tuple-element.111), channel_id=1, source_target_pairs={{0,1},{1,0},{2,3},{3,2},{4,5},{5,4},{6,7},{7,6},{8,9},{9,8},{10,11... | collective-permute-start | bytes 110600 | tf_op jit(solution)/shard_map/ppermute | solution.py:232
  39.5 1.6 %collective-permute-start.22 = (f32[64,128]{1,0:T(8,128)S(1)}, f32[64,128]{1,0:T(8,128)S(1)}, u32[]{:S(2)}, u32[]{:S(2)}) collective-permute-start(f32[64,128]{1,0:T(8,128)S(1)} %get-tuple-element.110), channel_id=1, source_target_pairs={{0,2},{1,3},{4,6},{5,7},{8,10},{9,11},{12,14},{13,15},{16,18},{17,... | collective-permute-start | bytes 98312 | tf_op jit(solution)/shard_map/ppermute | solution.py:232
  41.1 1.1 %collective-permute-start.21 = (f32[128,128]{1,0:T(8,128)S(1)}, f32[128,128]{1,0:T(8,128)S(1)}, u32[]{:S(2)}, u32[]{:S(2)}) collective-permute-start(f32[128,128]{1,0:T(8,128)S(1)} %get-tuple-element.109), channel_id=1, source_target_pairs={{0,28},{4,8},{8,4},{12,16},{16,12},{20,24},{24,20},{28,0},{1,29},{... | collective-permute-start | bytes 196616 | tf_op jit(solution)/shard_map/ppermute | solution.py:230
  42.1 1.3 %collective-permute-start.25 = (f32[88,128]{1,0:T(8,128)S(1)}, f32[88,128]{1,0:T(8,128)S(1)}, u32[]{:S(2)}, u32[]{:S(2)}) collective-permute-start(f32[88,128]{1,0:T(8,128)S(1)} %get-tuple-element.113), channel_id=1, source_target_pairs={{2,0},{3,1},{6,4},{7,5},{10,8},{11,9},{14,12},{15,13},{18,16},{19,... | collective-permute-start | bytes 135176 | tf_op jit(solution)/shard_map/ppermute | solution.py:232
  43.5 0.5 collective-permute-start.27
  44.9 3.2 %collective-permute-done.25.refs_4_ = f32[88,128]{1,0:T(8,128)S(1)} collective-permute-done((f32[88,128]{1,0:T(8,128)S(1)}, f32[88,128]{1,0:T(8,128)S(1)}, u32[]{:S(2)}, u32[]{:S(2)}) %collective-permute-start.25) | collective-permute-done | bytes 45088 | tf_op jit(solution)/shard_map/ppermute | solution.py:232
  48.4 1.2 %collective-permute-start.30 = (f32[72,128]{1,0:T(8,128)S(1)}, f32[72,128]{1,0:T(8,128)S(1)}, u32[]{:S(2)}, u32[]{:S(2)}) collective-permute-start(f32[72,128]{1,0:T(8,128)S(1)} %get-tuple-element.120), channel_id=1, source_target_pairs={{0,1},{1,0},{2,3},{3,2},{4,5},{5,4},{6,7},{7,6},{8,9},{9,8},{10,11... | collective-permute-start | bytes 110600 | tf_op jit(solution)/shard_map/ppermute | solution.py:232
  49.6 1.6 %collective-permute-start.29 = (f32[64,128]{1,0:T(8,128)S(1)}, f32[64,128]{1,0:T(8,128)S(1)}, u32[]{:S(2)}, u32[]{:S(2)}) collective-permute-start(f32[64,128]{1,0:T(8,128)S(1)} %get-tuple-element.119), channel_id=1, source_target_pairs={{0,2},{1,3},{4,6},{5,7},{8,10},{9,11},{12,14},{13,15},{16,18},{17,... | collective-permute-start | bytes 98312 | tf_op jit(solution)/shard_map/ppermute | solution.py:232
  51.2 1.5 %collective-permute-start.28 = (f32[128,128]{1,0:T(8,128)S(1)}, f32[128,128]{1,0:T(8,128)S(1)}, u32[]{:S(2)}, u32[]{:S(2)}) collective-permute-start(f32[128,128]{1,0:T(8,128)S(1)} %get-tuple-element.118), channel_id=1, source_target_pairs={{0,28},{4,8},{8,4},{12,16},{16,12},{20,24},{24,20},{28,0},{1,29},{... | collective-permute-start | bytes 196616 | tf_op jit(solution)/shard_map/ppermute | solution.py:230
  52.7 1.3 %collective-permute-start.32 = (f32[88,128]{1,0:T(8,128)S(1)}, f32[88,128]{1,0:T(8,128)S(1)}, u32[]{:S(2)}, u32[]{:S(2)}) collective-permute-start(f32[88,128]{1,0:T(8,128)S(1)} %get-tuple-element.122), channel_id=1, source_target_pairs={{2,0},{3,1},{6,4},{7,5},{10,8},{11,9},{14,12},{15,13},{18,16},{19,... | collective-permute-start | bytes 135176 | tf_op jit(solution)/shard_map/ppermute | solution.py:232
  55.5 3.2 %collective-permute-done.32.refs_4_ = f32[88,128]{1,0:T(8,128)S(1)} collective-permute-done((f32[88,128]{1,0:T(8,128)S(1)}, f32[88,128]{1,0:T(8,128)S(1)}, u32[]{:S(2)}, u32[]{:S(2)}) %collective-permute-start.32) | collective-permute-done | bytes 45088 | tf_op jit(solution)/shard_map/ppermute | solution.py:232
  59.0 1.2 %collective-permute-start.37 = (f32[72,128]{1,0:T(8,128)S(1)}, f32[72,128]{1,0:T(8,128)S(1)}, u32[]{:S(2)}, u32[]{:S(2)}) collective-permute-start(f32[72,128]{1,0:T(8,128)S(1)} %get-tuple-element.129), channel_id=1, source_target_pairs={{0,1},{1,0},{2,3},{3,2},{4,5},{5,4},{6,7},{7,6},{8,9},{9,8},{10,11... | collective-permute-start | bytes 110600 | tf_op jit(solution)/shard_map/ppermute | solution.py:232
  60.2 1.6 %collective-permute-start.36 = (f32[64,128]{1,0:T(8,128)S(1)}, f32[64,128]{1,0:T(8,128)S(1)}, u32[]{:S(2)}, u32[]{:S(2)}) collective-permute-start(f32[64,128]{1,0:T(8,128)S(1)} %get-tuple-element.128), channel_id=1, source_target_pairs={{0,2},{1,3},{4,6},{5,7},{8,10},{9,11},{12,14},{13,15},{16,18},{17,... | collective-permute-start | bytes 98312 | tf_op jit(solution)/shard_map/ppermute | solution.py:232
  61.8 0.8 collective-permute-start.35
  62.9 1.3 %collective-permute-start.39 = (f32[88,128]{1,0:T(8,128)S(1)}, f32[88,128]{1,0:T(8,128)S(1)}, u32[]{:S(2)}, u32[]{:S(2)}) collective-permute-start(f32[88,128]{1,0:T(8,128)S(1)} %get-tuple-element.131), channel_id=1, source_target_pairs={{2,0},{3,1},{6,4},{7,5},{10,8},{11,9},{14,12},{15,13},{18,16},{19,... | collective-permute-start | bytes 135176 | tf_op jit(solution)/shard_map/ppermute | solution.py:232
  65.6 3.2 %collective-permute-done.39.refs_4_ = f32[88,128]{1,0:T(8,128)S(1)} collective-permute-done((f32[88,128]{1,0:T(8,128)S(1)}, f32[88,128]{1,0:T(8,128)S(1)}, u32[]{:S(2)}, u32[]{:S(2)}) %collective-permute-start.39) | collective-permute-done | bytes 45088 | tf_op jit(solution)/shard_map/ppermute | solution.py:232
  69.1 1.0 %collective-permute-start.44 = (f32[72,128]{1,0:T(8,128)S(1)}, f32[72,128]{1,0:T(8,128)S(1)}, u32[]{:S(2)}, u32[]{:S(2)}) collective-permute-start(f32[72,128]{1,0:T(8,128)S(1)} %get-tuple-element.138), channel_id=1, source_target_pairs={{0,1},{1,0},{2,3},{3,2},{4,5},{5,4},{6,7},{7,6},{8,9},{9,8},{10,11... | collective-permute-start | bytes 110600 | tf_op jit(solution)/shard_map/ppermute | solution.py:232
  70.1 1.6 %collective-permute-start.43 = (f32[64,128]{1,0:T(8,128)S(1)}, f32[64,128]{1,0:T(8,128)S(1)}, u32[]{:S(2)}, u32[]{:S(2)}) collective-permute-start(f32[64,128]{1,0:T(8,128)S(1)} %get-tuple-element.137), channel_id=1, source_target_pairs={{0,2},{1,3},{4,6},{5,7},{8,10},{9,11},{12,14},{13,15},{16,18},{17,... | collective-permute-start | bytes 98312 | tf_op jit(solution)/shard_map/ppermute | solution.py:232
  71.7 1.6 %collective-permute-start.42 = (f32[128,128]{1,0:T(8,128)S(1)}, f32[128,128]{1,0:T(8,128)S(1)}, u32[]{:S(2)}, u32[]{:S(2)}) collective-permute-start(f32[128,128]{1,0:T(8,128)S(1)} %get-tuple-element.136), channel_id=1, source_target_pairs={{0,28},{4,8},{8,4},{12,16},{16,12},{20,24},{24,20},{28,0},{1,29},{... | collective-permute-start | bytes 196616 | tf_op jit(solution)/shard_map/ppermute | solution.py:230
  73.4 1.3 %collective-permute-start.46 = (f32[88,128]{1,0:T(8,128)S(1)}, f32[88,128]{1,0:T(8,128)S(1)}, u32[]{:S(2)}, u32[]{:S(2)}) collective-permute-start(f32[88,128]{1,0:T(8,128)S(1)} %get-tuple-element.140), channel_id=1, source_target_pairs={{2,0},{3,1},{6,4},{7,5},{10,8},{11,9},{14,12},{15,13},{18,16},{19,... | collective-permute-start | bytes 135176 | tf_op jit(solution)/shard_map/ppermute | solution.py:232
  76.2 3.2 %collective-permute-done.46.refs_4_ = f32[88,128]{1,0:T(8,128)S(1)} collective-permute-done((f32[88,128]{1,0:T(8,128)S(1)}, f32[88,128]{1,0:T(8,128)S(1)}, u32[]{:S(2)}, u32[]{:S(2)}) %collective-permute-start.46) | collective-permute-done | bytes 45088 | tf_op jit(solution)/shard_map/ppermute | solution.py:232
  79.7 1.0 %collective-permute-start.51 = (f32[72,128]{1,0:T(8,128)S(1)}, f32[72,128]{1,0:T(8,128)S(1)}, u32[]{:S(2)}, u32[]{:S(2)}) collective-permute-start(f32[72,128]{1,0:T(8,128)S(1)} %get-tuple-element.153), channel_id=1, source_target_pairs={{0,1},{1,0},{2,3},{3,2},{4,5},{5,4},{6,7},{7,6},{8,9},{9,8},{10,11... | collective-permute-start | bytes 110600 | tf_op jit(solution)/shard_map/ppermute | solution.py:232
  80.7 1.6 %collective-permute-start.50 = (f32[64,128]{1,0:T(8,128)S(1)}, f32[64,128]{1,0:T(8,128)S(1)}, u32[]{:S(2)}, u32[]{:S(2)}) collective-permute-start(f32[64,128]{1,0:T(8,128)S(1)} %get-tuple-element.152), channel_id=1, source_target_pairs={{0,2},{1,3},{4,6},{5,7},{8,10},{9,11},{12,14},{13,15},{16,18},{17,... | collective-permute-start | bytes 98312 | tf_op jit(solution)/shard_map/ppermute | solution.py:232
  82.3 1.1 %collective-permute-start.49 = (f32[128,128]{1,0:T(8,128)S(1)}, f32[128,128]{1,0:T(8,128)S(1)}, u32[]{:S(2)}, u32[]{:S(2)}) collective-permute-start(f32[128,128]{1,0:T(8,128)S(1)} %get-tuple-element.151), channel_id=1, source_target_pairs={{0,28},{4,8},{8,4},{12,16},{16,12},{20,24},{24,20},{28,0},{1,29},{... | collective-permute-start | bytes 196616 | tf_op jit(solution)/shard_map/ppermute | solution.py:230
  83.3 1.3 %collective-permute-start.53 = (f32[88,128]{1,0:T(8,128)S(1)}, f32[88,128]{1,0:T(8,128)S(1)}, u32[]{:S(2)}, u32[]{:S(2)}) collective-permute-start(f32[88,128]{1,0:T(8,128)S(1)} %get-tuple-element.155), channel_id=1, source_target_pairs={{2,0},{3,1},{6,4},{7,5},{10,8},{11,9},{14,12},{15,13},{18,16},{19,... | collective-permute-start | bytes 135176 | tf_op jit(solution)/shard_map/ppermute | solution.py:232
  85.2 0.8 local7.1
  86.1 3.2 %collective-permute-done.53.refs_4_ = f32[88,128]{1,0:T(8,128)S(1)} collective-permute-done((f32[88,128]{1,0:T(8,128)S(1)}, f32[88,128]{1,0:T(8,128)S(1)}, u32[]{:S(2)}, u32[]{:S(2)}) %collective-permute-start.53) | collective-permute-done | bytes 45088 | tf_op jit(solution)/shard_map/ppermute | solution.py:232
  89.3 0.9 final.1
  (81 shorter events, 11.3 us)
Async XLA Ops:
  2.5 10.4 %collective-permute-start.2 = (f32[80,128]{1,0:T(8,128)S(1)}, f32[80,128]{1,0:T(8,128)S(1)}, u32[]{:S(2)}, u32[]{:S(2)}) collective-permute-start(f32[80,128]{1,0:T(8,128)S(1)} %get-tuple-element.87), channel_id=1, source_target_pairs={{0,1},{1,0},{2,3},{3,2},{4,5},{5,4},{6,7},{7,6},{8,9},{9,8},{10,11... | collective-permute-start | bytes 122888 | tf_op jit(solution)/shard_map/ppermute | solution.py:232
  5.5 7.3 %collective-permute-start.1 = (f32[72,128]{1,0:T(8,128)S(1)}, f32[72,128]{1,0:T(8,128)S(1)}, u32[]{:S(2)}, u32[]{:S(2)}) collective-permute-start(f32[72,128]{1,0:T(8,128)S(1)} %get-tuple-element.86), channel_id=1, source_target_pairs={{0,2},{1,3},{4,6},{5,7},{8,10},{9,11},{12,14},{13,15},{16,18},{17,... | collective-permute-start | bytes 110600 | tf_op jit(solution)/shard_map/ppermute | solution.py:232
  9.0 8.5 %collective-permute-start = (f32[136,128]{1,0:T(8,128)S(1)}, f32[136,128]{1,0:T(8,128)S(1)}, u32[]{:S(2)}, u32[]{:S(2)}) collective-permute-start(f32[136,128]{1,0:T(8,128)S(1)} %get-tuple-element.85), channel_id=1, source_target_pairs={{0,28},{4,8},{8,4},{12,16},{16,12},{20,24},{24,20},{28,0},{1,29},{... | collective-permute-start | bytes 208904 | tf_op jit(solution)/shard_map/ppermute | solution.py:230
  11.5 6.0 %collective-permute-start.3 = (f32[104,128]{1,0:T(8,128)S(1)}, f32[104,128]{1,0:T(8,128)S(1)}, u32[]{:S(2)}, u32[]{:S(2)}) collective-permute-start(f32[104,128]{1,0:T(8,128)S(1)} %get-tuple-element.88), channel_id=1, source_target_pairs={{0,3},{1,2},{2,1},{3,0},{4,7},{5,6},{6,5},{7,4},{8,11},{9,10},{10,... | collective-permute-start | bytes 159752 | tf_op jit(solution)/shard_map/ppermute | solution.py:232
  11.5 6.0 %collective-permute-start.4 = (f32[96,128]{1,0:T(8,128)S(1)}, f32[96,128]{1,0:T(8,128)S(1)}, u32[]{:S(2)}, u32[]{:S(2)}) collective-permute-start(f32[96,128]{1,0:T(8,128)S(1)} %get-tuple-element.89), channel_id=1, source_target_pairs={{2,0},{3,1},{6,4},{7,5},{10,8},{11,9},{14,12},{15,13},{18,16},{19,... | collective-permute-start | bytes 147464 | tf_op jit(solution)/shard_map/ppermute | solution.py:232
  12.9 1.4 %collective-permute-start.6 = (f32[88,128]{1,0:T(8,128)S(1)}, f32[88,128]{1,0:T(8,128)S(1)}, u32[]{:S(2)}, u32[]{:S(2)}) collective-permute-start(f32[88,128]{1,0:T(8,128)S(1)} %get-tuple-element.91), channel_id=1, source_target_pairs={{0,4},{4,0},{8,12},{12,8},{16,20},{20,16},{24,28},{28,24},{1,5},{5... | collective-permute-start | bytes 135176 | tf_op jit(solution)/shard_map/ppermute | solution.py:233
  17.8 5.2 %collective-permute-start.9 = (f32[72,128]{1,0:T(8,128)S(1)}, f32[72,128]{1,0:T(8,128)S(1)}, u32[]{:S(2)}, u32[]{:S(2)}) collective-permute-start(f32[72,128]{1,0:T(8,128)S(1)} %get-tuple-element.95), channel_id=1, source_target_pairs={{0,1},{1,0},{2,3},{3,2},{4,5},{5,4},{6,7},{7,6},{8,9},{9,8},{10,11... | collective-permute-start | bytes 110600 | tf_op jit(solution)/shard_map/ppermute | solution.py:232
  19.0 4.0 %collective-permute-start.8 = (f32[64,128]{1,0:T(8,128)S(1)}, f32[64,128]{1,0:T(8,128)S(1)}, u32[]{:S(2)}, u32[]{:S(2)}) collective-permute-start(f32[64,128]{1,0:T(8,128)S(1)} %get-tuple-element.94), channel_id=1, source_target_pairs={{0,2},{1,3},{4,6},{5,7},{8,10},{9,11},{12,14},{13,15},{16,18},{17,... | collective-permute-start | bytes 98312 | tf_op jit(solution)/shard_map/ppermute | solution.py:232
  20.6 7.0 %collective-permute-start.7 = (f32[128,128]{1,0:T(8,128)S(1)}, f32[128,128]{1,0:T(8,128)S(1)}, u32[]{:S(2)}, u32[]{:S(2)}) collective-permute-start(f32[128,128]{1,0:T(8,128)S(1)} %get-tuple-element.93), channel_id=1, source_target_pairs={{0,28},{4,8},{8,4},{12,16},{16,12},{20,24},{24,20},{28,0},{1,29},{... | collective-permute-start | bytes 196616 | tf_op jit(solution)/shard_map/ppermute | solution.py:230
  20.8 6.8 %collective-permute-start.10 = (f32[96,128]{1,0:T(8,128)S(1)}, f32[96,128]{1,0:T(8,128)S(1)}, u32[]{:S(2)}, u32[]{:S(2)}) collective-permute-start(f32[96,128]{1,0:T(8,128)S(1)} %get-tuple-element.96), channel_id=1, source_target_pairs={{0,3},{1,2},{2,1},{3,0},{4,7},{5,6},{6,5},{7,4},{8,11},{9,10},{10,... | collective-permute-start | bytes 147464 | tf_op jit(solution)/shard_map/ppermute | solution.py:232
  21.7 5.9 %collective-permute-start.11 = (f32[88,128]{1,0:T(8,128)S(1)}, f32[88,128]{1,0:T(8,128)S(1)}, u32[]{:S(2)}, u32[]{:S(2)}) collective-permute-start(f32[88,128]{1,0:T(8,128)S(1)} %get-tuple-element.97), channel_id=1, source_target_pairs={{2,0},{3,1},{6,4},{7,5},{10,8},{11,9},{14,12},{15,13},{18,16},{19,... | collective-permute-start | bytes 135176 | tf_op jit(solution)/shard_map/ppermute | solution.py:232
  23.0 1.4 %collective-permute-start.13 = (f32[80,128]{1,0:T(8,128)S(1)}, f32[80,128]{1,0:T(8,128)S(1)}, u32[]{:S(2)}, u32[]{:S(2)}) collective-permute-start(f32[80,128]{1,0:T(8,128)S(1)} %get-tuple-element.99), channel_id=1, source_target_pairs={{0,4},{4,0},{8,12},{12,8},{16,20},{20,16},{24,28},{28,24},{1,5},{5... | collective-permute-start | bytes 122888 | tf_op jit(solution)/shard_map/ppermute | solution.py:233
  27.9 5.7 %collective-permute-start.16 = (f32[72,128]{1,0:T(8,128)S(1)}, f32[72,128]{1,0:T(8,128)S(1)}, u32[]{:S(2)}, u32[]{:S(2)}) collective-permute-start(f32[72,128]{1,0:T(8,128)S(1)} %get-tuple-element.103), channel_id=1, source_target_pairs={{0,1},{1,0},{2,3},{3,2},{4,5},{5,4},{6,7},{7,6},{8,9},{9,8},{10,11... | collective-permute-start | bytes 110600 | tf_op jit(solution)/shard_map/ppermute | solution.py:232
  28.9 4.7 %collective-permute-start.15 = (f32[64,128]{1,0:T(8,128)S(1)}, f32[64,128]{1,0:T(8,128)S(1)}, u32[]{:S(2)}, u32[]{:S(2)}) collective-permute-start(f32[64,128]{1,0:T(8,128)S(1)} %get-tuple-element.102), channel_id=1, source_target_pairs={{0,2},{1,3},{4,6},{5,7},{8,10},{9,11},{12,14},{13,15},{16,18},{17,... | collective-permute-start | bytes 98312 | tf_op jit(solution)/shard_map/ppermute | solution.py:232
  30.5 7.7 %collective-permute-start.14 = (f32[128,128]{1,0:T(8,128)S(1)}, f32[128,128]{1,0:T(8,128)S(1)}, u32[]{:S(2)}, u32[]{:S(2)}) collective-permute-start(f32[128,128]{1,0:T(8,128)S(1)} %get-tuple-element.101), channel_id=1, source_target_pairs={{0,28},{4,8},{8,4},{12,16},{16,12},{20,24},{24,20},{28,0},{1,29},{... | collective-permute-start | bytes 196616 | tf_op jit(solution)/shard_map/ppermute | solution.py:230
  32.0 6.2 %collective-permute-start.17 = (f32[96,128]{1,0:T(8,128)S(1)}, f32[96,128]{1,0:T(8,128)S(1)}, u32[]{:S(2)}, u32[]{:S(2)}) collective-permute-start(f32[96,128]{1,0:T(8,128)S(1)} %get-tuple-element.104), channel_id=1, source_target_pairs={{0,3},{1,2},{2,1},{3,0},{4,7},{5,6},{6,5},{7,4},{8,11},{9,10},{10,... | collective-permute-start | bytes 147464 | tf_op jit(solution)/shard_map/ppermute | solution.py:232
  32.2 5.9 %collective-permute-start.18 = (f32[88,128]{1,0:T(8,128)S(1)}, f32[88,128]{1,0:T(8,128)S(1)}, u32[]{:S(2)}, u32[]{:S(2)}) collective-permute-start(f32[88,128]{1,0:T(8,128)S(1)} %get-tuple-element.105), channel_id=1, source_target_pairs={{2,0},{3,1},{6,4},{7,5},{10,8},{11,9},{14,12},{15,13},{18,16},{19,... | collective-permute-start | bytes 135176 | tf_op jit(solution)/shard_map/ppermute | solution.py:232
  33.6 1.4 %collective-permute-start.20 = (f32[80,128]{1,0:T(8,128)S(1)}, f32[80,128]{1,0:T(8,128)S(1)}, u32[]{:S(2)}, u32[]{:S(2)}) collective-permute-start(f32[80,128]{1,0:T(8,128)S(1)} %get-tuple-element.107), channel_id=1, source_target_pairs={{0,4},{4,0},{8,12},{12,8},{16,20},{20,16},{24,28},{28,24},{1,5},{5... | collective-permute-start | bytes 122888 | tf_op jit(solution)/shard_map/ppermute | solution.py:233
  38.5 5.0 %collective-permute-start.23 = (f32[72,128]{1,0:T(8,128)S(1)}, f32[72,128]{1,0:T(8,128)S(1)}, u32[]{:S(2)}, u32[]{:S(2)}) collective-permute-start(f32[72,128]{1,0:T(8,128)S(1)} %get-tuple-element.111), channel_id=1, source_target_pairs={{0,1},{1,0},{2,3},{3,2},{4,5},{5,4},{6,7},{7,6},{8,9},{9,8},{10,11... | collective-permute-start | bytes 110600 | tf_op jit(solution)/shard_map/ppermute | solution.py:232
  39.5 4.0 %collective-permute-start.22 = (f32[64,128]{1,0:T(8,128)S(1)}, f32[64,128]{1,0:T(8,128)S(1)}, u32[]{:S(2)}, u32[]{:S(2)}) collective-permute-start(f32[64,128]{1,0:T(8,128)S(1)} %get-tuple-element.110), channel_id=1, source_target_pairs={{0,2},{1,3},{4,6},{5,7},{8,10},{9,11},{12,14},{13,15},{16,18},{17,... | collective-permute-start | bytes 98312 | tf_op jit(solution)/shard_map/ppermute | solution.py:232
  41.1 7.0 %collective-permute-start.21 = (f32[128,128]{1,0:T(8,128)S(1)}, f32[128,128]{1,0:T(8,128)S(1)}, u32[]{:S(2)}, u32[]{:S(2)}) collective-permute-start(f32[128,128]{1,0:T(8,128)S(1)} %get-tuple-element.109), channel_id=1, source_target_pairs={{0,28},{4,8},{8,4},{12,16},{16,12},{20,24},{24,20},{28,0},{1,29},{... | collective-permute-start | bytes 196616 | tf_op jit(solution)/shard_map/ppermute | solution.py:230
  42.1 5.9 %collective-permute-start.24 = (f32[96,128]{1,0:T(8,128)S(1)}, f32[96,128]{1,0:T(8,128)S(1)}, u32[]{:S(2)}, u32[]{:S(2)}) collective-permute-start(f32[96,128]{1,0:T(8,128)S(1)} %get-tuple-element.112), channel_id=1, source_target_pairs={{0,3},{1,2},{2,1},{3,0},{4,7},{5,6},{6,5},{7,4},{8,11},{9,10},{10,... | collective-permute-start | bytes 147464 | tf_op jit(solution)/shard_map/ppermute | solution.py:232
  42.1 5.9 %collective-permute-start.25 = (f32[88,128]{1,0:T(8,128)S(1)}, f32[88,128]{1,0:T(8,128)S(1)}, u32[]{:S(2)}, u32[]{:S(2)}) collective-permute-start(f32[88,128]{1,0:T(8,128)S(1)} %get-tuple-element.113), channel_id=1, source_target_pairs={{2,0},{3,1},{6,4},{7,5},{10,8},{11,9},{14,12},{15,13},{18,16},{19,... | collective-permute-start | bytes 135176 | tf_op jit(solution)/shard_map/ppermute | solution.py:232
  43.5 1.4 %collective-permute-start.27 = (f32[80,128]{1,0:T(8,128)S(1)}, f32[80,128]{1,0:T(8,128)S(1)}, u32[]{:S(2)}, u32[]{:S(2)}) collective-permute-start(f32[80,128]{1,0:T(8,128)S(1)} %get-tuple-element.115), channel_id=1, source_target_pairs={{0,4},{4,0},{8,12},{12,8},{16,20},{20,16},{24,28},{28,24},{1,5},{5... | collective-permute-start | bytes 122888 | tf_op jit(solution)/shard_map/ppermute | solution.py:233
  48.4 5.7 %collective-permute-start.30 = (f32[72,128]{1,0:T(8,128)S(1)}, f32[72,128]{1,0:T(8,128)S(1)}, u32[]{:S(2)}, u32[]{:S(2)}) collective-permute-start(f32[72,128]{1,0:T(8,128)S(1)} %get-tuple-element.120), channel_id=1, source_target_pairs={{0,1},{1,0},{2,3},{3,2},{4,5},{5,4},{6,7},{7,6},{8,9},{9,8},{10,11... | collective-permute-start | bytes 110600 | tf_op jit(solution)/shard_map/ppermute | solution.py:232
  49.6 4.4 %collective-permute-start.29 = (f32[64,128]{1,0:T(8,128)S(1)}, f32[64,128]{1,0:T(8,128)S(1)}, u32[]{:S(2)}, u32[]{:S(2)}) collective-permute-start(f32[64,128]{1,0:T(8,128)S(1)} %get-tuple-element.119), channel_id=1, source_target_pairs={{0,2},{1,3},{4,6},{5,7},{8,10},{9,11},{12,14},{13,15},{16,18},{17,... | collective-permute-start | bytes 98312 | tf_op jit(solution)/shard_map/ppermute | solution.py:232
  51.2 7.5 %collective-permute-start.28 = (f32[128,128]{1,0:T(8,128)S(1)}, f32[128,128]{1,0:T(8,128)S(1)}, u32[]{:S(2)}, u32[]{:S(2)}) collective-permute-start(f32[128,128]{1,0:T(8,128)S(1)} %get-tuple-element.118), channel_id=1, source_target_pairs={{0,28},{4,8},{8,4},{12,16},{16,12},{20,24},{24,20},{28,0},{1,29},{... | collective-permute-start | bytes 196616 | tf_op jit(solution)/shard_map/ppermute | solution.py:230
  52.7 5.9 %collective-permute-start.31 = (f32[96,128]{1,0:T(8,128)S(1)}, f32[96,128]{1,0:T(8,128)S(1)}, u32[]{:S(2)}, u32[]{:S(2)}) collective-permute-start(f32[96,128]{1,0:T(8,128)S(1)} %get-tuple-element.121), channel_id=1, source_target_pairs={{0,3},{1,2},{2,1},{3,0},{4,7},{5,6},{6,5},{7,4},{8,11},{9,10},{10,... | collective-permute-start | bytes 147464 | tf_op jit(solution)/shard_map/ppermute | solution.py:232
  52.7 5.9 %collective-permute-start.32 = (f32[88,128]{1,0:T(8,128)S(1)}, f32[88,128]{1,0:T(8,128)S(1)}, u32[]{:S(2)}, u32[]{:S(2)}) collective-permute-start(f32[88,128]{1,0:T(8,128)S(1)} %get-tuple-element.122), channel_id=1, source_target_pairs={{2,0},{3,1},{6,4},{7,5},{10,8},{11,9},{14,12},{15,13},{18,16},{19,... | collective-permute-start | bytes 135176 | tf_op jit(solution)/shard_map/ppermute | solution.py:232
  54.1 1.4 %collective-permute-start.34 = (f32[80,128]{1,0:T(8,128)S(1)}, f32[80,128]{1,0:T(8,128)S(1)}, u32[]{:S(2)}, u32[]{:S(2)}) collective-permute-start(f32[80,128]{1,0:T(8,128)S(1)} %get-tuple-element.124), channel_id=1, source_target_pairs={{0,4},{4,0},{8,12},{12,8},{16,20},{20,16},{24,28},{28,24},{1,5},{5... | collective-permute-start | bytes 122888 | tf_op jit(solution)/shard_map/ppermute | solution.py:233
  59.0 5.2 %collective-permute-start.37 = (f32[72,128]{1,0:T(8,128)S(1)}, f32[72,128]{1,0:T(8,128)S(1)}, u32[]{:S(2)}, u32[]{:S(2)}) collective-permute-start(f32[72,128]{1,0:T(8,128)S(1)} %get-tuple-element.129), channel_id=1, source_target_pairs={{0,1},{1,0},{2,3},{3,2},{4,5},{5,4},{6,7},{7,6},{8,9},{9,8},{10,11... | collective-permute-start | bytes 110600 | tf_op jit(solution)/shard_map/ppermute | solution.py:232
  60.2 4.0 %collective-permute-start.36 = (f32[64,128]{1,0:T(8,128)S(1)}, f32[64,128]{1,0:T(8,128)S(1)}, u32[]{:S(2)}, u32[]{:S(2)}) collective-permute-start(f32[64,128]{1,0:T(8,128)S(1)} %get-tuple-element.128), channel_id=1, source_target_pairs={{0,2},{1,3},{4,6},{5,7},{8,10},{9,11},{12,14},{13,15},{16,18},{17,... | collective-permute-start | bytes 98312 | tf_op jit(solution)/shard_map/ppermute | solution.py:232
  61.8 7.0 %collective-permute-start.35 = (f32[128,128]{1,0:T(8,128)S(1)}, f32[128,128]{1,0:T(8,128)S(1)}, u32[]{:S(2)}, u32[]{:S(2)}) collective-permute-start(f32[128,128]{1,0:T(8,128)S(1)} %get-tuple-element.127), channel_id=1, source_target_pairs={{0,28},{4,8},{8,4},{12,16},{16,12},{20,24},{24,20},{28,0},{1,29},{... | collective-permute-start | bytes 196616 | tf_op jit(solution)/shard_map/ppermute | solution.py:230
  62.6 6.2 %collective-permute-start.38 = (f32[96,128]{1,0:T(8,128)S(1)}, f32[96,128]{1,0:T(8,128)S(1)}, u32[]{:S(2)}, u32[]{:S(2)}) collective-permute-start(f32[96,128]{1,0:T(8,128)S(1)} %get-tuple-element.130), channel_id=1, source_target_pairs={{0,3},{1,2},{2,1},{3,0},{4,7},{5,6},{6,5},{7,4},{8,11},{9,10},{10,... | collective-permute-start | bytes 147464 | tf_op jit(solution)/shard_map/ppermute | solution.py:232
  62.9 5.9 %collective-permute-start.39 = (f32[88,128]{1,0:T(8,128)S(1)}, f32[88,128]{1,0:T(8,128)S(1)}, u32[]{:S(2)}, u32[]{:S(2)}) collective-permute-start(f32[88,128]{1,0:T(8,128)S(1)} %get-tuple-element.131), channel_id=1, source_target_pairs={{2,0},{3,1},{6,4},{7,5},{10,8},{11,9},{14,12},{15,13},{18,16},{19,... | collective-permute-start | bytes 135176 | tf_op jit(solution)/shard_map/ppermute | solution.py:232
  64.2 1.4 %collective-permute-start.41 = (f32[80,128]{1,0:T(8,128)S(1)}, f32[80,128]{1,0:T(8,128)S(1)}, u32[]{:S(2)}, u32[]{:S(2)}) collective-permute-start(f32[80,128]{1,0:T(8,128)S(1)} %get-tuple-element.133), channel_id=1, source_target_pairs={{0,4},{4,0},{8,12},{12,8},{16,20},{20,16},{24,28},{28,24},{1,5},{5... | collective-permute-start | bytes 122888 | tf_op jit(solution)/shard_map/ppermute | solution.py:233
  69.1 5.7 %collective-permute-start.44 = (f32[72,128]{1,0:T(8,128)S(1)}, f32[72,128]{1,0:T(8,128)S(1)}, u32[]{:S(2)}, u32[]{:S(2)}) collective-permute-start(f32[72,128]{1,0:T(8,128)S(1)} %get-tuple-element.138), channel_id=1, source_target_pairs={{0,1},{1,0},{2,3},{3,2},{4,5},{5,4},{6,7},{7,6},{8,9},{9,8},{10,11... | collective-permute-start | bytes 110600 | tf_op jit(solution)/shard_map/ppermute | solution.py:232
  70.1 4.7 %collective-permute-start.43 = (f32[64,128]{1,0:T(8,128)S(1)}, f32[64,128]{1,0:T(8,128)S(1)}, u32[]{:S(2)}, u32[]{:S(2)}) collective-permute-start(f32[64,128]{1,0:T(8,128)S(1)} %get-tuple-element.137), channel_id=1, source_target_pairs={{0,2},{1,3},{4,6},{5,7},{8,10},{9,11},{12,14},{13,15},{16,18},{17,... | collective-permute-start | bytes 98312 | tf_op jit(solution)/shard_map/ppermute | solution.py:232
  71.7 7.7 %collective-permute-start.42 = (f32[128,128]{1,0:T(8,128)S(1)}, f32[128,128]{1,0:T(8,128)S(1)}, u32[]{:S(2)}, u32[]{:S(2)}) collective-permute-start(f32[128,128]{1,0:T(8,128)S(1)} %get-tuple-element.136), channel_id=1, source_target_pairs={{0,28},{4,8},{8,4},{12,16},{16,12},{20,24},{24,20},{28,0},{1,29},{... | collective-permute-start | bytes 196616 | tf_op jit(solution)/shard_map/ppermute | solution.py:230
  73.2 6.2 %collective-permute-start.45 = (f32[96,128]{1,0:T(8,128)S(1)}, f32[96,128]{1,0:T(8,128)S(1)}, u32[]{:S(2)}, u32[]{:S(2)}) collective-permute-start(f32[96,128]{1,0:T(8,128)S(1)} %get-tuple-element.139), channel_id=1, source_target_pairs={{0,3},{1,2},{2,1},{3,0},{4,7},{5,6},{6,5},{7,4},{8,11},{9,10},{10,... | collective-permute-start | bytes 147464 | tf_op jit(solution)/shard_map/ppermute | solution.py:232
  73.4 5.9 %collective-permute-start.46 = (f32[88,128]{1,0:T(8,128)S(1)}, f32[88,128]{1,0:T(8,128)S(1)}, u32[]{:S(2)}, u32[]{:S(2)}) collective-permute-start(f32[88,128]{1,0:T(8,128)S(1)} %get-tuple-element.140), channel_id=1, source_target_pairs={{2,0},{3,1},{6,4},{7,5},{10,8},{11,9},{14,12},{15,13},{18,16},{19,... | collective-permute-start | bytes 135176 | tf_op jit(solution)/shard_map/ppermute | solution.py:232
  74.8 1.4 %collective-permute-start.48 = (f32[80,128]{1,0:T(8,128)S(1)}, f32[80,128]{1,0:T(8,128)S(1)}, u32[]{:S(2)}, u32[]{:S(2)}) collective-permute-start(f32[80,128]{1,0:T(8,128)S(1)} %get-tuple-element.142), channel_id=1, source_target_pairs={{0,4},{4,0},{8,12},{12,8},{16,20},{20,16},{24,28},{28,24},{1,5},{5... | collective-permute-start | bytes 122888 | tf_op jit(solution)/shard_map/ppermute | solution.py:233
  79.7 5.0 %collective-permute-start.51 = (f32[72,128]{1,0:T(8,128)S(1)}, f32[72,128]{1,0:T(8,128)S(1)}, u32[]{:S(2)}, u32[]{:S(2)}) collective-permute-start(f32[72,128]{1,0:T(8,128)S(1)} %get-tuple-element.153), channel_id=1, source_target_pairs={{0,1},{1,0},{2,3},{3,2},{4,5},{5,4},{6,7},{7,6},{8,9},{9,8},{10,11... | collective-permute-start | bytes 110600 | tf_op jit(solution)/shard_map/ppermute | solution.py:232
  80.7 4.0 %collective-permute-start.50 = (f32[64,128]{1,0:T(8,128)S(1)}, f32[64,128]{1,0:T(8,128)S(1)}, u32[]{:S(2)}, u32[]{:S(2)}) collective-permute-start(f32[64,128]{1,0:T(8,128)S(1)} %get-tuple-element.152), channel_id=1, source_target_pairs={{0,2},{1,3},{4,6},{5,7},{8,10},{9,11},{12,14},{13,15},{16,18},{17,... | collective-permute-start | bytes 98312 | tf_op jit(solution)/shard_map/ppermute | solution.py:232
  82.3 7.0 %collective-permute-start.49 = (f32[128,128]{1,0:T(8,128)S(1)}, f32[128,128]{1,0:T(8,128)S(1)}, u32[]{:S(2)}, u32[]{:S(2)}) collective-permute-start(f32[128,128]{1,0:T(8,128)S(1)} %get-tuple-element.151), channel_id=1, source_target_pairs={{0,28},{4,8},{8,4},{12,16},{16,12},{20,24},{24,20},{28,0},{1,29},{... | collective-permute-start | bytes 196616 | tf_op jit(solution)/shard_map/ppermute | solution.py:230
  83.3 5.9 %collective-permute-start.52 = (f32[96,128]{1,0:T(8,128)S(1)}, f32[96,128]{1,0:T(8,128)S(1)}, u32[]{:S(2)}, u32[]{:S(2)}) collective-permute-start(f32[96,128]{1,0:T(8,128)S(1)} %get-tuple-element.154), channel_id=1, source_target_pairs={{0,3},{1,2},{2,1},{3,0},{4,7},{5,6},{6,5},{7,4},{8,11},{9,10},{10,... | collective-permute-start | bytes 147464 | tf_op jit(solution)/shard_map/ppermute | solution.py:232
  83.3 5.9 %collective-permute-start.53 = (f32[88,128]{1,0:T(8,128)S(1)}, f32[88,128]{1,0:T(8,128)S(1)}, u32[]{:S(2)}, u32[]{:S(2)}) collective-permute-start(f32[88,128]{1,0:T(8,128)S(1)} %get-tuple-element.155), channel_id=1, source_target_pairs={{2,0},{3,1},{6,4},{7,5},{10,8},{11,9},{14,12},{15,13},{18,16},{19,... | collective-permute-start | bytes 135176 | tf_op jit(solution)/shard_map/ppermute | solution.py:232
  84.6 1.4 %collective-permute-start.54 = (f32[80,128]{1,0:T(8,128)S(1)}, f32[80,128]{1,0:T(8,128)S(1)}, u32[]{:S(2)}, u32[]{:S(2)}) collective-permute-start(f32[80,128]{1,0:T(8,128)S(1)} %get-tuple-element.156), channel_id=1, source_target_pairs={{0,4},{4,0},{8,12},{12,8},{16,20},{20,16},{24,28},{28,24},{1,5},{5... | collective-permute-start | bytes 122888 | tf_op jit(solution)/shard_map/ppermute | solution.py:233
  (8 other events, 10.4 us)

commit v10 on v7

--- a/solution.py
+++ b/solution.py
@@ -25,7 +25,7 @@
         self.rows, self.n, self.w, self.group = rows, rhs_count, width, group
         self.quarter = rows // COLORS
         self.lanes = group + self.quarter
-        self.distances = [1] + list(reversed(range(2, group)))
+        self.distances = list(reversed(range(1, group)))
         self.order, self.local, self.slot = 0, rows, 3 * rows
         self.table = 5 * rows
         self.dom_meta = -(-rows // 8) * 8
@@ -92,7 +92,7 @@
     copies = [
         pltpu.make_async_copy(src, dst, sems.at[i]) for i, (src, dst) in enumerate(zip(hbm, targets))
     ]
-    for copy in copies:
+    for copy in copies[7:] + copies[:7]:
         copy.start()
     for copy in copies[:5]:
         copy.wait()

time: 68.5 us -> 68.4 us (level)
    ppermute x8, starting transfers between devices: 8.65 us -> 11.1 us  [exchange(): got = [lax.ppermute(sends[0], 'dom', far_pairs)]]
    ppermute x24, starting transfers between devices: 29.4 us -> 27.9 us  [exchange(): got.append(lax.ppermute(send, 'sub', [(i, i ^ s) for i in range(group)]))]
    ppermute x16, starting transfers between devices: 2.6 us -> 1.17 us  [exchange(): lax.ppermute(send, 'dom', near_pairs)]
  transfers between devices with their start and end apart: 48 -> 48, of which waited for: 21 -> 24; matrix products, arithmetic and copies ran while one was open for 0% -> 0% of each run, Pallas kernels for 3% -> 3%
where the time goes in v10:
time: 68.4 us; the launch traced here: 68.2 us
  starting transfers between devices  40.1 us (59%)
  waiting for transfers between devices  20.1 us (29%)
  Pallas kernels  7.24 us (11%)
  between operations  0.79 us (1%)
    ppermute x24, starting transfers between devices, exchange(): got.append(lax.ppermute(send, 'sub', [(i, i ^ s) for i in range(group)]))  27.9 us
    ppermute x24, waiting for transfers between devices, exchange(): got.append(lax.ppermute(send, 'sub', [(i, i ^ s) for i in range(group)]))  19.7 us
    ppermute x8, starting transfers between devices, exchange(): got = [lax.ppermute(sends[0], 'dom', far_pairs)]  11.1 us
    pallas_call x17, Pallas kernels, call(): pl.pallas_call(body, name=name, in_specs=in_specs + [VMEM] * (len(ins) -...  7.24 us
  transfers between devices with their start and end apart: 48, of which 24 were waited for; matrix products, arithmetic and copies ran while one was open for 0% of the time, Pallas kernels for 3%

profile of v10, /device:TPU:0, one launch (start us, length us, event | category | flops | bytes accessed | tf_op | source)
XLA Modules:
  0.0 68.2 jit_solution(14814074709036046312)
XLA Ops:
  0.6 1.9 %first.1 = (s32[40]{0:T(128)S(4)}, bf16[8,6,128,128]{3,2,1,0:T(8,128)(2,1)S(1)}, bf16[8,128,128]{2,1,0:T(8,128)(2,1)S(1)}, f32[8,64,128]{2,1,0:T(8,128)S(1)}, f3...) custom-call(s32[8]{0:T(128)} %refs_0_.1, ...), custom_call_target="tpu_custom_call" | custom-call | tf_op jit(solution)/shard_map/first/pallas_call | solution.py:213
  2.6 4.0 %collective-permute-start.1 = (f32[72,128]{1,0:T(8,128)S(1)}, f32[72,128]{1,0:T(8,128)S(1)}, u32[]{:S(2)}, u32[]{:S(2)}) collective-permute-start(f32[72,128]{1,0:T(8,128)S(1)} %get-tuple-element.78), channel_id=1, source_target_pairs={{0,3},{1,2},{2,1},{3,0},{4,7},{5,6},{6,5},{7,4},{8,11},{9,10},{10,... | collective-permute-start | bytes 110600 | tf_op jit(solution)/shard_map/ppermute | solution.py:226
  6.5 2.8 %collective-permute-start = (f32[136,128]{1,0:T(8,128)S(1)}, f32[136,128]{1,0:T(8,128)S(1)}, u32[]{:S(2)}, u32[]{:S(2)}) collective-permute-start(f32[136,128]{1,0:T(8,128)S(1)} %get-tuple-element.77), channel_id=1, source_target_pairs={{0,28},{4,8},{8,4},{12,16},{16,12},{20,24},{24,20},{28,0},{1,29},{... | collective-permute-start | bytes 208904 | tf_op jit(solution)/shard_map/ppermute | solution.py:224
  9.8 0.5 collective-permute-start.3
  10.3 0.5 collective-permute-start.5
  11.0 2.2 %collective-permute-done.2.refs_2_.refs_8_ = f32[72,128]{1,0:T(8,128)S(1)} collective-permute-done((f32[72,128]{1,0:T(8,128)S(1)}, f32[72,128]{1,0:T(8,128)S(1)}, u32[]{:S(2)}, u32[]{:S(2)}) %collective-permute-start.2) | collective-permute-done | bytes 36896 | tf_op jit(solution)/shard_map/ppermute | solution.py:226
  14.1 1.6 %collective-permute-start.7 = (f32[64,128]{1,0:T(8,128)S(1)}, f32[64,128]{1,0:T(8,128)S(1)}, u32[]{:S(2)}, u32[]{:S(2)}) collective-permute-start(f32[64,128]{1,0:T(8,128)S(1)} %get-tuple-element.85), channel_id=1, source_target_pairs={{0,3},{1,2},{2,1},{3,0},{4,7},{5,6},{6,5},{7,4},{8,11},{9,10},{10,... | collective-permute-start | bytes 98312 | tf_op jit(solution)/shard_map/ppermute | solution.py:226
  15.7 0.7 %collective-permute-start.6 = (f32[128,128]{1,0:T(8,128)S(1)}, f32[128,128]{1,0:T(8,128)S(1)}, u32[]{:S(2)}, u32[]{:S(2)}) collective-permute-start(f32[128,128]{1,0:T(8,128)S(1)} %get-tuple-element.84), channel_id=1, source_target_pairs={{0,28},{4,8},{8,4},{12,16},{16,12},{20,24},{24,20},{28,0},{1,29},{... | collective-permute-start | bytes 196616 | tf_op jit(solution)/shard_map/ppermute | solution.py:224
  16.4 0.5 collective-permute-start.8
  16.9 1.5 %collective-permute-start.9 = (f32[64,128]{1,0:T(8,128)S(1)}, f32[64,128]{1,0:T(8,128)S(1)}, u32[]{:S(2)}, u32[]{:S(2)}) collective-permute-start(f32[64,128]{1,0:T(8,128)S(1)} %get-tuple-element.87), channel_id=1, source_target_pairs={{0,1},{1,0},{2,3},{3,2},{4,5},{5,4},{6,7},{7,6},{8,9},{9,8},{10,11... | collective-permute-start | bytes 98312 | tf_op jit(solution)/shard_map/ppermute | solution.py:226
  18.4 0.7 %collective-permute-done.7.refs_1_ = f32[64,128]{1,0:T(8,128)S(1)} collective-permute-done((f32[64,128]{1,0:T(8,128)S(1)}, f32[64,128]{1,0:T(8,128)S(1)}, u32[]{:S(2)}, u32[]{:S(2)}) %collective-permute-start.7) | collective-permute-done | bytes 32800 | tf_op jit(solution)/shard_map/ppermute | solution.py:226
  19.4 0.9 %collective-permute-done.8.refs_2_ = f32[64,128]{1,0:T(8,128)S(1)} collective-permute-done((f32[64,128]{1,0:T(8,128)S(1)}, f32[64,128]{1,0:T(8,128)S(1)}, u32[]{:S(2)}, u32[]{:S(2)}) %collective-permute-start.8) | collective-permute-done | bytes 32800 | tf_op jit(solution)/shard_map/ppermute | solution.py:226
  20.3 0.5 collective-permute-done.9.refs_3_
  21.5 1.5 %collective-permute-start.13 = (f32[64,128]{1,0:T(8,128)S(1)}, f32[64,128]{1,0:T(8,128)S(1)}, u32[]{:S(2)}, u32[]{:S(2)}) collective-permute-start(f32[64,128]{1,0:T(8,128)S(1)} %get-tuple-element.92), channel_id=1, source_target_pairs={{0,3},{1,2},{2,1},{3,0},{4,7},{5,6},{6,5},{7,4},{8,11},{9,10},{10,... | collective-permute-start | bytes 98312 | tf_op jit(solution)/shard_map/ppermute | solution.py:226
  23.0 1.8 %collective-permute-start.12 = (f32[128,128]{1,0:T(8,128)S(1)}, f32[128,128]{1,0:T(8,128)S(1)}, u32[]{:S(2)}, u32[]{:S(2)}) collective-permute-start(f32[128,128]{1,0:T(8,128)S(1)} %get-tuple-element.91), channel_id=1, source_target_pairs={{0,28},{4,8},{8,4},{12,16},{16,12},{20,24},{24,20},{28,0},{1,29},{... | collective-permute-start | bytes 196616 | tf_op jit(solution)/shard_map/ppermute | solution.py:224
  24.8 0.5 collective-permute-start.14
  25.3 0.5 collective-permute-start.15
  25.8 0.5 collective-permute-done.13.refs_1_
  26.6 2.1 %collective-permute-done.14.refs_2_ = f32[64,128]{1,0:T(8,128)S(1)} collective-permute-done((f32[64,128]{1,0:T(8,128)S(1)}, f32[64,128]{1,0:T(8,128)S(1)}, u32[]{:S(2)}, u32[]{:S(2)}) %collective-permute-start.14) | collective-permute-done | bytes 32800 | tf_op jit(solution)/shard_map/ppermute | solution.py:226
  29.5 1.6 %collective-permute-start.19 = (f32[64,128]{1,0:T(8,128)S(1)}, f32[64,128]{1,0:T(8,128)S(1)}, u32[]{:S(2)}, u32[]{:S(2)}) collective-permute-start(f32[64,128]{1,0:T(8,128)S(1)} %get-tuple-element.99), channel_id=1, source_target_pairs={{0,3},{1,2},{2,1},{3,0},{4,7},{5,6},{6,5},{7,4},{8,11},{9,10},{10,... | collective-permute-start | bytes 98312 | tf_op jit(solution)/shard_map/ppermute | solution.py:226
  31.1 0.7 %collective-permute-start.18 = (f32[128,128]{1,0:T(8,128)S(1)}, f32[128,128]{1,0:T(8,128)S(1)}, u32[]{:S(2)}, u32[]{:S(2)}) collective-permute-start(f32[128,128]{1,0:T(8,128)S(1)} %get-tuple-element.98), channel_id=1, source_target_pairs={{0,28},{4,8},{8,4},{12,16},{16,12},{20,24},{24,20},{28,0},{1,29},{... | collective-permute-start | bytes 196616 | tf_op jit(solution)/shard_map/ppermute | solution.py:224
  31.8 0.8 %collective-permute-start.20 = (f32[64,128]{1,0:T(8,128)S(1)}, f32[64,128]{1,0:T(8,128)S(1)}, u32[]{:S(2)}, u32[]{:S(2)}) collective-permute-start(f32[64,128]{1,0:T(8,128)S(1)} %get-tuple-element.100), channel_id=1, source_target_pairs={{0,2},{1,3},{2,0},{3,1},{4,6},{5,7},{6,4},{7,5},{8,10},{9,11},{10,... | collective-permute-start | bytes 98312 | tf_op jit(solution)/shard_map/ppermute | solution.py:226
  32.6 1.5 %collective-permute-start.21 = (f32[64,128]{1,0:T(8,128)S(1)}, f32[64,128]{1,0:T(8,128)S(1)}, u32[]{:S(2)}, u32[]{:S(2)}) collective-permute-start(f32[64,128]{1,0:T(8,128)S(1)} %get-tuple-element.101), channel_id=1, source_target_pairs={{0,1},{1,0},{2,3},{3,2},{4,5},{5,4},{6,7},{7,6},{8,9},{9,8},{10,11... | collective-permute-start | bytes 98312 | tf_op jit(solution)/shard_map/ppermute | solution.py:226
  34.8 0.9 %collective-permute-done.20.refs_2_ = f32[64,128]{1,0:T(8,128)S(1)} collective-permute-done((f32[64,128]{1,0:T(8,128)S(1)}, f32[64,128]{1,0:T(8,128)S(1)}, u32[]{:S(2)}, u32[]{:S(2)}) %collective-permute-start.20) | collective-permute-done | bytes 32800 | tf_op jit(solution)/shard_map/ppermute | solution.py:226
  35.7 0.8 %collective-permute-done.21.refs_3_ = f32[64,128]{1,0:T(8,128)S(1)} collective-permute-done((f32[64,128]{1,0:T(8,128)S(1)}, f32[64,128]{1,0:T(8,128)S(1)}, u32[]{:S(2)}, u32[]{:S(2)}) %collective-permute-start.21) | collective-permute-done | bytes 32800 | tf_op jit(solution)/shard_map/ppermute | solution.py:226
  36.9 1.5 %collective-permute-start.25 = (f32[64,128]{1,0:T(8,128)S(1)}, f32[64,128]{1,0:T(8,128)S(1)}, u32[]{:S(2)}, u32[]{:S(2)}) collective-permute-start(f32[64,128]{1,0:T(8,128)S(1)} %get-tuple-element.107), channel_id=1, source_target_pairs={{0,3},{1,2},{2,1},{3,0},{4,7},{5,6},{6,5},{7,4},{8,11},{9,10},{10,... | collective-permute-start | bytes 98312 | tf_op jit(solution)/shard_map/ppermute | solution.py:226
  38.4 1.8 %collective-permute-start.24 = (f32[128,128]{1,0:T(8,128)S(1)}, f32[128,128]{1,0:T(8,128)S(1)}, u32[]{:S(2)}, u32[]{:S(2)}) collective-permute-start(f32[128,128]{1,0:T(8,128)S(1)} %get-tuple-element.106), channel_id=1, source_target_pairs={{0,28},{4,8},{8,4},{12,16},{16,12},{20,24},{24,20},{28,0},{1,29},{... | collective-permute-start | bytes 196616 | tf_op jit(solution)/shard_map/ppermute | solution.py:224
  40.7 0.5 collective-permute-start.27
  41.2 0.5 collective-permute-done.25.refs_1_
  42.0 2.1 %collective-permute-done.26.refs_2_ = f32[64,128]{1,0:T(8,128)S(1)} collective-permute-done((f32[64,128]{1,0:T(8,128)S(1)}, f32[64,128]{1,0:T(8,128)S(1)}, u32[]{:S(2)}, u32[]{:S(2)}) %collective-permute-start.26) | collective-permute-done | bytes 32800 | tf_op jit(solution)/shard_map/ppermute | solution.py:226
  44.9 1.6 %collective-permute-start.31 = (f32[64,128]{1,0:T(8,128)S(1)}, f32[64,128]{1,0:T(8,128)S(1)}, u32[]{:S(2)}, u32[]{:S(2)}) collective-permute-start(f32[64,128]{1,0:T(8,128)S(1)} %get-tuple-element.115), channel_id=1, source_target_pairs={{0,3},{1,2},{2,1},{3,0},{4,7},{5,6},{6,5},{7,4},{8,11},{9,10},{10,... | collective-permute-start | bytes 98312 | tf_op jit(solution)/shard_map/ppermute | solution.py:226
  46.5 0.7 %collective-permute-start.30 = (f32[128,128]{1,0:T(8,128)S(1)}, f32[128,128]{1,0:T(8,128)S(1)}, u32[]{:S(2)}, u32[]{:S(2)}) collective-permute-start(f32[128,128]{1,0:T(8,128)S(1)} %get-tuple-element.114), channel_id=1, source_target_pairs={{0,28},{4,8},{8,4},{12,16},{16,12},{20,24},{24,20},{28,0},{1,29},{... | collective-permute-start | bytes 196616 | tf_op jit(solution)/shard_map/ppermute | solution.py:224
  47.2 0.8 %collective-permute-start.32 = (f32[64,128]{1,0:T(8,128)S(1)}, f32[64,128]{1,0:T(8,128)S(1)}, u32[]{:S(2)}, u32[]{:S(2)}) collective-permute-start(f32[64,128]{1,0:T(8,128)S(1)} %get-tuple-element.116), channel_id=1, source_target_pairs={{0,2},{1,3},{2,0},{3,1},{4,6},{5,7},{6,4},{7,5},{8,10},{9,11},{10,... | collective-permute-start | bytes 98312 | tf_op jit(solution)/shard_map/ppermute | solution.py:226
  48.0 1.5 %collective-permute-start.33 = (f32[64,128]{1,0:T(8,128)S(1)}, f32[64,128]{1,0:T(8,128)S(1)}, u32[]{:S(2)}, u32[]{:S(2)}) collective-permute-start(f32[64,128]{1,0:T(8,128)S(1)} %get-tuple-element.117), channel_id=1, source_target_pairs={{0,1},{1,0},{2,3},{3,2},{4,5},{5,4},{6,7},{7,6},{8,9},{9,8},{10,11... | collective-permute-start | bytes 98312 | tf_op jit(solution)/shard_map/ppermute | solution.py:226
  50.3 0.9 %collective-permute-done.32.refs_2_ = f32[64,128]{1,0:T(8,128)S(1)} collective-permute-done((f32[64,128]{1,0:T(8,128)S(1)}, f32[64,128]{1,0:T(8,128)S(1)}, u32[]{:S(2)}, u32[]{:S(2)}) %collective-permute-start.32) | collective-permute-done | bytes 32800 | tf_op jit(solution)/shard_map/ppermute | solution.py:226
  51.1 0.8 %collective-permute-done.33.refs_3_ = f32[64,128]{1,0:T(8,128)S(1)} collective-permute-done((f32[64,128]{1,0:T(8,128)S(1)}, f32[64,128]{1,0:T(8,128)S(1)}, u32[]{:S(2)}, u32[]{:S(2)}) %collective-permute-start.33) | collective-permute-done | bytes 32800 | tf_op jit(solution)/shard_map/ppermute | solution.py:226
  52.3 1.5 %collective-permute-start.37 = (f32[64,128]{1,0:T(8,128)S(1)}, f32[64,128]{1,0:T(8,128)S(1)}, u32[]{:S(2)}, u32[]{:S(2)}) collective-permute-start(f32[64,128]{1,0:T(8,128)S(1)} %get-tuple-element.123), channel_id=1, source_target_pairs={{0,3},{1,2},{2,1},{3,0},{4,7},{5,6},{6,5},{7,4},{8,11},{9,10},{10,... | collective-permute-start | bytes 98312 | tf_op jit(solution)/shard_map/ppermute | solution.py:226
  53.8 1.8 %collective-permute-start.36 = (f32[128,128]{1,0:T(8,128)S(1)}, f32[128,128]{1,0:T(8,128)S(1)}, u32[]{:S(2)}, u32[]{:S(2)}) collective-permute-start(f32[128,128]{1,0:T(8,128)S(1)} %get-tuple-element.122), channel_id=1, source_target_pairs={{0,28},{4,8},{8,4},{12,16},{16,12},{20,24},{24,20},{28,0},{1,29},{... | collective-permute-start | bytes 196616 | tf_op jit(solution)/shard_map/ppermute | solution.py:224
  56.1 0.5 collective-permute-start.39
  56.6 0.5 collective-permute-done.37.refs_1_
  57.4 2.1 %collective-permute-done.38.refs_2_ = f32[64,128]{1,0:T(8,128)S(1)} collective-permute-done((f32[64,128]{1,0:T(8,128)S(1)}, f32[64,128]{1,0:T(8,128)S(1)}, u32[]{:S(2)}, u32[]{:S(2)}) %collective-permute-start.38) | collective-permute-done | bytes 32800 | tf_op jit(solution)/shard_map/ppermute | solution.py:226
  60.3 1.6 %collective-permute-start.43 = (f32[64,128]{1,0:T(8,128)S(1)}, f32[64,128]{1,0:T(8,128)S(1)}, u32[]{:S(2)}, u32[]{:S(2)}) collective-permute-start(f32[64,128]{1,0:T(8,128)S(1)} %get-tuple-element.137), channel_id=1, source_target_pairs={{0,3},{1,2},{2,1},{3,0},{4,7},{5,6},{6,5},{7,4},{8,11},{9,10},{10,... | collective-permute-start | bytes 98312 | tf_op jit(solution)/shard_map/ppermute | solution.py:226
  61.9 0.7 %collective-permute-start.42 = (f32[128,128]{1,0:T(8,128)S(1)}, f32[128,128]{1,0:T(8,128)S(1)}, u32[]{:S(2)}, u32[]{:S(2)}) collective-permute-start(f32[128,128]{1,0:T(8,128)S(1)} %get-tuple-element.136), channel_id=1, source_target_pairs={{0,28},{4,8},{8,4},{12,16},{16,12},{20,24},{24,20},{28,0},{1,29},{... | collective-permute-start | bytes 196616 | tf_op jit(solution)/shard_map/ppermute | solution.py:224
  62.6 0.8 %collective-permute-start.44 = (f32[64,128]{1,0:T(8,128)S(1)}, f32[64,128]{1,0:T(8,128)S(1)}, u32[]{:S(2)}, u32[]{:S(2)}) collective-permute-start(f32[64,128]{1,0:T(8,128)S(1)} %get-tuple-element.138), channel_id=1, source_target_pairs={{0,2},{1,3},{2,0},{3,1},{4,6},{5,7},{6,4},{7,5},{8,10},{9,11},{10,... | collective-permute-start | bytes 98312 | tf_op jit(solution)/shard_map/ppermute | solution.py:226
  63.4 1.5 %collective-permute-start.45 = (f32[64,128]{1,0:T(8,128)S(1)}, f32[64,128]{1,0:T(8,128)S(1)}, u32[]{:S(2)}, u32[]{:S(2)}) collective-permute-start(f32[64,128]{1,0:T(8,128)S(1)} %get-tuple-element.139), channel_id=1, source_target_pairs={{0,1},{1,0},{2,3},{3,2},{4,5},{5,4},{6,7},{7,6},{8,9},{9,8},{10,11... | collective-permute-start | bytes 98312 | tf_op jit(solution)/shard_map/ppermute | solution.py:226
  65.4 0.9 %local7.1 = (f32[8,64,128]{2,1,0:T(8,128)S(1)}, f32[8,64,128]{2,1,0:T(8,128)}) custom-call(s32[40]{0:T(128)S(4)} %get-tuple-element.72.table, f32[8,64,128]{2,1,0:T(8,128)S(1)} %local6.1.resid, bf16[8,6,128,128]{3,2,1,0:T(8,128)(2,1)S(1)} %get-tuple-element.74.coupling, ...), custom_call_target="tpu_custom_call", output_to_operand_aliasing={{0}: (1, {})} | custom-call | tf_op jit(solution)/shard_map/local7/pallas_call | solution.py:213
  66.5 0.8 %collective-permute-done.45.refs_3_ = f32[64,128]{1,0:T(8,128)S(1)} collective-permute-done((f32[64,128]{1,0:T(8,128)S(1)}, f32[64,128]{1,0:T(8,128)S(1)}, u32[]{:S(2)}, u32[]{:S(2)}) %collective-permute-start.45) | collective-permute-done | bytes 32800 | tf_op jit(solution)/shard_map/ppermute | solution.py:226
  67.4 0.8 %final.1 = f32[8,64,128]{2,1,0:T(8,128)} custom-call(f32[8,64,128]{2,1,0:T(8,128)S(1)} %get-tuple-element.135.resid, f32[128,128]{1,0:T(8,128)S(1)} %collective-permute-done.42.refs_0_, f32[64,128]{1,0:T(8,128)S(1)} %collective-permute-done.43.refs_1_, f32[64,128]{1,0:T(8,128)S(1)} %collective-permute-done.44.refs_2_, ...), custom_call_target="tpu_custom_call" | custom-call | tf_op jit(solution)/shard_map/final/pallas_call | solution.py:213
  (65 shorter events, 9.3 us)
Async XLA Ops:
  2.6 7.8 %collective-permute-start.1 = (f32[72,128]{1,0:T(8,128)S(1)}, f32[72,128]{1,0:T(8,128)S(1)}, u32[]{:S(2)}, u32[]{:S(2)}) collective-permute-start(f32[72,128]{1,0:T(8,128)S(1)} %get-tuple-element.78), channel_id=1, source_target_pairs={{0,3},{1,2},{2,1},{3,0},{4,7},{5,6},{6,5},{7,4},{8,11},{9,10},{10,... | collective-permute-start | bytes 110600 | tf_op jit(solution)/shard_map/ppermute | solution.py:226
  6.5 7.2 %collective-permute-start = (f32[136,128]{1,0:T(8,128)S(1)}, f32[136,128]{1,0:T(8,128)S(1)}, u32[]{:S(2)}, u32[]{:S(2)}) collective-permute-start(f32[136,128]{1,0:T(8,128)S(1)} %get-tuple-element.77), channel_id=1, source_target_pairs={{0,28},{4,8},{8,4},{12,16},{16,12},{20,24},{24,20},{28,0},{1,29},{... | collective-permute-start | bytes 208904 | tf_op jit(solution)/shard_map/ppermute | solution.py:224
  9.3 4.0 %collective-permute-start.2 = (f32[72,128]{1,0:T(8,128)S(1)}, f32[72,128]{1,0:T(8,128)S(1)}, u32[]{:S(2)}, u32[]{:S(2)}) collective-permute-start(f32[72,128]{1,0:T(8,128)S(1)} %get-tuple-element.79), channel_id=1, source_target_pairs={{0,2},{1,3},{2,0},{3,1},{4,6},{5,7},{6,4},{7,5},{8,10},{9,11},{10,... | collective-permute-start | bytes 110600 | tf_op jit(solution)/shard_map/ppermute | solution.py:226
  9.8 4.0 %collective-permute-start.3 = (f32[72,128]{1,0:T(8,128)S(1)}, f32[72,128]{1,0:T(8,128)S(1)}, u32[]{:S(2)}, u32[]{:S(2)}) collective-permute-start(f32[72,128]{1,0:T(8,128)S(1)} %get-tuple-element.80), channel_id=1, source_target_pairs={{0,1},{1,0},{2,3},{3,2},{4,5},{5,4},{6,7},{7,6},{8,9},{9,8},{10,11... | collective-permute-start | bytes 110600 | tf_op jit(solution)/shard_map/ppermute | solution.py:226
  10.3 3.4 %collective-permute-start.4 = (f32[72,128]{1,0:T(8,128)S(1)}, f32[72,128]{1,0:T(8,128)S(1)}, u32[]{:S(2)}, u32[]{:S(2)}) collective-permute-start(f32[72,128]{1,0:T(8,128)S(1)} %get-tuple-element.81), channel_id=1, source_target_pairs={{0,4},{4,0},{8,12},{12,8},{16,20},{20,16},{24,28},{28,24},{1,5},{5... | collective-permute-start | bytes 110600 | tf_op jit(solution)/shard_map/ppermute | solution.py:227
  10.3 3.4 %collective-permute-start.5 = (f32[72,128]{1,0:T(8,128)S(1)}, f32[72,128]{1,0:T(8,128)S(1)}, u32[]{:S(2)}, u32[]{:S(2)}) collective-permute-start(f32[72,128]{1,0:T(8,128)S(1)} %get-tuple-element.82), channel_id=1, source_target_pairs={{0,4},{4,0},{8,12},{12,8},{16,20},{20,16},{24,28},{28,24},{1,5},{5... | collective-permute-start | bytes 110600 | tf_op jit(solution)/shard_map/ppermute | solution.py:227
  14.1 5.1 %collective-permute-start.7 = (f32[64,128]{1,0:T(8,128)S(1)}, f32[64,128]{1,0:T(8,128)S(1)}, u32[]{:S(2)}, u32[]{:S(2)}) collective-permute-start(f32[64,128]{1,0:T(8,128)S(1)} %get-tuple-element.85), channel_id=1, source_target_pairs={{0,3},{1,2},{2,1},{3,0},{4,7},{5,6},{6,5},{7,4},{8,11},{9,10},{10,... | collective-permute-start | bytes 98312 | tf_op jit(solution)/shard_map/ppermute | solution.py:226
  15.7 5.5 %collective-permute-start.6 = (f32[128,128]{1,0:T(8,128)S(1)}, f32[128,128]{1,0:T(8,128)S(1)}, u32[]{:S(2)}, u32[]{:S(2)}) collective-permute-start(f32[128,128]{1,0:T(8,128)S(1)} %get-tuple-element.84), channel_id=1, source_target_pairs={{0,28},{4,8},{8,4},{12,16},{16,12},{20,24},{24,20},{28,0},{1,29},{... | collective-permute-start | bytes 196616 | tf_op jit(solution)/shard_map/ppermute | solution.py:224
  16.4 3.9 %collective-permute-start.8 = (f32[64,128]{1,0:T(8,128)S(1)}, f32[64,128]{1,0:T(8,128)S(1)}, u32[]{:S(2)}, u32[]{:S(2)}) collective-permute-start(f32[64,128]{1,0:T(8,128)S(1)} %get-tuple-element.86), channel_id=1, source_target_pairs={{0,2},{1,3},{2,0},{3,1},{4,6},{5,7},{6,4},{7,5},{8,10},{9,11},{10,... | collective-permute-start | bytes 98312 | tf_op jit(solution)/shard_map/ppermute | solution.py:226
  16.9 3.9 %collective-permute-start.9 = (f32[64,128]{1,0:T(8,128)S(1)}, f32[64,128]{1,0:T(8,128)S(1)}, u32[]{:S(2)}, u32[]{:S(2)}) collective-permute-start(f32[64,128]{1,0:T(8,128)S(1)} %get-tuple-element.87), channel_id=1, source_target_pairs={{0,1},{1,0},{2,3},{3,2},{4,5},{5,4},{6,7},{7,6},{8,9},{9,8},{10,11... | collective-permute-start | bytes 98312 | tf_op jit(solution)/shard_map/ppermute | solution.py:226
  18.4 2.4 %collective-permute-start.10 = (f32[64,128]{1,0:T(8,128)S(1)}, f32[64,128]{1,0:T(8,128)S(1)}, u32[]{:S(2)}, u32[]{:S(2)}) collective-permute-start(f32[64,128]{1,0:T(8,128)S(1)} %get-tuple-element.88), channel_id=1, source_target_pairs={{0,4},{4,0},{8,12},{12,8},{16,20},{20,16},{24,28},{28,24},{1,5},{5... | collective-permute-start | bytes 98312 | tf_op jit(solution)/shard_map/ppermute | solution.py:227
  19.2 1.7 %collective-permute-start.11 = (f32[64,128]{1,0:T(8,128)S(1)}, f32[64,128]{1,0:T(8,128)S(1)}, u32[]{:S(2)}, u32[]{:S(2)}) collective-permute-start(f32[64,128]{1,0:T(8,128)S(1)} %get-tuple-element.89), channel_id=1, source_target_pairs={{0,4},{4,0},{8,12},{12,8},{16,20},{20,16},{24,28},{28,24},{1,5},{5... | collective-permute-start | bytes 98312 | tf_op jit(solution)/shard_map/ppermute | solution.py:227
  21.5 4.9 %collective-permute-start.13 = (f32[64,128]{1,0:T(8,128)S(1)}, f32[64,128]{1,0:T(8,128)S(1)}, u32[]{:S(2)}, u32[]{:S(2)}) collective-permute-start(f32[64,128]{1,0:T(8,128)S(1)} %get-tuple-element.92), channel_id=1, source_target_pairs={{0,3},{1,2},{2,1},{3,0},{4,7},{5,6},{6,5},{7,4},{8,11},{9,10},{10,... | collective-permute-start | bytes 98312 | tf_op jit(solution)/shard_map/ppermute | solution.py:226
  23.0 6.2 %collective-permute-start.12 = (f32[128,128]{1,0:T(8,128)S(1)}, f32[128,128]{1,0:T(8,128)S(1)}, u32[]{:S(2)}, u32[]{:S(2)}) collective-permute-start(f32[128,128]{1,0:T(8,128)S(1)} %get-tuple-element.91), channel_id=1, source_target_pairs={{0,28},{4,8},{8,4},{12,16},{16,12},{20,24},{24,20},{28,0},{1,29},{... | collective-permute-start | bytes 196616 | tf_op jit(solution)/shard_map/ppermute | solution.py:224
  24.8 3.9 %collective-permute-start.14 = (f32[64,128]{1,0:T(8,128)S(1)}, f32[64,128]{1,0:T(8,128)S(1)}, u32[]{:S(2)}, u32[]{:S(2)}) collective-permute-start(f32[64,128]{1,0:T(8,128)S(1)} %get-tuple-element.93), channel_id=1, source_target_pairs={{0,2},{1,3},{2,0},{3,1},{4,6},{5,7},{6,4},{7,5},{8,10},{9,11},{10,... | collective-permute-start | bytes 98312 | tf_op jit(solution)/shard_map/ppermute | solution.py:226
  25.3 3.9 %collective-permute-start.15 = (f32[64,128]{1,0:T(8,128)S(1)}, f32[64,128]{1,0:T(8,128)S(1)}, u32[]{:S(2)}, u32[]{:S(2)}) collective-permute-start(f32[64,128]{1,0:T(8,128)S(1)} %get-tuple-element.94), channel_id=1, source_target_pairs={{0,1},{1,0},{2,3},{3,2},{4,5},{5,4},{6,7},{7,6},{8,9},{9,8},{10,11... | collective-permute-start | bytes 98312 | tf_op jit(solution)/shard_map/ppermute | solution.py:226
  25.8 3.4 %collective-permute-start.16 = (f32[64,128]{1,0:T(8,128)S(1)}, f32[64,128]{1,0:T(8,128)S(1)}, u32[]{:S(2)}, u32[]{:S(2)}) collective-permute-start(f32[64,128]{1,0:T(8,128)S(1)} %get-tuple-element.95), channel_id=1, source_target_pairs={{0,4},{4,0},{8,12},{12,8},{16,20},{20,16},{24,28},{28,24},{1,5},{5... | collective-permute-start | bytes 98312 | tf_op jit(solution)/shard_map/ppermute | solution.py:227
  26.3 2.9 %collective-permute-start.17 = (f32[64,128]{1,0:T(8,128)S(1)}, f32[64,128]{1,0:T(8,128)S(1)}, u32[]{:S(2)}, u32[]{:S(2)}) collective-permute-start(f32[64,128]{1,0:T(8,128)S(1)} %get-tuple-element.96), channel_id=1, source_target_pairs={{0,4},{4,0},{8,12},{12,8},{16,20},{20,16},{24,28},{28,24},{1,5},{5... | collective-permute-start | bytes 98312 | tf_op jit(solution)/shard_map/ppermute | solution.py:227
  29.5 4.9 %collective-permute-start.19 = (f32[64,128]{1,0:T(8,128)S(1)}, f32[64,128]{1,0:T(8,128)S(1)}, u32[]{:S(2)}, u32[]{:S(2)}) collective-permute-start(f32[64,128]{1,0:T(8,128)S(1)} %get-tuple-element.99), channel_id=1, source_target_pairs={{0,3},{1,2},{2,1},{3,0},{4,7},{5,6},{6,5},{7,4},{8,11},{9,10},{10,... | collective-permute-start | bytes 98312 | tf_op jit(solution)/shard_map/ppermute | solution.py:226
  31.1 5.5 %collective-permute-start.18 = (f32[128,128]{1,0:T(8,128)S(1)}, f32[128,128]{1,0:T(8,128)S(1)}, u32[]{:S(2)}, u32[]{:S(2)}) collective-permute-start(f32[128,128]{1,0:T(8,128)S(1)} %get-tuple-element.98), channel_id=1, source_target_pairs={{0,28},{4,8},{8,4},{12,16},{16,12},{20,24},{24,20},{28,0},{1,29},{... | collective-permute-start | bytes 196616 | tf_op jit(solution)/shard_map/ppermute | solution.py:224
  31.8 3.9 %collective-permute-start.20 = (f32[64,128]{1,0:T(8,128)S(1)}, f32[64,128]{1,0:T(8,128)S(1)}, u32[]{:S(2)}, u32[]{:S(2)}) collective-permute-start(f32[64,128]{1,0:T(8,128)S(1)} %get-tuple-element.100), channel_id=1, source_target_pairs={{0,2},{1,3},{2,0},{3,1},{4,6},{5,7},{6,4},{7,5},{8,10},{9,11},{10,... | collective-permute-start | bytes 98312 | tf_op jit(solution)/shard_map/ppermute | solution.py:226
  32.6 3.9 %collective-permute-start.21 = (f32[64,128]{1,0:T(8,128)S(1)}, f32[64,128]{1,0:T(8,128)S(1)}, u32[]{:S(2)}, u32[]{:S(2)}) collective-permute-start(f32[64,128]{1,0:T(8,128)S(1)} %get-tuple-element.101), channel_id=1, source_target_pairs={{0,1},{1,0},{2,3},{3,2},{4,5},{5,4},{6,7},{7,6},{8,9},{9,8},{10,11... | collective-permute-start | bytes 98312 | tf_op jit(solution)/shard_map/ppermute | solution.py:226
  34.1 2.4 %collective-permute-start.22 = (f32[64,128]{1,0:T(8,128)S(1)}, f32[64,128]{1,0:T(8,128)S(1)}, u32[]{:S(2)}, u32[]{:S(2)}) collective-permute-start(f32[64,128]{1,0:T(8,128)S(1)} %get-tuple-element.102), channel_id=1, source_target_pairs={{0,4},{4,0},{8,12},{12,8},{16,20},{20,16},{24,28},{28,24},{1,5},{5... | collective-permute-start | bytes 98312 | tf_op jit(solution)/shard_map/ppermute | solution.py:227
  34.4 2.1 %collective-permute-start.23 = (f32[64,128]{1,0:T(8,128)S(1)}, f32[64,128]{1,0:T(8,128)S(1)}, u32[]{:S(2)}, u32[]{:S(2)}) collective-permute-start(f32[64,128]{1,0:T(8,128)S(1)} %get-tuple-element.103), channel_id=1, source_target_pairs={{0,4},{4,0},{8,12},{12,8},{16,20},{20,16},{24,28},{28,24},{1,5},{5... | collective-permute-start | bytes 98312 | tf_op jit(solution)/shard_map/ppermute | solution.py:227
  36.9 4.9 %collective-permute-start.25 = (f32[64,128]{1,0:T(8,128)S(1)}, f32[64,128]{1,0:T(8,128)S(1)}, u32[]{:S(2)}, u32[]{:S(2)}) collective-permute-start(f32[64,128]{1,0:T(8,128)S(1)} %get-tuple-element.107), channel_id=1, source_target_pairs={{0,3},{1,2},{2,1},{3,0},{4,7},{5,6},{6,5},{7,4},{8,11},{9,10},{10,... | collective-permute-start | bytes 98312 | tf_op jit(solution)/shard_map/ppermute | solution.py:226
  38.4 6.2 %collective-permute-start.24 = (f32[128,128]{1,0:T(8,128)S(1)}, f32[128,128]{1,0:T(8,128)S(1)}, u32[]{:S(2)}, u32[]{:S(2)}) collective-permute-start(f32[128,128]{1,0:T(8,128)S(1)} %get-tuple-element.106), channel_id=1, source_target_pairs={{0,28},{4,8},{8,4},{12,16},{16,12},{20,24},{24,20},{28,0},{1,29},{... | collective-permute-start | bytes 196616 | tf_op jit(solution)/shard_map/ppermute | solution.py:224
  40.2 3.9 %collective-permute-start.26 = (f32[64,128]{1,0:T(8,128)S(1)}, f32[64,128]{1,0:T(8,128)S(1)}, u32[]{:S(2)}, u32[]{:S(2)}) collective-permute-start(f32[64,128]{1,0:T(8,128)S(1)} %get-tuple-element.108), channel_id=1, source_target_pairs={{0,2},{1,3},{2,0},{3,1},{4,6},{5,7},{6,4},{7,5},{8,10},{9,11},{10,... | collective-permute-start | bytes 98312 | tf_op jit(solution)/shard_map/ppermute | solution.py:226
  40.7 3.9 %collective-permute-start.27 = (f32[64,128]{1,0:T(8,128)S(1)}, f32[64,128]{1,0:T(8,128)S(1)}, u32[]{:S(2)}, u32[]{:S(2)}) collective-permute-start(f32[64,128]{1,0:T(8,128)S(1)} %get-tuple-element.109), channel_id=1, source_target_pairs={{0,1},{1,0},{2,3},{3,2},{4,5},{5,4},{6,7},{7,6},{8,9},{9,8},{10,11... | collective-permute-start | bytes 98312 | tf_op jit(solution)/shard_map/ppermute | solution.py:226
  41.2 3.4 %collective-permute-start.28 = (f32[64,128]{1,0:T(8,128)S(1)}, f32[64,128]{1,0:T(8,128)S(1)}, u32[]{:S(2)}, u32[]{:S(2)}) collective-permute-start(f32[64,128]{1,0:T(8,128)S(1)} %get-tuple-element.110), channel_id=1, source_target_pairs={{0,4},{4,0},{8,12},{12,8},{16,20},{20,16},{24,28},{28,24},{1,5},{5... | collective-permute-start | bytes 98312 | tf_op jit(solution)/shard_map/ppermute | solution.py:227
  41.7 2.9 %collective-permute-start.29 = (f32[64,128]{1,0:T(8,128)S(1)}, f32[64,128]{1,0:T(8,128)S(1)}, u32[]{:S(2)}, u32[]{:S(2)}) collective-permute-start(f32[64,128]{1,0:T(8,128)S(1)} %get-tuple-element.111), channel_id=1, source_target_pairs={{0,4},{4,0},{8,12},{12,8},{16,20},{20,16},{24,28},{28,24},{1,5},{5... | collective-permute-start | bytes 98312 | tf_op jit(solution)/shard_map/ppermute | solution.py:227
  44.9 5.0 %collective-permute-start.31 = (f32[64,128]{1,0:T(8,128)S(1)}, f32[64,128]{1,0:T(8,128)S(1)}, u32[]{:S(2)}, u32[]{:S(2)}) collective-permute-start(f32[64,128]{1,0:T(8,128)S(1)} %get-tuple-element.115), channel_id=1, source_target_pairs={{0,3},{1,2},{2,1},{3,0},{4,7},{5,6},{6,5},{7,4},{8,11},{9,10},{10,... | collective-permute-start | bytes 98312 | tf_op jit(solution)/shard_map/ppermute | solution.py:226
  46.5 5.5 %collective-permute-start.30 = (f32[128,128]{1,0:T(8,128)S(1)}, f32[128,128]{1,0:T(8,128)S(1)}, u32[]{:S(2)}, u32[]{:S(2)}) collective-permute-start(f32[128,128]{1,0:T(8,128)S(1)} %get-tuple-element.114), channel_id=1, source_target_pairs={{0,28},{4,8},{8,4},{12,16},{16,12},{20,24},{24,20},{28,0},{1,29},{... | collective-permute-start | bytes 196616 | tf_op jit(solution)/shard_map/ppermute | solution.py:224
  47.2 3.9 %collective-permute-start.32 = (f32[64,128]{1,0:T(8,128)S(1)}, f32[64,128]{1,0:T(8,128)S(1)}, u32[]{:S(2)}, u32[]{:S(2)}) collective-permute-start(f32[64,128]{1,0:T(8,128)S(1)} %get-tuple-element.116), channel_id=1, source_target_pairs={{0,2},{1,3},{2,0},{3,1},{4,6},{5,7},{6,4},{7,5},{8,10},{9,11},{10,... | collective-permute-start | bytes 98312 | tf_op jit(solution)/shard_map/ppermute | solution.py:226
  48.0 3.9 %collective-permute-start.33 = (f32[64,128]{1,0:T(8,128)S(1)}, f32[64,128]{1,0:T(8,128)S(1)}, u32[]{:S(2)}, u32[]{:S(2)}) collective-permute-start(f32[64,128]{1,0:T(8,128)S(1)} %get-tuple-element.117), channel_id=1, source_target_pairs={{0,1},{1,0},{2,3},{3,2},{4,5},{5,4},{6,7},{7,6},{8,9},{9,8},{10,11... | collective-permute-start | bytes 98312 | tf_op jit(solution)/shard_map/ppermute | solution.py:226
  49.5 2.4 %collective-permute-start.34 = (f32[64,128]{1,0:T(8,128)S(1)}, f32[64,128]{1,0:T(8,128)S(1)}, u32[]{:S(2)}, u32[]{:S(2)}) collective-permute-start(f32[64,128]{1,0:T(8,128)S(1)} %get-tuple-element.118), channel_id=1, source_target_pairs={{0,4},{4,0},{8,12},{12,8},{16,20},{20,16},{24,28},{28,24},{1,5},{5... | collective-permute-start | bytes 98312 | tf_op jit(solution)/shard_map/ppermute | solution.py:227
  49.9 2.1 %collective-permute-start.35 = (f32[64,128]{1,0:T(8,128)S(1)}, f32[64,128]{1,0:T(8,128)S(1)}, u32[]{:S(2)}, u32[]{:S(2)}) collective-permute-start(f32[64,128]{1,0:T(8,128)S(1)} %get-tuple-element.119), channel_id=1, source_target_pairs={{0,4},{4,0},{8,12},{12,8},{16,20},{20,16},{24,28},{28,24},{1,5},{5... | collective-permute-start | bytes 98312 | tf_op jit(solution)/shard_map/ppermute | solution.py:227
  52.3 4.9 %collective-permute-start.37 = (f32[64,128]{1,0:T(8,128)S(1)}, f32[64,128]{1,0:T(8,128)S(1)}, u32[]{:S(2)}, u32[]{:S(2)}) collective-permute-start(f32[64,128]{1,0:T(8,128)S(1)} %get-tuple-element.123), channel_id=1, source_target_pairs={{0,3},{1,2},{2,1},{3,0},{4,7},{5,6},{6,5},{7,4},{8,11},{9,10},{10,... | collective-permute-start | bytes 98312 | tf_op jit(solution)/shard_map/ppermute | solution.py:226
  53.8 6.2 %collective-permute-start.36 = (f32[128,128]{1,0:T(8,128)S(1)}, f32[128,128]{1,0:T(8,128)S(1)}, u32[]{:S(2)}, u32[]{:S(2)}) collective-permute-start(f32[128,128]{1,0:T(8,128)S(1)} %get-tuple-element.122), channel_id=1, source_target_pairs={{0,28},{4,8},{8,4},{12,16},{16,12},{20,24},{24,20},{28,0},{1,29},{... | collective-permute-start | bytes 196616 | tf_op jit(solution)/shard_map/ppermute | solution.py:224
  55.6 3.9 %collective-permute-start.38 = (f32[64,128]{1,0:T(8,128)S(1)}, f32[64,128]{1,0:T(8,128)S(1)}, u32[]{:S(2)}, u32[]{:S(2)}) collective-permute-start(f32[64,128]{1,0:T(8,128)S(1)} %get-tuple-element.124), channel_id=1, source_target_pairs={{0,2},{1,3},{2,0},{3,1},{4,6},{5,7},{6,4},{7,5},{8,10},{9,11},{10,... | collective-permute-start | bytes 98312 | tf_op jit(solution)/shard_map/ppermute | solution.py:226
  56.1 3.9 %collective-permute-start.39 = (f32[64,128]{1,0:T(8,128)S(1)}, f32[64,128]{1,0:T(8,128)S(1)}, u32[]{:S(2)}, u32[]{:S(2)}) collective-permute-start(f32[64,128]{1,0:T(8,128)S(1)} %get-tuple-element.125), channel_id=1, source_target_pairs={{0,1},{1,0},{2,3},{3,2},{4,5},{5,4},{6,7},{7,6},{8,9},{9,8},{10,11... | collective-permute-start | bytes 98312 | tf_op jit(solution)/shard_map/ppermute | solution.py:226
  56.6 3.4 %collective-permute-start.40 = (f32[64,128]{1,0:T(8,128)S(1)}, f32[64,128]{1,0:T(8,128)S(1)}, u32[]{:S(2)}, u32[]{:S(2)}) collective-permute-start(f32[64,128]{1,0:T(8,128)S(1)} %get-tuple-element.126), channel_id=1, source_target_pairs={{0,4},{4,0},{8,12},{12,8},{16,20},{20,16},{24,28},{28,24},{1,5},{5... | collective-permute-start | bytes 98312 | tf_op jit(solution)/shard_map/ppermute | solution.py:227
  57.2 2.9 %collective-permute-start.41 = (f32[64,128]{1,0:T(8,128)S(1)}, f32[64,128]{1,0:T(8,128)S(1)}, u32[]{:S(2)}, u32[]{:S(2)}) collective-permute-start(f32[64,128]{1,0:T(8,128)S(1)} %get-tuple-element.127), channel_id=1, source_target_pairs={{0,4},{4,0},{8,12},{12,8},{16,20},{20,16},{24,28},{28,24},{1,5},{5... | collective-permute-start | bytes 98312 | tf_op jit(solution)/shard_map/ppermute | solution.py:227
  60.3 4.9 %collective-permute-start.43 = (f32[64,128]{1,0:T(8,128)S(1)}, f32[64,128]{1,0:T(8,128)S(1)}, u32[]{:S(2)}, u32[]{:S(2)}) collective-permute-start(f32[64,128]{1,0:T(8,128)S(1)} %get-tuple-element.137), channel_id=1, source_target_pairs={{0,3},{1,2},{2,1},{3,0},{4,7},{5,6},{6,5},{7,4},{8,11},{9,10},{10,... | collective-permute-start | bytes 98312 | tf_op jit(solution)/shard_map/ppermute | solution.py:226
  61.9 5.5 %collective-permute-start.42 = (f32[128,128]{1,0:T(8,128)S(1)}, f32[128,128]{1,0:T(8,128)S(1)}, u32[]{:S(2)}, u32[]{:S(2)}) collective-permute-start(f32[128,128]{1,0:T(8,128)S(1)} %get-tuple-element.136), channel_id=1, source_target_pairs={{0,28},{4,8},{8,4},{12,16},{16,12},{20,24},{24,20},{28,0},{1,29},{... | collective-permute-start | bytes 196616 | tf_op jit(solution)/shard_map/ppermute | solution.py:224
  62.6 3.9 %collective-permute-start.44 = (f32[64,128]{1,0:T(8,128)S(1)}, f32[64,128]{1,0:T(8,128)S(1)}, u32[]{:S(2)}, u32[]{:S(2)}) collective-permute-start(f32[64,128]{1,0:T(8,128)S(1)} %get-tuple-element.138), channel_id=1, source_target_pairs={{0,2},{1,3},{2,0},{3,1},{4,6},{5,7},{6,4},{7,5},{8,10},{9,11},{10,... | collective-permute-start | bytes 98312 | tf_op jit(solution)/shard_map/ppermute | solution.py:226
  63.4 3.9 %collective-permute-start.45 = (f32[64,128]{1,0:T(8,128)S(1)}, f32[64,128]{1,0:T(8,128)S(1)}, u32[]{:S(2)}, u32[]{:S(2)}) collective-permute-start(f32[64,128]{1,0:T(8,128)S(1)} %get-tuple-element.139), channel_id=1, source_target_pairs={{0,1},{1,0},{2,3},{3,2},{4,5},{5,4},{6,7},{7,6},{8,9},{9,8},{10,11... | collective-permute-start | bytes 98312 | tf_op jit(solution)/shard_map/ppermute | solution.py:226
  64.9 2.4 %collective-permute-start.46 = (f32[64,128]{1,0:T(8,128)S(1)}, f32[64,128]{1,0:T(8,128)S(1)}, u32[]{:S(2)}, u32[]{:S(2)}) collective-permute-start(f32[64,128]{1,0:T(8,128)S(1)} %get-tuple-element.140), channel_id=1, source_target_pairs={{0,4},{4,0},{8,12},{12,8},{16,20},{20,16},{24,28},{28,24},{1,5},{5... | collective-permute-start | bytes 98312 | tf_op jit(solution)/shard_map/ppermute | solution.py:227
  65.2 2.2 %collective-permute-start.47 = (f32[64,128]{1,0:T(8,128)S(1)}, f32[64,128]{1,0:T(8,128)S(1)}, u32[]{:S(2)}, u32[]{:S(2)}) collective-permute-start(f32[64,128]{1,0:T(8,128)S(1)} %get-tuple-element.141), channel_id=1, source_target_pairs={{0,4},{4,0},{8,12},{12,8},{16,20},{20,16},{24,28},{28,24},{1,5},{5... | collective-permute-start | bytes 98312 | tf_op jit(solution)/shard_map/ppermute | solution.py:227

commit v11 on v10

--- a/solution.py
+++ b/solution.py
@@ -66,15 +66,13 @@
     for p in range(plan.quarter):
         at = step % COLORS * plan.quarter + p
         j = table[plan.order + at]
-        both = dot(
-            changes[p],
-            jnp.concatenate([coupling[j, 5 - parity], coupling[j, 4 + parity]], axis=1),
-        )
-        far[pl.ds(p * plan.n, plan.n), :] = both[:, : plan.w]
-        near[p][pl.ds(0, plan.n), :] = both[:, plan.w :]
-        both = dot(changes[p], jnp.concatenate([coupling[j, 2], coupling[j, 3]], axis=1))
+        tiles = [coupling[j, k] for k in (2, 3, 5 - parity, 4 + parity)]
+        wide = dot(changes[p], jnp.concatenate(tiles, axis=1))
+        parts = [wide[:, k * plan.w : (k + 1) * plan.w] for k in range(4)]
+        far[pl.ds(p * plan.n, plan.n), :] = parts[2]
+        near[p][pl.ds(0, plan.n), :] = parts[3]
         for k in range(2):
-            terms.append((table[plan.slot + 2 * at + k], both[:, k * plan.w : (k + 1) * plan.w]))
+            terms.append((table[plan.slot + 2 * at + k], parts[k]))
     for lane, s in enumerate(plan.distances):
         total = jnp.zeros((plan.n, plan.w), jnp.float32)
         for slot, term in terms:

time: 68.4 us -> 68.4 us (level)
  no operation moved by 1% of the time
where the time goes in v11:
time: 68.4 us; the launch traced here: 68.2 us
  starting transfers between devices  40.1 us (59%)
  waiting for transfers between devices  20.1 us (29%)
  Pallas kernels  7.23 us (11%)
  between operations  0.8 us (1%)
    ppermute x24, starting transfers between devices, exchange(): got.append(lax.ppermute(send, 'sub', [(i, i ^ s) for i in range(group)]))  27.8 us
    ppermute x24, waiting for transfers between devices, exchange(): got.append(lax.ppermute(send, 'sub', [(i, i ^ s) for i in range(group)]))  19.8 us
    ppermute x8, starting transfers between devices, exchange(): got = [lax.ppermute(sends[0], 'dom', far_pairs)]  11.1 us
    pallas_call x17, Pallas kernels, call(): pl.pallas_call(body, name=name, in_specs=in_specs + [VMEM] * (len(ins) -...  7.23 us
  transfers between devices with their start and end apart: 48, of which 24 were waited for; matrix products, arithmetic and copies ran while one was open for 0% of the time, Pallas kernels for 3%

profile of v11, /device:TPU:0, one launch (start us, length us, event | category | flops | bytes accessed | tf_op | source)
XLA Modules:
  0.0 68.2 jit_solution(4172116372305269753)
XLA Ops:
  0.6 1.9 %first.1 = (s32[40]{0:T(128)S(4)}, bf16[8,6,128,128]{3,2,1,0:T(8,128)(2,1)S(1)}, bf16[8,128,128]{2,1,0:T(8,128)(2,1)S(1)}, f32[8,64,128]{2,1,0:T(8,128)S(1)}, f3...) custom-call(s32[8]{0:T(128)} %refs_0_.1, ...), custom_call_target="tpu_custom_call" | custom-call | tf_op jit(solution)/shard_map/first/pallas_call | solution.py:211
  2.6 4.0 %collective-permute-start.1 = (f32[72,128]{1,0:T(8,128)S(1)}, f32[72,128]{1,0:T(8,128)S(1)}, u32[]{:S(2)}, u32[]{:S(2)}) collective-permute-start(f32[72,128]{1,0:T(8,128)S(1)} %get-tuple-element.78), channel_id=1, source_target_pairs={{0,3},{1,2},{2,1},{3,0},{4,7},{5,6},{6,5},{7,4},{8,11},{9,10},{10,... | collective-permute-start | bytes 110600 | tf_op jit(solution)/shard_map/ppermute | solution.py:224
  6.5 2.8 %collective-permute-start = (f32[136,128]{1,0:T(8,128)S(1)}, f32[136,128]{1,0:T(8,128)S(1)}, u32[]{:S(2)}, u32[]{:S(2)}) collective-permute-start(f32[136,128]{1,0:T(8,128)S(1)} %get-tuple-element.77), channel_id=1, source_target_pairs={{0,28},{4,8},{8,4},{12,16},{16,12},{20,24},{24,20},{28,0},{1,29},{... | collective-permute-start | bytes 208904 | tf_op jit(solution)/shard_map/ppermute | solution.py:222
  9.8 0.5 collective-permute-start.3
  10.3 0.5 collective-permute-start.5
  11.0 2.2 %collective-permute-done.2.refs_2_.refs_8_ = f32[72,128]{1,0:T(8,128)S(1)} collective-permute-done((f32[72,128]{1,0:T(8,128)S(1)}, f32[72,128]{1,0:T(8,128)S(1)}, u32[]{:S(2)}, u32[]{:S(2)}) %collective-permute-start.2) | collective-permute-done | bytes 36896 | tf_op jit(solution)/shard_map/ppermute | solution.py:224
  14.1 1.6 %collective-permute-start.7 = (f32[64,128]{1,0:T(8,128)S(1)}, f32[64,128]{1,0:T(8,128)S(1)}, u32[]{:S(2)}, u32[]{:S(2)}) collective-permute-start(f32[64,128]{1,0:T(8,128)S(1)} %get-tuple-element.85), channel_id=1, source_target_pairs={{0,3},{1,2},{2,1},{3,0},{4,7},{5,6},{6,5},{7,4},{8,11},{9,10},{10,... | collective-permute-start | bytes 98312 | tf_op jit(solution)/shard_map/ppermute | solution.py:224
  15.7 0.7 %collective-permute-start.6 = (f32[128,128]{1,0:T(8,128)S(1)}, f32[128,128]{1,0:T(8,128)S(1)}, u32[]{:S(2)}, u32[]{:S(2)}) collective-permute-start(f32[128,128]{1,0:T(8,128)S(1)} %get-tuple-element.84), channel_id=1, source_target_pairs={{0,28},{4,8},{8,4},{12,16},{16,12},{20,24},{24,20},{28,0},{1,29},{... | collective-permute-start | bytes 196616 | tf_op jit(solution)/shard_map/ppermute | solution.py:222
  16.4 0.6 collective-permute-start.8
  17.0 1.5 %collective-permute-start.9 = (f32[64,128]{1,0:T(8,128)S(1)}, f32[64,128]{1,0:T(8,128)S(1)}, u32[]{:S(2)}, u32[]{:S(2)}) collective-permute-start(f32[64,128]{1,0:T(8,128)S(1)} %get-tuple-element.87), channel_id=1, source_target_pairs={{0,1},{1,0},{2,3},{3,2},{4,5},{5,4},{6,7},{7,6},{8,9},{9,8},{10,11... | collective-permute-start | bytes 98312 | tf_op jit(solution)/shard_map/ppermute | solution.py:224
  18.4 0.7 %collective-permute-done.7.refs_1_ = f32[64,128]{1,0:T(8,128)S(1)} collective-permute-done((f32[64,128]{1,0:T(8,128)S(1)}, f32[64,128]{1,0:T(8,128)S(1)}, u32[]{:S(2)}, u32[]{:S(2)}) %collective-permute-start.7) | collective-permute-done | bytes 32800 | tf_op jit(solution)/shard_map/ppermute | solution.py:224
  19.4 0.9 %collective-permute-done.8.refs_2_ = f32[64,128]{1,0:T(8,128)S(1)} collective-permute-done((f32[64,128]{1,0:T(8,128)S(1)}, f32[64,128]{1,0:T(8,128)S(1)}, u32[]{:S(2)}, u32[]{:S(2)}) %collective-permute-start.8) | collective-permute-done | bytes 32800 | tf_op jit(solution)/shard_map/ppermute | solution.py:224
  20.3 0.6 collective-permute-done.9.refs_3_
  21.5 1.5 %collective-permute-start.13 = (f32[64,128]{1,0:T(8,128)S(1)}, f32[64,128]{1,0:T(8,128)S(1)}, u32[]{:S(2)}, u32[]{:S(2)}) collective-permute-start(f32[64,128]{1,0:T(8,128)S(1)} %get-tuple-element.92), channel_id=1, source_target_pairs={{0,3},{1,2},{2,1},{3,0},{4,7},{5,6},{6,5},{7,4},{8,11},{9,10},{10,... | collective-permute-start | bytes 98312 | tf_op jit(solution)/shard_map/ppermute | solution.py:224
  23.0 1.8 %collective-permute-start.12 = (f32[128,128]{1,0:T(8,128)S(1)}, f32[128,128]{1,0:T(8,128)S(1)}, u32[]{:S(2)}, u32[]{:S(2)}) collective-permute-start(f32[128,128]{1,0:T(8,128)S(1)} %get-tuple-element.91), channel_id=1, source_target_pairs={{0,28},{4,8},{8,4},{12,16},{16,12},{20,24},{24,20},{28,0},{1,29},{... | collective-permute-start | bytes 196616 | tf_op jit(solution)/shard_map/ppermute | solution.py:222
  24.8 0.5 collective-permute-start.14
  25.3 0.5 collective-permute-start.15
  25.8 0.5 collective-permute-done.13.refs_1_
  26.6 2.1 %collective-permute-done.14.refs_2_ = f32[64,128]{1,0:T(8,128)S(1)} collective-permute-done((f32[64,128]{1,0:T(8,128)S(1)}, f32[64,128]{1,0:T(8,128)S(1)}, u32[]{:S(2)}, u32[]{:S(2)}) %collective-permute-start.14) | collective-permute-done | bytes 32800 | tf_op jit(solution)/shard_map/ppermute | solution.py:224
  29.5 1.6 %collective-permute-start.19 = (f32[64,128]{1,0:T(8,128)S(1)}, f32[64,128]{1,0:T(8,128)S(1)}, u32[]{:S(2)}, u32[]{:S(2)}) collective-permute-start(f32[64,128]{1,0:T(8,128)S(1)} %get-tuple-element.99), channel_id=1, source_target_pairs={{0,3},{1,2},{2,1},{3,0},{4,7},{5,6},{6,5},{7,4},{8,11},{9,10},{10,... | collective-permute-start | bytes 98312 | tf_op jit(solution)/shard_map/ppermute | solution.py:224
  31.1 0.7 %collective-permute-start.18 = (f32[128,128]{1,0:T(8,128)S(1)}, f32[128,128]{1,0:T(8,128)S(1)}, u32[]{:S(2)}, u32[]{:S(2)}) collective-permute-start(f32[128,128]{1,0:T(8,128)S(1)} %get-tuple-element.98), channel_id=1, source_target_pairs={{0,28},{4,8},{8,4},{12,16},{16,12},{20,24},{24,20},{28,0},{1,29},{... | collective-permute-start | bytes 196616 | tf_op jit(solution)/shard_map/ppermute | solution.py:222
  31.8 0.8 %collective-permute-start.20 = (f32[64,128]{1,0:T(8,128)S(1)}, f32[64,128]{1,0:T(8,128)S(1)}, u32[]{:S(2)}, u32[]{:S(2)}) collective-permute-start(f32[64,128]{1,0:T(8,128)S(1)} %get-tuple-element.100), channel_id=1, source_target_pairs={{0,2},{1,3},{2,0},{3,1},{4,6},{5,7},{6,4},{7,5},{8,10},{9,11},{10,... | collective-permute-start | bytes 98312 | tf_op jit(solution)/shard_map/ppermute | solution.py:224
  32.6 1.5 %collective-permute-start.21 = (f32[64,128]{1,0:T(8,128)S(1)}, f32[64,128]{1,0:T(8,128)S(1)}, u32[]{:S(2)}, u32[]{:S(2)}) collective-permute-start(f32[64,128]{1,0:T(8,128)S(1)} %get-tuple-element.101), channel_id=1, source_target_pairs={{0,1},{1,0},{2,3},{3,2},{4,5},{5,4},{6,7},{7,6},{8,9},{9,8},{10,11... | collective-permute-start | bytes 98312 | tf_op jit(solution)/shard_map/ppermute | solution.py:224
  34.8 0.9 %collective-permute-done.20.refs_2_ = f32[64,128]{1,0:T(8,128)S(1)} collective-permute-done((f32[64,128]{1,0:T(8,128)S(1)}, f32[64,128]{1,0:T(8,128)S(1)}, u32[]{:S(2)}, u32[]{:S(2)}) %collective-permute-start.20) | collective-permute-done | bytes 32800 | tf_op jit(solution)/shard_map/ppermute | solution.py:224
  35.7 0.8 %collective-permute-done.21.refs_3_ = f32[64,128]{1,0:T(8,128)S(1)} collective-permute-done((f32[64,128]{1,0:T(8,128)S(1)}, f32[64,128]{1,0:T(8,128)S(1)}, u32[]{:S(2)}, u32[]{:S(2)}) %collective-permute-start.21) | collective-permute-done | bytes 32800 | tf_op jit(solution)/shard_map/ppermute | solution.py:224
  36.9 1.5 %collective-permute-start.25 = (f32[64,128]{1,0:T(8,128)S(1)}, f32[64,128]{1,0:T(8,128)S(1)}, u32[]{:S(2)}, u32[]{:S(2)}) collective-permute-start(f32[64,128]{1,0:T(8,128)S(1)} %get-tuple-element.107), channel_id=1, source_target_pairs={{0,3},{1,2},{2,1},{3,0},{4,7},{5,6},{6,5},{7,4},{8,11},{9,10},{10,... | collective-permute-start | bytes 98312 | tf_op jit(solution)/shard_map/ppermute | solution.py:224
  38.4 1.8 %collective-permute-start.24 = (f32[128,128]{1,0:T(8,128)S(1)}, f32[128,128]{1,0:T(8,128)S(1)}, u32[]{:S(2)}, u32[]{:S(2)}) collective-permute-start(f32[128,128]{1,0:T(8,128)S(1)} %get-tuple-element.106), channel_id=1, source_target_pairs={{0,28},{4,8},{8,4},{12,16},{16,12},{20,24},{24,20},{28,0},{1,29},{... | collective-permute-start | bytes 196616 | tf_op jit(solution)/shard_map/ppermute | solution.py:222
  40.7 0.5 collective-permute-start.27
  41.2 0.5 collective-permute-done.25.refs_1_
  42.0 2.1 %collective-permute-done.26.refs_2_ = f32[64,128]{1,0:T(8,128)S(1)} collective-permute-done((f32[64,128]{1,0:T(8,128)S(1)}, f32[64,128]{1,0:T(8,128)S(1)}, u32[]{:S(2)}, u32[]{:S(2)}) %collective-permute-start.26) | collective-permute-done | bytes 32800 | tf_op jit(solution)/shard_map/ppermute | solution.py:224
  44.9 1.6 %collective-permute-start.31 = (f32[64,128]{1,0:T(8,128)S(1)}, f32[64,128]{1,0:T(8,128)S(1)}, u32[]{:S(2)}, u32[]{:S(2)}) collective-permute-start(f32[64,128]{1,0:T(8,128)S(1)} %get-tuple-element.115), channel_id=1, source_target_pairs={{0,3},{1,2},{2,1},{3,0},{4,7},{5,6},{6,5},{7,4},{8,11},{9,10},{10,... | collective-permute-start | bytes 98312 | tf_op jit(solution)/shard_map/ppermute | solution.py:224
  46.5 0.7 %collective-permute-start.30 = (f32[128,128]{1,0:T(8,128)S(1)}, f32[128,128]{1,0:T(8,128)S(1)}, u32[]{:S(2)}, u32[]{:S(2)}) collective-permute-start(f32[128,128]{1,0:T(8,128)S(1)} %get-tuple-element.114), channel_id=1, source_target_pairs={{0,28},{4,8},{8,4},{12,16},{16,12},{20,24},{24,20},{28,0},{1,29},{... | collective-permute-start | bytes 196616 | tf_op jit(solution)/shard_map/ppermute | solution.py:222
  47.2 0.8 %collective-permute-start.32 = (f32[64,128]{1,0:T(8,128)S(1)}, f32[64,128]{1,0:T(8,128)S(1)}, u32[]{:S(2)}, u32[]{:S(2)}) collective-permute-start(f32[64,128]{1,0:T(8,128)S(1)} %get-tuple-element.116), channel_id=1, source_target_pairs={{0,2},{1,3},{2,0},{3,1},{4,6},{5,7},{6,4},{7,5},{8,10},{9,11},{10,... | collective-permute-start | bytes 98312 | tf_op jit(solution)/shard_map/ppermute | solution.py:224
  48.0 1.5 %collective-permute-start.33 = (f32[64,128]{1,0:T(8,128)S(1)}, f32[64,128]{1,0:T(8,128)S(1)}, u32[]{:S(2)}, u32[]{:S(2)}) collective-permute-start(f32[64,128]{1,0:T(8,128)S(1)} %get-tuple-element.117), channel_id=1, source_target_pairs={{0,1},{1,0},{2,3},{3,2},{4,5},{5,4},{6,7},{7,6},{8,9},{9,8},{10,11... | collective-permute-start | bytes 98312 | tf_op jit(solution)/shard_map/ppermute | solution.py:224
  50.3 0.9 %collective-permute-done.32.refs_2_ = f32[64,128]{1,0:T(8,128)S(1)} collective-permute-done((f32[64,128]{1,0:T(8,128)S(1)}, f32[64,128]{1,0:T(8,128)S(1)}, u32[]{:S(2)}, u32[]{:S(2)}) %collective-permute-start.32) | collective-permute-done | bytes 32800 | tf_op jit(solution)/shard_map/ppermute | solution.py:224
  51.1 0.8 %collective-permute-done.33.refs_3_ = f32[64,128]{1,0:T(8,128)S(1)} collective-permute-done((f32[64,128]{1,0:T(8,128)S(1)}, f32[64,128]{1,0:T(8,128)S(1)}, u32[]{:S(2)}, u32[]{:S(2)}) %collective-permute-start.33) | collective-permute-done | bytes 32800 | tf_op jit(solution)/shard_map/ppermute | solution.py:224
  52.3 1.5 %collective-permute-start.37 = (f32[64,128]{1,0:T(8,128)S(1)}, f32[64,128]{1,0:T(8,128)S(1)}, u32[]{:S(2)}, u32[]{:S(2)}) collective-permute-start(f32[64,128]{1,0:T(8,128)S(1)} %get-tuple-element.123), channel_id=1, source_target_pairs={{0,3},{1,2},{2,1},{3,0},{4,7},{5,6},{6,5},{7,4},{8,11},{9,10},{10,... | collective-permute-start | bytes 98312 | tf_op jit(solution)/shard_map/ppermute | solution.py:224
  53.8 1.8 %collective-permute-start.36 = (f32[128,128]{1,0:T(8,128)S(1)}, f32[128,128]{1,0:T(8,128)S(1)}, u32[]{:S(2)}, u32[]{:S(2)}) collective-permute-start(f32[128,128]{1,0:T(8,128)S(1)} %get-tuple-element.122), channel_id=1, source_target_pairs={{0,28},{4,8},{8,4},{12,16},{16,12},{20,24},{24,20},{28,0},{1,29},{... | collective-permute-start | bytes 196616 | tf_op jit(solution)/shard_map/ppermute | solution.py:222
  56.1 0.5 collective-permute-start.39
  56.6 0.5 collective-permute-done.37.refs_1_
  57.4 2.1 %collective-permute-done.38.refs_2_ = f32[64,128]{1,0:T(8,128)S(1)} collective-permute-done((f32[64,128]{1,0:T(8,128)S(1)}, f32[64,128]{1,0:T(8,128)S(1)}, u32[]{:S(2)}, u32[]{:S(2)}) %collective-permute-start.38) | collective-permute-done | bytes 32800 | tf_op jit(solution)/shard_map/ppermute | solution.py:224
  60.3 1.6 %collective-permute-start.43 = (f32[64,128]{1,0:T(8,128)S(1)}, f32[64,128]{1,0:T(8,128)S(1)}, u32[]{:S(2)}, u32[]{:S(2)}) collective-permute-start(f32[64,128]{1,0:T(8,128)S(1)} %get-tuple-element.137), channel_id=1, source_target_pairs={{0,3},{1,2},{2,1},{3,0},{4,7},{5,6},{6,5},{7,4},{8,11},{9,10},{10,... | collective-permute-start | bytes 98312 | tf_op jit(solution)/shard_map/ppermute | solution.py:224
  61.9 0.7 %collective-permute-start.42 = (f32[128,128]{1,0:T(8,128)S(1)}, f32[128,128]{1,0:T(8,128)S(1)}, u32[]{:S(2)}, u32[]{:S(2)}) collective-permute-start(f32[128,128]{1,0:T(8,128)S(1)} %get-tuple-element.136), channel_id=1, source_target_pairs={{0,28},{4,8},{8,4},{12,16},{16,12},{20,24},{24,20},{28,0},{1,29},{... | collective-permute-start | bytes 196616 | tf_op jit(solution)/shard_map/ppermute | solution.py:222
  62.6 0.8 %collective-permute-start.44 = (f32[64,128]{1,0:T(8,128)S(1)}, f32[64,128]{1,0:T(8,128)S(1)}, u32[]{:S(2)}, u32[]{:S(2)}) collective-permute-start(f32[64,128]{1,0:T(8,128)S(1)} %get-tuple-element.138), channel_id=1, source_target_pairs={{0,2},{1,3},{2,0},{3,1},{4,6},{5,7},{6,4},{7,5},{8,10},{9,11},{10,... | collective-permute-start | bytes 98312 | tf_op jit(solution)/shard_map/ppermute | solution.py:224
  63.4 1.5 %collective-permute-start.45 = (f32[64,128]{1,0:T(8,128)S(1)}, f32[64,128]{1,0:T(8,128)S(1)}, u32[]{:S(2)}, u32[]{:S(2)}) collective-permute-start(f32[64,128]{1,0:T(8,128)S(1)} %get-tuple-element.139), channel_id=1, source_target_pairs={{0,1},{1,0},{2,3},{3,2},{4,5},{5,4},{6,7},{7,6},{8,9},{9,8},{10,11... | collective-permute-start | bytes 98312 | tf_op jit(solution)/shard_map/ppermute | solution.py:224
  65.4 0.9 %local7.1 = (f32[8,64,128]{2,1,0:T(8,128)S(1)}, f32[8,64,128]{2,1,0:T(8,128)}) custom-call(s32[40]{0:T(128)S(4)} %get-tuple-element.72.table, f32[8,64,128]{2,1,0:T(8,128)S(1)} %local6.1.resid, bf16[8,6,128,128]{3,2,1,0:T(8,128)(2,1)S(1)} %get-tuple-element.74.coupling, ...), custom_call_target="tpu_custom_call", output_to_operand_aliasing={{0}: (1, {})} | custom-call | tf_op jit(solution)/shard_map/local7/pallas_call | solution.py:211
  66.5 0.8 %collective-permute-done.45.refs_3_ = f32[64,128]{1,0:T(8,128)S(1)} collective-permute-done((f32[64,128]{1,0:T(8,128)S(1)}, f32[64,128]{1,0:T(8,128)S(1)}, u32[]{:S(2)}, u32[]{:S(2)}) %collective-permute-start.45) | collective-permute-done | bytes 32800 | tf_op jit(solution)/shard_map/ppermute | solution.py:224
  67.4 0.8 %final.1 = f32[8,64,128]{2,1,0:T(8,128)} custom-call(f32[8,64,128]{2,1,0:T(8,128)S(1)} %get-tuple-element.135.resid, f32[128,128]{1,0:T(8,128)S(1)} %collective-permute-done.42.refs_0_, f32[64,128]{1,0:T(8,128)S(1)} %collective-permute-done.43.refs_1_, f32[64,128]{1,0:T(8,128)S(1)} %collective-permute-done.44.refs_2_, ...), custom_call_target="tpu_custom_call" | custom-call | tf_op jit(solution)/shard_map/final/pallas_call | solution.py:211
  (65 shorter events, 9.3 us)
Async XLA Ops:
  2.6 7.8 %collective-permute-start.1 = (f32[72,128]{1,0:T(8,128)S(1)}, f32[72,128]{1,0:T(8,128)S(1)}, u32[]{:S(2)}, u32[]{:S(2)}) collective-permute-start(f32[72,128]{1,0:T(8,128)S(1)} %get-tuple-element.78), channel_id=1, source_target_pairs={{0,3},{1,2},{2,1},{3,0},{4,7},{5,6},{6,5},{7,4},{8,11},{9,10},{10,... | collective-permute-start | bytes 110600 | tf_op jit(solution)/shard_map/ppermute | solution.py:224
  6.5 7.2 %collective-permute-start = (f32[136,128]{1,0:T(8,128)S(1)}, f32[136,128]{1,0:T(8,128)S(1)}, u32[]{:S(2)}, u32[]{:S(2)}) collective-permute-start(f32[136,128]{1,0:T(8,128)S(1)} %get-tuple-element.77), channel_id=1, source_target_pairs={{0,28},{4,8},{8,4},{12,16},{16,12},{20,24},{24,20},{28,0},{1,29},{... | collective-permute-start | bytes 208904 | tf_op jit(solution)/shard_map/ppermute | solution.py:222
  9.3 4.0 %collective-permute-start.2 = (f32[72,128]{1,0:T(8,128)S(1)}, f32[72,128]{1,0:T(8,128)S(1)}, u32[]{:S(2)}, u32[]{:S(2)}) collective-permute-start(f32[72,128]{1,0:T(8,128)S(1)} %get-tuple-element.79), channel_id=1, source_target_pairs={{0,2},{1,3},{2,0},{3,1},{4,6},{5,7},{6,4},{7,5},{8,10},{9,11},{10,... | collective-permute-start | bytes 110600 | tf_op jit(solution)/shard_map/ppermute | solution.py:224
  9.8 4.0 %collective-permute-start.3 = (f32[72,128]{1,0:T(8,128)S(1)}, f32[72,128]{1,0:T(8,128)S(1)}, u32[]{:S(2)}, u32[]{:S(2)}) collective-permute-start(f32[72,128]{1,0:T(8,128)S(1)} %get-tuple-element.80), channel_id=1, source_target_pairs={{0,1},{1,0},{2,3},{3,2},{4,5},{5,4},{6,7},{7,6},{8,9},{9,8},{10,11... | collective-permute-start | bytes 110600 | tf_op jit(solution)/shard_map/ppermute | solution.py:224
  10.3 3.4 %collective-permute-start.4 = (f32[72,128]{1,0:T(8,128)S(1)}, f32[72,128]{1,0:T(8,128)S(1)}, u32[]{:S(2)}, u32[]{:S(2)}) collective-permute-start(f32[72,128]{1,0:T(8,128)S(1)} %get-tuple-element.81), channel_id=1, source_target_pairs={{0,4},{4,0},{8,12},{12,8},{16,20},{20,16},{24,28},{28,24},{1,5},{5... | collective-permute-start | bytes 110600 | tf_op jit(solution)/shard_map/ppermute | solution.py:225
  10.3 3.4 %collective-permute-start.5 = (f32[72,128]{1,0:T(8,128)S(1)}, f32[72,128]{1,0:T(8,128)S(1)}, u32[]{:S(2)}, u32[]{:S(2)}) collective-permute-start(f32[72,128]{1,0:T(8,128)S(1)} %get-tuple-element.82), channel_id=1, source_target_pairs={{0,4},{4,0},{8,12},{12,8},{16,20},{20,16},{24,28},{28,24},{1,5},{5... | collective-permute-start | bytes 110600 | tf_op jit(solution)/shard_map/ppermute | solution.py:225
  14.1 5.1 %collective-permute-start.7 = (f32[64,128]{1,0:T(8,128)S(1)}, f32[64,128]{1,0:T(8,128)S(1)}, u32[]{:S(2)}, u32[]{:S(2)}) collective-permute-start(f32[64,128]{1,0:T(8,128)S(1)} %get-tuple-element.85), channel_id=1, source_target_pairs={{0,3},{1,2},{2,1},{3,0},{4,7},{5,6},{6,5},{7,4},{8,11},{9,10},{10,... | collective-permute-start | bytes 98312 | tf_op jit(solution)/shard_map/ppermute | solution.py:224
  15.7 5.5 %collective-permute-start.6 = (f32[128,128]{1,0:T(8,128)S(1)}, f32[128,128]{1,0:T(8,128)S(1)}, u32[]{:S(2)}, u32[]{:S(2)}) collective-permute-start(f32[128,128]{1,0:T(8,128)S(1)} %get-tuple-element.84), channel_id=1, source_target_pairs={{0,28},{4,8},{8,4},{12,16},{16,12},{20,24},{24,20},{28,0},{1,29},{... | collective-permute-start | bytes 196616 | tf_op jit(solution)/shard_map/ppermute | solution.py:222
  16.4 3.9 %collective-permute-start.8 = (f32[64,128]{1,0:T(8,128)S(1)}, f32[64,128]{1,0:T(8,128)S(1)}, u32[]{:S(2)}, u32[]{:S(2)}) collective-permute-start(f32[64,128]{1,0:T(8,128)S(1)} %get-tuple-element.86), channel_id=1, source_target_pairs={{0,2},{1,3},{2,0},{3,1},{4,6},{5,7},{6,4},{7,5},{8,10},{9,11},{10,... | collective-permute-start | bytes 98312 | tf_op jit(solution)/shard_map/ppermute | solution.py:224
  17.0 3.9 %collective-permute-start.9 = (f32[64,128]{1,0:T(8,128)S(1)}, f32[64,128]{1,0:T(8,128)S(1)}, u32[]{:S(2)}, u32[]{:S(2)}) collective-permute-start(f32[64,128]{1,0:T(8,128)S(1)} %get-tuple-element.87), channel_id=1, source_target_pairs={{0,1},{1,0},{2,3},{3,2},{4,5},{5,4},{6,7},{7,6},{8,9},{9,8},{10,11... | collective-permute-start | bytes 98312 | tf_op jit(solution)/shard_map/ppermute | solution.py:224
  18.4 2.5 %collective-permute-start.10 = (f32[64,128]{1,0:T(8,128)S(1)}, f32[64,128]{1,0:T(8,128)S(1)}, u32[]{:S(2)}, u32[]{:S(2)}) collective-permute-start(f32[64,128]{1,0:T(8,128)S(1)} %get-tuple-element.88), channel_id=1, source_target_pairs={{0,4},{4,0},{8,12},{12,8},{16,20},{20,16},{24,28},{28,24},{1,5},{5... | collective-permute-start | bytes 98312 | tf_op jit(solution)/shard_map/ppermute | solution.py:225
  19.2 1.7 %collective-permute-start.11 = (f32[64,128]{1,0:T(8,128)S(1)}, f32[64,128]{1,0:T(8,128)S(1)}, u32[]{:S(2)}, u32[]{:S(2)}) collective-permute-start(f32[64,128]{1,0:T(8,128)S(1)} %get-tuple-element.89), channel_id=1, source_target_pairs={{0,4},{4,0},{8,12},{12,8},{16,20},{20,16},{24,28},{28,24},{1,5},{5... | collective-permute-start | bytes 98312 | tf_op jit(solution)/shard_map/ppermute | solution.py:225
  21.5 4.9 %collective-permute-start.13 = (f32[64,128]{1,0:T(8,128)S(1)}, f32[64,128]{1,0:T(8,128)S(1)}, u32[]{:S(2)}, u32[]{:S(2)}) collective-permute-start(f32[64,128]{1,0:T(8,128)S(1)} %get-tuple-element.92), channel_id=1, source_target_pairs={{0,3},{1,2},{2,1},{3,0},{4,7},{5,6},{6,5},{7,4},{8,11},{9,10},{10,... | collective-permute-start | bytes 98312 | tf_op jit(solution)/shard_map/ppermute | solution.py:224
  23.0 6.2 %collective-permute-start.12 = (f32[128,128]{1,0:T(8,128)S(1)}, f32[128,128]{1,0:T(8,128)S(1)}, u32[]{:S(2)}, u32[]{:S(2)}) collective-permute-start(f32[128,128]{1,0:T(8,128)S(1)} %get-tuple-element.91), channel_id=1, source_target_pairs={{0,28},{4,8},{8,4},{12,16},{16,12},{20,24},{24,20},{28,0},{1,29},{... | collective-permute-start | bytes 196616 | tf_op jit(solution)/shard_map/ppermute | solution.py:222
  24.8 3.9 %collective-permute-start.14 = (f32[64,128]{1,0:T(8,128)S(1)}, f32[64,128]{1,0:T(8,128)S(1)}, u32[]{:S(2)}, u32[]{:S(2)}) collective-permute-start(f32[64,128]{1,0:T(8,128)S(1)} %get-tuple-element.93), channel_id=1, source_target_pairs={{0,2},{1,3},{2,0},{3,1},{4,6},{5,7},{6,4},{7,5},{8,10},{9,11},{10,... | collective-permute-start | bytes 98312 | tf_op jit(solution)/shard_map/ppermute | solution.py:224
  25.3 3.9 %collective-permute-start.15 = (f32[64,128]{1,0:T(8,128)S(1)}, f32[64,128]{1,0:T(8,128)S(1)}, u32[]{:S(2)}, u32[]{:S(2)}) collective-permute-start(f32[64,128]{1,0:T(8,128)S(1)} %get-tuple-element.94), channel_id=1, source_target_pairs={{0,1},{1,0},{2,3},{3,2},{4,5},{5,4},{6,7},{7,6},{8,9},{9,8},{10,11... | collective-permute-start | bytes 98312 | tf_op jit(solution)/shard_map/ppermute | solution.py:224
  25.8 3.4 %collective-permute-start.16 = (f32[64,128]{1,0:T(8,128)S(1)}, f32[64,128]{1,0:T(8,128)S(1)}, u32[]{:S(2)}, u32[]{:S(2)}) collective-permute-start(f32[64,128]{1,0:T(8,128)S(1)} %get-tuple-element.95), channel_id=1, source_target_pairs={{0,4},{4,0},{8,12},{12,8},{16,20},{20,16},{24,28},{28,24},{1,5},{5... | collective-permute-start | bytes 98312 | tf_op jit(solution)/shard_map/ppermute | solution.py:225
  26.3 2.9 %collective-permute-start.17 = (f32[64,128]{1,0:T(8,128)S(1)}, f32[64,128]{1,0:T(8,128)S(1)}, u32[]{:S(2)}, u32[]{:S(2)}) collective-permute-start(f32[64,128]{1,0:T(8,128)S(1)} %get-tuple-element.96), channel_id=1, source_target_pairs={{0,4},{4,0},{8,12},{12,8},{16,20},{20,16},{24,28},{28,24},{1,5},{5... | collective-permute-start | bytes 98312 | tf_op jit(solution)/shard_map/ppermute | solution.py:225
  29.5 4.9 %collective-permute-start.19 = (f32[64,128]{1,0:T(8,128)S(1)}, f32[64,128]{1,0:T(8,128)S(1)}, u32[]{:S(2)}, u32[]{:S(2)}) collective-permute-start(f32[64,128]{1,0:T(8,128)S(1)} %get-tuple-element.99), channel_id=1, source_target_pairs={{0,3},{1,2},{2,1},{3,0},{4,7},{5,6},{6,5},{7,4},{8,11},{9,10},{10,... | collective-permute-start | bytes 98312 | tf_op jit(solution)/shard_map/ppermute | solution.py:224
  31.1 5.5 %collective-permute-start.18 = (f32[128,128]{1,0:T(8,128)S(1)}, f32[128,128]{1,0:T(8,128)S(1)}, u32[]{:S(2)}, u32[]{:S(2)}) collective-permute-start(f32[128,128]{1,0:T(8,128)S(1)} %get-tuple-element.98), channel_id=1, source_target_pairs={{0,28},{4,8},{8,4},{12,16},{16,12},{20,24},{24,20},{28,0},{1,29},{... | collective-permute-start | bytes 196616 | tf_op jit(solution)/shard_map/ppermute | solution.py:222
  31.8 3.9 %collective-permute-start.20 = (f32[64,128]{1,0:T(8,128)S(1)}, f32[64,128]{1,0:T(8,128)S(1)}, u32[]{:S(2)}, u32[]{:S(2)}) collective-permute-start(f32[64,128]{1,0:T(8,128)S(1)} %get-tuple-element.100), channel_id=1, source_target_pairs={{0,2},{1,3},{2,0},{3,1},{4,6},{5,7},{6,4},{7,5},{8,10},{9,11},{10,... | collective-permute-start | bytes 98312 | tf_op jit(solution)/shard_map/ppermute | solution.py:224
  32.6 3.9 %collective-permute-start.21 = (f32[64,128]{1,0:T(8,128)S(1)}, f32[64,128]{1,0:T(8,128)S(1)}, u32[]{:S(2)}, u32[]{:S(2)}) collective-permute-start(f32[64,128]{1,0:T(8,128)S(1)} %get-tuple-element.101), channel_id=1, source_target_pairs={{0,1},{1,0},{2,3},{3,2},{4,5},{5,4},{6,7},{7,6},{8,9},{9,8},{10,11... | collective-permute-start | bytes 98312 | tf_op jit(solution)/shard_map/ppermute | solution.py:224
  34.1 2.4 %collective-permute-start.22 = (f32[64,128]{1,0:T(8,128)S(1)}, f32[64,128]{1,0:T(8,128)S(1)}, u32[]{:S(2)}, u32[]{:S(2)}) collective-permute-start(f32[64,128]{1,0:T(8,128)S(1)} %get-tuple-element.102), channel_id=1, source_target_pairs={{0,4},{4,0},{8,12},{12,8},{16,20},{20,16},{24,28},{28,24},{1,5},{5... | collective-permute-start | bytes 98312 | tf_op jit(solution)/shard_map/ppermute | solution.py:225
  34.4 2.1 %collective-permute-start.23 = (f32[64,128]{1,0:T(8,128)S(1)}, f32[64,128]{1,0:T(8,128)S(1)}, u32[]{:S(2)}, u32[]{:S(2)}) collective-permute-start(f32[64,128]{1,0:T(8,128)S(1)} %get-tuple-element.103), channel_id=1, source_target_pairs={{0,4},{4,0},{8,12},{12,8},{16,20},{20,16},{24,28},{28,24},{1,5},{5... | collective-permute-start | bytes 98312 | tf_op jit(solution)/shard_map/ppermute | solution.py:225
  36.9 4.9 %collective-permute-start.25 = (f32[64,128]{1,0:T(8,128)S(1)}, f32[64,128]{1,0:T(8,128)S(1)}, u32[]{:S(2)}, u32[]{:S(2)}) collective-permute-start(f32[64,128]{1,0:T(8,128)S(1)} %get-tuple-element.107), channel_id=1, source_target_pairs={{0,3},{1,2},{2,1},{3,0},{4,7},{5,6},{6,5},{7,4},{8,11},{9,10},{10,... | collective-permute-start | bytes 98312 | tf_op jit(solution)/shard_map/ppermute | solution.py:224
  38.4 6.2 %collective-permute-start.24 = (f32[128,128]{1,0:T(8,128)S(1)}, f32[128,128]{1,0:T(8,128)S(1)}, u32[]{:S(2)}, u32[]{:S(2)}) collective-permute-start(f32[128,128]{1,0:T(8,128)S(1)} %get-tuple-element.106), channel_id=1, source_target_pairs={{0,28},{4,8},{8,4},{12,16},{16,12},{20,24},{24,20},{28,0},{1,29},{... | collective-permute-start | bytes 196616 | tf_op jit(solution)/shard_map/ppermute | solution.py:222
  40.2 3.9 %collective-permute-start.26 = (f32[64,128]{1,0:T(8,128)S(1)}, f32[64,128]{1,0:T(8,128)S(1)}, u32[]{:S(2)}, u32[]{:S(2)}) collective-permute-start(f32[64,128]{1,0:T(8,128)S(1)} %get-tuple-element.108), channel_id=1, source_target_pairs={{0,2},{1,3},{2,0},{3,1},{4,6},{5,7},{6,4},{7,5},{8,10},{9,11},{10,... | collective-permute-start | bytes 98312 | tf_op jit(solution)/shard_map/ppermute | solution.py:224
  40.7 3.9 %collective-permute-start.27 = (f32[64,128]{1,0:T(8,128)S(1)}, f32[64,128]{1,0:T(8,128)S(1)}, u32[]{:S(2)}, u32[]{:S(2)}) collective-permute-start(f32[64,128]{1,0:T(8,128)S(1)} %get-tuple-element.109), channel_id=1, source_target_pairs={{0,1},{1,0},{2,3},{3,2},{4,5},{5,4},{6,7},{7,6},{8,9},{9,8},{10,11... | collective-permute-start | bytes 98312 | tf_op jit(solution)/shard_map/ppermute | solution.py:224
  41.2 3.4 %collective-permute-start.28 = (f32[64,128]{1,0:T(8,128)S(1)}, f32[64,128]{1,0:T(8,128)S(1)}, u32[]{:S(2)}, u32[]{:S(2)}) collective-permute-start(f32[64,128]{1,0:T(8,128)S(1)} %get-tuple-element.110), channel_id=1, source_target_pairs={{0,4},{4,0},{8,12},{12,8},{16,20},{20,16},{24,28},{28,24},{1,5},{5... | collective-permute-start | bytes 98312 | tf_op jit(solution)/shard_map/ppermute | solution.py:225
  41.7 2.9 %collective-permute-start.29 = (f32[64,128]{1,0:T(8,128)S(1)}, f32[64,128]{1,0:T(8,128)S(1)}, u32[]{:S(2)}, u32[]{:S(2)}) collective-permute-start(f32[64,128]{1,0:T(8,128)S(1)} %get-tuple-element.111), channel_id=1, source_target_pairs={{0,4},{4,0},{8,12},{12,8},{16,20},{20,16},{24,28},{28,24},{1,5},{5... | collective-permute-start | bytes 98312 | tf_op jit(solution)/shard_map/ppermute | solution.py:225
  44.9 4.9 %collective-permute-start.31 = (f32[64,128]{1,0:T(8,128)S(1)}, f32[64,128]{1,0:T(8,128)S(1)}, u32[]{:S(2)}, u32[]{:S(2)}) collective-permute-start(f32[64,128]{1,0:T(8,128)S(1)} %get-tuple-element.115), channel_id=1, source_target_pairs={{0,3},{1,2},{2,1},{3,0},{4,7},{5,6},{6,5},{7,4},{8,11},{9,10},{10,... | collective-permute-start | bytes 98312 | tf_op jit(solution)/shard_map/ppermute | solution.py:224
  46.5 5.5 %collective-permute-start.30 = (f32[128,128]{1,0:T(8,128)S(1)}, f32[128,128]{1,0:T(8,128)S(1)}, u32[]{:S(2)}, u32[]{:S(2)}) collective-permute-start(f32[128,128]{1,0:T(8,128)S(1)} %get-tuple-element.114), channel_id=1, source_target_pairs={{0,28},{4,8},{8,4},{12,16},{16,12},{20,24},{24,20},{28,0},{1,29},{... | collective-permute-start | bytes 196616 | tf_op jit(solution)/shard_map/ppermute | solution.py:222
  47.2 3.9 %collective-permute-start.32 = (f32[64,128]{1,0:T(8,128)S(1)}, f32[64,128]{1,0:T(8,128)S(1)}, u32[]{:S(2)}, u32[]{:S(2)}) collective-permute-start(f32[64,128]{1,0:T(8,128)S(1)} %get-tuple-element.116), channel_id=1, source_target_pairs={{0,2},{1,3},{2,0},{3,1},{4,6},{5,7},{6,4},{7,5},{8,10},{9,11},{10,... | collective-permute-start | bytes 98312 | tf_op jit(solution)/shard_map/ppermute | solution.py:224
  48.0 3.9 %collective-permute-start.33 = (f32[64,128]{1,0:T(8,128)S(1)}, f32[64,128]{1,0:T(8,128)S(1)}, u32[]{:S(2)}, u32[]{:S(2)}) collective-permute-start(f32[64,128]{1,0:T(8,128)S(1)} %get-tuple-element.117), channel_id=1, source_target_pairs={{0,1},{1,0},{2,3},{3,2},{4,5},{5,4},{6,7},{7,6},{8,9},{9,8},{10,11... | collective-permute-start | bytes 98312 | tf_op jit(solution)/shard_map/ppermute | solution.py:224
  49.5 2.4 %collective-permute-start.34 = (f32[64,128]{1,0:T(8,128)S(1)}, f32[64,128]{1,0:T(8,128)S(1)}, u32[]{:S(2)}, u32[]{:S(2)}) collective-permute-start(f32[64,128]{1,0:T(8,128)S(1)} %get-tuple-element.118), channel_id=1, source_target_pairs={{0,4},{4,0},{8,12},{12,8},{16,20},{20,16},{24,28},{28,24},{1,5},{5... | collective-permute-start | bytes 98312 | tf_op jit(solution)/shard_map/ppermute | solution.py:225
  49.9 2.1 %collective-permute-start.35 = (f32[64,128]{1,0:T(8,128)S(1)}, f32[64,128]{1,0:T(8,128)S(1)}, u32[]{:S(2)}, u32[]{:S(2)}) collective-permute-start(f32[64,128]{1,0:T(8,128)S(1)} %get-tuple-element.119), channel_id=1, source_target_pairs={{0,4},{4,0},{8,12},{12,8},{16,20},{20,16},{24,28},{28,24},{1,5},{5... | collective-permute-start | bytes 98312 | tf_op jit(solution)/shard_map/ppermute | solution.py:225
  52.3 4.9 %collective-permute-start.37 = (f32[64,128]{1,0:T(8,128)S(1)}, f32[64,128]{1,0:T(8,128)S(1)}, u32[]{:S(2)}, u32[]{:S(2)}) collective-permute-start(f32[64,128]{1,0:T(8,128)S(1)} %get-tuple-element.123), channel_id=1, source_target_pairs={{0,3},{1,2},{2,1},{3,0},{4,7},{5,6},{6,5},{7,4},{8,11},{9,10},{10,... | collective-permute-start | bytes 98312 | tf_op jit(solution)/shard_map/ppermute | solution.py:224
  53.8 6.2 %collective-permute-start.36 = (f32[128,128]{1,0:T(8,128)S(1)}, f32[128,128]{1,0:T(8,128)S(1)}, u32[]{:S(2)}, u32[]{:S(2)}) collective-permute-start(f32[128,128]{1,0:T(8,128)S(1)} %get-tuple-element.122), channel_id=1, source_target_pairs={{0,28},{4,8},{8,4},{12,16},{16,12},{20,24},{24,20},{28,0},{1,29},{... | collective-permute-start | bytes 196616 | tf_op jit(solution)/shard_map/ppermute | solution.py:222
  55.6 3.9 %collective-permute-start.38 = (f32[64,128]{1,0:T(8,128)S(1)}, f32[64,128]{1,0:T(8,128)S(1)}, u32[]{:S(2)}, u32[]{:S(2)}) collective-permute-start(f32[64,128]{1,0:T(8,128)S(1)} %get-tuple-element.124), channel_id=1, source_target_pairs={{0,2},{1,3},{2,0},{3,1},{4,6},{5,7},{6,4},{7,5},{8,10},{9,11},{10,... | collective-permute-start | bytes 98312 | tf_op jit(solution)/shard_map/ppermute | solution.py:224
  56.1 3.9 %collective-permute-start.39 = (f32[64,128]{1,0:T(8,128)S(1)}, f32[64,128]{1,0:T(8,128)S(1)}, u32[]{:S(2)}, u32[]{:S(2)}) collective-permute-start(f32[64,128]{1,0:T(8,128)S(1)} %get-tuple-element.125), channel_id=1, source_target_pairs={{0,1},{1,0},{2,3},{3,2},{4,5},{5,4},{6,7},{7,6},{8,9},{9,8},{10,11... | collective-permute-start | bytes 98312 | tf_op jit(solution)/shard_map/ppermute | solution.py:224
  56.6 3.4 %collective-permute-start.40 = (f32[64,128]{1,0:T(8,128)S(1)}, f32[64,128]{1,0:T(8,128)S(1)}, u32[]{:S(2)}, u32[]{:S(2)}) collective-permute-start(f32[64,128]{1,0:T(8,128)S(1)} %get-tuple-element.126), channel_id=1, source_target_pairs={{0,4},{4,0},{8,12},{12,8},{16,20},{20,16},{24,28},{28,24},{1,5},{5... | collective-permute-start | bytes 98312 | tf_op jit(solution)/shard_map/ppermute | solution.py:225
  57.2 2.9 %collective-permute-start.41 = (f32[64,128]{1,0:T(8,128)S(1)}, f32[64,128]{1,0:T(8,128)S(1)}, u32[]{:S(2)}, u32[]{:S(2)}) collective-permute-start(f32[64,128]{1,0:T(8,128)S(1)} %get-tuple-element.127), channel_id=1, source_target_pairs={{0,4},{4,0},{8,12},{12,8},{16,20},{20,16},{24,28},{28,24},{1,5},{5... | collective-permute-start | bytes 98312 | tf_op jit(solution)/shard_map/ppermute | solution.py:225
  60.3 4.9 %collective-permute-start.43 = (f32[64,128]{1,0:T(8,128)S(1)}, f32[64,128]{1,0:T(8,128)S(1)}, u32[]{:S(2)}, u32[]{:S(2)}) collective-permute-start(f32[64,128]{1,0:T(8,128)S(1)} %get-tuple-element.137), channel_id=1, source_target_pairs={{0,3},{1,2},{2,1},{3,0},{4,7},{5,6},{6,5},{7,4},{8,11},{9,10},{10,... | collective-permute-start | bytes 98312 | tf_op jit(solution)/shard_map/ppermute | solution.py:224
  61.9 5.5 %collective-permute-start.42 = (f32[128,128]{1,0:T(8,128)S(1)}, f32[128,128]{1,0:T(8,128)S(1)}, u32[]{:S(2)}, u32[]{:S(2)}) collective-permute-start(f32[128,128]{1,0:T(8,128)S(1)} %get-tuple-element.136), channel_id=1, source_target_pairs={{0,28},{4,8},{8,4},{12,16},{16,12},{20,24},{24,20},{28,0},{1,29},{... | collective-permute-start | bytes 196616 | tf_op jit(solution)/shard_map/ppermute | solution.py:222
  62.6 3.9 %collective-permute-start.44 = (f32[64,128]{1,0:T(8,128)S(1)}, f32[64,128]{1,0:T(8,128)S(1)}, u32[]{:S(2)}, u32[]{:S(2)}) collective-permute-start(f32[64,128]{1,0:T(8,128)S(1)} %get-tuple-element.138), channel_id=1, source_target_pairs={{0,2},{1,3},{2,0},{3,1},{4,6},{5,7},{6,4},{7,5},{8,10},{9,11},{10,... | collective-permute-start | bytes 98312 | tf_op jit(solution)/shard_map/ppermute | solution.py:224
  63.4 3.9 %collective-permute-start.45 = (f32[64,128]{1,0:T(8,128)S(1)}, f32[64,128]{1,0:T(8,128)S(1)}, u32[]{:S(2)}, u32[]{:S(2)}) collective-permute-start(f32[64,128]{1,0:T(8,128)S(1)} %get-tuple-element.139), channel_id=1, source_target_pairs={{0,1},{1,0},{2,3},{3,2},{4,5},{5,4},{6,7},{7,6},{8,9},{9,8},{10,11... | collective-permute-start | bytes 98312 | tf_op jit(solution)/shard_map/ppermute | solution.py:224
  64.9 2.4 %collective-permute-start.46 = (f32[64,128]{1,0:T(8,128)S(1)}, f32[64,128]{1,0:T(8,128)S(1)}, u32[]{:S(2)}, u32[]{:S(2)}) collective-permute-start(f32[64,128]{1,0:T(8,128)S(1)} %get-tuple-element.140), channel_id=1, source_target_pairs={{0,4},{4,0},{8,12},{12,8},{16,20},{20,16},{24,28},{28,24},{1,5},{5... | collective-permute-start | bytes 98312 | tf_op jit(solution)/shard_map/ppermute | solution.py:225
  65.2 2.2 %collective-permute-start.47 = (f32[64,128]{1,0:T(8,128)S(1)}, f32[64,128]{1,0:T(8,128)S(1)}, u32[]{:S(2)}, u32[]{:S(2)}) collective-permute-start(f32[64,128]{1,0:T(8,128)S(1)} %get-tuple-element.141), channel_id=1, source_target_pairs={{0,4},{4,0},{8,12},{12,8},{16,20},{20,16},{24,28},{28,24},{1,5},{5... | collective-permute-start | bytes 98312 | tf_op jit(solution)/shard_map/ppermute | solution.py:225

commit v12 on v10

--- a/solution.py
+++ b/solution.py
@@ -89,10 +89,11 @@
     color, local_target, group_peer, group_list, dom_target = scratch[:5]
     sems = scratch[5]
     targets = (color, group_peer, group_list, dom_target, local_target, rhs, diag, coupling)
-    copies = [
-        pltpu.make_async_copy(src, dst, sems.at[i]) for i, (src, dst) in enumerate(zip(hbm, targets))
-    ]
-    for copy in copies[7:] + copies[:7]:
+    pieces = list(zip(hbm[:7], targets[:7]))
+    for part in (pl.ds(2, coupling.shape[1] - 2), pl.ds(0, 2)):
+        pieces.append((hbm[7].at[:, part], coupling.at[:, part]))
+    copies = [pltpu.make_async_copy(src, dst, sems.at[i]) for i, (src, dst) in enumerate(pieces)]
+    for copy in copies[7:8] + copies[:7] + copies[8:]:
         copy.start()
     for copy in copies[:5]:
         copy.wait()
@@ -136,6 +137,7 @@
     for at in range(plan.rows):
         meta = jnp.where(line == at, dom_target[1 - parity, table[plan.order + at]], meta)
     sends[0][pl.ds(plan.quarter * plan.n, plan.dom_meta), :] = meta.astype(jnp.float32)
+    copies[8].wait()
 
 
 def step_kernel(plan, step, table, resid, diag, coupling, *refs):
@@ -247,7 +249,7 @@
         ]
         + plan.types(0),
         scratch_shapes=[pltpu.SMEM(shape, jnp.int32) for shape in table_scratch]
-        + [pltpu.SemaphoreType.DMA((len(hbm),))],
+        + [pltpu.SemaphoreType.DMA((len(hbm) + 1,))],
     )
     sols = [sol]
     got = meta = None

time: 68.4 us -> 68.2 us (level)
  no operation moved by 1% of the time
where the time goes in v12:
time: 68.2 us; the launch traced here: 68.1 us
  starting transfers between devices  40.1 us (59%)
  waiting for transfers between devices  20.1 us (29%)
  Pallas kernels  7.1 us (10%)
  between operations  0.79 us (1%)
    ppermute x24, starting transfers between devices, exchange(): got.append(lax.ppermute(send, 'sub', [(i, i ^ s) for i in range(group)]))  27.8 us
    ppermute x24, waiting for transfers between devices, exchange(): got.append(lax.ppermute(send, 'sub', [(i, i ^ s) for i in range(group)]))  19.7 us
    ppermute x8, starting transfers between devices, exchange(): got = [lax.ppermute(sends[0], 'dom', far_pairs)]  11.1 us
    pallas_call x17, Pallas kernels, call(): pl.pallas_call(body, name=name, in_specs=in_specs + [VMEM] * (len(ins) -...  7.1 us
  transfers between devices with their start and end apart: 48, of which 24 were waited for; matrix products, arithmetic and copies ran while one was open for 0% of the time, Pallas kernels for 3%

profile of v12, /device:TPU:0, one launch (start us, length us, event | category | flops | bytes accessed | tf_op | source)
XLA Modules:
  0.0 68.1 jit_solution(17606549981498582443)
XLA Ops:
  0.6 1.8 %first.1 = (s32[40]{0:T(128)S(4)}, bf16[8,6,128,128]{3,2,1,0:T(8,128)(2,1)S(1)}, bf16[8,128,128]{2,1,0:T(8,128)(2,1)S(1)}, f32[8,64,128]{2,1,0:T(8,128)S(1)}, f3...) custom-call(s32[8]{0:T(128)} %refs_0_.1, ...), custom_call_target="tpu_custom_call" | custom-call | tf_op jit(solution)/shard_map/first/pallas_call | solution.py:215
  2.4 4.0 %collective-permute-start.1 = (f32[72,128]{1,0:T(8,128)S(1)}, f32[72,128]{1,0:T(8,128)S(1)}, u32[]{:S(2)}, u32[]{:S(2)}) collective-permute-start(f32[72,128]{1,0:T(8,128)S(1)} %get-tuple-element.78), channel_id=1, source_target_pairs={{0,3},{1,2},{2,1},{3,0},{4,7},{5,6},{6,5},{7,4},{8,11},{9,10},{10,... | collective-permute-start | bytes 110600 | tf_op jit(solution)/shard_map/ppermute | solution.py:228
  6.4 2.8 %collective-permute-start = (f32[136,128]{1,0:T(8,128)S(1)}, f32[136,128]{1,0:T(8,128)S(1)}, u32[]{:S(2)}, u32[]{:S(2)}) collective-permute-start(f32[136,128]{1,0:T(8,128)S(1)} %get-tuple-element.77), channel_id=1, source_target_pairs={{0,28},{4,8},{8,4},{12,16},{16,12},{20,24},{24,20},{28,0},{1,29},{... | collective-permute-start | bytes 208904 | tf_op jit(solution)/shard_map/ppermute | solution.py:226
  9.7 0.5 collective-permute-start.3
  10.2 0.5 collective-permute-start.5
  10.9 2.2 %collective-permute-done.2.refs_2_.refs_8_ = f32[72,128]{1,0:T(8,128)S(1)} collective-permute-done((f32[72,128]{1,0:T(8,128)S(1)}, f32[72,128]{1,0:T(8,128)S(1)}, u32[]{:S(2)}, u32[]{:S(2)}) %collective-permute-start.2) | collective-permute-done | bytes 36896 | tf_op jit(solution)/shard_map/ppermute | solution.py:228
  14.0 1.6 %collective-permute-start.7 = (f32[64,128]{1,0:T(8,128)S(1)}, f32[64,128]{1,0:T(8,128)S(1)}, u32[]{:S(2)}, u32[]{:S(2)}) collective-permute-start(f32[64,128]{1,0:T(8,128)S(1)} %get-tuple-element.85), channel_id=1, source_target_pairs={{0,3},{1,2},{2,1},{3,0},{4,7},{5,6},{6,5},{7,4},{8,11},{9,10},{10,... | collective-permute-start | bytes 98312 | tf_op jit(solution)/shard_map/ppermute | solution.py:228
  15.5 0.7 %collective-permute-start.6 = (f32[128,128]{1,0:T(8,128)S(1)}, f32[128,128]{1,0:T(8,128)S(1)}, u32[]{:S(2)}, u32[]{:S(2)}) collective-permute-start(f32[128,128]{1,0:T(8,128)S(1)} %get-tuple-element.84), channel_id=1, source_target_pairs={{0,28},{4,8},{8,4},{12,16},{16,12},{20,24},{24,20},{28,0},{1,29},{... | collective-permute-start | bytes 196616 | tf_op jit(solution)/shard_map/ppermute | solution.py:226
  16.2 0.5 collective-permute-start.8
  16.8 1.5 %collective-permute-start.9 = (f32[64,128]{1,0:T(8,128)S(1)}, f32[64,128]{1,0:T(8,128)S(1)}, u32[]{:S(2)}, u32[]{:S(2)}) collective-permute-start(f32[64,128]{1,0:T(8,128)S(1)} %get-tuple-element.87), channel_id=1, source_target_pairs={{0,1},{1,0},{2,3},{3,2},{4,5},{5,4},{6,7},{7,6},{8,9},{9,8},{10,11... | collective-permute-start | bytes 98312 | tf_op jit(solution)/shard_map/ppermute | solution.py:228
  18.3 0.7 %collective-permute-done.7.refs_1_ = f32[64,128]{1,0:T(8,128)S(1)} collective-permute-done((f32[64,128]{1,0:T(8,128)S(1)}, f32[64,128]{1,0:T(8,128)S(1)}, u32[]{:S(2)}, u32[]{:S(2)}) %collective-permute-start.7) | collective-permute-done | bytes 32800 | tf_op jit(solution)/shard_map/ppermute | solution.py:228
  19.2 0.9 %collective-permute-done.8.refs_2_ = f32[64,128]{1,0:T(8,128)S(1)} collective-permute-done((f32[64,128]{1,0:T(8,128)S(1)}, f32[64,128]{1,0:T(8,128)S(1)}, u32[]{:S(2)}, u32[]{:S(2)}) %collective-permute-start.8) | collective-permute-done | bytes 32800 | tf_op jit(solution)/shard_map/ppermute | solution.py:228
  20.1 0.5 collective-permute-done.9.refs_3_
  21.3 1.5 %collective-permute-start.13 = (f32[64,128]{1,0:T(8,128)S(1)}, f32[64,128]{1,0:T(8,128)S(1)}, u32[]{:S(2)}, u32[]{:S(2)}) collective-permute-start(f32[64,128]{1,0:T(8,128)S(1)} %get-tuple-element.92), channel_id=1, source_target_pairs={{0,3},{1,2},{2,1},{3,0},{4,7},{5,6},{6,5},{7,4},{8,11},{9,10},{10,... | collective-permute-start | bytes 98312 | tf_op jit(solution)/shard_map/ppermute | solution.py:228
  22.8 1.8 %collective-permute-start.12 = (f32[128,128]{1,0:T(8,128)S(1)}, f32[128,128]{1,0:T(8,128)S(1)}, u32[]{:S(2)}, u32[]{:S(2)}) collective-permute-start(f32[128,128]{1,0:T(8,128)S(1)} %get-tuple-element.91), channel_id=1, source_target_pairs={{0,28},{4,8},{8,4},{12,16},{16,12},{20,24},{24,20},{28,0},{1,29},{... | collective-permute-start | bytes 196616 | tf_op jit(solution)/shard_map/ppermute | solution.py:226
  25.1 0.5 collective-permute-start.15
  25.7 0.5 collective-permute-done.13.refs_1_
  26.4 2.1 %collective-permute-done.14.refs_2_ = f32[64,128]{1,0:T(8,128)S(1)} collective-permute-done((f32[64,128]{1,0:T(8,128)S(1)}, f32[64,128]{1,0:T(8,128)S(1)}, u32[]{:S(2)}, u32[]{:S(2)}) %collective-permute-start.14) | collective-permute-done | bytes 32800 | tf_op jit(solution)/shard_map/ppermute | solution.py:228
  29.4 1.6 %collective-permute-start.19 = (f32[64,128]{1,0:T(8,128)S(1)}, f32[64,128]{1,0:T(8,128)S(1)}, u32[]{:S(2)}, u32[]{:S(2)}) collective-permute-start(f32[64,128]{1,0:T(8,128)S(1)} %get-tuple-element.99), channel_id=1, source_target_pairs={{0,3},{1,2},{2,1},{3,0},{4,7},{5,6},{6,5},{7,4},{8,11},{9,10},{10,... | collective-permute-start | bytes 98312 | tf_op jit(solution)/shard_map/ppermute | solution.py:228
  30.9 0.7 %collective-permute-start.18 = (f32[128,128]{1,0:T(8,128)S(1)}, f32[128,128]{1,0:T(8,128)S(1)}, u32[]{:S(2)}, u32[]{:S(2)}) collective-permute-start(f32[128,128]{1,0:T(8,128)S(1)} %get-tuple-element.98), channel_id=1, source_target_pairs={{0,28},{4,8},{8,4},{12,16},{16,12},{20,24},{24,20},{28,0},{1,29},{... | collective-permute-start | bytes 196616 | tf_op jit(solution)/shard_map/ppermute | solution.py:226
  31.6 0.8 %collective-permute-start.20 = (f32[64,128]{1,0:T(8,128)S(1)}, f32[64,128]{1,0:T(8,128)S(1)}, u32[]{:S(2)}, u32[]{:S(2)}) collective-permute-start(f32[64,128]{1,0:T(8,128)S(1)} %get-tuple-element.100), channel_id=1, source_target_pairs={{0,2},{1,3},{2,0},{3,1},{4,6},{5,7},{6,4},{7,5},{8,10},{9,11},{10,... | collective-permute-start | bytes 98312 | tf_op jit(solution)/shard_map/ppermute | solution.py:228
  32.5 1.5 %collective-permute-start.21 = (f32[64,128]{1,0:T(8,128)S(1)}, f32[64,128]{1,0:T(8,128)S(1)}, u32[]{:S(2)}, u32[]{:S(2)}) collective-permute-start(f32[64,128]{1,0:T(8,128)S(1)} %get-tuple-element.101), channel_id=1, source_target_pairs={{0,1},{1,0},{2,3},{3,2},{4,5},{5,4},{6,7},{7,6},{8,9},{9,8},{10,11... | collective-permute-start | bytes 98312 | tf_op jit(solution)/shard_map/ppermute | solution.py:228
  34.7 0.9 %collective-permute-done.20.refs_2_ = f32[64,128]{1,0:T(8,128)S(1)} collective-permute-done((f32[64,128]{1,0:T(8,128)S(1)}, f32[64,128]{1,0:T(8,128)S(1)}, u32[]{:S(2)}, u32[]{:S(2)}) %collective-permute-start.20) | collective-permute-done | bytes 32800 | tf_op jit(solution)/shard_map/ppermute | solution.py:228
  35.6 0.8 %collective-permute-done.21.refs_3_ = f32[64,128]{1,0:T(8,128)S(1)} collective-permute-done((f32[64,128]{1,0:T(8,128)S(1)}, f32[64,128]{1,0:T(8,128)S(1)}, u32[]{:S(2)}, u32[]{:S(2)}) %collective-permute-start.21) | collective-permute-done | bytes 32800 | tf_op jit(solution)/shard_map/ppermute | solution.py:228
  36.7 1.5 %collective-permute-start.25 = (f32[64,128]{1,0:T(8,128)S(1)}, f32[64,128]{1,0:T(8,128)S(1)}, u32[]{:S(2)}, u32[]{:S(2)}) collective-permute-start(f32[64,128]{1,0:T(8,128)S(1)} %get-tuple-element.107), channel_id=1, source_target_pairs={{0,3},{1,2},{2,1},{3,0},{4,7},{5,6},{6,5},{7,4},{8,11},{9,10},{10,... | collective-permute-start | bytes 98312 | tf_op jit(solution)/shard_map/ppermute | solution.py:228
  38.2 1.8 %collective-permute-start.24 = (f32[128,128]{1,0:T(8,128)S(1)}, f32[128,128]{1,0:T(8,128)S(1)}, u32[]{:S(2)}, u32[]{:S(2)}) collective-permute-start(f32[128,128]{1,0:T(8,128)S(1)} %get-tuple-element.106), channel_id=1, source_target_pairs={{0,28},{4,8},{8,4},{12,16},{16,12},{20,24},{24,20},{28,0},{1,29},{... | collective-permute-start | bytes 196616 | tf_op jit(solution)/shard_map/ppermute | solution.py:226
  40.0 0.5 collective-permute-start.26
  40.5 0.5 collective-permute-start.27
  41.1 0.5 collective-permute-done.25.refs_1_
  41.8 2.1 %collective-permute-done.26.refs_2_ = f32[64,128]{1,0:T(8,128)S(1)} collective-permute-done((f32[64,128]{1,0:T(8,128)S(1)}, f32[64,128]{1,0:T(8,128)S(1)}, u32[]{:S(2)}, u32[]{:S(2)}) %collective-permute-start.26) | collective-permute-done | bytes 32800 | tf_op jit(solution)/shard_map/ppermute | solution.py:228
  44.8 1.6 %collective-permute-start.31 = (f32[64,128]{1,0:T(8,128)S(1)}, f32[64,128]{1,0:T(8,128)S(1)}, u32[]{:S(2)}, u32[]{:S(2)}) collective-permute-start(f32[64,128]{1,0:T(8,128)S(1)} %get-tuple-element.115), channel_id=1, source_target_pairs={{0,3},{1,2},{2,1},{3,0},{4,7},{5,6},{6,5},{7,4},{8,11},{9,10},{10,... | collective-permute-start | bytes 98312 | tf_op jit(solution)/shard_map/ppermute | solution.py:228
  46.3 0.7 %collective-permute-start.30 = (f32[128,128]{1,0:T(8,128)S(1)}, f32[128,128]{1,0:T(8,128)S(1)}, u32[]{:S(2)}, u32[]{:S(2)}) collective-permute-start(f32[128,128]{1,0:T(8,128)S(1)} %get-tuple-element.114), channel_id=1, source_target_pairs={{0,28},{4,8},{8,4},{12,16},{16,12},{20,24},{24,20},{28,0},{1,29},{... | collective-permute-start | bytes 196616 | tf_op jit(solution)/shard_map/ppermute | solution.py:226
  47.1 0.8 %collective-permute-start.32 = (f32[64,128]{1,0:T(8,128)S(1)}, f32[64,128]{1,0:T(8,128)S(1)}, u32[]{:S(2)}, u32[]{:S(2)}) collective-permute-start(f32[64,128]{1,0:T(8,128)S(1)} %get-tuple-element.116), channel_id=1, source_target_pairs={{0,2},{1,3},{2,0},{3,1},{4,6},{5,7},{6,4},{7,5},{8,10},{9,11},{10,... | collective-permute-start | bytes 98312 | tf_op jit(solution)/shard_map/ppermute | solution.py:228
  47.9 1.5 %collective-permute-start.33 = (f32[64,128]{1,0:T(8,128)S(1)}, f32[64,128]{1,0:T(8,128)S(1)}, u32[]{:S(2)}, u32[]{:S(2)}) collective-permute-start(f32[64,128]{1,0:T(8,128)S(1)} %get-tuple-element.117), channel_id=1, source_target_pairs={{0,1},{1,0},{2,3},{3,2},{4,5},{5,4},{6,7},{7,6},{8,9},{9,8},{10,11... | collective-permute-start | bytes 98312 | tf_op jit(solution)/shard_map/ppermute | solution.py:228
  50.1 0.9 %collective-permute-done.32.refs_2_ = f32[64,128]{1,0:T(8,128)S(1)} collective-permute-done((f32[64,128]{1,0:T(8,128)S(1)}, f32[64,128]{1,0:T(8,128)S(1)}, u32[]{:S(2)}, u32[]{:S(2)}) %collective-permute-start.32) | collective-permute-done | bytes 32800 | tf_op jit(solution)/shard_map/ppermute | solution.py:228
  51.0 0.8 %collective-permute-done.33.refs_3_ = f32[64,128]{1,0:T(8,128)S(1)} collective-permute-done((f32[64,128]{1,0:T(8,128)S(1)}, f32[64,128]{1,0:T(8,128)S(1)}, u32[]{:S(2)}, u32[]{:S(2)}) %collective-permute-start.33) | collective-permute-done | bytes 32800 | tf_op jit(solution)/shard_map/ppermute | solution.py:228
  52.1 1.5 %collective-permute-start.37 = (f32[64,128]{1,0:T(8,128)S(1)}, f32[64,128]{1,0:T(8,128)S(1)}, u32[]{:S(2)}, u32[]{:S(2)}) collective-permute-start(f32[64,128]{1,0:T(8,128)S(1)} %get-tuple-element.123), channel_id=1, source_target_pairs={{0,3},{1,2},{2,1},{3,0},{4,7},{5,6},{6,5},{7,4},{8,11},{9,10},{10,... | collective-permute-start | bytes 98312 | tf_op jit(solution)/shard_map/ppermute | solution.py:228
  53.6 1.8 %collective-permute-start.36 = (f32[128,128]{1,0:T(8,128)S(1)}, f32[128,128]{1,0:T(8,128)S(1)}, u32[]{:S(2)}, u32[]{:S(2)}) collective-permute-start(f32[128,128]{1,0:T(8,128)S(1)} %get-tuple-element.122), channel_id=1, source_target_pairs={{0,28},{4,8},{8,4},{12,16},{16,12},{20,24},{24,20},{28,0},{1,29},{... | collective-permute-start | bytes 196616 | tf_op jit(solution)/shard_map/ppermute | solution.py:226
  55.9 0.5 collective-permute-start.39
  56.5 0.5 collective-permute-done.37.refs_1_
  57.2 2.1 %collective-permute-done.38.refs_2_ = f32[64,128]{1,0:T(8,128)S(1)} collective-permute-done((f32[64,128]{1,0:T(8,128)S(1)}, f32[64,128]{1,0:T(8,128)S(1)}, u32[]{:S(2)}, u32[]{:S(2)}) %collective-permute-start.38) | collective-permute-done | bytes 32800 | tf_op jit(solution)/shard_map/ppermute | solution.py:228
  60.2 1.6 %collective-permute-start.43 = (f32[64,128]{1,0:T(8,128)S(1)}, f32[64,128]{1,0:T(8,128)S(1)}, u32[]{:S(2)}, u32[]{:S(2)}) collective-permute-start(f32[64,128]{1,0:T(8,128)S(1)} %get-tuple-element.137), channel_id=1, source_target_pairs={{0,3},{1,2},{2,1},{3,0},{4,7},{5,6},{6,5},{7,4},{8,11},{9,10},{10,... | collective-permute-start | bytes 98312 | tf_op jit(solution)/shard_map/ppermute | solution.py:228
  61.7 0.7 %collective-permute-start.42 = (f32[128,128]{1,0:T(8,128)S(1)}, f32[128,128]{1,0:T(8,128)S(1)}, u32[]{:S(2)}, u32[]{:S(2)}) collective-permute-start(f32[128,128]{1,0:T(8,128)S(1)} %get-tuple-element.136), channel_id=1, source_target_pairs={{0,28},{4,8},{8,4},{12,16},{16,12},{20,24},{24,20},{28,0},{1,29},{... | collective-permute-start | bytes 196616 | tf_op jit(solution)/shard_map/ppermute | solution.py:226
  62.5 0.8 %collective-permute-start.44 = (f32[64,128]{1,0:T(8,128)S(1)}, f32[64,128]{1,0:T(8,128)S(1)}, u32[]{:S(2)}, u32[]{:S(2)}) collective-permute-start(f32[64,128]{1,0:T(8,128)S(1)} %get-tuple-element.138), channel_id=1, source_target_pairs={{0,2},{1,3},{2,0},{3,1},{4,6},{5,7},{6,4},{7,5},{8,10},{9,11},{10,... | collective-permute-start | bytes 98312 | tf_op jit(solution)/shard_map/ppermute | solution.py:228
  63.3 1.5 %collective-permute-start.45 = (f32[64,128]{1,0:T(8,128)S(1)}, f32[64,128]{1,0:T(8,128)S(1)}, u32[]{:S(2)}, u32[]{:S(2)}) collective-permute-start(f32[64,128]{1,0:T(8,128)S(1)} %get-tuple-element.139), channel_id=1, source_target_pairs={{0,1},{1,0},{2,3},{3,2},{4,5},{5,4},{6,7},{7,6},{8,9},{9,8},{10,11... | collective-permute-start | bytes 98312 | tf_op jit(solution)/shard_map/ppermute | solution.py:228
  65.3 0.9 %local7.1 = (f32[8,64,128]{2,1,0:T(8,128)S(1)}, f32[8,64,128]{2,1,0:T(8,128)}) custom-call(s32[40]{0:T(128)S(4)} %get-tuple-element.72.table, f32[8,64,128]{2,1,0:T(8,128)S(1)} %local6.1.resid, bf16[8,6,128,128]{3,2,1,0:T(8,128)(2,1)S(1)} %get-tuple-element.74.coupling, ...), custom_call_target="tpu_custom_call", output_to_operand_aliasing={{0}: (1, {})} | custom-call | tf_op jit(solution)/shard_map/local7/pallas_call | solution.py:215
  66.4 0.8 %collective-permute-done.45.refs_3_ = f32[64,128]{1,0:T(8,128)S(1)} collective-permute-done((f32[64,128]{1,0:T(8,128)S(1)}, f32[64,128]{1,0:T(8,128)S(1)}, u32[]{:S(2)}, u32[]{:S(2)}) %collective-permute-start.45) | collective-permute-done | bytes 32800 | tf_op jit(solution)/shard_map/ppermute | solution.py:228
  67.2 0.8 %final.1 = f32[8,64,128]{2,1,0:T(8,128)} custom-call(f32[8,64,128]{2,1,0:T(8,128)S(1)} %get-tuple-element.135.resid, f32[128,128]{1,0:T(8,128)S(1)} %collective-permute-done.42.refs_0_, f32[64,128]{1,0:T(8,128)S(1)} %collective-permute-done.43.refs_1_, f32[64,128]{1,0:T(8,128)S(1)} %collective-permute-done.44.refs_2_, ...), custom_call_target="tpu_custom_call" | custom-call | tf_op jit(solution)/shard_map/final/pallas_call | solution.py:215
  (65 shorter events, 9.3 us)
Async XLA Ops:
  2.4 7.8 %collective-permute-start.1 = (f32[72,128]{1,0:T(8,128)S(1)}, f32[72,128]{1,0:T(8,128)S(1)}, u32[]{:S(2)}, u32[]{:S(2)}) collective-permute-start(f32[72,128]{1,0:T(8,128)S(1)} %get-tuple-element.78), channel_id=1, source_target_pairs={{0,3},{1,2},{2,1},{3,0},{4,7},{5,6},{6,5},{7,4},{8,11},{9,10},{10,... | collective-permute-start | bytes 110600 | tf_op jit(solution)/shard_map/ppermute | solution.py:228
  6.4 7.2 %collective-permute-start = (f32[136,128]{1,0:T(8,128)S(1)}, f32[136,128]{1,0:T(8,128)S(1)}, u32[]{:S(2)}, u32[]{:S(2)}) collective-permute-start(f32[136,128]{1,0:T(8,128)S(1)} %get-tuple-element.77), channel_id=1, source_target_pairs={{0,28},{4,8},{8,4},{12,16},{16,12},{20,24},{24,20},{28,0},{1,29},{... | collective-permute-start | bytes 208904 | tf_op jit(solution)/shard_map/ppermute | solution.py:226
  9.2 4.0 %collective-permute-start.2 = (f32[72,128]{1,0:T(8,128)S(1)}, f32[72,128]{1,0:T(8,128)S(1)}, u32[]{:S(2)}, u32[]{:S(2)}) collective-permute-start(f32[72,128]{1,0:T(8,128)S(1)} %get-tuple-element.79), channel_id=1, source_target_pairs={{0,2},{1,3},{2,0},{3,1},{4,6},{5,7},{6,4},{7,5},{8,10},{9,11},{10,... | collective-permute-start | bytes 110600 | tf_op jit(solution)/shard_map/ppermute | solution.py:228
  9.7 4.0 %collective-permute-start.3 = (f32[72,128]{1,0:T(8,128)S(1)}, f32[72,128]{1,0:T(8,128)S(1)}, u32[]{:S(2)}, u32[]{:S(2)}) collective-permute-start(f32[72,128]{1,0:T(8,128)S(1)} %get-tuple-element.80), channel_id=1, source_target_pairs={{0,1},{1,0},{2,3},{3,2},{4,5},{5,4},{6,7},{7,6},{8,9},{9,8},{10,11... | collective-permute-start | bytes 110600 | tf_op jit(solution)/shard_map/ppermute | solution.py:228
  10.2 3.4 %collective-permute-start.4 = (f32[72,128]{1,0:T(8,128)S(1)}, f32[72,128]{1,0:T(8,128)S(1)}, u32[]{:S(2)}, u32[]{:S(2)}) collective-permute-start(f32[72,128]{1,0:T(8,128)S(1)} %get-tuple-element.81), channel_id=1, source_target_pairs={{0,4},{4,0},{8,12},{12,8},{16,20},{20,16},{24,28},{28,24},{1,5},{5... | collective-permute-start | bytes 110600 | tf_op jit(solution)/shard_map/ppermute | solution.py:229
  10.2 3.4 %collective-permute-start.5 = (f32[72,128]{1,0:T(8,128)S(1)}, f32[72,128]{1,0:T(8,128)S(1)}, u32[]{:S(2)}, u32[]{:S(2)}) collective-permute-start(f32[72,128]{1,0:T(8,128)S(1)} %get-tuple-element.82), channel_id=1, source_target_pairs={{0,4},{4,0},{8,12},{12,8},{16,20},{20,16},{24,28},{28,24},{1,5},{5... | collective-permute-start | bytes 110600 | tf_op jit(solution)/shard_map/ppermute | solution.py:229
  14.0 5.1 %collective-permute-start.7 = (f32[64,128]{1,0:T(8,128)S(1)}, f32[64,128]{1,0:T(8,128)S(1)}, u32[]{:S(2)}, u32[]{:S(2)}) collective-permute-start(f32[64,128]{1,0:T(8,128)S(1)} %get-tuple-element.85), channel_id=1, source_target_pairs={{0,3},{1,2},{2,1},{3,0},{4,7},{5,6},{6,5},{7,4},{8,11},{9,10},{10,... | collective-permute-start | bytes 98312 | tf_op jit(solution)/shard_map/ppermute | solution.py:228
  15.5 5.5 %collective-permute-start.6 = (f32[128,128]{1,0:T(8,128)S(1)}, f32[128,128]{1,0:T(8,128)S(1)}, u32[]{:S(2)}, u32[]{:S(2)}) collective-permute-start(f32[128,128]{1,0:T(8,128)S(1)} %get-tuple-element.84), channel_id=1, source_target_pairs={{0,28},{4,8},{8,4},{12,16},{16,12},{20,24},{24,20},{28,0},{1,29},{... | collective-permute-start | bytes 196616 | tf_op jit(solution)/shard_map/ppermute | solution.py:226
  16.2 3.9 %collective-permute-start.8 = (f32[64,128]{1,0:T(8,128)S(1)}, f32[64,128]{1,0:T(8,128)S(1)}, u32[]{:S(2)}, u32[]{:S(2)}) collective-permute-start(f32[64,128]{1,0:T(8,128)S(1)} %get-tuple-element.86), channel_id=1, source_target_pairs={{0,2},{1,3},{2,0},{3,1},{4,6},{5,7},{6,4},{7,5},{8,10},{9,11},{10,... | collective-permute-start | bytes 98312 | tf_op jit(solution)/shard_map/ppermute | solution.py:228
  16.8 3.9 %collective-permute-start.9 = (f32[64,128]{1,0:T(8,128)S(1)}, f32[64,128]{1,0:T(8,128)S(1)}, u32[]{:S(2)}, u32[]{:S(2)}) collective-permute-start(f32[64,128]{1,0:T(8,128)S(1)} %get-tuple-element.87), channel_id=1, source_target_pairs={{0,1},{1,0},{2,3},{3,2},{4,5},{5,4},{6,7},{7,6},{8,9},{9,8},{10,11... | collective-permute-start | bytes 98312 | tf_op jit(solution)/shard_map/ppermute | solution.py:228
  18.3 2.4 %collective-permute-start.10 = (f32[64,128]{1,0:T(8,128)S(1)}, f32[64,128]{1,0:T(8,128)S(1)}, u32[]{:S(2)}, u32[]{:S(2)}) collective-permute-start(f32[64,128]{1,0:T(8,128)S(1)} %get-tuple-element.88), channel_id=1, source_target_pairs={{0,4},{4,0},{8,12},{12,8},{16,20},{20,16},{24,28},{28,24},{1,5},{5... | collective-permute-start | bytes 98312 | tf_op jit(solution)/shard_map/ppermute | solution.py:229
  19.0 1.7 %collective-permute-start.11 = (f32[64,128]{1,0:T(8,128)S(1)}, f32[64,128]{1,0:T(8,128)S(1)}, u32[]{:S(2)}, u32[]{:S(2)}) collective-permute-start(f32[64,128]{1,0:T(8,128)S(1)} %get-tuple-element.89), channel_id=1, source_target_pairs={{0,4},{4,0},{8,12},{12,8},{16,20},{20,16},{24,28},{28,24},{1,5},{5... | collective-permute-start | bytes 98312 | tf_op jit(solution)/shard_map/ppermute | solution.py:229
  21.3 4.9 %collective-permute-start.13 = (f32[64,128]{1,0:T(8,128)S(1)}, f32[64,128]{1,0:T(8,128)S(1)}, u32[]{:S(2)}, u32[]{:S(2)}) collective-permute-start(f32[64,128]{1,0:T(8,128)S(1)} %get-tuple-element.92), channel_id=1, source_target_pairs={{0,3},{1,2},{2,1},{3,0},{4,7},{5,6},{6,5},{7,4},{8,11},{9,10},{10,... | collective-permute-start | bytes 98312 | tf_op jit(solution)/shard_map/ppermute | solution.py:228
  22.8 6.2 %collective-permute-start.12 = (f32[128,128]{1,0:T(8,128)S(1)}, f32[128,128]{1,0:T(8,128)S(1)}, u32[]{:S(2)}, u32[]{:S(2)}) collective-permute-start(f32[128,128]{1,0:T(8,128)S(1)} %get-tuple-element.91), channel_id=1, source_target_pairs={{0,28},{4,8},{8,4},{12,16},{16,12},{20,24},{24,20},{28,0},{1,29},{... | collective-permute-start | bytes 196616 | tf_op jit(solution)/shard_map/ppermute | solution.py:226
  24.6 3.9 %collective-permute-start.14 = (f32[64,128]{1,0:T(8,128)S(1)}, f32[64,128]{1,0:T(8,128)S(1)}, u32[]{:S(2)}, u32[]{:S(2)}) collective-permute-start(f32[64,128]{1,0:T(8,128)S(1)} %get-tuple-element.93), channel_id=1, source_target_pairs={{0,2},{1,3},{2,0},{3,1},{4,6},{5,7},{6,4},{7,5},{8,10},{9,11},{10,... | collective-permute-start | bytes 98312 | tf_op jit(solution)/shard_map/ppermute | solution.py:228
  25.1 3.9 %collective-permute-start.15 = (f32[64,128]{1,0:T(8,128)S(1)}, f32[64,128]{1,0:T(8,128)S(1)}, u32[]{:S(2)}, u32[]{:S(2)}) collective-permute-start(f32[64,128]{1,0:T(8,128)S(1)} %get-tuple-element.94), channel_id=1, source_target_pairs={{0,1},{1,0},{2,3},{3,2},{4,5},{5,4},{6,7},{7,6},{8,9},{9,8},{10,11... | collective-permute-start | bytes 98312 | tf_op jit(solution)/shard_map/ppermute | solution.py:228
  25.7 3.4 %collective-permute-start.16 = (f32[64,128]{1,0:T(8,128)S(1)}, f32[64,128]{1,0:T(8,128)S(1)}, u32[]{:S(2)}, u32[]{:S(2)}) collective-permute-start(f32[64,128]{1,0:T(8,128)S(1)} %get-tuple-element.95), channel_id=1, source_target_pairs={{0,4},{4,0},{8,12},{12,8},{16,20},{20,16},{24,28},{28,24},{1,5},{5... | collective-permute-start | bytes 98312 | tf_op jit(solution)/shard_map/ppermute | solution.py:229
  26.2 2.9 %collective-permute-start.17 = (f32[64,128]{1,0:T(8,128)S(1)}, f32[64,128]{1,0:T(8,128)S(1)}, u32[]{:S(2)}, u32[]{:S(2)}) collective-permute-start(f32[64,128]{1,0:T(8,128)S(1)} %get-tuple-element.96), channel_id=1, source_target_pairs={{0,4},{4,0},{8,12},{12,8},{16,20},{20,16},{24,28},{28,24},{1,5},{5... | collective-permute-start | bytes 98312 | tf_op jit(solution)/shard_map/ppermute | solution.py:229
  29.4 4.9 %collective-permute-start.19 = (f32[64,128]{1,0:T(8,128)S(1)}, f32[64,128]{1,0:T(8,128)S(1)}, u32[]{:S(2)}, u32[]{:S(2)}) collective-permute-start(f32[64,128]{1,0:T(8,128)S(1)} %get-tuple-element.99), channel_id=1, source_target_pairs={{0,3},{1,2},{2,1},{3,0},{4,7},{5,6},{6,5},{7,4},{8,11},{9,10},{10,... | collective-permute-start | bytes 98312 | tf_op jit(solution)/shard_map/ppermute | solution.py:228
  30.9 5.5 %collective-permute-start.18 = (f32[128,128]{1,0:T(8,128)S(1)}, f32[128,128]{1,0:T(8,128)S(1)}, u32[]{:S(2)}, u32[]{:S(2)}) collective-permute-start(f32[128,128]{1,0:T(8,128)S(1)} %get-tuple-element.98), channel_id=1, source_target_pairs={{0,28},{4,8},{8,4},{12,16},{16,12},{20,24},{24,20},{28,0},{1,29},{... | collective-permute-start | bytes 196616 | tf_op jit(solution)/shard_map/ppermute | solution.py:226
  31.6 3.9 %collective-permute-start.20 = (f32[64,128]{1,0:T(8,128)S(1)}, f32[64,128]{1,0:T(8,128)S(1)}, u32[]{:S(2)}, u32[]{:S(2)}) collective-permute-start(f32[64,128]{1,0:T(8,128)S(1)} %get-tuple-element.100), channel_id=1, source_target_pairs={{0,2},{1,3},{2,0},{3,1},{4,6},{5,7},{6,4},{7,5},{8,10},{9,11},{10,... | collective-permute-start | bytes 98312 | tf_op jit(solution)/shard_map/ppermute | solution.py:228
  32.5 3.9 %collective-permute-start.21 = (f32[64,128]{1,0:T(8,128)S(1)}, f32[64,128]{1,0:T(8,128)S(1)}, u32[]{:S(2)}, u32[]{:S(2)}) collective-permute-start(f32[64,128]{1,0:T(8,128)S(1)} %get-tuple-element.101), channel_id=1, source_target_pairs={{0,1},{1,0},{2,3},{3,2},{4,5},{5,4},{6,7},{7,6},{8,9},{9,8},{10,11... | collective-permute-start | bytes 98312 | tf_op jit(solution)/shard_map/ppermute | solution.py:228
  34.0 2.4 %collective-permute-start.22 = (f32[64,128]{1,0:T(8,128)S(1)}, f32[64,128]{1,0:T(8,128)S(1)}, u32[]{:S(2)}, u32[]{:S(2)}) collective-permute-start(f32[64,128]{1,0:T(8,128)S(1)} %get-tuple-element.102), channel_id=1, source_target_pairs={{0,4},{4,0},{8,12},{12,8},{16,20},{20,16},{24,28},{28,24},{1,5},{5... | collective-permute-start | bytes 98312 | tf_op jit(solution)/shard_map/ppermute | solution.py:229
  34.2 2.1 %collective-permute-start.23 = (f32[64,128]{1,0:T(8,128)S(1)}, f32[64,128]{1,0:T(8,128)S(1)}, u32[]{:S(2)}, u32[]{:S(2)}) collective-permute-start(f32[64,128]{1,0:T(8,128)S(1)} %get-tuple-element.103), channel_id=1, source_target_pairs={{0,4},{4,0},{8,12},{12,8},{16,20},{20,16},{24,28},{28,24},{1,5},{5... | collective-permute-start | bytes 98312 | tf_op jit(solution)/shard_map/ppermute | solution.py:229
  36.7 4.9 %collective-permute-start.25 = (f32[64,128]{1,0:T(8,128)S(1)}, f32[64,128]{1,0:T(8,128)S(1)}, u32[]{:S(2)}, u32[]{:S(2)}) collective-permute-start(f32[64,128]{1,0:T(8,128)S(1)} %get-tuple-element.107), channel_id=1, source_target_pairs={{0,3},{1,2},{2,1},{3,0},{4,7},{5,6},{6,5},{7,4},{8,11},{9,10},{10,... | collective-permute-start | bytes 98312 | tf_op jit(solution)/shard_map/ppermute | solution.py:228
  38.2 6.2 %collective-permute-start.24 = (f32[128,128]{1,0:T(8,128)S(1)}, f32[128,128]{1,0:T(8,128)S(1)}, u32[]{:S(2)}, u32[]{:S(2)}) collective-permute-start(f32[128,128]{1,0:T(8,128)S(1)} %get-tuple-element.106), channel_id=1, source_target_pairs={{0,28},{4,8},{8,4},{12,16},{16,12},{20,24},{24,20},{28,0},{1,29},{... | collective-permute-start | bytes 196616 | tf_op jit(solution)/shard_map/ppermute | solution.py:226
  40.0 3.9 %collective-permute-start.26 = (f32[64,128]{1,0:T(8,128)S(1)}, f32[64,128]{1,0:T(8,128)S(1)}, u32[]{:S(2)}, u32[]{:S(2)}) collective-permute-start(f32[64,128]{1,0:T(8,128)S(1)} %get-tuple-element.108), channel_id=1, source_target_pairs={{0,2},{1,3},{2,0},{3,1},{4,6},{5,7},{6,4},{7,5},{8,10},{9,11},{10,... | collective-permute-start | bytes 98312 | tf_op jit(solution)/shard_map/ppermute | solution.py:228
  40.5 3.9 %collective-permute-start.27 = (f32[64,128]{1,0:T(8,128)S(1)}, f32[64,128]{1,0:T(8,128)S(1)}, u32[]{:S(2)}, u32[]{:S(2)}) collective-permute-start(f32[64,128]{1,0:T(8,128)S(1)} %get-tuple-element.109), channel_id=1, source_target_pairs={{0,1},{1,0},{2,3},{3,2},{4,5},{5,4},{6,7},{7,6},{8,9},{9,8},{10,11... | collective-permute-start | bytes 98312 | tf_op jit(solution)/shard_map/ppermute | solution.py:228
  41.1 3.4 %collective-permute-start.28 = (f32[64,128]{1,0:T(8,128)S(1)}, f32[64,128]{1,0:T(8,128)S(1)}, u32[]{:S(2)}, u32[]{:S(2)}) collective-permute-start(f32[64,128]{1,0:T(8,128)S(1)} %get-tuple-element.110), channel_id=1, source_target_pairs={{0,4},{4,0},{8,12},{12,8},{16,20},{20,16},{24,28},{28,24},{1,5},{5... | collective-permute-start | bytes 98312 | tf_op jit(solution)/shard_map/ppermute | solution.py:229
  41.6 2.9 %collective-permute-start.29 = (f32[64,128]{1,0:T(8,128)S(1)}, f32[64,128]{1,0:T(8,128)S(1)}, u32[]{:S(2)}, u32[]{:S(2)}) collective-permute-start(f32[64,128]{1,0:T(8,128)S(1)} %get-tuple-element.111), channel_id=1, source_target_pairs={{0,4},{4,0},{8,12},{12,8},{16,20},{20,16},{24,28},{28,24},{1,5},{5... | collective-permute-start | bytes 98312 | tf_op jit(solution)/shard_map/ppermute | solution.py:229
  44.8 5.0 %collective-permute-start.31 = (f32[64,128]{1,0:T(8,128)S(1)}, f32[64,128]{1,0:T(8,128)S(1)}, u32[]{:S(2)}, u32[]{:S(2)}) collective-permute-start(f32[64,128]{1,0:T(8,128)S(1)} %get-tuple-element.115), channel_id=1, source_target_pairs={{0,3},{1,2},{2,1},{3,0},{4,7},{5,6},{6,5},{7,4},{8,11},{9,10},{10,... | collective-permute-start | bytes 98312 | tf_op jit(solution)/shard_map/ppermute | solution.py:228
  46.3 5.5 %collective-permute-start.30 = (f32[128,128]{1,0:T(8,128)S(1)}, f32[128,128]{1,0:T(8,128)S(1)}, u32[]{:S(2)}, u32[]{:S(2)}) collective-permute-start(f32[128,128]{1,0:T(8,128)S(1)} %get-tuple-element.114), channel_id=1, source_target_pairs={{0,28},{4,8},{8,4},{12,16},{16,12},{20,24},{24,20},{28,0},{1,29},{... | collective-permute-start | bytes 196616 | tf_op jit(solution)/shard_map/ppermute | solution.py:226
  47.1 3.9 %collective-permute-start.32 = (f32[64,128]{1,0:T(8,128)S(1)}, f32[64,128]{1,0:T(8,128)S(1)}, u32[]{:S(2)}, u32[]{:S(2)}) collective-permute-start(f32[64,128]{1,0:T(8,128)S(1)} %get-tuple-element.116), channel_id=1, source_target_pairs={{0,2},{1,3},{2,0},{3,1},{4,6},{5,7},{6,4},{7,5},{8,10},{9,11},{10,... | collective-permute-start | bytes 98312 | tf_op jit(solution)/shard_map/ppermute | solution.py:228
  47.9 3.9 %collective-permute-start.33 = (f32[64,128]{1,0:T(8,128)S(1)}, f32[64,128]{1,0:T(8,128)S(1)}, u32[]{:S(2)}, u32[]{:S(2)}) collective-permute-start(f32[64,128]{1,0:T(8,128)S(1)} %get-tuple-element.117), channel_id=1, source_target_pairs={{0,1},{1,0},{2,3},{3,2},{4,5},{5,4},{6,7},{7,6},{8,9},{9,8},{10,11... | collective-permute-start | bytes 98312 | tf_op jit(solution)/shard_map/ppermute | solution.py:228
  49.4 2.4 %collective-permute-start.34 = (f32[64,128]{1,0:T(8,128)S(1)}, f32[64,128]{1,0:T(8,128)S(1)}, u32[]{:S(2)}, u32[]{:S(2)}) collective-permute-start(f32[64,128]{1,0:T(8,128)S(1)} %get-tuple-element.118), channel_id=1, source_target_pairs={{0,4},{4,0},{8,12},{12,8},{16,20},{20,16},{24,28},{28,24},{1,5},{5... | collective-permute-start | bytes 98312 | tf_op jit(solution)/shard_map/ppermute | solution.py:229
  49.7 2.1 %collective-permute-start.35 = (f32[64,128]{1,0:T(8,128)S(1)}, f32[64,128]{1,0:T(8,128)S(1)}, u32[]{:S(2)}, u32[]{:S(2)}) collective-permute-start(f32[64,128]{1,0:T(8,128)S(1)} %get-tuple-element.119), channel_id=1, source_target_pairs={{0,4},{4,0},{8,12},{12,8},{16,20},{20,16},{24,28},{28,24},{1,5},{5... | collective-permute-start | bytes 98312 | tf_op jit(solution)/shard_map/ppermute | solution.py:229
  52.1 4.9 %collective-permute-start.37 = (f32[64,128]{1,0:T(8,128)S(1)}, f32[64,128]{1,0:T(8,128)S(1)}, u32[]{:S(2)}, u32[]{:S(2)}) collective-permute-start(f32[64,128]{1,0:T(8,128)S(1)} %get-tuple-element.123), channel_id=1, source_target_pairs={{0,3},{1,2},{2,1},{3,0},{4,7},{5,6},{6,5},{7,4},{8,11},{9,10},{10,... | collective-permute-start | bytes 98312 | tf_op jit(solution)/shard_map/ppermute | solution.py:228
  53.6 6.2 %collective-permute-start.36 = (f32[128,128]{1,0:T(8,128)S(1)}, f32[128,128]{1,0:T(8,128)S(1)}, u32[]{:S(2)}, u32[]{:S(2)}) collective-permute-start(f32[128,128]{1,0:T(8,128)S(1)} %get-tuple-element.122), channel_id=1, source_target_pairs={{0,28},{4,8},{8,4},{12,16},{16,12},{20,24},{24,20},{28,0},{1,29},{... | collective-permute-start | bytes 196616 | tf_op jit(solution)/shard_map/ppermute | solution.py:226
  55.4 3.9 %collective-permute-start.38 = (f32[64,128]{1,0:T(8,128)S(1)}, f32[64,128]{1,0:T(8,128)S(1)}, u32[]{:S(2)}, u32[]{:S(2)}) collective-permute-start(f32[64,128]{1,0:T(8,128)S(1)} %get-tuple-element.124), channel_id=1, source_target_pairs={{0,2},{1,3},{2,0},{3,1},{4,6},{5,7},{6,4},{7,5},{8,10},{9,11},{10,... | collective-permute-start | bytes 98312 | tf_op jit(solution)/shard_map/ppermute | solution.py:228
  55.9 3.9 %collective-permute-start.39 = (f32[64,128]{1,0:T(8,128)S(1)}, f32[64,128]{1,0:T(8,128)S(1)}, u32[]{:S(2)}, u32[]{:S(2)}) collective-permute-start(f32[64,128]{1,0:T(8,128)S(1)} %get-tuple-element.125), channel_id=1, source_target_pairs={{0,1},{1,0},{2,3},{3,2},{4,5},{5,4},{6,7},{7,6},{8,9},{9,8},{10,11... | collective-permute-start | bytes 98312 | tf_op jit(solution)/shard_map/ppermute | solution.py:228
  56.5 3.4 %collective-permute-start.40 = (f32[64,128]{1,0:T(8,128)S(1)}, f32[64,128]{1,0:T(8,128)S(1)}, u32[]{:S(2)}, u32[]{:S(2)}) collective-permute-start(f32[64,128]{1,0:T(8,128)S(1)} %get-tuple-element.126), channel_id=1, source_target_pairs={{0,4},{4,0},{8,12},{12,8},{16,20},{20,16},{24,28},{28,24},{1,5},{5... | collective-permute-start | bytes 98312 | tf_op jit(solution)/shard_map/ppermute | solution.py:229
  57.0 2.9 %collective-permute-start.41 = (f32[64,128]{1,0:T(8,128)S(1)}, f32[64,128]{1,0:T(8,128)S(1)}, u32[]{:S(2)}, u32[]{:S(2)}) collective-permute-start(f32[64,128]{1,0:T(8,128)S(1)} %get-tuple-element.127), channel_id=1, source_target_pairs={{0,4},{4,0},{8,12},{12,8},{16,20},{20,16},{24,28},{28,24},{1,5},{5... | collective-permute-start | bytes 98312 | tf_op jit(solution)/shard_map/ppermute | solution.py:229
  60.2 4.9 %collective-permute-start.43 = (f32[64,128]{1,0:T(8,128)S(1)}, f32[64,128]{1,0:T(8,128)S(1)}, u32[]{:S(2)}, u32[]{:S(2)}) collective-permute-start(f32[64,128]{1,0:T(8,128)S(1)} %get-tuple-element.137), channel_id=1, source_target_pairs={{0,3},{1,2},{2,1},{3,0},{4,7},{5,6},{6,5},{7,4},{8,11},{9,10},{10,... | collective-permute-start | bytes 98312 | tf_op jit(solution)/shard_map/ppermute | solution.py:228
  61.7 5.5 %collective-permute-start.42 = (f32[128,128]{1,0:T(8,128)S(1)}, f32[128,128]{1,0:T(8,128)S(1)}, u32[]{:S(2)}, u32[]{:S(2)}) collective-permute-start(f32[128,128]{1,0:T(8,128)S(1)} %get-tuple-element.136), channel_id=1, source_target_pairs={{0,28},{4,8},{8,4},{12,16},{16,12},{20,24},{24,20},{28,0},{1,29},{... | collective-permute-start | bytes 196616 | tf_op jit(solution)/shard_map/ppermute | solution.py:226
  62.5 3.9 %collective-permute-start.44 = (f32[64,128]{1,0:T(8,128)S(1)}, f32[64,128]{1,0:T(8,128)S(1)}, u32[]{:S(2)}, u32[]{:S(2)}) collective-permute-start(f32[64,128]{1,0:T(8,128)S(1)} %get-tuple-element.138), channel_id=1, source_target_pairs={{0,2},{1,3},{2,0},{3,1},{4,6},{5,7},{6,4},{7,5},{8,10},{9,11},{10,... | collective-permute-start | bytes 98312 | tf_op jit(solution)/shard_map/ppermute | solution.py:228
  63.3 3.9 %collective-permute-start.45 = (f32[64,128]{1,0:T(8,128)S(1)}, f32[64,128]{1,0:T(8,128)S(1)}, u32[]{:S(2)}, u32[]{:S(2)}) collective-permute-start(f32[64,128]{1,0:T(8,128)S(1)} %get-tuple-element.139), channel_id=1, source_target_pairs={{0,1},{1,0},{2,3},{3,2},{4,5},{5,4},{6,7},{7,6},{8,9},{9,8},{10,11... | collective-permute-start | bytes 98312 | tf_op jit(solution)/shard_map/ppermute | solution.py:228
  64.8 2.4 %collective-permute-start.46 = (f32[64,128]{1,0:T(8,128)S(1)}, f32[64,128]{1,0:T(8,128)S(1)}, u32[]{:S(2)}, u32[]{:S(2)}) collective-permute-start(f32[64,128]{1,0:T(8,128)S(1)} %get-tuple-element.140), channel_id=1, source_target_pairs={{0,4},{4,0},{8,12},{12,8},{16,20},{20,16},{24,28},{28,24},{1,5},{5... | collective-permute-start | bytes 98312 | tf_op jit(solution)/shard_map/ppermute | solution.py:229
  65.1 2.1 %collective-permute-start.47 = (f32[64,128]{1,0:T(8,128)S(1)}, f32[64,128]{1,0:T(8,128)S(1)}, u32[]{:S(2)}, u32[]{:S(2)}) collective-permute-start(f32[64,128]{1,0:T(8,128)S(1)} %get-tuple-element.141), channel_id=1, source_target_pairs={{0,4},{4,0},{8,12},{12,8},{16,20},{20,16},{24,28},{28,24},{1,5},{5... | collective-permute-start | bytes 98312 | tf_op jit(solution)/shard_map/ppermute | solution.py:229
